TPU v7x, 32 devices: a whole 2x2x4 slice. The times are simulated.
32 devices in a mesh: batch: 4 (over y, x), expert: 8 (over z, core).
Axes of the slice: x: 2, y: 2, z: 4, core: 2. Of those that a mesh axis runs over, the one named last changes fastest.
Arguments:
- tokens: bfloat16 [256, 4096], P(('batch', 'expert')), may hold values from -6 to 6
- expert_ids: int32 [256, 8], P(('batch', 'expert')), may hold values from 0 to 15, all different within a row; in each aligned block of 8 rows (0 to 7, 8 to 15, ...) at most 8 rows name the same one
- route_weights: float32 [256, 8], P(('batch', 'expert')), may hold values from 0.1 to 1
- in_weights: bfloat16 [16, 1536, 2, 4096], P('expert', 'batch'), may hold values from -0.09375 to 0.09375
- out_weights: bfloat16 [16, 1536, 4096], P('expert', 'batch'), may hold values from -0.15625 to 0.15625
Outputs:
- combined: bfloat16 [256, 4096], P(('batch', 'expert'))
Inputs may be any that keep to these rules, and one draw needn't show every extreme that they name: `expert_ids`: each row names 8 different experts. Among the 8 rows of one device no expert is named more than 8 times, a bound that some block reaches.
All inputs are finite; a program needn't handle non-finite values.
Results may differ from a plain program's by a relative error of at most 0.0057.
Values may be sent and summed in bfloat16 or wider, within the bound.
No kernel may reach another device: no remote copies, remote signals or barrier semaphores. Data moves between devices by JAX's collectives and lax.ppermute only.
A program may use at most 192 MiB of HBM per device.

v0:
```python
import jax
import jax.numpy as jnp
from jax import lax
from jax.sharding import PartitionSpec as P


def expand(row_block, weight_piece):
    mixed = jnp.einsum(
        "red,efcd->recf", row_block, weight_piece, preferred_element_type=jnp.float32
    )
    return (jax.nn.silu(mixed[:, :, 0]) * mixed[:, :, 1]).astype(jnp.bfloat16)


def shrink(hidden, weight_piece):
    return jnp.einsum("ref,efd->red", hidden, weight_piece, preferred_element_type=jnp.float32)


def body(tokens, expert_ids, route_weights, in_weights, out_weights):
    tok_dev, model_width = tokens.shape
    top_count = expert_ids.shape[1]
    exp_dev = in_weights.shape[0]
    groups = lax.axis_size("expert")
    experts = exp_dev * groups
    slot_most = 2 * tok_dev * top_count // experts
    slot_total = groups * slot_most * exp_dev
    pair_count = tok_dev * top_count
    flat_ids = expert_ids.reshape(-1)
    onehot = (flat_ids[:, None] == jnp.arange(experts, dtype=jnp.int32)[None, :]).astype(jnp.int32)
    slot_rank = jnp.sum((jnp.cumsum(onehot, axis=0) - onehot) * onehot, axis=1)
    owner_dev = flat_ids // exp_dev
    local_expert = flat_ids % exp_dev
    slot_index = (owner_dev * slot_most + slot_rank) * exp_dev + local_expert
    placed = (slot_index[:, None] == jnp.arange(slot_total, dtype=jnp.int32)[None, :]).astype(
        jnp.bfloat16
    )
    token_of = jnp.arange(pair_count, dtype=jnp.int32) // top_count
    token_hot = (token_of[:, None] == jnp.arange(tok_dev, dtype=jnp.int32)[None, :]).astype(
        jnp.bfloat16
    )
    dispatch_map = jnp.dot(placed.T, token_hot, preferred_element_type=jnp.float32).astype(
        jnp.bfloat16
    )
    outgoing = jnp.dot(dispatch_map, tokens, preferred_element_type=jnp.float32).astype(
        jnp.bfloat16
    )
    outgoing = outgoing.reshape(groups * slot_most, exp_dev, model_width)
    arrived = lax.all_to_all(outgoing, "expert", split_axis=0, concat_axis=0, tiled=True)
    every_row = lax.all_gather(arrived, "batch", axis=0, tiled=True)
    produced = lax.psum_scatter(
        shrink(expand(every_row, in_weights), out_weights), "batch", scatter_dimension=0, tiled=True
    )
    results = produced.astype(jnp.bfloat16)
    returned_rows = lax.all_to_all(results, "expert", split_axis=0, concat_axis=0, tiled=True)
    returned_rows = returned_rows.reshape(slot_total, model_width)
    picked = returned_rows[slot_index].reshape(tok_dev, top_count, model_width)
    combined = jnp.sum(route_weights[:, :, None] * picked.astype(jnp.float32), axis=1)
    return combined.astype(jnp.bfloat16)


def solution(mesh):
    return jax.shard_map(
        body,
        mesh=mesh,
        in_specs=(
            P(("batch", "expert"), None),
            P(("batch", "expert"), None),
            P(("batch", "expert"), None),
            P("expert", "batch", None, None),
            P("expert", "batch", None),
        ),
        out_specs=P(("batch", "expert"), None),
        check_vma=False,
    )
```

profile of v0, /device:TPU:0, one launch (start us, length us, event | category | flops | bytes accessed | tf_op | source)
XLA Modules:
  0.0 255.9 jit_solution(11157953728648017484)
XLA Ops:
  6.5 0.0 copy-start
  6.5 0.0 all-gather.2.cloned.1.call-start
  6.5 0.8 reshape.166
  7.3 0.1 fusion.13
  7.4 0.1 reduce_window_sum.11
  7.5 0.2 select_reduce_fusion
  7.7 0.0 copy-done
  7.7 0.7 convolution_convert_fusion
  8.5 0.7 reshape.167
  9.2 32.7 %all_to_all.10 = bf16[64,2,4096]{2,1,0:T(2,128)(2,1)S(1)} all-to-all(bf16[64,2,4096]{2,1,0:T(2,128)(2,1)S(1)} %reshape.167), channel_id=1, replica_groups=mesh['batch'=4,'expert'=8] {'expert'}, dimensions={0} | all-to-all | bytes 2097152 | tf_op jit(solution)/shard_map/all_to_all | solution.py:47
  41.9 1.6 copy.13
  43.4 0.0 all-gather.2.cloned.1.call-update
  43.5 0.0 reduce-scatter.2.cloned.1.call-start
  43.5 51.7 %all-gather.2.cloned.1.call-done = bf16[256,2,4096]{2,0,1:T(8,128)(2,1)} async-done(((bf16[64,2,4096]{2,0,1:T(8,128)(2,1)}), bf16[256,2,4096]{2,0,1:T(8,128)(2,1)}) %all-gather.2.cloned.1.call-update) | async-done | bytes 4194320 | tf_op jit(solution)/shard_map/all_gather | solution.py:48
  95.2 21.4 %fusion.3 = f32[256,2,2,384]{3,0,2,1:T(8,128)S(1)} fusion(bf16[2,384,2,4096]{3,2,1,0:T(2,128)(2,1)} %param.8, bf16[256,2,4096]{2,0,1:T(8,128)(2,1)} %all-gather.2.cloned.1.call-done), kind=kOutput, calls=%fused_computation.6 | convolution fusion | flops 3221225472 | bytes 18350080 | tf_op jit(solution)/shard_map/red,efcd->recf/dot_general | solution.py:8
  116.6 8.4 %convolution_bitcast_fusion = f32[256,2,4096]{2,0,1:T(8,128)} fusion(bf16[2,384,4096]{2,1,0:T(8,128)(2,1)} %param.9, f32[256,2,2,384]{3,0,2,1:T(8,128)S(1)} %fusion.3), kind=kOutput, calls=%fused_computation.3 | convolution fusion | flops 1611792384 | bytes 16252928 | tf_op jit(solution)/shard_map/ref,efd->red/dot_general | solution.py:15
  125.0 0.0 copy-start.1
  125.0 0.0 reduce-scatter.2.cloned.1.call-update
  125.1 86.6 %reduce-scatter.2.cloned.1.call-done = f32[64,2,4096]{2,0,1:T(8,128)} async-done(((f32[256,2,4096]{2,0,1:T(8,128)}), f32[64,2,4096]{2,0,1:T(8,128)}) %reduce-scatter.2.cloned.1.call-update) | async-done | bytes 2097168 | tf_op jit(solution)/shard_map/reduce_scatter | solution.py:49
  211.6 1.7 convert_element_type.30
  213.4 0.0 copy-start.2
  213.4 2.1 copy.16
  215.5 4.6 %all-to-all-start.1 = ((bf16[64,2,4096]{2,1,0:T(2,128)(2,1)}), bf16[64,2,4096]{2,1,0:T(2,128)(2,1)S(1)}, u32[]{:S(2)}, u32[]{:S(2)}) async-start(bf16[64,2,4096]{2,1,0:T(2,128)(2,1)} %copy.16), calls=%async_computation.2 | async-start | bytes 2097152 | tf_op jit(solution)/shard_map/all_to_all | solution.py:53
  220.1 0.0 copy-done.1
  220.1 0.1 reshape.169
  220.2 26.5 %all-to-all-done.1 = bf16[64,2,4096]{2,1,0:T(2,128)(2,1)S(1)} async-done(((bf16[64,2,4096]{2,1,0:T(2,128)(2,1)}), bf16[64,2,4096]{2,1,0:T(2,128)(2,1)S(1)}, u32[]{:S(2)}, u32[]{:S(2)}) %all-to-all-start.1) | async-done | bytes 1048608 | tf_op jit(solution)/shard_map/all_to_all | solution.py:53
  246.7 0.4 reshape.168
  247.1 0.9 gather_fusion
  248.0 0.0 copy-done.2
  248.0 1.1 fusion.8
  (3 shorter events, 0.0 us)
Async XLA Ops:
  6.5 1.2 copy-start
  6.5 88.7 %all-gather.2.cloned.1.call-start = ((), (), s32[]{:S(2)}) async-start(), calls=%async_computation.3 | async-start | bytes 5242880 | tf_op jit(solution)/shard_map/all_gather | solution.py:48
  43.5 168.2 %reduce-scatter.2.cloned.1.call-start = ((), (), s32[]{:S(2)}) async-start(), calls=%async_computation.4 | async-start | bytes 10485760 | tf_op jit(solution)/shard_map/reduce_scatter | solution.py:49
  125.0 95.0 %copy-start.1 = (s32[8,8]{1,0:T(8,128)S(1)}, s32[8,8]{1,0:T(8,128)}, u32[]{:S(2)}) copy-start(s32[8,8]{1,0:T(8,128)} %param.6) | copy-start | bytes 772
  213.4 34.6 %copy-start.2 = (f32[8,8]{1,0:T(8,128)S(1)}, f32[8,8]{1,0:T(8,128)}, u32[]{:S(2)}) copy-start(f32[8,8]{1,0:T(8,128)} %param.7) | copy-start | bytes 772
  215.5 31.2 %all-to-all-start.1 = ((bf16[64,2,4096]{2,1,0:T(2,128)(2,1)}), bf16[64,2,4096]{2,1,0:T(2,128)(2,1)S(1)}, u32[]{:S(2)}, u32[]{:S(2)}) async-start(bf16[64,2,4096]{2,1,0:T(2,128)(2,1)} %copy.16), calls=%async_computation.2 | async-start | bytes 2097152 | tf_op jit(solution)/shard_map/all_to_all | solution.py:53
Sparse Core Ops, SparseCore 0:
  43.6 51.6 all-gather.1
  125.2 86.4 reduce-scatter.1
where the time goes:
time: 256 us
  waiting for transfers between devices  165 us (64%)
  blocking collectives  32.7 us (13%)
  matrix products  30.5 us (12%)
  between operations  13.5 us (5%)
  local copies, waits for them, and re-layouts  6.52 us (3%)
  starting transfers between devices  4.65 us (2%)
  other arithmetic  3.19 us (1%)
    reduce_scatter x1, waiting for transfers between devices, body(): lax.psum_scatter(shrink(expand(every_row, in_weights), out_weights), 'bat...  86.6 us
    all_gather x1, waiting for transfers between devices, body(): every_row = lax.all_gather(arrived, 'batch', axis=0, tiled=True)  51.7 us
    all_to_all x1, blocking collectives, body(): lax.all_to_all(outgoing, 'expert', split_axis=0, concat_axis=0, tiled=True)  32.7 us
    all_to_all x1, waiting for transfers between devices, body(): lax.all_to_all(results, 'expert', split_axis=0, concat_axis=0, tiled=True)  26.5 us
    dot_general x1, matrix products, expand(): jnp.einsum('red,efcd->recf', row_block, weight_piece, preferred_element_t...  21.4 us
    dot_general x1, matrix products, shrink(): jnp.einsum('ref,efd->red', hidden, weight_piece, preferred_element_type=j...  8.4 us
  transfers between devices with their start and end apart: 3, of which 3 were waited for; matrix products, arithmetic and copies ran while one was open for 0% of the time, Pallas kernels for 0%

commit v1 on v0

v1 whole, which is shorter than its diff:
```python
import functools

import jax
import jax.numpy as jnp
from jax import lax
from jax.experimental import pallas as pl
from jax.experimental.pallas import tpu as pltpu
from jax.sharding import PartitionSpec as P

LANES = 128
MIB = 1 << 20


def swap(block, axis, flips):
    size = lax.axis_size(axis)
    return lax.ppermute(block, axis, [(i, i ^ flips) for i in range(size)])


def gather_over(block, axis, steps):
    return jnp.concatenate([block] + [swap(block, axis, step) for step in steps], axis=0)


def packed_weights(expert_ids, route_weights, experts, width):
    onehot = expert_ids[:, :, None] == jnp.arange(experts, dtype=jnp.int32)
    dense = jnp.sum(jnp.where(onehot, route_weights[:, :, None], 0.0), axis=1)
    parts = []
    for _ in range(3):
        part = dense.astype(jnp.bfloat16)
        parts.append(part)
        dense = dense - part.astype(jnp.float32)
    packed = jnp.concatenate(parts, axis=1)
    return jnp.pad(packed, ((0, 0), (0, width - packed.shape[1])))


def load_kernel(in_ref, out_ref, in_vmem, out_vmem, sems):
    tiles = in_vmem.shape[0]
    copies = []
    for t in range(tiles):
        copies.append(
            pltpu.make_async_copy(
                in_ref.at[:, :, pl.ds(t * LANES, LANES)], in_vmem.at[t], sems.at[t]
            )
        )
    copies.append(pltpu.make_async_copy(out_ref, out_vmem, sems.at[tiles]))
    for copy in copies:
        copy.start()
    for copy in copies:
        copy.wait()


def load_weights(w_in, w_out):
    units, _, width = w_in.shape
    tiles = width // LANES
    return pl.pallas_call(
        load_kernel,
        out_shape=(
            pltpu.VMEM((tiles, units, 2, LANES), w_in.dtype),
            pltpu.VMEM(w_out.shape, w_out.dtype),
        ),
        in_specs=[pl.BlockSpec(memory_space=pltpu.HBM)] * 2,
        out_specs=[pl.BlockSpec(memory_space=pltpu.VMEM)] * 2,
        scratch_shapes=[pltpu.SemaphoreType.DMA((tiles + 1,))],
        compiler_params=pltpu.CompilerParams(vmem_limit_bytes=2 * MIB),
        cost_estimate=pl.CostEstimate(
            flops=0, bytes_accessed=2 * (w_in.size + w_out.size), transcendentals=0
        ),
    )(*(pltpu.with_memory_space_constraint(w, pltpu.HBM) for w in (w_in, w_out)))


def expert_kernel(exp_dev, select_ref, x_ref, win_ref, wout_ref, send_ref, keep_ref, mixed, hidden):
    halves, half_rows, _ = x_ref.shape
    rows = halves * half_rows
    tiles, lines, _ = win_ref.shape
    width = tiles * LANES
    per = lines // exp_dev
    x = x_ref[:, :, :width].reshape(rows, width)
    tail = x_ref[:, :, width:].reshape(rows, x_ref.shape[2] - width)
    contract_last = (((1,), (1,)), ((), ()))
    scale = lax.dot_general(
        select_ref[...], tail, contract_last, preferred_element_type=jnp.float32
    )
    for e in range(exp_dev):
        w = jnp.concatenate([win_ref[t, pl.ds(e * per, per), :] for t in range(tiles)], axis=1)
        both = lax.dot_general(w, x, contract_last, preferred_element_type=jnp.float32)
        for r in range(0, rows, LANES):
            mixed[...] = both[:, r : r + LANES]
            gate = mixed[pl.ds(0, per // 2, stride=2), :]
            up = mixed[pl.ds(1, per // 2, stride=2), :]
            act = gate / (1.0 + jnp.exp(-gate)) * up * scale[e : e + 1, r : r + LANES]
            hidden[pl.ds(e * per // 2, per // 2), r : r + LANES] = act.astype(jnp.bfloat16)
    chunk = min(512, width)
    for c in range(0, width, chunk):
        part = lax.dot_general(
            hidden[...],
            wout_ref[:, c : c + chunk],
            (((0,), (0,)), ((), ())),
            preferred_element_type=jnp.float32,
        )
        keep_ref[:, c : c + chunk] = part[:half_rows]
        send_ref[:, c : c + chunk] = part[half_rows:].astype(jnp.bfloat16)


def run_experts(select, x, win, wout, exp_dev):
    halves, half_rows, packed_width = x.shape
    tiles, lines, _ = win.shape
    width = tiles * LANES
    block = min(half_rows, 128)
    return pl.pallas_call(
        functools.partial(expert_kernel, exp_dev),
        grid=(half_rows // block,),
        out_shape=(
            jax.ShapeDtypeStruct((half_rows, width), jnp.bfloat16),
            jax.ShapeDtypeStruct((half_rows, width), jnp.float32),
        ),
        in_specs=[
            pl.BlockSpec(select.shape, lambda i: (0, 0)),
            pl.BlockSpec((halves, block, packed_width), lambda i: (0, i, 0)),
            pl.BlockSpec(memory_space=pltpu.VMEM),
            pl.BlockSpec(memory_space=pltpu.VMEM),
        ],
        out_specs=[
            pl.BlockSpec((block, width), lambda i: (i, 0)),
            pl.BlockSpec((block, width), lambda i: (i, 0)),
        ],
        scratch_shapes=[
            pltpu.VMEM((lines // exp_dev, LANES), jnp.float32),
            pltpu.VMEM((lines // 2, halves * block), jnp.bfloat16),
        ],
        compiler_params=pltpu.CompilerParams(vmem_limit_bytes=16 * MIB),
        cost_estimate=pl.CostEstimate(
            flops=3 * halves * half_rows * width * lines,
            bytes_accessed=2 * x.size + 6 * half_rows * width,
            transcendentals=halves * half_rows * lines // 2,
        ),
    )(select, x, win, wout)


def body(tokens, expert_ids, route_weights, in_weights, out_weights):
    tok_dev, width = tokens.shape
    exp_dev, units = in_weights.shape[:2]
    groups = lax.axis_size("expert")
    planes = lax.axis_size("batch")
    chips = groups // 2
    experts = exp_dev * groups
    tail = -(-3 * experts // LANES) * LANES

    win, wout = load_weights(
        in_weights.reshape(exp_dev * units, 2, width), out_weights.reshape(exp_dev * units, width)
    )
    win = win.reshape(width // LANES, exp_dev * units * 2, LANES)

    packed = packed_weights(expert_ids, route_weights, experts, tail)
    x = jnp.concatenate([tokens, packed], axis=1)
    x = gather_over(x, "expert", [2 * i for i in range(1, chips)])
    x = gather_over(x, "batch", range(1, planes))
    half_rows = x.shape[0]
    x = gather_over(x, "expert", [1]).reshape(2, half_rows, width + tail)

    wanted = lax.axis_index("expert") * exp_dev + jnp.arange(exp_dev, dtype=jnp.int32)
    column = jnp.arange(tail, dtype=jnp.int32)
    select = (column[None, :] % experts == wanted[:, None]) & (column < 3 * experts)[None, :]
    select = jnp.pad(select.astype(jnp.bfloat16), ((0, -exp_dev % 16), (0, 0)))

    send, total = run_experts(select, x, win, wout, exp_dev)
    total = total + swap(send, "expert", 1).astype(jnp.float32)
    for axis, steps in (
        ("batch", list(range(1, planes))),
        ("expert", [2 * i for i in range(1, chips)]),
    ):
        size = total.shape[0] // (len(steps) + 1)
        pieces = [total[i * size : (i + 1) * size] for i in range(len(steps) + 1)]
        total = pieces[0]
        for i, step in enumerate(steps):
            total = total + swap(pieces[i + 1].astype(jnp.bfloat16), axis, step).astype(jnp.float32)
    return total.astype(jnp.bfloat16)


def solution(mesh):
    return jax.shard_map(
        body,
        mesh=mesh,
        in_specs=(
            P(("batch", "expert"), None),
            P(("batch", "expert"), None),
            P(("batch", "expert"), None),
            P("expert", "batch", None, None),
            P("expert", "batch", None),
        ),
        out_specs=P(("batch", "expert"), None),
        check_vma=False,
    )
```

time: 256 us -> 73.5 us (0.29)
  waiting for transfers between devices: 165 us -> 33.8 us
  blocking collectives: 32.7 us -> 0 us
  matrix products: 30.5 us -> 0 us
  between operations: 13.5 us -> 0.1 us
  starting transfers between devices: 4.65 us -> 17.8 us
  Pallas kernels: 0 us -> 12.7 us
    reduce_scatter x1 -> x0, waiting for transfers between devices: 86.6 us -> none  [body(): lax.psum_scatter(shrink(expand(every_row, in_weights), out_weights), 'bat...]
    all_gather x1 -> x0, waiting for transfers between devices: 51.7 us -> none  [body(): every_row = lax.all_gather(arrived, 'batch', axis=0, tiled=True)]
    ppermute x0 -> x14, waiting for transfers between devices: none -> 33.8 us  [swap(): return lax.ppermute(block, axis, [(i, i ^ flips) for i in range(size)])]
    all_to_all x1 -> x0, blocking collectives: 32.7 us -> none  [body(): lax.all_to_all(outgoing, 'expert', split_axis=0, concat_axis=0, tiled=True)]
    dot_general x3 -> x0, matrix products: 30.5 us -> none  [the longest x1 21.4 us: expand(): jnp.einsum('red,efcd->recf', row_block, weight_piece, preferred_element_t...]
    all_to_all x1 -> x0, waiting for transfers between devices: 26.5 us -> none  [body(): lax.all_to_all(results, 'expert', split_axis=0, concat_axis=0, tiled=True)]
    ppermute x0 -> x14, starting transfers between devices: none -> 17.8 us  [swap(): return lax.ppermute(block, axis, [(i, i ^ flips) for i in range(size)])]
    pallas_call x0 -> x2, Pallas kernels: none -> 12.7 us  [the longest x1 7.31 us: load_weights(): pl.pallas_call(load_kernel, out_shape=(pltpu.VMEM((tiles, units, 2, LANES...]
  transfers between devices with their start and end apart: 3 -> 14, of which waited for: 3 -> 10; matrix products, arithmetic and copies ran while one was open for 0% -> 5% of each run, Pallas kernels for 0% -> 10%
where the time goes in v1:
time: 73.5 us; the launch traced here: 73.3 us
  waiting for transfers between devices  33.8 us (46%)
  starting transfers between devices  17.8 us (24%)
  Pallas kernels  12.7 us (17%)
  other arithmetic  4.48 us (6%)
  local copies, waits for them, and re-layouts  4.35 us (6%)
    ppermute x14, waiting for transfers between devices, swap(): return lax.ppermute(block, axis, [(i, i ^ flips) for i in range(size)])  33.8 us
    ppermute x14, starting transfers between devices, swap(): return lax.ppermute(block, axis, [(i, i ^ flips) for i in range(size)])  17.8 us
    pallas_call x1, Pallas kernels, load_weights(): pl.pallas_call(load_kernel, out_shape=(pltpu.VMEM((tiles, units, 2, LANES...  7.31 us
    pallas_call x1, Pallas kernels, run_experts(): pl.pallas_call(functools.partial(expert_kernel, exp_dev), grid=(half_rows...  5.43 us
    unnamed x5, local copies, waits for them, and re-layouts  3.38 us
    unnamed x1, other arithmetic  1.47 us
  transfers between devices with their start and end apart: 14, of which 10 were waited for; matrix products, arithmetic and copies ran while one was open for 5% of the time, Pallas kernels for 10%

profile of v1, /device:TPU:0, one launch (start us, length us, event | category | flops | bytes accessed | tf_op | source)
XLA Modules:
  0.0 73.3 jit_solution(17112005189555475935)
XLA Ops:
  0.0 0.8 %select_reduce_fusion = f32[8,16]{1,0:T(8,128)S(1)} fusion(f32[8,8]{1,0:T(8,128)} %param.7, s32[8,8]{1,0:T(8,128)} %param.6), kind=kLoop, calls=%fused_computation.25 | loop fusion | flops 2944 | bytes 1024 | tf_op jit(solution)/shard_map/reduce_sum | solution.py:25
  0.8 0.1 fusion.10
  0.9 1.5 %constant_dynamic-update-slice_fusion.6 = (bf16[128,4224]{1,0:T(8,128)(2,1)}, bf16[256,4224]{1,0:T(8,128)(2,1)S(1)}, bf16[8,4224]{1,0:T(8,128)(2,1)S(1)}) fusion(bf16[8,128]{1,0:T(8,128)(2,1)S(1)} %fusion.10, bf16[8,4096]{1,0:T(8,128)(2,1)} %param.5), kind=kLoop, calls=%fused_computation.16 | loop fusion | flops 135166 | bytes 270336
  2.4 4.0 %collective-permute-start.1 = (bf16[8,4224]{1,0:T(8,128)(2,1)S(1)}, bf16[8,4224]{1,0:T(8,128)(2,1)S(1)}, u32[]{:S(2)}, u32[]{:S(2)}) collective-permute-start(bf16[8,4224]{1,0:T(8,128)(2,1)S(1)} %get-tuple-element.37), channel_id=1, source_target_pairs={{0,4},{1,5},{2,6},{3,7},{4,0},{5,1},{6,2},{7,3},{8,12},{9,13},{10,... | collective-permute-start | bytes 202760 | tf_op jit(solution)/shard_map/ppermute | solution.py:16
  6.4 1.6 %collective-permute-start = (bf16[8,4224]{1,0:T(8,128)(2,1)S(1)}, bf16[8,4224]{1,0:T(8,128)(2,1)S(1)}, u32[]{:S(2)}, u32[]{:S(2)}) collective-permute-start(bf16[8,4224]{1,0:T(8,128)(2,1)S(1)} %get-tuple-element.37), channel_id=1, source_target_pairs={{0,2},{1,3},{2,0},{3,1},{4,6},{5,7},{6,4},{7,5},{8,10},{9,11},{10,... | collective-permute-start | bytes 202760 | tf_op jit(solution)/shard_map/ppermute | solution.py:16
  8.0 0.0 collective-permute-start.2
  8.0 1.5 %collective-permute-done.1 = bf16[8,4224]{1,0:T(8,128)(2,1)S(1)} collective-permute-done((bf16[8,4224]{1,0:T(8,128)(2,1)S(1)}, bf16[8,4224]{1,0:T(8,128)(2,1)S(1)}, u32[]{:S(2)}, u32[]{:S(2)}) %collective-permute-start.1) | collective-permute-done | bytes 67616 | tf_op jit(solution)/shard_map/ppermute | solution.py:16
  9.5 1.2 %collective-permute-done = bf16[8,4224]{1,0:T(8,128)(2,1)S(1)} collective-permute-done((bf16[8,4224]{1,0:T(8,128)(2,1)S(1)}, bf16[8,4224]{1,0:T(8,128)(2,1)S(1)}, u32[]{:S(2)}, u32[]{:S(2)}) %collective-permute-start) | collective-permute-done | bytes 67616 | tf_op jit(solution)/shard_map/ppermute | solution.py:16
  10.7 3.4 %collective-permute-done.2 = bf16[8,4224]{1,0:T(8,128)(2,1)S(1)} collective-permute-done((bf16[8,4224]{1,0:T(8,128)(2,1)S(1)}, bf16[8,4224]{1,0:T(8,128)(2,1)S(1)}, u32[]{:S(2)}, u32[]{:S(2)}) %collective-permute-start.2) | collective-permute-done | bytes 67616 | tf_op jit(solution)/shard_map/ppermute | solution.py:16
  14.1 0.9 %pad_maximum_fusion = bf16[32,4224]{1,0:T(8,128)(2,1)S(1)} fusion(bf16[8,4224]{1,0:T(8,128)(2,1)S(1)} %collective-permute-done.2, bf16[8,4224]{1,0:T(8,128)(2,1)S(1)} %collective-permute-done.1, bf16[8,4224]{1,0:T(8,128)(2,1)S(1)} %collective-permute-done, bf16[8,128]{1,0:T(8,128)(2,1)S(1)} %fusion.10, bf16[8,4096]{1,0:T(8,128)(2,1)} %param.5), kind=kLoop, calls=%fused_computation.4 | loop fusion | flops 1351680 | bytes 540672 | tf_op jit(solution)/shard_map/concatenate | solution.py:20
  14.9 2.5 %collective-permute-start.5 = (bf16[32,4224]{1,0:T(8,128)(2,1)S(1)}, bf16[32,4224]{1,0:T(8,128)(2,1)S(1)}, u32[]{:S(2)}, u32[]{:S(2)}) collective-permute-start(bf16[32,4224]{1,0:T(8,128)(2,1)S(1)} %pad_maximum_fusion), channel_id=1, source_target_pairs={{0,24},{8,16},{16,8},{24,0},{1,25},{9,17},{17,9},{25,1},{2,26},{10... | collective-permute-start | bytes 811016 | tf_op jit(solution)/shard_map/ppermute | solution.py:16
  17.4 0.5 collective-permute-start.4
  17.9 0.5 collective-permute-start.3
  18.5 0.6 constant_dynamic-update-slice_fusion.5
  19.1 0.6 constant_dynamic-update-slice_fusion.4
  19.7 0.6 constant_dynamic-update-slice_fusion.3
  20.4 8.0 %collective-permute-done.3 = bf16[32,4224]{1,0:T(8,128)(2,1)S(1)} collective-permute-done((bf16[32,4224]{1,0:T(8,128)(2,1)S(1)}, bf16[32,4224]{1,0:T(8,128)(2,1)S(1)}, u32[]{:S(2)}, u32[]{:S(2)}) %collective-permute-start.3) | collective-permute-done | bytes 270368 | tf_op jit(solution)/shard_map/ppermute | solution.py:16
  28.4 0.7 %constant_dynamic-update-slice_fusion.2 = (bf16[128,4224]{1,0:T(8,128)(2,1)}, bf16[256,4224]{1,0:T(8,128)(2,1)S(1)}) fusion(bf16[128,4224]{1,0:T(8,128)(2,1)} %get-tuple-element.29, bf16[32,4224]{1,0:T(8,128)(2,1)S(1)} %collective-permute-done.3, bf16[256,4224]{1,0:T(8,128)(2,1)S(1)} %get-tuple-element.30), kind=kLoop, calls=%fused_computation.12 | loop fusion | bytes 811008
  29.1 0.0 collective-permute-done.4
  29.1 0.7 %constant_dynamic-update-slice_fusion.1 = (bf16[128,4224]{1,0:T(8,128)(2,1)}, bf16[256,4224]{1,0:T(8,128)(2,1)S(1)}) fusion(bf16[128,4224]{1,0:T(8,128)(2,1)} %get-tuple-element.24, bf16[32,4224]{1,0:T(8,128)(2,1)S(1)} %collective-permute-done.4, bf16[256,4224]{1,0:T(8,128)(2,1)S(1)} %get-tuple-element.25), kind=kLoop, calls=%fused_computation.11 | loop fusion | bytes 811008
  29.9 0.0 collective-permute-done.5
  29.9 0.8 %constant_dynamic-update-slice_fusion = (bf16[128,4224]{1,0:T(8,128)(2,1)}, bf16[256,4224]{1,0:T(8,128)(2,1)S(1)}) fusion(bf16[128,4224]{1,0:T(8,128)(2,1)} %get-tuple-element.22, bf16[32,4224]{1,0:T(8,128)(2,1)S(1)} %collective-permute-done.5, bf16[256,4224]{1,0:T(8,128)(2,1)S(1)} %get-tuple-element.23), kind=kLoop, calls=%fused_computation.10 | loop fusion | bytes 811008 | tf_op jit(solution)/shard_map/concatenate | solution.py:20
  30.7 0.0 collective-permute-start.6
  30.7 7.3 %shard_map.55 = (bf16[32,768,2,128]{3,2,1,0:T(2,128)(2,1)S(1)}, bf16[768,4096]{1,0:T(8,128)(2,1)S(1)}) custom-call(bf16[768,2,4096]{2,1,0:T(2,128)(2,1)} %bitcast.6, bf16[768,4096]{1,0:T(8,128)(2,1)} %bitcast.7), custom_call_target="tpu_custom_call" | custom-call | bytes 18874368 | tf_op jit(solution)/shard_map/pallas_call | solution.py:54
  38.0 0.1 compare_and_fusion
  38.1 0.0 collective-permute-done.6
  38.1 0.1 constant_dynamic-update-slice_fusion.7
  38.2 5.4 %shard_map.56 = (bf16[128,4096]{1,0:T(8,128)(2,1)S(1)}, f32[128,4096]{1,0:T(8,128)S(1)}) custom-call(bf16[16,128]{1,0:T(8,128)(2,1)S(1)} %pad_convert_fusion.select_ref, bf16[2,128,4224]{2,1,0:T(8,128)(2,1)S(1)} %bitcast.5, bf16[32,1536,128]{2,1,0:T(8,128)(2,1)S(1)} %bitcast.4, bf16[768,4096]{1,0:T(8,128)(2,1)S(1)} %get-tuple-element.10.wout_ref), custom_call_target="tpu_custom_call" | custom-call | flops 4831838208 | bytes 5308416 | tf_op jit(solution)/shard_map/pallas_call | solution.py:108
  43.7 0.6 collective-permute-start.7
  44.3 2.3 %collective-permute-done.7 = bf16[128,4096]{1,0:T(8,128)(2,1)S(1)} collective-permute-done((bf16[128,4096]{1,0:T(8,128)(2,1)S(1)}, bf16[128,4096]{1,0:T(8,128)(2,1)S(1)}, u32[]{:S(2)}, u32[]{:S(2)}) %collective-permute-start.7) | collective-permute-done | bytes 1048608 | tf_op jit(solution)/shard_map/ppermute | solution.py:16
  46.6 0.4 fusion.13
  46.9 0.1 fusion.14
  47.0 1.5 %collective-permute-start.8 = (bf16[32,4096]{1,0:T(8,128)(2,1)S(1)}, bf16[32,4096]{1,0:T(8,128)(2,1)S(1)}, u32[]{:S(2)}, u32[]{:S(2)}) collective-permute-start(bf16[32,4096]{1,0:T(8,128)(2,1)S(1)} %get-tuple-element.17), channel_id=1, source_target_pairs={{0,8},{8,0},{16,24},{24,16},{1,9},{9,1},{17,25},{25,17},{2,10},{10... | collective-permute-start | bytes 786440 | tf_op jit(solution)/shard_map/ppermute | solution.py:16
  48.6 0.7 collective-permute-start.10
  49.2 1.3 %collective-permute-start.9 = (bf16[32,4096]{1,0:T(8,128)(2,1)S(1)}, bf16[32,4096]{1,0:T(8,128)(2,1)S(1)}, u32[]{:S(2)}, u32[]{:S(2)}) collective-permute-start(bf16[32,4096]{1,0:T(8,128)(2,1)S(1)} %get-tuple-element.19), channel_id=1, source_target_pairs={{0,16},{8,24},{16,0},{24,8},{1,17},{9,25},{17,1},{25,9},{2,18},{10... | collective-permute-start | bytes 786440 | tf_op jit(solution)/shard_map/ppermute | solution.py:16
  50.6 5.6 %collective-permute-done.8 = bf16[32,4096]{1,0:T(8,128)(2,1)S(1)} collective-permute-done((bf16[32,4096]{1,0:T(8,128)(2,1)S(1)}, bf16[32,4096]{1,0:T(8,128)(2,1)S(1)}, u32[]{:S(2)}, u32[]{:S(2)}) %collective-permute-start.8) | collective-permute-done | bytes 262176 | tf_op jit(solution)/shard_map/ppermute | solution.py:16
  56.2 5.3 %collective-permute-done.10 = bf16[32,4096]{1,0:T(8,128)(2,1)S(1)} collective-permute-done((bf16[32,4096]{1,0:T(8,128)(2,1)S(1)}, bf16[32,4096]{1,0:T(8,128)(2,1)S(1)}, u32[]{:S(2)}, u32[]{:S(2)}) %collective-permute-start.10) | collective-permute-done | bytes 262176 | tf_op jit(solution)/shard_map/ppermute | solution.py:16
  61.5 1.4 %collective-permute-done.9 = bf16[32,4096]{1,0:T(8,128)(2,1)S(1)} collective-permute-done((bf16[32,4096]{1,0:T(8,128)(2,1)S(1)}, bf16[32,4096]{1,0:T(8,128)(2,1)S(1)}, u32[]{:S(2)}, u32[]{:S(2)}) %collective-permute-start.9) | collective-permute-done | bytes 262176 | tf_op jit(solution)/shard_map/ppermute | solution.py:16
  62.9 0.1 fusion.11
  63.0 0.9 %collective-permute-start.11 = (bf16[8,4096]{1,0:T(8,128)(2,1)S(1)}, bf16[8,4096]{1,0:T(8,128)(2,1)S(1)}, u32[]{:S(2)}, u32[]{:S(2)}) collective-permute-start(bf16[8,4096]{1,0:T(8,128)(2,1)S(1)} %get-tuple-element.26), channel_id=1, source_target_pairs={{0,2},{1,3},{2,0},{3,1},{4,6},{5,7},{6,4},{7,5},{8,10},{9,11},{10,... | collective-permute-start | bytes 196616 | tf_op jit(solution)/shard_map/ppermute | solution.py:16
  63.9 3.5 %collective-permute-start.13 = (bf16[8,4096]{1,0:T(8,128)(2,1)S(1)}, bf16[8,4096]{1,0:T(8,128)(2,1)S(1)}, u32[]{:S(2)}, u32[]{:S(2)}) collective-permute-start(bf16[8,4096]{1,0:T(8,128)(2,1)S(1)} %get-tuple-element.27), channel_id=1, source_target_pairs={{0,6},{1,7},{2,4},{3,5},{4,2},{5,3},{6,0},{7,1},{8,14},{9,15},{10,... | collective-permute-start | bytes 196616 | tf_op jit(solution)/shard_map/ppermute | solution.py:16
  67.4 0.0 collective-permute-start.12
  67.5 0.0 collective-permute-done.11
  67.5 3.1 %collective-permute-done.13 = bf16[8,4096]{1,0:T(8,128)(2,1)S(1)} collective-permute-done((bf16[8,4096]{1,0:T(8,128)(2,1)S(1)}, bf16[8,4096]{1,0:T(8,128)(2,1)S(1)}, u32[]{:S(2)}, u32[]{:S(2)}) %collective-permute-start.13) | collective-permute-done | bytes 65568 | tf_op jit(solution)/shard_map/ppermute | solution.py:16
  70.5 2.1 %collective-permute-done.12 = bf16[8,4096]{1,0:T(8,128)(2,1)S(1)} collective-permute-done((bf16[8,4096]{1,0:T(8,128)(2,1)S(1)}, bf16[8,4096]{1,0:T(8,128)(2,1)S(1)}, u32[]{:S(2)}, u32[]{:S(2)}) %collective-permute-start.12) | collective-permute-done | bytes 65568 | tf_op jit(solution)/shard_map/ppermute | solution.py:16
  72.6 0.7 fusion.4
  (6 shorter events, 0.0 us)
Async XLA Ops:
  2.4 7.1 %collective-permute-start.1 = (bf16[8,4224]{1,0:T(8,128)(2,1)S(1)}, bf16[8,4224]{1,0:T(8,128)(2,1)S(1)}, u32[]{:S(2)}, u32[]{:S(2)}) collective-permute-start(bf16[8,4224]{1,0:T(8,128)(2,1)S(1)} %get-tuple-element.37), channel_id=1, source_target_pairs={{0,4},{1,5},{2,6},{3,7},{4,0},{5,1},{6,2},{7,3},{8,12},{9,13},{10,... | collective-permute-start | bytes 202760 | tf_op jit(solution)/shard_map/ppermute | solution.py:16
  6.4 4.3 %collective-permute-start = (bf16[8,4224]{1,0:T(8,128)(2,1)S(1)}, bf16[8,4224]{1,0:T(8,128)(2,1)S(1)}, u32[]{:S(2)}, u32[]{:S(2)}) collective-permute-start(bf16[8,4224]{1,0:T(8,128)(2,1)S(1)} %get-tuple-element.37), channel_id=1, source_target_pairs={{0,2},{1,3},{2,0},{3,1},{4,6},{5,7},{6,4},{7,5},{8,10},{9,11},{10,... | collective-permute-start | bytes 202760 | tf_op jit(solution)/shard_map/ppermute | solution.py:16
  8.0 6.1 %collective-permute-start.2 = (bf16[8,4224]{1,0:T(8,128)(2,1)S(1)}, bf16[8,4224]{1,0:T(8,128)(2,1)S(1)}, u32[]{:S(2)}, u32[]{:S(2)}) collective-permute-start(bf16[8,4224]{1,0:T(8,128)(2,1)S(1)} %get-tuple-element.37), channel_id=1, source_target_pairs={{0,6},{1,7},{2,4},{3,5},{4,2},{5,3},{6,0},{7,1},{8,14},{9,15},{10,... | collective-permute-start | bytes 202760 | tf_op jit(solution)/shard_map/ppermute | solution.py:16
  14.9 15.0 %collective-permute-start.5 = (bf16[32,4224]{1,0:T(8,128)(2,1)S(1)}, bf16[32,4224]{1,0:T(8,128)(2,1)S(1)}, u32[]{:S(2)}, u32[]{:S(2)}) collective-permute-start(bf16[32,4224]{1,0:T(8,128)(2,1)S(1)} %pad_maximum_fusion), channel_id=1, source_target_pairs={{0,24},{8,16},{16,8},{24,0},{1,25},{9,17},{17,9},{25,1},{2,26},{10... | collective-permute-start | bytes 811016 | tf_op jit(solution)/shard_map/ppermute | solution.py:16
  17.4 11.7 %collective-permute-start.4 = (bf16[32,4224]{1,0:T(8,128)(2,1)S(1)}, bf16[32,4224]{1,0:T(8,128)(2,1)S(1)}, u32[]{:S(2)}, u32[]{:S(2)}) collective-permute-start(bf16[32,4224]{1,0:T(8,128)(2,1)S(1)} %pad_maximum_fusion), channel_id=1, source_target_pairs={{0,16},{8,24},{16,0},{24,8},{1,17},{9,25},{17,1},{25,9},{2,18},{10... | collective-permute-start | bytes 811016 | tf_op jit(solution)/shard_map/ppermute | solution.py:16
  17.9 10.5 %collective-permute-start.3 = (bf16[32,4224]{1,0:T(8,128)(2,1)S(1)}, bf16[32,4224]{1,0:T(8,128)(2,1)S(1)}, u32[]{:S(2)}, u32[]{:S(2)}) collective-permute-start(bf16[32,4224]{1,0:T(8,128)(2,1)S(1)} %pad_maximum_fusion), channel_id=1, source_target_pairs={{0,8},{8,0},{16,24},{24,16},{1,9},{9,1},{17,25},{25,17},{2,10},{10... | collective-permute-start | bytes 811016 | tf_op jit(solution)/shard_map/ppermute | solution.py:16
  30.7 7.4 %collective-permute-start.6 = (bf16[128,4224]{1,0:T(8,128)(2,1)}, bf16[128,4224]{1,0:T(8,128)(2,1)S(1)}, u32[]{:S(2)}, u32[]{:S(2)}) collective-permute-start(bf16[128,4224]{1,0:T(8,128)(2,1)} %get-tuple-element.20), channel_id=1, source_target_pairs={{0,1},{1,0},{2,3},{3,2},{4,5},{5,4},{6,7},{7,6},{8,9},{9,8},{10,11... | collective-permute-start | bytes 3244040 | tf_op jit(solution)/shard_map/ppermute | solution.py:16
  43.7 2.9 %collective-permute-start.7 = (bf16[128,4096]{1,0:T(8,128)(2,1)S(1)}, bf16[128,4096]{1,0:T(8,128)(2,1)S(1)}, u32[]{:S(2)}, u32[]{:S(2)}) collective-permute-start(bf16[128,4096]{1,0:T(8,128)(2,1)S(1)} %get-tuple-element.12), channel_id=1, source_target_pairs={{0,1},{1,0},{2,3},{3,2},{4,5},{5,4},{6,7},{7,6},{8,9},{9,8},{10,11... | collective-permute-start | bytes 3145736 | tf_op jit(solution)/shard_map/ppermute | solution.py:16
  47.0 9.2 %collective-permute-start.8 = (bf16[32,4096]{1,0:T(8,128)(2,1)S(1)}, bf16[32,4096]{1,0:T(8,128)(2,1)S(1)}, u32[]{:S(2)}, u32[]{:S(2)}) collective-permute-start(bf16[32,4096]{1,0:T(8,128)(2,1)S(1)} %get-tuple-element.17), channel_id=1, source_target_pairs={{0,8},{8,0},{16,24},{24,16},{1,9},{9,1},{17,25},{25,17},{2,10},{10... | collective-permute-start | bytes 786440 | tf_op jit(solution)/shard_map/ppermute | solution.py:16
  48.6 12.9 %collective-permute-start.10 = (bf16[32,4096]{1,0:T(8,128)(2,1)S(1)}, bf16[32,4096]{1,0:T(8,128)(2,1)S(1)}, u32[]{:S(2)}, u32[]{:S(2)}) collective-permute-start(bf16[32,4096]{1,0:T(8,128)(2,1)S(1)} %get-tuple-element.18), channel_id=1, source_target_pairs={{0,24},{8,16},{16,8},{24,0},{1,25},{9,17},{17,9},{25,1},{2,26},{10... | collective-permute-start | bytes 786440 | tf_op jit(solution)/shard_map/ppermute | solution.py:16
  49.2 13.6 %collective-permute-start.9 = (bf16[32,4096]{1,0:T(8,128)(2,1)S(1)}, bf16[32,4096]{1,0:T(8,128)(2,1)S(1)}, u32[]{:S(2)}, u32[]{:S(2)}) collective-permute-start(bf16[32,4096]{1,0:T(8,128)(2,1)S(1)} %get-tuple-element.19), channel_id=1, source_target_pairs={{0,16},{8,24},{16,0},{24,8},{1,17},{9,25},{17,1},{25,9},{2,18},{10... | collective-permute-start | bytes 786440 | tf_op jit(solution)/shard_map/ppermute | solution.py:16
  63.0 4.4 %collective-permute-start.11 = (bf16[8,4096]{1,0:T(8,128)(2,1)S(1)}, bf16[8,4096]{1,0:T(8,128)(2,1)S(1)}, u32[]{:S(2)}, u32[]{:S(2)}) collective-permute-start(bf16[8,4096]{1,0:T(8,128)(2,1)S(1)} %get-tuple-element.26), channel_id=1, source_target_pairs={{0,2},{1,3},{2,0},{3,1},{4,6},{5,7},{6,4},{7,5},{8,10},{9,11},{10,... | collective-permute-start | bytes 196616 | tf_op jit(solution)/shard_map/ppermute | solution.py:16
  63.9 6.6 %collective-permute-start.13 = (bf16[8,4096]{1,0:T(8,128)(2,1)S(1)}, bf16[8,4096]{1,0:T(8,128)(2,1)S(1)}, u32[]{:S(2)}, u32[]{:S(2)}) collective-permute-start(bf16[8,4096]{1,0:T(8,128)(2,1)S(1)} %get-tuple-element.27), channel_id=1, source_target_pairs={{0,6},{1,7},{2,4},{3,5},{4,2},{5,3},{6,0},{7,1},{8,14},{9,15},{10,... | collective-permute-start | bytes 196616 | tf_op jit(solution)/shard_map/ppermute | solution.py:16
  67.4 5.2 %collective-permute-start.12 = (bf16[8,4096]{1,0:T(8,128)(2,1)S(1)}, bf16[8,4096]{1,0:T(8,128)(2,1)S(1)}, u32[]{:S(2)}, u32[]{:S(2)}) collective-permute-start(bf16[8,4096]{1,0:T(8,128)(2,1)S(1)} %get-tuple-element.28), channel_id=1, source_target_pairs={{0,4},{1,5},{2,6},{3,7},{4,0},{5,1},{6,2},{7,3},{8,12},{9,13},{10,... | collective-permute-start | bytes 196616 | tf_op jit(solution)/shard_map/ppermute | solution.py:16

commit v2 on v1

v2 whole, which is shorter than its diff:
```python
import functools

import jax
import jax.numpy as jnp
from jax import lax
from jax.experimental import pallas as pl
from jax.experimental.pallas import tpu as pltpu
from jax.sharding import PartitionSpec as P

LANES = 128
MIB = 1 << 20
VMEM = pl.BlockSpec(memory_space=pltpu.VMEM)


def swap(block, axis, flips):
    size = lax.axis_size(axis)
    return lax.ppermute(block, axis, [(i, i ^ flips) for i in range(size)])


def pack_kernel(experts, tokens_ref, ids_ref, weights_ref, packed_ref):
    rows, width = tokens_ref.shape
    tail = packed_ref.shape[1] - width
    packed_ref[:, :width] = tokens_ref[...]
    lane = lax.broadcasted_iota(jnp.int32, (rows, tail), 1)
    expert = lane % experts
    part = lane // experts
    dense = jnp.zeros((rows, tail), jnp.float32)
    for k in range(ids_ref.shape[1]):
        dense += jnp.where(ids_ref[:, k : k + 1] == expert, weights_ref[:, k : k + 1], 0.0)
    result = jnp.zeros((rows, tail), jnp.float32)
    for step in range(3):
        rounded = dense.astype(jnp.bfloat16).astype(jnp.float32)
        result = jnp.where(part == step, rounded, result)
        dense = dense - rounded
    packed_ref[:, width:] = result.astype(jnp.bfloat16)


def pack(tokens, expert_ids, route_weights, experts):
    rows, width = tokens.shape
    tail = -(-3 * experts // LANES) * LANES
    return pl.pallas_call(
        functools.partial(pack_kernel, experts),
        out_shape=jax.ShapeDtypeStruct((rows, width + tail), jnp.bfloat16),
        in_specs=[VMEM] * 3,
        out_specs=VMEM,
        compiler_params=pltpu.CompilerParams(vmem_limit_bytes=2 * MIB),
    )(tokens, expert_ids, route_weights)


def stack_kernel(*refs):
    out_ref = refs[-1]
    start = 0
    for ref in refs[:-1]:
        out_ref[start : start + ref.shape[0], :] = ref[...]
        start += ref.shape[0]


def stack(blocks):
    rows = sum(block.shape[0] for block in blocks)
    return pl.pallas_call(
        stack_kernel,
        out_shape=jax.ShapeDtypeStruct((rows, blocks[0].shape[1]), blocks[0].dtype),
        in_specs=[VMEM] * len(blocks),
        out_specs=VMEM,
        compiler_params=pltpu.CompilerParams(vmem_limit_bytes=4 * MIB),
    )(*blocks)


def load_kernel(in_ref, out_ref, in_vmem, out_vmem, sems):
    tiles = in_vmem.shape[0]
    copies = [
        pltpu.make_async_copy(in_ref.at[:, :, pl.ds(t * LANES, LANES)], in_vmem.at[t], sems.at[t])
        for t in range(tiles)
    ]
    copies.append(pltpu.make_async_copy(out_ref, out_vmem, sems.at[tiles]))
    for copy in copies:
        copy.start()
    for copy in copies:
        copy.wait()


def load_weights(w_in, w_out):
    units, _, width = w_in.shape
    tiles = width // LANES
    win, wout = pl.pallas_call(
        load_kernel,
        out_shape=(
            pltpu.VMEM((tiles, units, 2, LANES), w_in.dtype),
            pltpu.VMEM(w_out.shape, w_out.dtype),
        ),
        in_specs=[pl.BlockSpec(memory_space=pltpu.HBM)] * 2,
        out_specs=[VMEM] * 2,
        scratch_shapes=[pltpu.SemaphoreType.DMA((tiles + 1,))],
        compiler_params=pltpu.CompilerParams(vmem_limit_bytes=2 * MIB),
        cost_estimate=pl.CostEstimate(
            flops=0, bytes_accessed=4 * (w_in.size + w_out.size), transcendentals=0
        ),
    )(*(pltpu.with_memory_space_constraint(w, pltpu.HBM) for w in (w_in, w_out)))
    return win.reshape(tiles, units * 2, LANES), wout


def expert_kernel(exp_dev, half, *refs):
    select_ref = refs[0]
    x_refs = refs[1 : 1 + 2 * half]
    win_ref, wout_ref, send_ref, keep_ref, mixed, hidden = refs[1 + 2 * half :]
    lines = win_ref.shape[1]
    width = win_ref.shape[0] * LANES
    per = lines // exp_dev
    block = x_refs[0].shape[0]
    rows = 2 * half * block
    x = jnp.concatenate([ref[:, :width] for ref in x_refs], axis=0)
    tail = jnp.concatenate([ref[:, width:] for ref in x_refs], axis=0)
    contract_last = (((1,), (1,)), ((), ()))
    scale = lax.dot_general(
        select_ref[...], tail, contract_last, preferred_element_type=jnp.float32
    )
    for e in range(exp_dev):
        w = jnp.concatenate(
            [win_ref[t, pl.ds(e * per, per), :] for t in range(win_ref.shape[0])], axis=1
        )
        both = lax.dot_general(w, x, contract_last, preferred_element_type=jnp.float32)
        for r in range(0, rows, LANES):
            mixed[...] = both[:, r : r + LANES]
            gate = mixed[pl.ds(0, per // 2, stride=2), :]
            up = mixed[pl.ds(1, per // 2, stride=2), :]
            act = gate / (1.0 + jnp.exp(-gate)) * up * scale[e : e + 1, r : r + LANES]
            hidden[pl.ds(e * per // 2, per // 2), r : r + LANES] = act.astype(jnp.bfloat16)
    chunk = min(512, width)
    for c in range(0, width, chunk):
        part = lax.dot_general(
            hidden[...],
            wout_ref[:, c : c + chunk],
            (((0,), (0,)), ((), ())),
            preferred_element_type=jnp.float32,
        )
        for b in range(half):
            keep_ref[b, :, c : c + chunk] = part[b * block : (b + 1) * block]
            other = part[(half + b) * block : (half + b + 1) * block]
            send_ref[b, :, c : c + chunk] = other.astype(jnp.bfloat16)


def run_experts(select, blocks, win, wout, exp_dev):
    half = len(blocks) // 2
    block_rows, packed_width = blocks[0].shape
    width = wout.shape[1]
    lines = win.shape[1]
    block = min(block_rows, max(16, 128 // half))
    rows = 2 * half * block
    out_block = pl.BlockSpec((half, block, width), lambda i: (0, i, 0))
    planned = 2 * rows * (2 * packed_width + 3 * width) + rows * (4 * lines + 4 * width)
    return pl.pallas_call(
        functools.partial(expert_kernel, exp_dev, half),
        grid=(block_rows // block,),
        out_shape=(
            jax.ShapeDtypeStruct((half, block_rows, width), jnp.bfloat16),
            jax.ShapeDtypeStruct((half, block_rows, width), jnp.float32),
        ),
        in_specs=[
            pl.BlockSpec(select.shape, lambda i: (0, 0)),
            *[pl.BlockSpec((block, packed_width), lambda i: (i, 0))] * (2 * half),
            VMEM,
            VMEM,
        ],
        out_specs=[out_block, out_block],
        scratch_shapes=[
            pltpu.VMEM((lines // exp_dev, LANES), jnp.float32),
            pltpu.VMEM((lines // 2, rows), jnp.bfloat16),
        ],
        compiler_params=pltpu.CompilerParams(vmem_limit_bytes=planned + 2 * MIB),
        cost_estimate=pl.CostEstimate(
            flops=6 * half * block_rows * width * lines,
            bytes_accessed=4 * half * block_rows * packed_width + 6 * half * block_rows * width,
            transcendentals=half * block_rows * lines,
        ),
    )(select, *blocks, win, wout)


def body(tokens, expert_ids, route_weights, in_weights, out_weights):
    tok_dev, width = tokens.shape
    exp_dev, units = in_weights.shape[:2]
    groups = lax.axis_size("expert")
    planes = lax.axis_size("batch")
    chips = groups // 2
    experts = exp_dev * groups
    far = planes - 1
    w_in = in_weights.reshape(exp_dev * units, 2, width)
    w_out = out_weights.reshape(exp_dev * units, width)

    x = pack(tokens, expert_ids, route_weights, experts)
    along = [swap(x, "expert", 2 * r) for r in range(1, chips)]
    across = swap(x, "batch", far)
    mine = stack([x] + along)
    mine, across, w_in = lax.optimization_barrier((mine, across, w_in))
    blocks = [swap(mine, "batch", b) for b in range(1, far)]
    others = [swap(across, "expert", 2 * r) for r in range(1, chips)]
    win, wout = load_weights(w_in, w_out)
    blocks, others, win = lax.optimization_barrier((blocks, others, win))
    blocks = [mine] + blocks + [stack([across] + others)]
    blocks = blocks + [swap(block, "expert", 1) for block in blocks]

    tail = x.shape[1] - width
    wanted = lax.axis_index("expert") * exp_dev + jnp.arange(exp_dev, dtype=jnp.int32)
    column = jnp.arange(tail, dtype=jnp.int32)
    select = (column[None, :] % experts == wanted[:, None]) & (column < 3 * experts)[None, :]
    select = jnp.pad(select.astype(jnp.bfloat16), ((0, -exp_dev % 16), (0, 0)))

    send, total = run_experts(select, blocks, win, wout, exp_dev)
    total = total + swap(send, "expert", 1).astype(jnp.float32)
    rounded = total.astype(jnp.bfloat16)
    mine = total[0]
    for b in range(1, far):
        mine = mine + swap(rounded[b], "batch", b).astype(jnp.float32)
    across = total[far, :tok_dev]
    for r in range(1, chips):
        piece = rounded[far, r * tok_dev : (r + 1) * tok_dev]
        across = across + swap(piece, "expert", 2 * r).astype(jnp.float32)
    result = mine[:tok_dev] + swap(across.astype(jnp.bfloat16), "batch", far).astype(jnp.float32)
    rounded = mine.astype(jnp.bfloat16)
    for r in range(1, chips):
        piece = rounded[r * tok_dev : (r + 1) * tok_dev]
        result = result + swap(piece, "expert", 2 * r).astype(jnp.float32)
    return result.astype(jnp.bfloat16)


def solution(mesh):
    return jax.shard_map(
        body,
        mesh=mesh,
        in_specs=(
            P(("batch", "expert"), None),
            P(("batch", "expert"), None),
            P(("batch", "expert"), None),
            P("expert", "batch", None, None),
            P("expert", "batch", None),
        ),
        out_specs=P(("batch", "expert"), None),
        check_vma=False,
    )
```

time: 73.5 us -> 62.8 us (0.85)
  waiting for transfers between devices: 33.8 us -> 18.2 us
  starting transfers between devices: 17.8 us -> 27.9 us
  other arithmetic: 4.48 us -> 1.28 us
  local copies, waits for them, and re-layouts: 4.35 us -> 2.28 us
    ppermute x14 -> x23, waiting for transfers between devices: 33.8 us -> 18.2 us  [swap(): return lax.ppermute(block, axis, [(i, i ^ flips) for i in range(size)])]
    ppermute x14 -> x23, starting transfers between devices: 17.8 us -> 27.9 us  [swap(): return lax.ppermute(block, axis, [(i, i ^ flips) for i in range(size)])]
    unnamed x1 -> x0, other arithmetic: 1.47 us -> none
    unnamed x5 -> x6, local copies, waits for them, and re-layouts: 3.38 us -> 2.21 us
    concatenate x2 -> x0, other arithmetic: 0.94 us -> none  [the longest x1 0.86 us: gather_over(): jnp.concatenate([block] + [swap(block, axis, step) for step in steps], ax...]
    concatenate x2 -> x0, local copies, waits for them, and re-layouts: 0.89 us -> none  [gather_over(): jnp.concatenate([block] + [swap(block, axis, step) for step in steps], ax...]
    reduce_sum x1 -> x0, other arithmetic: 0.79 us -> none  [packed_weights(): dense = jnp.sum(jnp.where(onehot, route_weights[:, :, None], 0.0), axis=1)]
    pallas_call x1 -> x4, Pallas kernels: 5.43 us -> 5.52 us  [the longest x1 5.38 us: run_experts(): pl.pallas_call(functools.partial(expert_kernel, exp_dev, half), grid=(blo...]
  transfers between devices with their start and end apart: 14 -> 23, of which waited for: 10 -> 13; matrix products, arithmetic and copies ran while one was open for 5% -> 0% of each run, Pallas kernels for 10% -> 12%
where the time goes in v2:
time: 62.8 us; the launch traced here: 62.6 us
  starting transfers between devices  27.9 us (44%)
  waiting for transfers between devices  18.2 us (29%)
  Pallas kernels  12.8 us (20%)
  local copies, waits for them, and re-layouts  2.28 us (4%)
  other arithmetic  1.28 us (2%)
    ppermute x23, starting transfers between devices, swap(): return lax.ppermute(block, axis, [(i, i ^ flips) for i in range(size)])  27.9 us
    ppermute x23, waiting for transfers between devices, swap(): return lax.ppermute(block, axis, [(i, i ^ flips) for i in range(size)])  18.2 us
    pallas_call x1, Pallas kernels, load_weights(): pl.pallas_call(load_kernel, out_shape=(pltpu.VMEM((tiles, units, 2, LANES...  7.31 us
    pallas_call x1, Pallas kernels, run_experts(): pl.pallas_call(functools.partial(expert_kernel, exp_dev, half), grid=(blo...  5.38 us
    unnamed x6, local copies, waits for them, and re-layouts  2.21 us
  transfers between devices with their start and end apart: 23, of which 13 were waited for; matrix products, arithmetic and copies ran while one was open for 0% of the time, Pallas kernels for 12%

profile of v2, /device:TPU:0, one launch (start us, length us, event | category | flops | bytes accessed | tf_op | source)
XLA Modules:
  0.0 62.6 jit_solution(11370679085511829957)
XLA Ops:
  0.0 0.0 copy-start
  0.0 0.8 %copy-done = bf16[8,4096]{1,0:T(8,128)(2,1)S(1)} copy-done((bf16[8,4096]{1,0:T(8,128)(2,1)S(1)}, bf16[8,4096]{1,0:T(8,128)(2,1)}, u32[]{:S(2)}) %copy-start) | copy-done | bytes 65560
  0.8 0.0 copy-start.1
  0.8 0.7 %copy-done.1 = s32[8,8]{1,0:T(8,128)S(1)} copy-done((s32[8,8]{1,0:T(8,128)S(1)}, s32[8,8]{1,0:T(8,128)}, u32[]{:S(2)}) %copy-start.1) | copy-done | bytes 280
  1.5 0.0 copy-start.2
  1.5 0.7 %copy-done.2 = f32[8,8]{1,0:T(8,128)S(1)} copy-done((f32[8,8]{1,0:T(8,128)S(1)}, f32[8,8]{1,0:T(8,128)}, u32[]{:S(2)}) %copy-start.2) | copy-done | bytes 280
  2.2 0.1 shard_map.55.refs_0_
  2.3 5.1 %collective-permute-start.2 = (bf16[8,4224]{1,0:T(8,128)(2,1)S(1)}, bf16[8,4224]{1,0:T(8,128)(2,1)S(1)}, u32[]{:S(2)}, u32[]{:S(2)}) collective-permute-start(bf16[8,4224]{1,0:T(8,128)(2,1)S(1)} %shard_map.55.refs_0_), channel_id=1, source_target_pairs={{0,6},{1,7},{2,4},{3,5},{4,2},{5,3},{6,0},{7,1},{8,14},{9,15},{10,... | collective-permute-start | bytes 202760 | tf_op jit(solution)/shard_map/ppermute | solution.py:17
  7.4 0.0 collective-permute-start.1
  7.4 0.6 %collective-permute-start = (bf16[8,4224]{1,0:T(8,128)(2,1)S(1)}, bf16[8,4224]{1,0:T(8,128)(2,1)S(1)}, u32[]{:S(2)}, u32[]{:S(2)}) collective-permute-start(bf16[8,4224]{1,0:T(8,128)(2,1)S(1)} %shard_map.55.refs_0_), channel_id=1, source_target_pairs={{0,2},{1,3},{2,0},{3,1},{4,6},{5,7},{6,4},{7,5},{8,10},{9,11},{10,... | collective-permute-start | bytes 202760 | tf_op jit(solution)/shard_map/ppermute | solution.py:17
  8.1 2.6 %collective-permute-start.3 = (bf16[8,4224]{1,0:T(8,128)(2,1)S(1)}, bf16[8,4224]{1,0:T(8,128)(2,1)S(1)}, u32[]{:S(2)}, u32[]{:S(2)}) collective-permute-start(bf16[8,4224]{1,0:T(8,128)(2,1)S(1)} %shard_map.55.refs_0_), channel_id=1, source_target_pairs={{0,24},{8,16},{16,8},{24,0},{1,25},{9,17},{17,9},{25,1},{2,26},{10... | collective-permute-start | bytes 202760 | tf_op jit(solution)/shard_map/ppermute | solution.py:17
  10.7 0.0 collective-permute-done.2.refs_3_
  10.7 2.5 %collective-permute-done.1.refs_2_ = bf16[8,4224]{1,0:T(8,128)(2,1)S(1)} collective-permute-done((bf16[8,4224]{1,0:T(8,128)(2,1)S(1)}, bf16[8,4224]{1,0:T(8,128)(2,1)S(1)}, u32[]{:S(2)}, u32[]{:S(2)}) %collective-permute-start.1) | collective-permute-done | bytes 67616 | tf_op jit(solution)/shard_map/ppermute | solution.py:17
  13.2 0.0 collective-permute-done.refs_1_
  13.2 0.0 collective-permute-done.3.refs_0_
  13.3 1.7 %collective-permute-start.5 = (bf16[32,4224]{1,0:T(8,128)(2,1)S(1)}, bf16[32,4224]{1,0:T(8,128)(2,1)S(1)}, u32[]{:S(2)}, u32[]{:S(2)}) collective-permute-start(bf16[32,4224]{1,0:T(8,128)(2,1)S(1)} %shard_map.56.refs_1_), channel_id=1, source_target_pairs={{0,16},{8,24},{16,0},{24,8},{1,17},{9,25},{17,1},{25,9},{2,18},{10... | collective-permute-start | bytes 811016 | tf_op jit(solution)/shard_map/ppermute | solution.py:17
  14.9 1.5 %collective-permute-start.4 = (bf16[32,4224]{1,0:T(8,128)(2,1)S(1)}, bf16[32,4224]{1,0:T(8,128)(2,1)S(1)}, u32[]{:S(2)}, u32[]{:S(2)}) collective-permute-start(bf16[32,4224]{1,0:T(8,128)(2,1)S(1)} %shard_map.56.refs_1_), channel_id=1, source_target_pairs={{0,8},{8,0},{16,24},{24,16},{1,9},{9,1},{17,25},{25,17},{2,10},{10... | collective-permute-start | bytes 811016 | tf_op jit(solution)/shard_map/ppermute | solution.py:17
  16.4 3.6 %collective-permute-start.8 = (bf16[8,4224]{1,0:T(8,128)(2,1)S(1)}, bf16[8,4224]{1,0:T(8,128)(2,1)S(1)}, u32[]{:S(2)}, u32[]{:S(2)}) collective-permute-start(bf16[8,4224]{1,0:T(8,128)(2,1)S(1)} %collective-permute-done.3.refs_0_), channel_id=1, source_target_pairs={{0,6},{1,7},{2,4},{3,5},{4,2},{5,3},{6,0},{7,1},{8,14},{9,15},{10,... | collective-permute-start | bytes 202760 | tf_op jit(solution)/shard_map/ppermute | solution.py:17
  20.0 0.0 collective-permute-start.7
  20.0 0.8 %collective-permute-start.6 = (bf16[8,4224]{1,0:T(8,128)(2,1)S(1)}, bf16[8,4224]{1,0:T(8,128)(2,1)S(1)}, u32[]{:S(2)}, u32[]{:S(2)}) collective-permute-start(bf16[8,4224]{1,0:T(8,128)(2,1)S(1)} %collective-permute-done.3.refs_0_), channel_id=1, source_target_pairs={{0,2},{1,3},{2,0},{3,1},{4,6},{5,7},{6,4},{7,5},{8,10},{9,11},{10,... | collective-permute-start | bytes 202760 | tf_op jit(solution)/shard_map/ppermute | solution.py:17
  20.8 7.3 %shard_map.57 = (bf16[32,768,2,128]{3,2,1,0:T(2,128)(2,1)S(1)}, bf16[768,4096]{1,0:T(8,128)(2,1)S(1)}) custom-call(bf16[768,2,4096]{2,1,0:T(2,128)(2,1)} %bitcast.31, bf16[768,4096]{1,0:T(8,128)(2,1)} %bitcast.32), custom_call_target="tpu_custom_call" | custom-call | bytes 37748736 | tf_op jit(solution)/shard_map/pallas_call | solution.py:85
  28.1 0.0 collective-permute-done.8.refs_3_
  28.1 0.1 collective-permute-start.9
  28.2 0.0 collective-permute-done.7.refs_2_
  28.2 0.0 collective-permute-done.6.refs_1_
  28.2 0.0 collective-permute-done.5.refs_3_
  28.3 0.0 collective-permute-done.4.refs_2_
  28.3 0.5 collective-permute-start.12
  28.8 0.1 collective-permute-start.10
  28.9 0.4 collective-permute-start.11
  29.3 0.1 compare_and_fusion
  29.4 0.3 collective-permute-done.9.refs_5_
  29.8 0.4 collective-permute-done.12.refs_8_
  30.1 0.4 collective-permute-done.10.refs_6_
  30.5 0.4 collective-permute-done.11.refs_7_
  30.9 5.4 %shard_map.59 = (bf16[4,32,4096]{2,1,0:T(8,128)(2,1)S(1)}, f32[4,32,4096]{2,1,0:T(8,128)S(1)}) custom-call(bf16[16,128]{1,0:T(8,128)(2,1)S(1)} %pad_convert_fusion.refs_0_, bf16[32,4224]{1,0:T(8,128)(2,1)S(1)} %shard_map.56.refs_1_, bf16[32,4224]{1,0:T(8,128)(2,1)S(1)} %collective-permute-done.4.refs_2_, ...), custom_call_target="tpu_custom_call" | custom-call | flops 4831838208 | bytes 5308416 | tf_op jit(solution)/shard_map/pallas_call | solution.py:151
  36.3 0.3 collective-permute-start.13
  36.6 2.4 %collective-permute-done.13 = bf16[4,32,4096]{2,1,0:T(8,128)(2,1)S(1)} collective-permute-done((bf16[4,32,4096]{2,1,0:T(8,128)(2,1)S(1)}, bf16[4,32,4096]{2,1,0:T(8,128)(2,1)S(1)}, u32[]{:S(2)}, u32[]{:S(2)}) %collective-permute-start.13) | collective-permute-done | bytes 1048608 | tf_op jit(solution)/shard_map/ppermute | solution.py:17
  39.0 0.4 fusion.12
  39.4 1.3 %collective-permute-start.16 = (bf16[8,4096]{1,0:T(8,128)(2,1)S(1)}, bf16[8,4096]{1,0:T(8,128)(2,1)S(1)}, u32[]{:S(2)}, u32[]{:S(2)}) collective-permute-start(bf16[8,4096]{1,0:T(8,128)(2,1)S(1)} %get-tuple-element.35), channel_id=1, source_target_pairs={{0,2},{1,3},{2,0},{3,1},{4,6},{5,7},{6,4},{7,5},{8,10},{9,11},{10,... | collective-permute-start | bytes 196616 | tf_op jit(solution)/shard_map/ppermute | solution.py:17
  40.7 2.4 %collective-permute-start.18 = (bf16[8,4096]{1,0:T(8,128)(2,1)S(1)}, bf16[8,4096]{1,0:T(8,128)(2,1)S(1)}, u32[]{:S(2)}, u32[]{:S(2)}) collective-permute-start(bf16[8,4096]{1,0:T(8,128)(2,1)S(1)} %get-tuple-element.36), channel_id=1, source_target_pairs={{0,6},{1,7},{2,4},{3,5},{4,2},{5,3},{6,0},{7,1},{8,14},{9,15},{10,... | collective-permute-start | bytes 196616 | tf_op jit(solution)/shard_map/ppermute | solution.py:17
  43.2 0.5 collective-permute-start.17
  43.7 0.6 collective-permute-start.14
  44.3 0.5 collective-permute-start.15
  44.8 0.0 collective-permute-done.16
  44.8 2.5 %collective-permute-done.18 = bf16[8,4096]{1,0:T(8,128)(2,1)S(1)} collective-permute-done((bf16[8,4096]{1,0:T(8,128)(2,1)S(1)}, bf16[8,4096]{1,0:T(8,128)(2,1)S(1)}, u32[]{:S(2)}, u32[]{:S(2)}) %collective-permute-start.18) | collective-permute-done | bytes 65568 | tf_op jit(solution)/shard_map/ppermute | solution.py:17
  47.3 2.8 %collective-permute-done.17 = bf16[8,4096]{1,0:T(8,128)(2,1)S(1)} collective-permute-done((bf16[8,4096]{1,0:T(8,128)(2,1)S(1)}, bf16[8,4096]{1,0:T(8,128)(2,1)S(1)}, u32[]{:S(2)}, u32[]{:S(2)}) %collective-permute-start.17) | collective-permute-done | bytes 65568 | tf_op jit(solution)/shard_map/ppermute | solution.py:17
  50.2 0.5 collective-permute-start.19
  50.7 1.0 %collective-permute-done.14 = bf16[32,4096]{1,0:T(8,128)(2,1)S(1)} collective-permute-done((bf16[32,4096]{1,0:T(8,128)(2,1)S(1)}, bf16[32,4096]{1,0:T(8,128)(2,1)S(1)}, u32[]{:S(2)}, u32[]{:S(2)}) %collective-permute-start.14) | collective-permute-done | bytes 262176 | tf_op jit(solution)/shard_map/ppermute | solution.py:17
  51.7 0.2 collective-permute-done.15
  51.9 0.1 fusion.10
  52.1 2.0 %collective-permute-start.20 = (bf16[8,4096]{1,0:T(8,128)(2,1)S(1)}, bf16[8,4096]{1,0:T(8,128)(2,1)S(1)}, u32[]{:S(2)}, u32[]{:S(2)}) collective-permute-start(bf16[8,4096]{1,0:T(8,128)(2,1)S(1)} %get-tuple-element.40), channel_id=1, source_target_pairs={{0,2},{1,3},{2,0},{3,1},{4,6},{5,7},{6,4},{7,5},{8,10},{9,11},{10,... | collective-permute-start | bytes 196616 | tf_op jit(solution)/shard_map/ppermute | solution.py:17
  54.0 2.7 %collective-permute-start.22 = (bf16[8,4096]{1,0:T(8,128)(2,1)S(1)}, bf16[8,4096]{1,0:T(8,128)(2,1)S(1)}, u32[]{:S(2)}, u32[]{:S(2)}) collective-permute-start(bf16[8,4096]{1,0:T(8,128)(2,1)S(1)} %get-tuple-element.41), channel_id=1, source_target_pairs={{0,6},{1,7},{2,4},{3,5},{4,2},{5,3},{6,0},{7,1},{8,14},{9,15},{10,... | collective-permute-start | bytes 196616 | tf_op jit(solution)/shard_map/ppermute | solution.py:17
  56.7 0.0 collective-permute-start.21
  56.7 0.0 collective-permute-done.19
  56.7 0.4 collective-permute-done.20
  57.1 3.0 %collective-permute-done.22 = bf16[8,4096]{1,0:T(8,128)(2,1)S(1)} collective-permute-done((bf16[8,4096]{1,0:T(8,128)(2,1)S(1)}, bf16[8,4096]{1,0:T(8,128)(2,1)S(1)}, u32[]{:S(2)}, u32[]{:S(2)}) %collective-permute-start.22) | collective-permute-done | bytes 65568 | tf_op jit(solution)/shard_map/ppermute | solution.py:17
  60.1 1.8 %collective-permute-done.21 = bf16[8,4096]{1,0:T(8,128)(2,1)S(1)} collective-permute-done((bf16[8,4096]{1,0:T(8,128)(2,1)S(1)}, bf16[8,4096]{1,0:T(8,128)(2,1)S(1)}, u32[]{:S(2)}, u32[]{:S(2)}) %collective-permute-start.21) | collective-permute-done | bytes 65568 | tf_op jit(solution)/shard_map/ppermute | solution.py:17
  61.9 0.7 %fusion.9 = bf16[8,4096]{1,0:T(8,128)(2,1)} fusion(f32[32,4096]{1,0:T(8,128)S(1)} %get-tuple-element.32, bf16[8,4096]{1,0:T(8,128)(2,1)S(1)} %collective-permute-done.22, bf16[8,4096]{1,0:T(8,128)(2,1)S(1)} %collective-permute-done.21, bf16[8,4096]{1,0:T(8,128)(2,1)S(1)} %collective-permute-done.20, bf16[8,4096]{1,0:T(8,128)(2,1)S(1)} %collective-permute-done.19), kind=kLoop, calls=%fused_computation.15 | loop fusion | flops 294912 | bytes 458752 | tf_op jit(solution)/shard_map/convert_element_type | solution.py:222
  (10 shorter events, 0.2 us)
Async XLA Ops:
  0.0 0.8 %copy-start = (bf16[8,4096]{1,0:T(8,128)(2,1)S(1)}, bf16[8,4096]{1,0:T(8,128)(2,1)}, u32[]{:S(2)}) copy-start(bf16[8,4096]{1,0:T(8,128)(2,1)} %tokens_ref.1) | copy-start | bytes 196612
  0.8 0.7 %copy-start.1 = (s32[8,8]{1,0:T(8,128)S(1)}, s32[8,8]{1,0:T(8,128)}, u32[]{:S(2)}) copy-start(s32[8,8]{1,0:T(8,128)} %ids_ref.1) | copy-start | bytes 772
  1.5 0.7 %copy-start.2 = (f32[8,8]{1,0:T(8,128)S(1)}, f32[8,8]{1,0:T(8,128)}, u32[]{:S(2)}) copy-start(f32[8,8]{1,0:T(8,128)} %weights_ref.1) | copy-start | bytes 772
  2.3 8.4 %collective-permute-start.2 = (bf16[8,4224]{1,0:T(8,128)(2,1)S(1)}, bf16[8,4224]{1,0:T(8,128)(2,1)S(1)}, u32[]{:S(2)}, u32[]{:S(2)}) collective-permute-start(bf16[8,4224]{1,0:T(8,128)(2,1)S(1)} %shard_map.55.refs_0_), channel_id=1, source_target_pairs={{0,6},{1,7},{2,4},{3,5},{4,2},{5,3},{6,0},{7,1},{8,14},{9,15},{10,... | collective-permute-start | bytes 202760 | tf_op jit(solution)/shard_map/ppermute | solution.py:17
  7.4 5.8 %collective-permute-start.1 = (bf16[8,4224]{1,0:T(8,128)(2,1)S(1)}, bf16[8,4224]{1,0:T(8,128)(2,1)S(1)}, u32[]{:S(2)}, u32[]{:S(2)}) collective-permute-start(bf16[8,4224]{1,0:T(8,128)(2,1)S(1)} %shard_map.55.refs_0_), channel_id=1, source_target_pairs={{0,4},{1,5},{2,6},{3,7},{4,0},{5,1},{6,2},{7,3},{8,12},{9,13},{10,... | collective-permute-start | bytes 202760 | tf_op jit(solution)/shard_map/ppermute | solution.py:17
  7.4 5.8 %collective-permute-start = (bf16[8,4224]{1,0:T(8,128)(2,1)S(1)}, bf16[8,4224]{1,0:T(8,128)(2,1)S(1)}, u32[]{:S(2)}, u32[]{:S(2)}) collective-permute-start(bf16[8,4224]{1,0:T(8,128)(2,1)S(1)} %shard_map.55.refs_0_), channel_id=1, source_target_pairs={{0,2},{1,3},{2,0},{3,1},{4,6},{5,7},{6,4},{7,5},{8,10},{9,11},{10,... | collective-permute-start | bytes 202760 | tf_op jit(solution)/shard_map/ppermute | solution.py:17
  8.1 5.2 %collective-permute-start.3 = (bf16[8,4224]{1,0:T(8,128)(2,1)S(1)}, bf16[8,4224]{1,0:T(8,128)(2,1)S(1)}, u32[]{:S(2)}, u32[]{:S(2)}) collective-permute-start(bf16[8,4224]{1,0:T(8,128)(2,1)S(1)} %shard_map.55.refs_0_), channel_id=1, source_target_pairs={{0,24},{8,16},{16,8},{24,0},{1,25},{9,17},{17,9},{25,1},{2,26},{10... | collective-permute-start | bytes 202760 | tf_op jit(solution)/shard_map/ppermute | solution.py:17
  13.3 15.0 %collective-permute-start.5 = (bf16[32,4224]{1,0:T(8,128)(2,1)S(1)}, bf16[32,4224]{1,0:T(8,128)(2,1)S(1)}, u32[]{:S(2)}, u32[]{:S(2)}) collective-permute-start(bf16[32,4224]{1,0:T(8,128)(2,1)S(1)} %shard_map.56.refs_1_), channel_id=1, source_target_pairs={{0,16},{8,24},{16,0},{24,8},{1,17},{9,25},{17,1},{25,9},{2,18},{10... | collective-permute-start | bytes 811016 | tf_op jit(solution)/shard_map/ppermute | solution.py:17
  14.9 13.3 %collective-permute-start.4 = (bf16[32,4224]{1,0:T(8,128)(2,1)S(1)}, bf16[32,4224]{1,0:T(8,128)(2,1)S(1)}, u32[]{:S(2)}, u32[]{:S(2)}) collective-permute-start(bf16[32,4224]{1,0:T(8,128)(2,1)S(1)} %shard_map.56.refs_1_), channel_id=1, source_target_pairs={{0,8},{8,0},{16,24},{24,16},{1,9},{9,1},{17,25},{25,17},{2,10},{10... | collective-permute-start | bytes 811016 | tf_op jit(solution)/shard_map/ppermute | solution.py:17
  16.4 11.7 %collective-permute-start.8 = (bf16[8,4224]{1,0:T(8,128)(2,1)S(1)}, bf16[8,4224]{1,0:T(8,128)(2,1)S(1)}, u32[]{:S(2)}, u32[]{:S(2)}) collective-permute-start(bf16[8,4224]{1,0:T(8,128)(2,1)S(1)} %collective-permute-done.3.refs_0_), channel_id=1, source_target_pairs={{0,6},{1,7},{2,4},{3,5},{4,2},{5,3},{6,0},{7,1},{8,14},{9,15},{10,... | collective-permute-start | bytes 202760 | tf_op jit(solution)/shard_map/ppermute | solution.py:17
  20.0 8.2 %collective-permute-start.7 = (bf16[8,4224]{1,0:T(8,128)(2,1)S(1)}, bf16[8,4224]{1,0:T(8,128)(2,1)S(1)}, u32[]{:S(2)}, u32[]{:S(2)}) collective-permute-start(bf16[8,4224]{1,0:T(8,128)(2,1)S(1)} %collective-permute-done.3.refs_0_), channel_id=1, source_target_pairs={{0,4},{1,5},{2,6},{3,7},{4,0},{5,1},{6,2},{7,3},{8,12},{9,13},{10,... | collective-permute-start | bytes 202760 | tf_op jit(solution)/shard_map/ppermute | solution.py:17
  20.0 8.2 %collective-permute-start.6 = (bf16[8,4224]{1,0:T(8,128)(2,1)S(1)}, bf16[8,4224]{1,0:T(8,128)(2,1)S(1)}, u32[]{:S(2)}, u32[]{:S(2)}) collective-permute-start(bf16[8,4224]{1,0:T(8,128)(2,1)S(1)} %collective-permute-done.3.refs_0_), channel_id=1, source_target_pairs={{0,2},{1,3},{2,0},{3,1},{4,6},{5,7},{6,4},{7,5},{8,10},{9,11},{10,... | collective-permute-start | bytes 202760 | tf_op jit(solution)/shard_map/ppermute | solution.py:17
  28.1 1.6 %collective-permute-start.9 = (bf16[32,4224]{1,0:T(8,128)(2,1)S(1)}, bf16[32,4224]{1,0:T(8,128)(2,1)S(1)}, u32[]{:S(2)}, u32[]{:S(2)}) collective-permute-start(bf16[32,4224]{1,0:T(8,128)(2,1)S(1)} %shard_map.56.refs_1_), channel_id=1, source_target_pairs={{0,1},{1,0},{2,3},{3,2},{4,5},{5,4},{6,7},{7,6},{8,9},{9,8},{10,11... | collective-permute-start | bytes 811016 | tf_op jit(solution)/shard_map/ppermute | solution.py:17
  28.3 1.8 %collective-permute-start.12 = (bf16[32,4224]{1,0:T(8,128)(2,1)S(1)}, bf16[32,4224]{1,0:T(8,128)(2,1)S(1)}, u32[]{:S(2)}, u32[]{:S(2)}) collective-permute-start(bf16[32,4224]{1,0:T(8,128)(2,1)S(1)} %shard_map.58.refs_4_), channel_id=1, source_target_pairs={{0,1},{1,0},{2,3},{3,2},{4,5},{5,4},{6,7},{7,6},{8,9},{9,8},{10,11... | collective-permute-start | bytes 811016 | tf_op jit(solution)/shard_map/ppermute | solution.py:17
  28.8 1.7 %collective-permute-start.10 = (bf16[32,4224]{1,0:T(8,128)(2,1)S(1)}, bf16[32,4224]{1,0:T(8,128)(2,1)S(1)}, u32[]{:S(2)}, u32[]{:S(2)}) collective-permute-start(bf16[32,4224]{1,0:T(8,128)(2,1)S(1)} %collective-permute-done.4.refs_2_), channel_id=1, source_target_pairs={{0,1},{1,0},{2,3},{3,2},{4,5},{5,4},{6,7},{7,6},{8,9},{9,8},{10,11... | collective-permute-start | bytes 811016 | tf_op jit(solution)/shard_map/ppermute | solution.py:17
  28.9 2.0 %collective-permute-start.11 = (bf16[32,4224]{1,0:T(8,128)(2,1)S(1)}, bf16[32,4224]{1,0:T(8,128)(2,1)S(1)}, u32[]{:S(2)}, u32[]{:S(2)}) collective-permute-start(bf16[32,4224]{1,0:T(8,128)(2,1)S(1)} %collective-permute-done.5.refs_3_), channel_id=1, source_target_pairs={{0,1},{1,0},{2,3},{3,2},{4,5},{5,4},{6,7},{7,6},{8,9},{9,8},{10,11... | collective-permute-start | bytes 811016 | tf_op jit(solution)/shard_map/ppermute | solution.py:17
  36.3 2.7 %collective-permute-start.13 = (bf16[4,32,4096]{2,1,0:T(8,128)(2,1)S(1)}, bf16[4,32,4096]{2,1,0:T(8,128)(2,1)S(1)}, u32[]{:S(2)}, u32[]{:S(2)}) collective-permute-start(bf16[4,32,4096]{2,1,0:T(8,128)(2,1)S(1)} %get-tuple-element.30), channel_id=1, source_target_pairs={{0,1},{1,0},{2,3},{3,2},{4,5},{5,4},{6,7},{7,6},{8,9},{9,8},{10,11... | collective-permute-start | bytes 3145736 | tf_op jit(solution)/shard_map/ppermute | solution.py:17
  39.4 5.4 %collective-permute-start.16 = (bf16[8,4096]{1,0:T(8,128)(2,1)S(1)}, bf16[8,4096]{1,0:T(8,128)(2,1)S(1)}, u32[]{:S(2)}, u32[]{:S(2)}) collective-permute-start(bf16[8,4096]{1,0:T(8,128)(2,1)S(1)} %get-tuple-element.35), channel_id=1, source_target_pairs={{0,2},{1,3},{2,0},{3,1},{4,6},{5,7},{6,4},{7,5},{8,10},{9,11},{10,... | collective-permute-start | bytes 196616 | tf_op jit(solution)/shard_map/ppermute | solution.py:17
  40.7 6.6 %collective-permute-start.18 = (bf16[8,4096]{1,0:T(8,128)(2,1)S(1)}, bf16[8,4096]{1,0:T(8,128)(2,1)S(1)}, u32[]{:S(2)}, u32[]{:S(2)}) collective-permute-start(bf16[8,4096]{1,0:T(8,128)(2,1)S(1)} %get-tuple-element.36), channel_id=1, source_target_pairs={{0,6},{1,7},{2,4},{3,5},{4,2},{5,3},{6,0},{7,1},{8,14},{9,15},{10,... | collective-permute-start | bytes 196616 | tf_op jit(solution)/shard_map/ppermute | solution.py:17
  43.2 6.9 %collective-permute-start.17 = (bf16[8,4096]{1,0:T(8,128)(2,1)S(1)}, bf16[8,4096]{1,0:T(8,128)(2,1)S(1)}, u32[]{:S(2)}, u32[]{:S(2)}) collective-permute-start(bf16[8,4096]{1,0:T(8,128)(2,1)S(1)} %get-tuple-element.37), channel_id=1, source_target_pairs={{0,4},{1,5},{2,6},{3,7},{4,0},{5,1},{6,2},{7,3},{8,12},{9,13},{10,... | collective-permute-start | bytes 196616 | tf_op jit(solution)/shard_map/ppermute | solution.py:17
  43.7 8.0 %collective-permute-start.14 = (bf16[32,4096]{1,0:T(8,128)(2,1)S(1)}, bf16[32,4096]{1,0:T(8,128)(2,1)S(1)}, u32[]{:S(2)}, u32[]{:S(2)}) collective-permute-start(bf16[32,4096]{1,0:T(8,128)(2,1)S(1)} %get-tuple-element.38), channel_id=1, source_target_pairs={{0,8},{8,0},{16,24},{24,16},{1,9},{9,1},{17,25},{25,17},{2,10},{10... | collective-permute-start | bytes 786440 | tf_op jit(solution)/shard_map/ppermute | solution.py:17
  44.3 7.6 %collective-permute-start.15 = (bf16[32,4096]{1,0:T(8,128)(2,1)S(1)}, bf16[32,4096]{1,0:T(8,128)(2,1)S(1)}, u32[]{:S(2)}, u32[]{:S(2)}) collective-permute-start(bf16[32,4096]{1,0:T(8,128)(2,1)S(1)} %get-tuple-element.39), channel_id=1, source_target_pairs={{0,16},{8,24},{16,0},{24,8},{1,17},{9,25},{17,1},{25,9},{2,18},{10... | collective-permute-start | bytes 786440 | tf_op jit(solution)/shard_map/ppermute | solution.py:17
  50.2 6.5 %collective-permute-start.19 = (bf16[8,4096]{1,0:T(8,128)(2,1)S(1)}, bf16[8,4096]{1,0:T(8,128)(2,1)S(1)}, u32[]{:S(2)}, u32[]{:S(2)}) collective-permute-start(bf16[8,4096]{1,0:T(8,128)(2,1)S(1)} %fusion.5), channel_id=1, source_target_pairs={{0,24},{8,16},{16,8},{24,0},{1,25},{9,17},{17,9},{25,1},{2,26},{10... | collective-permute-start | bytes 196616 | tf_op jit(solution)/shard_map/ppermute | solution.py:17
  52.1 5.0 %collective-permute-start.20 = (bf16[8,4096]{1,0:T(8,128)(2,1)S(1)}, bf16[8,4096]{1,0:T(8,128)(2,1)S(1)}, u32[]{:S(2)}, u32[]{:S(2)}) collective-permute-start(bf16[8,4096]{1,0:T(8,128)(2,1)S(1)} %get-tuple-element.40), channel_id=1, source_target_pairs={{0,2},{1,3},{2,0},{3,1},{4,6},{5,7},{6,4},{7,5},{8,10},{9,11},{10,... | collective-permute-start | bytes 196616 | tf_op jit(solution)/shard_map/ppermute | solution.py:17
  54.0 6.1 %collective-permute-start.22 = (bf16[8,4096]{1,0:T(8,128)(2,1)S(1)}, bf16[8,4096]{1,0:T(8,128)(2,1)S(1)}, u32[]{:S(2)}, u32[]{:S(2)}) collective-permute-start(bf16[8,4096]{1,0:T(8,128)(2,1)S(1)} %get-tuple-element.41), channel_id=1, source_target_pairs={{0,6},{1,7},{2,4},{3,5},{4,2},{5,3},{6,0},{7,1},{8,14},{9,15},{10,... | collective-permute-start | bytes 196616 | tf_op jit(solution)/shard_map/ppermute | solution.py:17
  56.7 5.2 %collective-permute-start.21 = (bf16[8,4096]{1,0:T(8,128)(2,1)S(1)}, bf16[8,4096]{1,0:T(8,128)(2,1)S(1)}, u32[]{:S(2)}, u32[]{:S(2)}) collective-permute-start(bf16[8,4096]{1,0:T(8,128)(2,1)S(1)} %get-tuple-element.42), channel_id=1, source_target_pairs={{0,4},{1,5},{2,6},{3,7},{4,0},{5,1},{6,2},{7,3},{8,12},{9,13},{10,... | collective-permute-start | bytes 196616 | tf_op jit(solution)/shard_map/ppermute | solution.py:17

commit v3 on v2

--- a/solution.py
+++ b/solution.py
@@ -10,6 +10,11 @@
 LANES = 128
 MIB = 1 << 20
 VMEM = pl.BlockSpec(memory_space=pltpu.VMEM)
+HBM = pl.BlockSpec(memory_space=pltpu.HBM)
+
+
+def in_hbm(*arrays):
+    return [pltpu.with_memory_space_constraint(array, pltpu.HBM) for array in arrays]
 
 
 def swap(block, axis, flips):
@@ -17,7 +22,19 @@
     return lax.ppermute(block, axis, [(i, i ^ flips) for i in range(size)])
 
 
-def pack_kernel(experts, tokens_ref, ids_ref, weights_ref, packed_ref):
+def pack_kernel(
+    experts, tokens_hbm, ids_hbm, weights_hbm, packed_ref, tokens_ref, ids_ref, weights_ref, sems
+):
+    copies = [
+        pltpu.make_async_copy(source, target, sems.at[i])
+        for i, (source, target) in enumerate(
+            ((ids_hbm, ids_ref), (weights_hbm, weights_ref), (tokens_hbm, tokens_ref))
+        )
+    ]
+    for copy in copies:
+        copy.start()
+    for copy in copies:
+        copy.wait()
     rows, width = tokens_ref.shape
     tail = packed_ref.shape[1] - width
     packed_ref[:, :width] = tokens_ref[...]
@@ -41,68 +58,79 @@
     return pl.pallas_call(
         functools.partial(pack_kernel, experts),
         out_shape=jax.ShapeDtypeStruct((rows, width + tail), jnp.bfloat16),
-        in_specs=[VMEM] * 3,
+        in_specs=[HBM] * 3,
         out_specs=VMEM,
+        scratch_shapes=[
+            pltpu.VMEM(tokens.shape, tokens.dtype),
+            pltpu.VMEM(expert_ids.shape, expert_ids.dtype),
+            pltpu.VMEM(route_weights.shape, route_weights.dtype),
+            pltpu.SemaphoreType.DMA((3,)),
+        ],
         compiler_params=pltpu.CompilerParams(vmem_limit_bytes=2 * MIB),
-    )(tokens, expert_ids, route_weights)
+    )(*in_hbm(tokens, expert_ids, route_weights))
 
 
 def stack_kernel(*refs):
     out_ref = refs[-1]
     start = 0
-    for ref in refs[:-1]:
+    for ref in refs[1:-2]:
         out_ref[start : start + ref.shape[0], :] = ref[...]
         start += ref.shape[0]
 
 
-def stack(blocks):
+def stack(win, blocks):
     rows = sum(block.shape[0] for block in blocks)
     return pl.pallas_call(
         stack_kernel,
-        out_shape=jax.ShapeDtypeStruct((rows, blocks[0].shape[1]), blocks[0].dtype),
-        in_specs=[VMEM] * len(blocks),
-        out_specs=VMEM,
-        compiler_params=pltpu.CompilerParams(vmem_limit_bytes=4 * MIB),
-    )(*blocks)
-
-
-def load_kernel(in_ref, out_ref, in_vmem, out_vmem, sems):
+        out_shape=(
+            pltpu.VMEM(win.shape, win.dtype),
+            jax.ShapeDtypeStruct((rows, blocks[0].shape[1]), blocks[0].dtype),
+        ),
+        in_specs=[VMEM] * (1 + len(blocks)),
+        out_specs=[VMEM] * 2,
+        input_output_aliases={0: 0},
+        compiler_params=pltpu.CompilerParams(vmem_limit_bytes=2 * MIB),
+    )(pltpu.with_memory_space_constraint(win, pltpu.VMEM), *blocks)
+
+
+def load_kernel(in_ref, in_vmem, sems):
     tiles = in_vmem.shape[0]
     copies = [
         pltpu.make_async_copy(in_ref.at[:, :, pl.ds(t * LANES, LANES)], in_vmem.at[t], sems.at[t])
         for t in range(tiles)
     ]
-    copies.append(pltpu.make_async_copy(out_ref, out_vmem, sems.at[tiles]))
     for copy in copies:
         copy.start()
     for copy in copies:
         copy.wait()
 
 
-def load_weights(w_in, w_out):
+def load_weights(w_in):
     units, _, width = w_in.shape
     tiles = width // LANES
-    win, wout = pl.pallas_call(
+    loaded = pl.pallas_call(
         load_kernel,
-        out_shape=(
-            pltpu.VMEM((tiles, units, 2, LANES), w_in.dtype),
-            pltpu.VMEM(w_out.shape, w_out.dtype),
-        ),
-        in_specs=[pl.BlockSpec(memory_space=pltpu.HBM)] * 2,
-        out_specs=[VMEM] * 2,
-        scratch_shapes=[pltpu.SemaphoreType.DMA((tiles + 1,))],
+        out_shape=pltpu.VMEM((tiles, units, 2, LANES), w_in.dtype),
+        in_specs=[HBM],
+        out_specs=VMEM,
+        scratch_shapes=[pltpu.SemaphoreType.DMA((tiles,))],
         compiler_params=pltpu.CompilerParams(vmem_limit_bytes=2 * MIB),
-        cost_estimate=pl.CostEstimate(
-            flops=0, bytes_accessed=4 * (w_in.size + w_out.size), transcendentals=0
-        ),
-    )(*(pltpu.with_memory_space_constraint(w, pltpu.HBM) for w in (w_in, w_out)))
-    return win.reshape(tiles, units * 2, LANES), wout
-
-
-def expert_kernel(exp_dev, half, *refs):
-    select_ref = refs[0]
+        cost_estimate=pl.CostEstimate(flops=0, bytes_accessed=4 * w_in.size, transcendentals=0),
+    )(*in_hbm(w_in))
+    return loaded.reshape(tiles, units * 2, LANES)
+
+
+def expert_kernel(exp_dev, experts, half, *refs):
+    group_ref = refs[0]
     x_refs = refs[1 : 1 + 2 * half]
-    win_ref, wout_ref, send_ref, keep_ref, mixed, hidden = refs[1 + 2 * half :]
+    win_ref, wout_hbm, send_ref, keep_ref, mixed, hidden, wout_ref, sem = refs[1 + 2 * half :]
+    first = pl.program_id(0) == 0
+    load = pltpu.make_async_copy(wout_hbm, wout_ref, sem)
+
+    @pl.when(first)
+    def _():
+        load.start()
+
     lines = win_ref.shape[1]
     width = win_ref.shape[0] * LANES
     per = lines // exp_dev
@@ -111,8 +139,11 @@
     x = jnp.concatenate([ref[:, :width] for ref in x_refs], axis=0)
     tail = jnp.concatenate([ref[:, width:] for ref in x_refs], axis=0)
     contract_last = (((1,), (1,)), ((), ()))
+    column = lax.broadcasted_iota(jnp.int32, (16, tail.shape[1]), 1)
+    wanted = lax.broadcasted_iota(jnp.int32, (16, tail.shape[1]), 0) + group_ref[0] * exp_dev
+    select = (column % experts == wanted) & (column < 3 * experts)
     scale = lax.dot_general(
-        select_ref[...], tail, contract_last, preferred_element_type=jnp.float32
+        select.astype(jnp.bfloat16), tail, contract_last, preferred_element_type=jnp.float32
     )
     for e in range(exp_dev):
         w = jnp.concatenate(
@@ -125,6 +156,11 @@
             up = mixed[pl.ds(1, per // 2, stride=2), :]
             act = gate / (1.0 + jnp.exp(-gate)) * up * scale[e : e + 1, r : r + LANES]
             hidden[pl.ds(e * per // 2, per // 2), r : r + LANES] = act.astype(jnp.bfloat16)
+
+    @pl.when(first)
+    def _():
+        load.wait()
+
     chunk = min(512, width)
     for c in range(0, width, chunk):
         part = lax.dot_general(
@@ -139,7 +175,7 @@
             send_ref[b, :, c : c + chunk] = other.astype(jnp.bfloat16)
 
 
-def run_experts(select, blocks, win, wout, exp_dev):
+def run_experts(group, blocks, win, wout, exp_dev, experts):
     half = len(blocks) // 2
     block_rows, packed_width = blocks[0].shape
     width = wout.shape[1]
@@ -149,30 +185,32 @@
     out_block = pl.BlockSpec((half, block, width), lambda i: (0, i, 0))
     planned = 2 * rows * (2 * packed_width + 3 * width) + rows * (4 * lines + 4 * width)
     return pl.pallas_call(
-        functools.partial(expert_kernel, exp_dev, half),
+        functools.partial(expert_kernel, exp_dev, experts, half),
         grid=(block_rows // block,),
         out_shape=(
             jax.ShapeDtypeStruct((half, block_rows, width), jnp.bfloat16),
             jax.ShapeDtypeStruct((half, block_rows, width), jnp.float32),
         ),
         in_specs=[
-            pl.BlockSpec(select.shape, lambda i: (0, 0)),
+            pl.BlockSpec(memory_space=pltpu.SMEM),
             *[pl.BlockSpec((block, packed_width), lambda i: (i, 0))] * (2 * half),
             VMEM,
-            VMEM,
+            HBM,
         ],
         out_specs=[out_block, out_block],
         scratch_shapes=[
             pltpu.VMEM((lines // exp_dev, LANES), jnp.float32),
             pltpu.VMEM((lines // 2, rows), jnp.bfloat16),
+            pltpu.VMEM(wout.shape, wout.dtype),
+            pltpu.SemaphoreType.DMA,
         ],
-        compiler_params=pltpu.CompilerParams(vmem_limit_bytes=planned + 2 * MIB),
+        compiler_params=pltpu.CompilerParams(vmem_limit_bytes=planned + 2 * wout.size + 2 * MIB),
         cost_estimate=pl.CostEstimate(
             flops=6 * half * block_rows * width * lines,
             bytes_accessed=4 * half * block_rows * packed_width + 6 * half * block_rows * width,
             transcendentals=half * block_rows * lines,
         ),
-    )(select, *blocks, win, wout)
+    )(group, *blocks, pltpu.with_memory_space_constraint(win, pltpu.VMEM), *in_hbm(wout))
 
 
 def body(tokens, expert_ids, route_weights, in_weights, out_weights):
@@ -187,24 +225,20 @@
     w_out = out_weights.reshape(exp_dev * units, width)
 
     x = pack(tokens, expert_ids, route_weights, experts)
+    group = lax.axis_index("expert").astype(jnp.int32).reshape(1)
+    x, w_in, group = lax.optimization_barrier((x, w_in, group))
     along = [swap(x, "expert", 2 * r) for r in range(1, chips)]
     across = swap(x, "batch", far)
-    mine = stack([x] + along)
-    mine, across, w_in = lax.optimization_barrier((mine, across, w_in))
-    blocks = [swap(mine, "batch", b) for b in range(1, far)]
+    win = load_weights(w_in)
+    along, across, win = lax.optimization_barrier((along, across, win))
+    win, mine = stack(win, [x] + along)
+    blocks = [mine] + [swap(mine, "batch", b) for b in range(1, far)]
     others = [swap(across, "expert", 2 * r) for r in range(1, chips)]
-    win, wout = load_weights(w_in, w_out)
-    blocks, others, win = lax.optimization_barrier((blocks, others, win))
-    blocks = [mine] + blocks + [stack([across] + others)]
+    win, last = stack(win, [across] + others)
+    blocks.append(last)
     blocks = blocks + [swap(block, "expert", 1) for block in blocks]
 
-    tail = x.shape[1] - width
-    wanted = lax.axis_index("expert") * exp_dev + jnp.arange(exp_dev, dtype=jnp.int32)
-    column = jnp.arange(tail, dtype=jnp.int32)
-    select = (column[None, :] % experts == wanted[:, None]) & (column < 3 * experts)[None, :]
-    select = jnp.pad(select.astype(jnp.bfloat16), ((0, -exp_dev % 16), (0, 0)))
-
-    send, total = run_experts(select, blocks, win, wout, exp_dev)
+    send, total = run_experts(group, blocks, win, w_out, exp_dev, experts)
     total = total + swap(send, "expert", 1).astype(jnp.float32)
     rounded = total.astype(jnp.bfloat16)
     mine = total[0]

time: 62.8 us -> 62.7 us (level)
  local copies, waits for them, and re-layouts: 2.28 us -> 0.07 us
  Pallas kernels: 12.8 us -> 14.4 us
  starting transfers between devices: 27.9 us -> 29.2 us
  waiting for transfers between devices: 18.2 us -> 17.5 us
    unnamed x6 -> x0, local copies, waits for them, and re-layouts: 2.21 us -> none
    ppermute x23, starting transfers between devices: 27.9 us -> 29.2 us  [swap(): return lax.ppermute(block, axis, [(i, i ^ flips) for i in range(size)])]
    pallas_call x1, Pallas kernels: 0.1 us -> 1 us  [pack(): pl.pallas_call(functools.partial(pack_kernel, experts), out_shape=jax.Sha...]
    pallas_call x4, Pallas kernels: 12.7 us -> 13.4 us  [the longest x1 8.05 us: run_experts(): pl.pallas_call(functools.partial(expert_kernel, exp_dev, experts, half),...]
    ppermute x23, waiting for transfers between devices: 18.2 us -> 17.5 us  [swap(): return lax.ppermute(block, axis, [(i, i ^ flips) for i in range(size)])]
  transfers between devices with their start and end apart: 23 -> 23, of which waited for: 13 -> 11; matrix products, arithmetic and copies ran while one was open for 0% -> 0% of each run, Pallas kernels for 12% -> 9%
where the time goes in v3:
time: 62.7 us; the launch traced here: 62.5 us
  starting transfers between devices  29.2 us (47%)
  waiting for transfers between devices  17.5 us (28%)
  Pallas kernels  14.4 us (23%)
  other arithmetic  1.19 us (2%)
    ppermute x23, starting transfers between devices, swap(): return lax.ppermute(block, axis, [(i, i ^ flips) for i in range(size)])  29.2 us
    ppermute x23, waiting for transfers between devices, swap(): return lax.ppermute(block, axis, [(i, i ^ flips) for i in range(size)])  17.5 us
    pallas_call x1, Pallas kernels, run_experts(): pl.pallas_call(functools.partial(expert_kernel, exp_dev, experts, half),...  8.05 us
    pallas_call x1, Pallas kernels, load_weights(): pl.pallas_call(load_kernel, out_shape=pltpu.VMEM((tiles, units, 2, LANES)...  5.36 us
  transfers between devices with their start and end apart: 23, of which 11 were waited for; matrix products, arithmetic and copies ran while one was open for 0% of the time, Pallas kernels for 9%

profile of v3, /device:TPU:0, one launch (start us, length us, event | category | flops | bytes accessed | tf_op | source)
XLA Modules:
  0.0 62.5 jit_solution(5869425364685357510)
XLA Ops:
  0.0 1.0 %shard_map.55.refs_1_ = bf16[8,4224]{1,0:T(8,128)(2,1)S(1)} custom-call(bf16[8,4096]{1,0:T(8,128)(2,1)} %tokens_hbm.1, s32[8,8]{1,0:T(8,128)} %ids_hbm.1, f32[8,8]{1,0:T(8,128)} %weights_hbm.1), custom_call_target="tpu_custom_call" | custom-call | tf_op jit(solution)/shard_map/pallas_call | solution.py:58
  1.0 4.0 %collective-permute-start.3 = (bf16[8,4224]{1,0:T(8,128)(2,1)S(1)}, bf16[8,4224]{1,0:T(8,128)(2,1)S(1)}, u32[]{:S(2)}, u32[]{:S(2)}) collective-permute-start(bf16[8,4224]{1,0:T(8,128)(2,1)S(1)} %shard_map.55.refs_1_), channel_id=1, source_target_pairs={{0,24},{8,16},{16,8},{24,0},{1,25},{9,17},{17,9},{25,1},{2,26},{10... | collective-permute-start | bytes 202760 | tf_op jit(solution)/shard_map/ppermute | solution.py:22
  5.0 3.6 %collective-permute-start.2 = (bf16[8,4224]{1,0:T(8,128)(2,1)S(1)}, bf16[8,4224]{1,0:T(8,128)(2,1)S(1)}, u32[]{:S(2)}, u32[]{:S(2)}) collective-permute-start(bf16[8,4224]{1,0:T(8,128)(2,1)S(1)} %shard_map.55.refs_1_), channel_id=1, source_target_pairs={{0,6},{1,7},{2,4},{3,5},{4,2},{5,3},{6,0},{7,1},{8,14},{9,15},{10,... | collective-permute-start | bytes 202760 | tf_op jit(solution)/shard_map/ppermute | solution.py:22
  8.6 0.0 collective-permute-start.1
  8.6 0.8 %collective-permute-start = (bf16[8,4224]{1,0:T(8,128)(2,1)S(1)}, bf16[8,4224]{1,0:T(8,128)(2,1)S(1)}, u32[]{:S(2)}, u32[]{:S(2)}) collective-permute-start(bf16[8,4224]{1,0:T(8,128)(2,1)S(1)} %shard_map.55.refs_1_), channel_id=1, source_target_pairs={{0,2},{1,3},{2,0},{3,1},{4,6},{5,7},{6,4},{7,5},{8,10},{9,11},{10,... | collective-permute-start | bytes 202760 | tf_op jit(solution)/shard_map/ppermute | solution.py:22
  9.4 5.4 %shard_map.56 = bf16[32,768,2,128]{3,2,1,0:T(2,128)(2,1)S(1)} custom-call(bf16[768,2,4096]{2,1,0:T(2,128)(2,1)} %bitcast.32), custom_call_target="tpu_custom_call" | custom-call | bytes 25165824 | tf_op jit(solution)/shard_map/pallas_call | solution.py:111
  14.7 0.0 collective-permute-done.3.refs_1_
  14.7 0.0 collective-permute-done.2.refs_4_
  14.7 0.0 collective-permute-done.1.refs_3_
  14.8 0.0 collective-permute-done.refs_2_
  14.8 0.6 collective-permute-start.5
  15.4 0.3 collective-permute-start.4
  15.7 3.8 %collective-permute-start.8 = (bf16[8,4224]{1,0:T(8,128)(2,1)S(1)}, bf16[8,4224]{1,0:T(8,128)(2,1)S(1)}, u32[]{:S(2)}, u32[]{:S(2)}) collective-permute-start(bf16[8,4224]{1,0:T(8,128)(2,1)S(1)} %collective-permute-done.3.refs_1_), channel_id=1, source_target_pairs={{0,6},{1,7},{2,4},{3,5},{4,2},{5,3},{6,0},{7,1},{8,14},{9,15},{10,... | collective-permute-start | bytes 202760 | tf_op jit(solution)/shard_map/ppermute | solution.py:22
  19.5 0.0 collective-permute-start.7
  19.5 0.6 collective-permute-start.6
  20.1 1.8 %collective-permute-done.8.refs_4_ = bf16[8,4224]{1,0:T(8,128)(2,1)S(1)} collective-permute-done((bf16[8,4224]{1,0:T(8,128)(2,1)S(1)}, bf16[8,4224]{1,0:T(8,128)(2,1)S(1)}, u32[]{:S(2)}, u32[]{:S(2)}) %collective-permute-start.8) | collective-permute-done | bytes 67616 | tf_op jit(solution)/shard_map/ppermute | solution.py:22
  21.9 0.0 collective-permute-start.9
  21.9 2.8 %collective-permute-done.7.refs_3_ = bf16[8,4224]{1,0:T(8,128)(2,1)S(1)} collective-permute-done((bf16[8,4224]{1,0:T(8,128)(2,1)S(1)}, bf16[8,4224]{1,0:T(8,128)(2,1)S(1)}, u32[]{:S(2)}, u32[]{:S(2)}) %collective-permute-start.7) | collective-permute-done | bytes 67616 | tf_op jit(solution)/shard_map/ppermute | solution.py:22
  24.7 0.0 collective-permute-done.6.refs_2_
  24.7 0.1 collective-permute-start.12
  24.8 0.0 collective-permute-done.5.refs_3_
  24.8 0.5 collective-permute-start.11
  25.3 0.0 collective-permute-done.4.refs_2_
  25.3 0.1 collective-permute-start.10
  25.4 0.0 collective-permute-done.9.refs_5_
  25.4 0.9 %collective-permute-done.12.refs_8_ = bf16[32,4224]{1,0:T(8,128)(2,1)S(1)} collective-permute-done((bf16[32,4224]{1,0:T(8,128)(2,1)S(1)}, bf16[32,4224]{1,0:T(8,128)(2,1)S(1)}, u32[]{:S(2)}, u32[]{:S(2)}) %collective-permute-start.12) | collective-permute-done | bytes 270368 | tf_op jit(solution)/shard_map/ppermute | solution.py:22
  26.3 0.4 collective-permute-done.11.refs_7_
  26.7 0.4 collective-permute-done.10.refs_6_
  27.1 8.1 %shard_map.59 = (bf16[4,32,4096]{2,1,0:T(8,128)(2,1)S(1)}, f32[4,32,4096]{2,1,0:T(8,128)S(1)}) custom-call(s32[1]{0:T(128)} %bitcast.1.refs_0_, bf16[32,4224]{1,0:T(8,128)(2,1)S(1)} %get-tuple-element.26.refs_1_, bf16[32,4224]{1,0:T(8,128)(2,1)S(1)} %collective-permute-done.4.refs_2_, bf16[32,4224]{1,0:T(8,128)(2,1)S(1)} %collective-permute-done.5.refs_3_, ...), custom_call_target="tpu_custom_call" | custom-call | flops 4831838208 | bytes 5308416 | tf_op jit(solution)/shard_map/pallas_call | solution.py:187
  35.2 0.2 collective-permute-start.13
  35.4 2.5 %collective-permute-done.13 = bf16[4,32,4096]{2,1,0:T(8,128)(2,1)S(1)} collective-permute-done((bf16[4,32,4096]{2,1,0:T(8,128)(2,1)S(1)}, bf16[4,32,4096]{2,1,0:T(8,128)(2,1)S(1)}, u32[]{:S(2)}, u32[]{:S(2)}) %collective-permute-start.13) | collective-permute-done | bytes 1048608 | tf_op jit(solution)/shard_map/ppermute | solution.py:22
  37.9 0.4 fusion.12
  38.3 0.6 %collective-permute-start.16 = (bf16[8,4096]{1,0:T(8,128)(2,1)S(1)}, bf16[8,4096]{1,0:T(8,128)(2,1)S(1)}, u32[]{:S(2)}, u32[]{:S(2)}) collective-permute-start(bf16[8,4096]{1,0:T(8,128)(2,1)S(1)} %get-tuple-element.37), channel_id=1, source_target_pairs={{0,2},{1,3},{2,0},{3,1},{4,6},{5,7},{6,4},{7,5},{8,10},{9,11},{10,... | collective-permute-start | bytes 196616 | tf_op jit(solution)/shard_map/ppermute | solution.py:22
  38.9 2.9 %collective-permute-start.18 = (bf16[8,4096]{1,0:T(8,128)(2,1)S(1)}, bf16[8,4096]{1,0:T(8,128)(2,1)S(1)}, u32[]{:S(2)}, u32[]{:S(2)}) collective-permute-start(bf16[8,4096]{1,0:T(8,128)(2,1)S(1)} %get-tuple-element.38), channel_id=1, source_target_pairs={{0,6},{1,7},{2,4},{3,5},{4,2},{5,3},{6,0},{7,1},{8,14},{9,15},{10,... | collective-permute-start | bytes 196616 | tf_op jit(solution)/shard_map/ppermute | solution.py:22
  41.8 0.0 collective-permute-start.17
  41.9 1.6 %collective-permute-start.14 = (bf16[32,4096]{1,0:T(8,128)(2,1)S(1)}, bf16[32,4096]{1,0:T(8,128)(2,1)S(1)}, u32[]{:S(2)}, u32[]{:S(2)}) collective-permute-start(bf16[32,4096]{1,0:T(8,128)(2,1)S(1)} %get-tuple-element.40), channel_id=1, source_target_pairs={{0,8},{8,0},{16,24},{24,16},{1,9},{9,1},{17,25},{25,17},{2,10},{10... | collective-permute-start | bytes 786440 | tf_op jit(solution)/shard_map/ppermute | solution.py:22
  43.5 1.5 %collective-permute-start.15 = (bf16[32,4096]{1,0:T(8,128)(2,1)S(1)}, bf16[32,4096]{1,0:T(8,128)(2,1)S(1)}, u32[]{:S(2)}, u32[]{:S(2)}) collective-permute-start(bf16[32,4096]{1,0:T(8,128)(2,1)S(1)} %get-tuple-element.41), channel_id=1, source_target_pairs={{0,16},{8,24},{16,0},{24,8},{1,17},{9,25},{17,1},{25,9},{2,18},{10... | collective-permute-start | bytes 786440 | tf_op jit(solution)/shard_map/ppermute | solution.py:22
  45.0 0.0 collective-permute-done.16
  45.0 1.2 %collective-permute-done.18 = bf16[8,4096]{1,0:T(8,128)(2,1)S(1)} collective-permute-done((bf16[8,4096]{1,0:T(8,128)(2,1)S(1)}, bf16[8,4096]{1,0:T(8,128)(2,1)S(1)}, u32[]{:S(2)}, u32[]{:S(2)}) %collective-permute-start.18) | collective-permute-done | bytes 65568 | tf_op jit(solution)/shard_map/ppermute | solution.py:22
  46.2 2.0 %collective-permute-done.17 = bf16[8,4096]{1,0:T(8,128)(2,1)S(1)} collective-permute-done((bf16[8,4096]{1,0:T(8,128)(2,1)S(1)}, bf16[8,4096]{1,0:T(8,128)(2,1)S(1)}, u32[]{:S(2)}, u32[]{:S(2)}) %collective-permute-start.17) | collective-permute-done | bytes 65568 | tf_op jit(solution)/shard_map/ppermute | solution.py:22
  48.2 2.5 %collective-permute-start.19 = (bf16[8,4096]{1,0:T(8,128)(2,1)S(1)}, bf16[8,4096]{1,0:T(8,128)(2,1)S(1)}, u32[]{:S(2)}, u32[]{:S(2)}) collective-permute-start(bf16[8,4096]{1,0:T(8,128)(2,1)S(1)} %fusion.5), channel_id=1, source_target_pairs={{0,24},{8,16},{16,8},{24,0},{1,25},{9,17},{17,9},{25,1},{2,26},{10... | collective-permute-start | bytes 196616 | tf_op jit(solution)/shard_map/ppermute | solution.py:22
  50.7 0.0 collective-permute-done.14
  50.7 0.2 collective-permute-done.15
  51.0 0.1 fusion.10
  51.1 2.7 %collective-permute-start.20 = (bf16[8,4096]{1,0:T(8,128)(2,1)S(1)}, bf16[8,4096]{1,0:T(8,128)(2,1)S(1)}, u32[]{:S(2)}, u32[]{:S(2)}) collective-permute-start(bf16[8,4096]{1,0:T(8,128)(2,1)S(1)} %get-tuple-element.42), channel_id=1, source_target_pairs={{0,2},{1,3},{2,0},{3,1},{4,6},{5,7},{6,4},{7,5},{8,10},{9,11},{10,... | collective-permute-start | bytes 196616 | tf_op jit(solution)/shard_map/ppermute | solution.py:22
  53.7 2.9 %collective-permute-start.22 = (bf16[8,4096]{1,0:T(8,128)(2,1)S(1)}, bf16[8,4096]{1,0:T(8,128)(2,1)S(1)}, u32[]{:S(2)}, u32[]{:S(2)}) collective-permute-start(bf16[8,4096]{1,0:T(8,128)(2,1)S(1)} %get-tuple-element.43), channel_id=1, source_target_pairs={{0,6},{1,7},{2,4},{3,5},{4,2},{5,3},{6,0},{7,1},{8,14},{9,15},{10,... | collective-permute-start | bytes 196616 | tf_op jit(solution)/shard_map/ppermute | solution.py:22
  56.7 0.0 collective-permute-start.21
  56.7 0.0 collective-permute-done.19
  56.7 0.0 collective-permute-done.20
  56.7 3.1 %collective-permute-done.22 = bf16[8,4096]{1,0:T(8,128)(2,1)S(1)} collective-permute-done((bf16[8,4096]{1,0:T(8,128)(2,1)S(1)}, bf16[8,4096]{1,0:T(8,128)(2,1)S(1)}, u32[]{:S(2)}, u32[]{:S(2)}) %collective-permute-start.22) | collective-permute-done | bytes 65568 | tf_op jit(solution)/shard_map/ppermute | solution.py:22
  59.8 2.0 %collective-permute-done.21 = bf16[8,4096]{1,0:T(8,128)(2,1)S(1)} collective-permute-done((bf16[8,4096]{1,0:T(8,128)(2,1)S(1)}, bf16[8,4096]{1,0:T(8,128)(2,1)S(1)}, u32[]{:S(2)}, u32[]{:S(2)}) %collective-permute-start.21) | collective-permute-done | bytes 65568 | tf_op jit(solution)/shard_map/ppermute | solution.py:22
  61.8 0.7 %fusion.9 = bf16[8,4096]{1,0:T(8,128)(2,1)} fusion(f32[32,4096]{1,0:T(8,128)S(1)} %get-tuple-element.34, bf16[8,4096]{1,0:T(8,128)(2,1)S(1)} %collective-permute-done.22, bf16[8,4096]{1,0:T(8,128)(2,1)S(1)} %collective-permute-done.21, bf16[8,4096]{1,0:T(8,128)(2,1)S(1)} %collective-permute-done.20, bf16[8,4096]{1,0:T(8,128)(2,1)S(1)} %collective-permute-done.19), kind=kLoop, calls=%fused_computation.15 | loop fusion | flops 294912 | bytes 458752 | tf_op jit(solution)/shard_map/convert_element_type | solution.py:256
  (6 shorter events, 0.1 us)
Async XLA Ops:
  1.0 13.7 %collective-permute-start.3 = (bf16[8,4224]{1,0:T(8,128)(2,1)S(1)}, bf16[8,4224]{1,0:T(8,128)(2,1)S(1)}, u32[]{:S(2)}, u32[]{:S(2)}) collective-permute-start(bf16[8,4224]{1,0:T(8,128)(2,1)S(1)} %shard_map.55.refs_1_), channel_id=1, source_target_pairs={{0,24},{8,16},{16,8},{24,0},{1,25},{9,17},{17,9},{25,1},{2,26},{10... | collective-permute-start | bytes 202760 | tf_op jit(solution)/shard_map/ppermute | solution.py:22
  5.0 9.8 %collective-permute-start.2 = (bf16[8,4224]{1,0:T(8,128)(2,1)S(1)}, bf16[8,4224]{1,0:T(8,128)(2,1)S(1)}, u32[]{:S(2)}, u32[]{:S(2)}) collective-permute-start(bf16[8,4224]{1,0:T(8,128)(2,1)S(1)} %shard_map.55.refs_1_), channel_id=1, source_target_pairs={{0,6},{1,7},{2,4},{3,5},{4,2},{5,3},{6,0},{7,1},{8,14},{9,15},{10,... | collective-permute-start | bytes 202760 | tf_op jit(solution)/shard_map/ppermute | solution.py:22
  8.6 6.2 %collective-permute-start.1 = (bf16[8,4224]{1,0:T(8,128)(2,1)S(1)}, bf16[8,4224]{1,0:T(8,128)(2,1)S(1)}, u32[]{:S(2)}, u32[]{:S(2)}) collective-permute-start(bf16[8,4224]{1,0:T(8,128)(2,1)S(1)} %shard_map.55.refs_1_), channel_id=1, source_target_pairs={{0,4},{1,5},{2,6},{3,7},{4,0},{5,1},{6,2},{7,3},{8,12},{9,13},{10,... | collective-permute-start | bytes 202760 | tf_op jit(solution)/shard_map/ppermute | solution.py:22
  8.6 6.2 %collective-permute-start = (bf16[8,4224]{1,0:T(8,128)(2,1)S(1)}, bf16[8,4224]{1,0:T(8,128)(2,1)S(1)}, u32[]{:S(2)}, u32[]{:S(2)}) collective-permute-start(bf16[8,4224]{1,0:T(8,128)(2,1)S(1)} %shard_map.55.refs_1_), channel_id=1, source_target_pairs={{0,2},{1,3},{2,0},{3,1},{4,6},{5,7},{6,4},{7,5},{8,10},{9,11},{10,... | collective-permute-start | bytes 202760 | tf_op jit(solution)/shard_map/ppermute | solution.py:22
  14.8 10.0 %collective-permute-start.5 = (bf16[32,4224]{1,0:T(8,128)(2,1)S(1)}, bf16[32,4224]{1,0:T(8,128)(2,1)S(1)}, u32[]{:S(2)}, u32[]{:S(2)}) collective-permute-start(bf16[32,4224]{1,0:T(8,128)(2,1)S(1)} %get-tuple-element.26.refs_1_), channel_id=1, source_target_pairs={{0,16},{8,24},{16,0},{24,8},{1,17},{9,25},{17,1},{25,9},{2,18},{10... | collective-permute-start | bytes 811016 | tf_op jit(solution)/shard_map/ppermute | solution.py:22
  15.4 9.9 %collective-permute-start.4 = (bf16[32,4224]{1,0:T(8,128)(2,1)S(1)}, bf16[32,4224]{1,0:T(8,128)(2,1)S(1)}, u32[]{:S(2)}, u32[]{:S(2)}) collective-permute-start(bf16[32,4224]{1,0:T(8,128)(2,1)S(1)} %get-tuple-element.26.refs_1_), channel_id=1, source_target_pairs={{0,8},{8,0},{16,24},{24,16},{1,9},{9,1},{17,25},{25,17},{2,10},{10... | collective-permute-start | bytes 811016 | tf_op jit(solution)/shard_map/ppermute | solution.py:22
  15.7 6.2 %collective-permute-start.8 = (bf16[8,4224]{1,0:T(8,128)(2,1)S(1)}, bf16[8,4224]{1,0:T(8,128)(2,1)S(1)}, u32[]{:S(2)}, u32[]{:S(2)}) collective-permute-start(bf16[8,4224]{1,0:T(8,128)(2,1)S(1)} %collective-permute-done.3.refs_1_), channel_id=1, source_target_pairs={{0,6},{1,7},{2,4},{3,5},{4,2},{5,3},{6,0},{7,1},{8,14},{9,15},{10,... | collective-permute-start | bytes 202760 | tf_op jit(solution)/shard_map/ppermute | solution.py:22
  19.5 5.2 %collective-permute-start.7 = (bf16[8,4224]{1,0:T(8,128)(2,1)S(1)}, bf16[8,4224]{1,0:T(8,128)(2,1)S(1)}, u32[]{:S(2)}, u32[]{:S(2)}) collective-permute-start(bf16[8,4224]{1,0:T(8,128)(2,1)S(1)} %collective-permute-done.3.refs_1_), channel_id=1, source_target_pairs={{0,4},{1,5},{2,6},{3,7},{4,0},{5,1},{6,2},{7,3},{8,12},{9,13},{10,... | collective-permute-start | bytes 202760 | tf_op jit(solution)/shard_map/ppermute | solution.py:22
  19.5 5.2 %collective-permute-start.6 = (bf16[8,4224]{1,0:T(8,128)(2,1)S(1)}, bf16[8,4224]{1,0:T(8,128)(2,1)S(1)}, u32[]{:S(2)}, u32[]{:S(2)}) collective-permute-start(bf16[8,4224]{1,0:T(8,128)(2,1)S(1)} %collective-permute-done.3.refs_1_), channel_id=1, source_target_pairs={{0,2},{1,3},{2,0},{3,1},{4,6},{5,7},{6,4},{7,5},{8,10},{9,11},{10,... | collective-permute-start | bytes 202760 | tf_op jit(solution)/shard_map/ppermute | solution.py:22
  21.9 3.5 %collective-permute-start.9 = (bf16[32,4224]{1,0:T(8,128)(2,1)S(1)}, bf16[32,4224]{1,0:T(8,128)(2,1)S(1)}, u32[]{:S(2)}, u32[]{:S(2)}) collective-permute-start(bf16[32,4224]{1,0:T(8,128)(2,1)S(1)} %get-tuple-element.26.refs_1_), channel_id=1, source_target_pairs={{0,1},{1,0},{2,3},{3,2},{4,5},{5,4},{6,7},{7,6},{8,9},{9,8},{10,11... | collective-permute-start | bytes 811016 | tf_op jit(solution)/shard_map/ppermute | solution.py:22
  24.7 1.6 %collective-permute-start.12 = (bf16[32,4224]{1,0:T(8,128)(2,1)S(1)}, bf16[32,4224]{1,0:T(8,128)(2,1)S(1)}, u32[]{:S(2)}, u32[]{:S(2)}) collective-permute-start(bf16[32,4224]{1,0:T(8,128)(2,1)S(1)} %get-tuple-element.29.refs_4_), channel_id=1, source_target_pairs={{0,1},{1,0},{2,3},{3,2},{4,5},{5,4},{6,7},{7,6},{8,9},{9,8},{10,11... | collective-permute-start | bytes 811016 | tf_op jit(solution)/shard_map/ppermute | solution.py:22
  24.8 1.9 %collective-permute-start.11 = (bf16[32,4224]{1,0:T(8,128)(2,1)S(1)}, bf16[32,4224]{1,0:T(8,128)(2,1)S(1)}, u32[]{:S(2)}, u32[]{:S(2)}) collective-permute-start(bf16[32,4224]{1,0:T(8,128)(2,1)S(1)} %collective-permute-done.5.refs_3_), channel_id=1, source_target_pairs={{0,1},{1,0},{2,3},{3,2},{4,5},{5,4},{6,7},{7,6},{8,9},{9,8},{10,11... | collective-permute-start | bytes 811016 | tf_op jit(solution)/shard_map/ppermute | solution.py:22
  25.3 1.8 %collective-permute-start.10 = (bf16[32,4224]{1,0:T(8,128)(2,1)S(1)}, bf16[32,4224]{1,0:T(8,128)(2,1)S(1)}, u32[]{:S(2)}, u32[]{:S(2)}) collective-permute-start(bf16[32,4224]{1,0:T(8,128)(2,1)S(1)} %collective-permute-done.4.refs_2_), channel_id=1, source_target_pairs={{0,1},{1,0},{2,3},{3,2},{4,5},{5,4},{6,7},{7,6},{8,9},{9,8},{10,11... | collective-permute-start | bytes 811016 | tf_op jit(solution)/shard_map/ppermute | solution.py:22
  35.2 2.7 %collective-permute-start.13 = (bf16[4,32,4096]{2,1,0:T(8,128)(2,1)S(1)}, bf16[4,32,4096]{2,1,0:T(8,128)(2,1)S(1)}, u32[]{:S(2)}, u32[]{:S(2)}) collective-permute-start(bf16[4,32,4096]{2,1,0:T(8,128)(2,1)S(1)} %get-tuple-element.32), channel_id=1, source_target_pairs={{0,1},{1,0},{2,3},{3,2},{4,5},{5,4},{6,7},{7,6},{8,9},{9,8},{10,11... | collective-permute-start | bytes 3145736 | tf_op jit(solution)/shard_map/ppermute | solution.py:22
  38.3 6.7 %collective-permute-start.16 = (bf16[8,4096]{1,0:T(8,128)(2,1)S(1)}, bf16[8,4096]{1,0:T(8,128)(2,1)S(1)}, u32[]{:S(2)}, u32[]{:S(2)}) collective-permute-start(bf16[8,4096]{1,0:T(8,128)(2,1)S(1)} %get-tuple-element.37), channel_id=1, source_target_pairs={{0,2},{1,3},{2,0},{3,1},{4,6},{5,7},{6,4},{7,5},{8,10},{9,11},{10,... | collective-permute-start | bytes 196616 | tf_op jit(solution)/shard_map/ppermute | solution.py:22
  38.9 7.2 %collective-permute-start.18 = (bf16[8,4096]{1,0:T(8,128)(2,1)S(1)}, bf16[8,4096]{1,0:T(8,128)(2,1)S(1)}, u32[]{:S(2)}, u32[]{:S(2)}) collective-permute-start(bf16[8,4096]{1,0:T(8,128)(2,1)S(1)} %get-tuple-element.38), channel_id=1, source_target_pairs={{0,6},{1,7},{2,4},{3,5},{4,2},{5,3},{6,0},{7,1},{8,14},{9,15},{10,... | collective-permute-start | bytes 196616 | tf_op jit(solution)/shard_map/ppermute | solution.py:22
  41.8 6.3 %collective-permute-start.17 = (bf16[8,4096]{1,0:T(8,128)(2,1)S(1)}, bf16[8,4096]{1,0:T(8,128)(2,1)S(1)}, u32[]{:S(2)}, u32[]{:S(2)}) collective-permute-start(bf16[8,4096]{1,0:T(8,128)(2,1)S(1)} %get-tuple-element.39), channel_id=1, source_target_pairs={{0,4},{1,5},{2,6},{3,7},{4,0},{5,1},{6,2},{7,3},{8,12},{9,13},{10,... | collective-permute-start | bytes 196616 | tf_op jit(solution)/shard_map/ppermute | solution.py:22
  41.9 8.8 %collective-permute-start.14 = (bf16[32,4096]{1,0:T(8,128)(2,1)S(1)}, bf16[32,4096]{1,0:T(8,128)(2,1)S(1)}, u32[]{:S(2)}, u32[]{:S(2)}) collective-permute-start(bf16[32,4096]{1,0:T(8,128)(2,1)S(1)} %get-tuple-element.40), channel_id=1, source_target_pairs={{0,8},{8,0},{16,24},{24,16},{1,9},{9,1},{17,25},{25,17},{2,10},{10... | collective-permute-start | bytes 786440 | tf_op jit(solution)/shard_map/ppermute | solution.py:22
  43.5 7.5 %collective-permute-start.15 = (bf16[32,4096]{1,0:T(8,128)(2,1)S(1)}, bf16[32,4096]{1,0:T(8,128)(2,1)S(1)}, u32[]{:S(2)}, u32[]{:S(2)}) collective-permute-start(bf16[32,4096]{1,0:T(8,128)(2,1)S(1)} %get-tuple-element.41), channel_id=1, source_target_pairs={{0,16},{8,24},{16,0},{24,8},{1,17},{9,25},{17,1},{25,9},{2,18},{10... | collective-permute-start | bytes 786440 | tf_op jit(solution)/shard_map/ppermute | solution.py:22
  48.2 8.4 %collective-permute-start.19 = (bf16[8,4096]{1,0:T(8,128)(2,1)S(1)}, bf16[8,4096]{1,0:T(8,128)(2,1)S(1)}, u32[]{:S(2)}, u32[]{:S(2)}) collective-permute-start(bf16[8,4096]{1,0:T(8,128)(2,1)S(1)} %fusion.5), channel_id=1, source_target_pairs={{0,24},{8,16},{16,8},{24,0},{1,25},{9,17},{17,9},{25,1},{2,26},{10... | collective-permute-start | bytes 196616 | tf_op jit(solution)/shard_map/ppermute | solution.py:22
  51.1 5.6 %collective-permute-start.20 = (bf16[8,4096]{1,0:T(8,128)(2,1)S(1)}, bf16[8,4096]{1,0:T(8,128)(2,1)S(1)}, u32[]{:S(2)}, u32[]{:S(2)}) collective-permute-start(bf16[8,4096]{1,0:T(8,128)(2,1)S(1)} %get-tuple-element.42), channel_id=1, source_target_pairs={{0,2},{1,3},{2,0},{3,1},{4,6},{5,7},{6,4},{7,5},{8,10},{9,11},{10,... | collective-permute-start | bytes 196616 | tf_op jit(solution)/shard_map/ppermute | solution.py:22
  53.7 6.1 %collective-permute-start.22 = (bf16[8,4096]{1,0:T(8,128)(2,1)S(1)}, bf16[8,4096]{1,0:T(8,128)(2,1)S(1)}, u32[]{:S(2)}, u32[]{:S(2)}) collective-permute-start(bf16[8,4096]{1,0:T(8,128)(2,1)S(1)} %get-tuple-element.43), channel_id=1, source_target_pairs={{0,6},{1,7},{2,4},{3,5},{4,2},{5,3},{6,0},{7,1},{8,14},{9,15},{10,... | collective-permute-start | bytes 196616 | tf_op jit(solution)/shard_map/ppermute | solution.py:22
  56.7 5.2 %collective-permute-start.21 = (bf16[8,4096]{1,0:T(8,128)(2,1)S(1)}, bf16[8,4096]{1,0:T(8,128)(2,1)S(1)}, u32[]{:S(2)}, u32[]{:S(2)}) collective-permute-start(bf16[8,4096]{1,0:T(8,128)(2,1)S(1)} %get-tuple-element.44), channel_id=1, source_target_pairs={{0,4},{1,5},{2,6},{3,7},{4,0},{5,1},{6,2},{7,3},{8,12},{9,13},{10,... | collective-permute-start | bytes 196616 | tf_op jit(solution)/shard_map/ppermute | solution.py:22

commit v4 on v3

v4 whole, which is shorter than its diff:
```python
import functools

import jax
import jax.numpy as jnp
from jax import lax
from jax.experimental import pallas as pl
from jax.experimental.pallas import tpu as pltpu
from jax.sharding import PartitionSpec as P

LANES = 128
MIB = 1 << 20
VMEM = pl.BlockSpec(memory_space=pltpu.VMEM)
HBM = pl.BlockSpec(memory_space=pltpu.HBM)


def in_hbm(*arrays):
    return [pltpu.with_memory_space_constraint(array, pltpu.HBM) for array in arrays]


def swap(block, axis, flips):
    size = lax.axis_size(axis)
    return lax.ppermute(block, axis, [(i, i ^ flips) for i in range(size)])


def exchange(blocks):
    return lax.all_to_all(blocks, "chip", split_axis=0, concat_axis=0, tiled=True)


def pack_kernel(
    experts,
    tokens_hbm,
    ids_hbm,
    weights_hbm,
    packed_ref,
    repeated_ref,
    tokens_ref,
    ids_ref,
    weights_ref,
    sems,
):
    copies = [
        pltpu.make_async_copy(source, target, sems.at[i])
        for i, (source, target) in enumerate(
            ((ids_hbm, ids_ref), (weights_hbm, weights_ref), (tokens_hbm, tokens_ref))
        )
    ]
    for copy in copies:
        copy.start()
    for copy in copies:
        copy.wait()
    rows, width = tokens_ref.shape
    tail = packed_ref.shape[1] - width
    packed_ref[:, :width] = tokens_ref[...]
    lane = lax.broadcasted_iota(jnp.int32, (rows, tail), 1)
    expert = lane % experts
    part = lane // experts
    dense = jnp.zeros((rows, tail), jnp.float32)
    for k in range(ids_ref.shape[1]):
        dense += jnp.where(ids_ref[:, k : k + 1] == expert, weights_ref[:, k : k + 1], 0.0)
    result = jnp.zeros((rows, tail), jnp.float32)
    for step in range(3):
        rounded = dense.astype(jnp.bfloat16).astype(jnp.float32)
        result = jnp.where(part == step, rounded, result)
        dense = dense - rounded
    packed_ref[:, width:] = result.astype(jnp.bfloat16)
    for start in range(0, repeated_ref.shape[0], rows):
        repeated_ref[start : start + rows, :] = packed_ref[...]


def pack(tokens, expert_ids, route_weights, experts, times):
    rows, width = tokens.shape
    tail = -(-3 * experts // LANES) * LANES
    return pl.pallas_call(
        functools.partial(pack_kernel, experts),
        out_shape=(
            jax.ShapeDtypeStruct((rows, width + tail), jnp.bfloat16),
            jax.ShapeDtypeStruct((times * rows, width + tail), jnp.bfloat16),
        ),
        in_specs=[HBM] * 3,
        out_specs=[VMEM] * 2,
        scratch_shapes=[
            pltpu.VMEM(tokens.shape, tokens.dtype),
            pltpu.VMEM(expert_ids.shape, expert_ids.dtype),
            pltpu.VMEM(route_weights.shape, route_weights.dtype),
            pltpu.SemaphoreType.DMA((3,)),
        ],
        compiler_params=pltpu.CompilerParams(vmem_limit_bytes=2 * MIB),
    )(*in_hbm(tokens, expert_ids, route_weights))


def repeat_kernel(block_ref, out_ref):
    rows = block_ref.shape[0]
    for start in range(0, out_ref.shape[0], rows):
        out_ref[start : start + rows, :] = block_ref[...]


def repeat(block, times):
    rows, width = block.shape
    return pl.pallas_call(
        repeat_kernel,
        out_shape=jax.ShapeDtypeStruct((times * rows, width), block.dtype),
        in_specs=[VMEM],
        out_specs=VMEM,
        compiler_params=pltpu.CompilerParams(vmem_limit_bytes=2 * MIB),
    )(block)


def expert_kernel(exp_dev, experts, half, one_step, *refs):
    group_ref = refs[0]
    x_refs = refs[1 : 1 + 2 * half]
    win_hbm, wout_hbm, send_ref, keep_ref = refs[1 + 2 * half : 5 + 2 * half]
    win_pairs, wout_ref, mixed, hidden, in_sems, out_sems = refs[5 + 2 * half :]
    _, tiles, units, _, _ = win_pairs.shape
    parts, _, chunk = wout_ref.shape
    win_ref = win_pairs.reshape(exp_dev, tiles, 2 * units, LANES)
    in_loads = [
        [
            pltpu.make_async_copy(
                win_hbm.at[pl.ds(e * units, units), :, pl.ds(t * LANES, LANES)],
                win_pairs.at[e, t],
                in_sems.at[e, t],
            )
            for t in range(tiles)
        ]
        for e in range(exp_dev)
    ]
    out_loads = [
        pltpu.make_async_copy(
            wout_hbm.at[:, pl.ds(p * chunk, chunk)], wout_ref.at[p], out_sems.at[p]
        )
        for p in range(parts)
    ]

    def on_first(loads, act):
        def run():
            for load in loads:
                act(load)

        if one_step:
            run()
        else:
            pl.when(pl.program_id(0) == 0)(run)

    every = [load for loads in in_loads for load in loads] + out_loads
    on_first(every, lambda load: load.start())

    width = tiles * LANES
    block = x_refs[0].shape[0]
    rows = 2 * half * block
    tail = jnp.concatenate([ref[:, width:] for ref in x_refs], axis=0)
    contract_last = (((1,), (1,)), ((), ()))
    column = lax.broadcasted_iota(jnp.int32, (16, tail.shape[1]), 1)
    wanted = lax.broadcasted_iota(jnp.int32, (16, tail.shape[1]), 0) + group_ref[0] * exp_dev
    select = (column % experts == wanted) & (column < 3 * experts)
    scale = lax.dot_general(
        select.astype(jnp.bfloat16), tail, contract_last, preferred_element_type=jnp.float32
    )
    step = tiles // 2
    for e in range(exp_dev):
        both = 0.0
        for t in range(0, tiles, step):
            on_first(in_loads[e][t : t + step], lambda load: load.wait())
            w = jnp.concatenate([win_ref[e, u] for u in range(t, t + step)], axis=1)
            lanes = slice(t * LANES, (t + step) * LANES)
            x = jnp.concatenate([ref[:, lanes] for ref in x_refs], axis=0)
            both += lax.dot_general(w, x, contract_last, preferred_element_type=jnp.float32)
        for r in range(0, rows, LANES):
            mixed[...] = both[:, r : r + LANES]
            gate = mixed[pl.ds(0, units, stride=2), :]
            up = mixed[pl.ds(1, units, stride=2), :]
            act = gate / (1.0 + jnp.exp(-gate)) * up * scale[e : e + 1, r : r + LANES]
            hidden[pl.ds(e * units, units), r : r + LANES] = act.astype(jnp.bfloat16)
    for p in range(parts):
        on_first(out_loads[p : p + 1], lambda load: load.wait())
        part = lax.dot_general(
            hidden[...],
            wout_ref[p],
            (((0,), (0,)), ((), ())),
            preferred_element_type=jnp.float32,
        )
        lanes = slice(p * chunk, (p + 1) * chunk)
        for b in range(half):
            keep_ref[b, :, lanes] = part[b * block : (b + 1) * block]
            other = part[(half + b) * block : (half + b + 1) * block]
            send_ref[b, :, lanes] = other.astype(jnp.bfloat16)


def run_experts(group, blocks, win, wout, exp_dev, experts):
    half = len(blocks) // 2
    block_rows, packed_width = blocks[0].shape
    lines, width = wout.shape
    tiles = width // LANES
    parts = 4
    block = min(block_rows, max(16, 128 // half))
    rows = 2 * half * block
    steps = block_rows // block
    if steps == 1:
        x_block, out_block, grid = VMEM, VMEM, ()
    else:
        x_block = pl.BlockSpec((block, packed_width), lambda i: (i, 0))
        out_block = pl.BlockSpec((half, block, width), lambda i: (0, i, 0))
        grid = (steps,)
    windows = 0 if steps == 1 else 2 * rows * (2 * packed_width + 3 * width)
    scratch = 2 * (win.size + wout.size) + rows * (10 * lines + 6 * width)
    return pl.pallas_call(
        functools.partial(expert_kernel, exp_dev, experts, half, steps == 1),
        grid=grid,
        out_shape=(
            jax.ShapeDtypeStruct((half, block_rows, width), jnp.bfloat16),
            jax.ShapeDtypeStruct((half, block_rows, width), jnp.float32),
        ),
        in_specs=[
            pl.BlockSpec(memory_space=pltpu.SMEM),
            *[x_block] * (2 * half),
            HBM,
            HBM,
        ],
        out_specs=[out_block, out_block],
        scratch_shapes=[
            pltpu.VMEM((exp_dev, tiles, lines // exp_dev, 2, LANES), win.dtype),
            pltpu.VMEM((parts, lines, width // parts), wout.dtype),
            pltpu.VMEM((2 * lines // exp_dev, LANES), jnp.float32),
            pltpu.VMEM((lines, rows), jnp.bfloat16),
            pltpu.SemaphoreType.DMA((exp_dev, tiles)),
            pltpu.SemaphoreType.DMA((parts,)),
        ],
        compiler_params=pltpu.CompilerParams(vmem_limit_bytes=windows + scratch + 4 * MIB),
        cost_estimate=pl.CostEstimate(
            flops=12 * half * block_rows * width * lines,
            bytes_accessed=4 * half * block_rows * packed_width + 6 * half * block_rows * width,
            transcendentals=2 * half * block_rows * lines,
        ),
    )(group, *blocks, *in_hbm(win, wout))


def body(tokens, expert_ids, route_weights, in_weights, out_weights):
    tok_dev, width = tokens.shape
    exp_dev, units = in_weights.shape[:2]
    planes = lax.axis_size("batch")
    chips = lax.axis_size("chip")
    experts = exp_dev * lax.axis_size("core") * chips
    far = planes - 1
    w_in = in_weights.reshape(exp_dev * units, 2, width)
    w_out = out_weights.reshape(exp_dev * units, width)

    group = lax.axis_index(("chip", "core")).astype(jnp.int32).reshape(1)
    x, repeated = pack(tokens, expert_ids, route_weights, experts, chips)
    across = swap(x, "batch", far)
    mine = exchange(repeated)
    blocks = [mine] + [swap(mine, "batch", b) for b in range(1, far)]
    blocks.append(exchange(repeat(across, chips)))
    blocks = blocks + [swap(block, "core", 1) for block in blocks]

    send, total = run_experts(group, blocks, w_in, w_out, exp_dev, experts)
    total = total + swap(send, "core", 1).astype(jnp.float32)
    rounded = total.astype(jnp.bfloat16)
    mine = total[0]
    for b in range(1, far):
        mine = mine + swap(rounded[b], "batch", b).astype(jnp.float32)
    across = exchange(rounded[far]).reshape(chips, tok_dev, width).astype(jnp.float32).sum(0)
    across = swap(across.astype(jnp.bfloat16), "batch", far)
    mine = exchange(mine.astype(jnp.bfloat16)).reshape(chips, tok_dev, width)
    result = mine.astype(jnp.float32).sum(0) + across.astype(jnp.float32)
    return result.astype(jnp.bfloat16)


def solution(mesh):
    planes, groups = mesh.devices.shape
    mesh = jax.sharding.Mesh(
        mesh.devices.reshape(planes, groups // 2, 2), ("batch", "chip", "core")
    )
    expert = ("chip", "core")
    tokens = P(("batch",) + expert, None)
    return jax.shard_map(
        body,
        mesh=mesh,
        in_specs=(
            tokens,
            tokens,
            tokens,
            P(expert, "batch", None, None),
            P(expert, "batch", None),
        ),
        out_specs=tokens,
        check_vma=False,
    )
```

time: 62.7 us -> 76.5 us (1.22)
  waiting for transfers between devices: 17.5 us -> 27.7 us
  Pallas kernels: 14.4 us -> 17.6 us
  starting transfers between devices: 29.2 us -> 28 us
    ppermute x23 -> x11, starting transfers between devices: 29.2 us -> 10.6 us  [swap(): return lax.ppermute(block, axis, [(i, i ^ flips) for i in range(size)])]
    all_to_all x0 -> x4, waiting for transfers between devices: none -> 18.1 us  [exchange(): lax.all_to_all(blocks, 'chip', split_axis=0, concat_axis=0, tiled=True)]
    all_to_all x0 -> x4, starting transfers between devices: none -> 17.4 us  [exchange(): lax.all_to_all(blocks, 'chip', split_axis=0, concat_axis=0, tiled=True)]
    ppermute x23 -> x11, waiting for transfers between devices: 17.5 us -> 9.66 us  [swap(): return lax.ppermute(block, axis, [(i, i ^ flips) for i in range(size)])]
    pallas_call x5 -> x3, Pallas kernels: 14.4 us -> 17.7 us  [the longest x1 15.2 us: run_experts(): pl.pallas_call(functools.partial(expert_kernel, exp_dev, experts, half, s...]
    all_to_all x0 -> x1, other arithmetic: none -> 0.77 us  [exchange(): lax.all_to_all(blocks, 'chip', split_axis=0, concat_axis=0, tiled=True)]
  transfers between devices with their start and end apart: 23 -> 15, of which waited for: 11 -> 12; matrix products, arithmetic and copies ran while one was open for 0% -> 1% of each run, Pallas kernels for 9% -> 1%
where the time goes in v4:
time: 76.5 us; the launch traced here: 76 us
  starting transfers between devices  28 us (37%)
  waiting for transfers between devices  27.7 us (36%)
  Pallas kernels  17.6 us (23%)
  other arithmetic  1.83 us (2%)
    all_to_all x4, waiting for transfers between devices, exchange(): lax.all_to_all(blocks, 'chip', split_axis=0, concat_axis=0, tiled=True)  18.1 us
    all_to_all x4, starting transfers between devices, exchange(): lax.all_to_all(blocks, 'chip', split_axis=0, concat_axis=0, tiled=True)  17.4 us
    pallas_call x1, Pallas kernels, run_experts(): pl.pallas_call(functools.partial(expert_kernel, exp_dev, experts, half, s...  15.2 us
    ppermute x11, starting transfers between devices, swap(): return lax.ppermute(block, axis, [(i, i ^ flips) for i in range(size)])  10.6 us
    ppermute x11, waiting for transfers between devices, swap(): return lax.ppermute(block, axis, [(i, i ^ flips) for i in range(size)])  9.66 us
    pallas_call x1, Pallas kernels, pack(): pl.pallas_call(functools.partial(pack_kernel, experts), out_shape=(jax.Sh...  1.7 us
  transfers between devices with their start and end apart: 15, of which 12 were waited for; matrix products, arithmetic and copies ran while one was open for 1% of the time, Pallas kernels for 1%

profile of v4, /device:TPU:0, one launch (start us, length us, event | category | flops | bytes accessed | tf_op | source)
XLA Modules:
  0.0 76.0 jit_solution(11185155664306367964)
XLA Ops:
  0.0 1.7 %shard_map.55 = (bf16[8,4224]{1,0:T(8,128)(2,1)S(1)}, bf16[32,4224]{1,0:T(8,128)(2,1)}) custom-call(bf16[8,4096]{1,0:T(8,128)(2,1)} %tokens_hbm.1, s32[8,8]{1,0:T(8,128)} %ids_hbm.1, f32[8,8]{1,0:T(8,128)} %weights_hbm.1), custom_call_target="tpu_custom_call" | custom-call | tf_op jit(solution)/shard_map/pallas_call | solution.py:73
  1.7 6.3 %all-to-all-start = ((bf16[4,8,4224]{2,1,0:T(8,128)(2,1)}), bf16[4,8,4224]{2,1,0:T(8,128)(2,1)S(1)}, u32[]{:S(2)}, u32[]{:S(2)}) async-start(bf16[4,8,4224]{2,1,0:T(8,128)(2,1)} %bitcast.1), calls=%async_computation | async-start | bytes 540672 | tf_op jit(solution)/shard_map/all_to_all | solution.py:26
  8.0 2.4 %collective-permute-start.2 = (bf16[8,4224]{1,0:T(8,128)(2,1)S(1)}, bf16[8,4224]{1,0:T(8,128)(2,1)S(1)}, u32[]{:S(2)}, u32[]{:S(2)}) collective-permute-start(bf16[8,4224]{1,0:T(8,128)(2,1)S(1)} %get-tuple-element.10), channel_id=1, source_target_pairs={{0,24},{8,16},{16,8},{24,0},{1,25},{9,17},{17,9},{25,1},{2,26},{10... | collective-permute-start | bytes 202760 | tf_op jit(solution)/shard_map/ppermute | solution.py:22
  10.5 2.7 %collective-permute-done.2.block_ref = bf16[8,4224]{1,0:T(8,128)(2,1)S(1)} collective-permute-done((bf16[8,4224]{1,0:T(8,128)(2,1)S(1)}, bf16[8,4224]{1,0:T(8,128)(2,1)S(1)}, u32[]{:S(2)}, u32[]{:S(2)}) %collective-permute-start.2) | collective-permute-done | bytes 67616 | tf_op jit(solution)/shard_map/ppermute | solution.py:22
  13.2 0.7 shard_map.56
  13.9 3.2 %all-to-all-done = bf16[4,8,4224]{2,1,0:T(8,128)(2,1)S(1)} async-done(((bf16[4,8,4224]{2,1,0:T(8,128)(2,1)}), bf16[4,8,4224]{2,1,0:T(8,128)(2,1)S(1)}, u32[]{:S(2)}, u32[]{:S(2)}) %all-to-all-start) | async-done | bytes 270368 | tf_op jit(solution)/shard_map/all_to_all | solution.py:26
  17.1 3.4 %all-to-all-start.1 = ((bf16[4,8,4224]{2,1,0:T(8,128)(2,1)}), bf16[4,8,4224]{2,1,0:T(8,128)(2,1)S(1)}, u32[]{:S(2)}, u32[]{:S(2)}) async-start(bf16[4,8,4224]{2,1,0:T(8,128)(2,1)} %bitcast.3), calls=%async_computation.1 | async-start | bytes 540672 | tf_op jit(solution)/shard_map/all_to_all | solution.py:26
  20.6 1.6 %collective-permute-start.1 = (bf16[32,4224]{1,0:T(8,128)(2,1)S(1)}, bf16[32,4224]{1,0:T(8,128)(2,1)S(1)}, u32[]{:S(2)}, u32[]{:S(2)}) collective-permute-start(bf16[32,4224]{1,0:T(8,128)(2,1)S(1)} %bitcast.25), channel_id=1, source_target_pairs={{0,16},{8,24},{16,0},{24,8},{1,17},{9,25},{17,1},{25,9},{2,18},{10... | collective-permute-start | bytes 811016 | tf_op jit(solution)/shard_map/ppermute | solution.py:22
  22.2 1.5 %collective-permute-start = (bf16[32,4224]{1,0:T(8,128)(2,1)S(1)}, bf16[32,4224]{1,0:T(8,128)(2,1)S(1)}, u32[]{:S(2)}, u32[]{:S(2)}) collective-permute-start(bf16[32,4224]{1,0:T(8,128)(2,1)S(1)} %bitcast.26), channel_id=1, source_target_pairs={{0,8},{8,0},{16,24},{24,16},{1,9},{9,1},{17,25},{25,17},{2,10},{10... | collective-permute-start | bytes 811016 | tf_op jit(solution)/shard_map/ppermute | solution.py:22
  23.7 0.0 collective-permute-start.3
  23.7 4.0 %all-to-all-done.1 = bf16[4,8,4224]{2,1,0:T(8,128)(2,1)S(1)} async-done(((bf16[4,8,4224]{2,1,0:T(8,128)(2,1)}), bf16[4,8,4224]{2,1,0:T(8,128)(2,1)S(1)}, u32[]{:S(2)}, u32[]{:S(2)}) %all-to-all-start.1) | async-done | bytes 270368 | tf_op jit(solution)/shard_map/all_to_all | solution.py:26
  27.6 0.0 collective-permute-start.6
  27.6 0.0 collective-permute-done.1.refs_3_
  27.6 0.5 collective-permute-start.5
  28.1 0.5 collective-permute-done.refs_2_
  28.6 0.0 collective-permute-start.4
  28.6 0.0 collective-permute-done.3.refs_5_
  28.6 0.5 collective-permute-done.6.refs_8_
  29.2 0.4 collective-permute-done.5.refs_7_
  29.6 0.6 collective-permute-done.4.refs_6_
  30.2 15.2 %shard_map.57 = (bf16[4,32,4096]{2,1,0:T(8,128)(2,1)S(1)}, f32[4,32,4096]{2,1,0:T(8,128)S(1)}) custom-call(s32[1]{0:T(128)} %bitcast.refs_0_, bf16[32,4224]{1,0:T(8,128)(2,1)S(1)} %bitcast.28, bf16[32,4224]{1,0:T(8,128)(2,1)S(1)} %collective-permute-done.refs_2_, bf16[32,4224]{1,0:T(8,128)(2,1)S(1)} %collective-permute-done.1.refs_3_, ...), custom_call_target="tpu_custom_call" | custom-call | flops 4831838208 | bytes 5308416 | tf_op jit(solution)/shard_map/pallas_call | solution.py:205
  45.4 0.2 collective-permute-start.7
  45.6 2.5 %collective-permute-done.7 = bf16[4,32,4096]{2,1,0:T(8,128)(2,1)S(1)} collective-permute-done((bf16[4,32,4096]{2,1,0:T(8,128)(2,1)S(1)}, bf16[4,32,4096]{2,1,0:T(8,128)(2,1)S(1)}, u32[]{:S(2)}, u32[]{:S(2)}) %collective-permute-start.7) | collective-permute-done | bytes 1048608 | tf_op jit(solution)/shard_map/ppermute | solution.py:22
  48.2 0.3 fusion.4
  48.5 0.7 slice_bitcast_fusion.1
  49.2 1.3 %collective-permute-start.9 = (bf16[32,4096]{1,0:T(8,128)(2,1)S(1)}, bf16[32,4096]{1,0:T(8,128)(2,1)S(1)}, u32[]{:S(2)}, u32[]{:S(2)}) collective-permute-start(bf16[32,4096]{1,0:T(8,128)(2,1)S(1)} %get-tuple-element.16), channel_id=1, source_target_pairs={{0,16},{8,24},{16,0},{24,8},{1,17},{9,25},{17,1},{25,9},{2,18},{10... | collective-permute-start | bytes 786440 | tf_op jit(solution)/shard_map/ppermute | solution.py:22
  50.5 1.5 %collective-permute-start.8 = (bf16[32,4096]{1,0:T(8,128)(2,1)S(1)}, bf16[32,4096]{1,0:T(8,128)(2,1)S(1)}, u32[]{:S(2)}, u32[]{:S(2)}) collective-permute-start(bf16[32,4096]{1,0:T(8,128)(2,1)S(1)} %get-tuple-element.17), channel_id=1, source_target_pairs={{0,8},{8,0},{16,24},{24,16},{1,9},{9,1},{17,25},{25,17},{2,10},{10... | collective-permute-start | bytes 786440 | tf_op jit(solution)/shard_map/ppermute | solution.py:22
  52.0 4.2 %all-to-all-start.3 = ((bf16[4,8,4096]{2,1,0:T(8,128)(2,1)}), bf16[4,8,4096]{2,1,0:T(8,128)(2,1)S(1)}, u32[]{:S(2)}, u32[]{:S(2)}) async-start(bf16[4,8,4096]{2,1,0:T(8,128)(2,1)} %get-tuple-element.15), calls=%async_computation.3 | async-start | bytes 524288 | tf_op jit(solution)/shard_map/all_to_all | solution.py:26
  56.2 1.4 %collective-permute-done.9 = bf16[32,4096]{1,0:T(8,128)(2,1)S(1)} collective-permute-done((bf16[32,4096]{1,0:T(8,128)(2,1)S(1)}, bf16[32,4096]{1,0:T(8,128)(2,1)S(1)}, u32[]{:S(2)}, u32[]{:S(2)}) %collective-permute-start.9) | collective-permute-done | bytes 262176 | tf_op jit(solution)/shard_map/ppermute | solution.py:22
  57.6 1.0 %collective-permute-done.8 = bf16[32,4096]{1,0:T(8,128)(2,1)S(1)} collective-permute-done((bf16[32,4096]{1,0:T(8,128)(2,1)S(1)}, bf16[32,4096]{1,0:T(8,128)(2,1)S(1)}, u32[]{:S(2)}, u32[]{:S(2)}) %collective-permute-start.8) | collective-permute-done | bytes 262176 | tf_op jit(solution)/shard_map/ppermute | solution.py:22
  58.6 0.8 %fusion.3 = bf16[4,8,4096]{2,1,0:T(8,128)(2,1)} fusion(bf16[32,4096]{1,0:T(8,128)(2,1)S(1)} %collective-permute-done.9, bf16[32,4096]{1,0:T(8,128)(2,1)S(1)} %collective-permute-done.8, f32[4,32,4096]{2,1,0:T(8,128)S(1)} %get-tuple-element.14), kind=kLoop, calls=%fused_computation.6 | loop fusion | flops 655360 | bytes 1310720 | tf_op jit(solution)/shard_map/all_to_all | solution.py:26
  59.4 5.5 %all-to-all-done.3 = bf16[4,8,4096]{2,1,0:T(8,128)(2,1)S(1)} async-done(((bf16[4,8,4096]{2,1,0:T(8,128)(2,1)}), bf16[4,8,4096]{2,1,0:T(8,128)(2,1)S(1)}, u32[]{:S(2)}, u32[]{:S(2)}) %all-to-all-start.3) | async-done | bytes 262176 | tf_op jit(solution)/shard_map/all_to_all | solution.py:26
  64.9 3.4 %all-to-all-start.2 = ((bf16[4,8,4096]{2,1,0:T(8,128)(2,1)}), bf16[4,8,4096]{2,1,0:T(8,128)(2,1)S(1)}, u32[]{:S(2)}, u32[]{:S(2)}) async-start(bf16[4,8,4096]{2,1,0:T(8,128)(2,1)} %fusion.3), calls=%async_computation.2 | async-start | bytes 524288 | tf_op jit(solution)/shard_map/all_to_all | solution.py:26
  68.3 1.6 %collective-permute-start.10 = (bf16[8,4096]{1,0:T(8,128)(2,1)S(1)}, bf16[8,4096]{1,0:T(8,128)(2,1)S(1)}, u32[]{:S(2)}, u32[]{:S(2)}) collective-permute-start(bf16[8,4096]{1,0:T(8,128)(2,1)S(1)} %reduce_sum.22), channel_id=1, source_target_pairs={{0,24},{8,16},{16,8},{24,0},{1,25},{9,17},{17,9},{25,1},{2,26},{10... | collective-permute-start | bytes 196616 | tf_op jit(solution)/shard_map/ppermute | solution.py:22
  69.9 5.4 %all-to-all-done.2 = bf16[4,8,4096]{2,1,0:T(8,128)(2,1)S(1)} async-done(((bf16[4,8,4096]{2,1,0:T(8,128)(2,1)}), bf16[4,8,4096]{2,1,0:T(8,128)(2,1)S(1)}, u32[]{:S(2)}, u32[]{:S(2)}) %all-to-all-start.2) | async-done | bytes 262176 | tf_op jit(solution)/shard_map/all_to_all | solution.py:26
  75.3 0.0 collective-permute-done.10
  75.4 0.7 add_convert_fusion
  (2 shorter events, 0.1 us)
Async XLA Ops:
  1.7 15.4 %all-to-all-start = ((bf16[4,8,4224]{2,1,0:T(8,128)(2,1)}), bf16[4,8,4224]{2,1,0:T(8,128)(2,1)S(1)}, u32[]{:S(2)}, u32[]{:S(2)}) async-start(bf16[4,8,4224]{2,1,0:T(8,128)(2,1)} %bitcast.1), calls=%async_computation | async-start | bytes 540672 | tf_op jit(solution)/shard_map/all_to_all | solution.py:26
  8.0 5.2 %collective-permute-start.2 = (bf16[8,4224]{1,0:T(8,128)(2,1)S(1)}, bf16[8,4224]{1,0:T(8,128)(2,1)S(1)}, u32[]{:S(2)}, u32[]{:S(2)}) collective-permute-start(bf16[8,4224]{1,0:T(8,128)(2,1)S(1)} %get-tuple-element.10), channel_id=1, source_target_pairs={{0,24},{8,16},{16,8},{24,0},{1,25},{9,17},{17,9},{25,1},{2,26},{10... | collective-permute-start | bytes 202760 | tf_op jit(solution)/shard_map/ppermute | solution.py:22
  17.1 10.5 %all-to-all-start.1 = ((bf16[4,8,4224]{2,1,0:T(8,128)(2,1)}), bf16[4,8,4224]{2,1,0:T(8,128)(2,1)S(1)}, u32[]{:S(2)}, u32[]{:S(2)}) async-start(bf16[4,8,4224]{2,1,0:T(8,128)(2,1)} %bitcast.3), calls=%async_computation.1 | async-start | bytes 540672 | tf_op jit(solution)/shard_map/all_to_all | solution.py:26
  20.6 7.0 %collective-permute-start.1 = (bf16[32,4224]{1,0:T(8,128)(2,1)S(1)}, bf16[32,4224]{1,0:T(8,128)(2,1)S(1)}, u32[]{:S(2)}, u32[]{:S(2)}) collective-permute-start(bf16[32,4224]{1,0:T(8,128)(2,1)S(1)} %bitcast.25), channel_id=1, source_target_pairs={{0,16},{8,24},{16,0},{24,8},{1,17},{9,25},{17,1},{25,9},{2,18},{10... | collective-permute-start | bytes 811016 | tf_op jit(solution)/shard_map/ppermute | solution.py:22
  22.2 6.5 %collective-permute-start = (bf16[32,4224]{1,0:T(8,128)(2,1)S(1)}, bf16[32,4224]{1,0:T(8,128)(2,1)S(1)}, u32[]{:S(2)}, u32[]{:S(2)}) collective-permute-start(bf16[32,4224]{1,0:T(8,128)(2,1)S(1)} %bitcast.26), channel_id=1, source_target_pairs={{0,8},{8,0},{16,24},{24,16},{1,9},{9,1},{17,25},{25,17},{2,10},{10... | collective-permute-start | bytes 811016 | tf_op jit(solution)/shard_map/ppermute | solution.py:22
  23.7 5.0 %collective-permute-start.3 = (bf16[32,4224]{1,0:T(8,128)(2,1)S(1)}, bf16[32,4224]{1,0:T(8,128)(2,1)S(1)}, u32[]{:S(2)}, u32[]{:S(2)}) collective-permute-start(bf16[32,4224]{1,0:T(8,128)(2,1)S(1)} %bitcast.27), channel_id=1, source_target_pairs={{0,1},{1,0},{2,3},{3,2},{4,5},{5,4},{6,7},{7,6},{8,9},{9,8},{10,11... | collective-permute-start | bytes 811016 | tf_op jit(solution)/shard_map/ppermute | solution.py:22
  27.6 1.5 %collective-permute-start.6 = (bf16[32,4224]{1,0:T(8,128)(2,1)S(1)}, bf16[32,4224]{1,0:T(8,128)(2,1)S(1)}, u32[]{:S(2)}, u32[]{:S(2)}) collective-permute-start(bf16[32,4224]{1,0:T(8,128)(2,1)S(1)} %bitcast.29), channel_id=1, source_target_pairs={{0,1},{1,0},{2,3},{3,2},{4,5},{5,4},{6,7},{7,6},{8,9},{9,8},{10,11... | collective-permute-start | bytes 811016 | tf_op jit(solution)/shard_map/ppermute | solution.py:22
  27.6 1.9 %collective-permute-start.5 = (bf16[32,4224]{1,0:T(8,128)(2,1)S(1)}, bf16[32,4224]{1,0:T(8,128)(2,1)S(1)}, u32[]{:S(2)}, u32[]{:S(2)}) collective-permute-start(bf16[32,4224]{1,0:T(8,128)(2,1)S(1)} %collective-permute-done.1.refs_3_), channel_id=1, source_target_pairs={{0,1},{1,0},{2,3},{3,2},{4,5},{5,4},{6,7},{7,6},{8,9},{9,8},{10,11... | collective-permute-start | bytes 811016 | tf_op jit(solution)/shard_map/ppermute | solution.py:22
  28.6 1.5 %collective-permute-start.4 = (bf16[32,4224]{1,0:T(8,128)(2,1)S(1)}, bf16[32,4224]{1,0:T(8,128)(2,1)S(1)}, u32[]{:S(2)}, u32[]{:S(2)}) collective-permute-start(bf16[32,4224]{1,0:T(8,128)(2,1)S(1)} %collective-permute-done.refs_2_), channel_id=1, source_target_pairs={{0,1},{1,0},{2,3},{3,2},{4,5},{5,4},{6,7},{7,6},{8,9},{9,8},{10,11... | collective-permute-start | bytes 811016 | tf_op jit(solution)/shard_map/ppermute | solution.py:22
  45.4 2.7 %collective-permute-start.7 = (bf16[4,32,4096]{2,1,0:T(8,128)(2,1)S(1)}, bf16[4,32,4096]{2,1,0:T(8,128)(2,1)S(1)}, u32[]{:S(2)}, u32[]{:S(2)}) collective-permute-start(bf16[4,32,4096]{2,1,0:T(8,128)(2,1)S(1)} %get-tuple-element.12), channel_id=1, source_target_pairs={{0,1},{1,0},{2,3},{3,2},{4,5},{5,4},{6,7},{7,6},{8,9},{9,8},{10,11... | collective-permute-start | bytes 3145736 | tf_op jit(solution)/shard_map/ppermute | solution.py:22
  49.2 8.4 %collective-permute-start.9 = (bf16[32,4096]{1,0:T(8,128)(2,1)S(1)}, bf16[32,4096]{1,0:T(8,128)(2,1)S(1)}, u32[]{:S(2)}, u32[]{:S(2)}) collective-permute-start(bf16[32,4096]{1,0:T(8,128)(2,1)S(1)} %get-tuple-element.16), channel_id=1, source_target_pairs={{0,16},{8,24},{16,0},{24,8},{1,17},{9,25},{17,1},{25,9},{2,18},{10... | collective-permute-start | bytes 786440 | tf_op jit(solution)/shard_map/ppermute | solution.py:22
  50.5 8.1 %collective-permute-start.8 = (bf16[32,4096]{1,0:T(8,128)(2,1)S(1)}, bf16[32,4096]{1,0:T(8,128)(2,1)S(1)}, u32[]{:S(2)}, u32[]{:S(2)}) collective-permute-start(bf16[32,4096]{1,0:T(8,128)(2,1)S(1)} %get-tuple-element.17), channel_id=1, source_target_pairs={{0,8},{8,0},{16,24},{24,16},{1,9},{9,1},{17,25},{25,17},{2,10},{10... | collective-permute-start | bytes 786440 | tf_op jit(solution)/shard_map/ppermute | solution.py:22
  52.0 12.8 %all-to-all-start.3 = ((bf16[4,8,4096]{2,1,0:T(8,128)(2,1)}), bf16[4,8,4096]{2,1,0:T(8,128)(2,1)S(1)}, u32[]{:S(2)}, u32[]{:S(2)}) async-start(bf16[4,8,4096]{2,1,0:T(8,128)(2,1)} %get-tuple-element.15), calls=%async_computation.3 | async-start | bytes 524288 | tf_op jit(solution)/shard_map/all_to_all | solution.py:26
  64.9 10.5 %all-to-all-start.2 = ((bf16[4,8,4096]{2,1,0:T(8,128)(2,1)}), bf16[4,8,4096]{2,1,0:T(8,128)(2,1)S(1)}, u32[]{:S(2)}, u32[]{:S(2)}) async-start(bf16[4,8,4096]{2,1,0:T(8,128)(2,1)} %fusion.3), calls=%async_computation.2 | async-start | bytes 524288 | tf_op jit(solution)/shard_map/all_to_all | solution.py:26
  68.3 7.0 %collective-permute-start.10 = (bf16[8,4096]{1,0:T(8,128)(2,1)S(1)}, bf16[8,4096]{1,0:T(8,128)(2,1)S(1)}, u32[]{:S(2)}, u32[]{:S(2)}) collective-permute-start(bf16[8,4096]{1,0:T(8,128)(2,1)S(1)} %reduce_sum.22), channel_id=1, source_target_pairs={{0,24},{8,16},{16,8},{24,0},{1,25},{9,17},{17,9},{25,1},{2,26},{10... | collective-permute-start | bytes 196616 | tf_op jit(solution)/shard_map/ppermute | solution.py:22

commit v5 on v3

v5 whole, which is shorter than its diff:
```python
import functools

import jax
import jax.numpy as jnp
from jax import lax
from jax.experimental import pallas as pl
from jax.experimental.pallas import tpu as pltpu
from jax.sharding import PartitionSpec as P

LANES = 128
MIB = 1 << 20
VMEM = pl.BlockSpec(memory_space=pltpu.VMEM)
HBM = pl.BlockSpec(memory_space=pltpu.HBM)


def in_hbm(*arrays):
    return [pltpu.with_memory_space_constraint(array, pltpu.HBM) for array in arrays]


def swap(block, axis, flips):
    size = lax.axis_size(axis)
    return lax.ppermute(block, axis, [(i, i ^ flips) for i in range(size)])


def pack_kernel(
    experts, tokens_hbm, ids_hbm, weights_hbm, packed_ref, tokens_ref, ids_ref, weights_ref, sems
):
    copies = [
        pltpu.make_async_copy(source, target, sems.at[i])
        for i, (source, target) in enumerate(
            ((ids_hbm, ids_ref), (weights_hbm, weights_ref), (tokens_hbm, tokens_ref))
        )
    ]
    for copy in copies:
        copy.start()
    for copy in copies:
        copy.wait()
    rows, width = tokens_ref.shape
    tail = packed_ref.shape[1] - width
    packed_ref[:, :width] = tokens_ref[...]
    lane = lax.broadcasted_iota(jnp.int32, (rows, tail), 1)
    expert = lane % experts
    part = lane // experts
    dense = jnp.zeros((rows, tail), jnp.float32)
    for k in range(ids_ref.shape[1]):
        dense += jnp.where(ids_ref[:, k : k + 1] == expert, weights_ref[:, k : k + 1], 0.0)
    result = jnp.zeros((rows, tail), jnp.float32)
    for step in range(3):
        rounded = dense.astype(jnp.bfloat16).astype(jnp.float32)
        result = jnp.where(part == step, rounded, result)
        dense = dense - rounded
    packed_ref[:, width:] = result.astype(jnp.bfloat16)


def pack(tokens, expert_ids, route_weights, experts):
    rows, width = tokens.shape
    tail = -(-3 * experts // LANES) * LANES
    return pl.pallas_call(
        functools.partial(pack_kernel, experts),
        out_shape=jax.ShapeDtypeStruct((rows, width + tail), jnp.bfloat16),
        in_specs=[HBM] * 3,
        out_specs=VMEM,
        scratch_shapes=[
            pltpu.VMEM(tokens.shape, tokens.dtype),
            pltpu.VMEM(expert_ids.shape, expert_ids.dtype),
            pltpu.VMEM(route_weights.shape, route_weights.dtype),
            pltpu.SemaphoreType.DMA((3,)),
        ],
        compiler_params=pltpu.CompilerParams(vmem_limit_bytes=2 * MIB),
    )(*in_hbm(tokens, expert_ids, route_weights))


def stack_kernel(first_ref, second_ref, out_ref):
    rows = first_ref.shape[0]
    out_ref[:rows, :] = first_ref[...]
    out_ref[rows:, :] = second_ref[...]


def stack(first, second):
    rows, width = first.shape
    return pl.pallas_call(
        stack_kernel,
        out_shape=jax.ShapeDtypeStruct((rows + second.shape[0], width), first.dtype),
        in_specs=[VMEM] * 2,
        out_specs=VMEM,
        compiler_params=pltpu.CompilerParams(vmem_limit_bytes=2 * MIB),
    )(first, second)


def load_kernel(in_ref, in_vmem, sems):
    tiles = in_vmem.shape[0]
    copies = [
        pltpu.make_async_copy(in_ref.at[:, :, pl.ds(t * LANES, LANES)], in_vmem.at[t], sems.at[t])
        for t in range(tiles)
    ]
    for copy in copies:
        copy.start()
    for copy in copies:
        copy.wait()


def load_weights(w_in):
    units, _, width = w_in.shape
    tiles = width // LANES
    loaded = pl.pallas_call(
        load_kernel,
        out_shape=pltpu.VMEM((tiles, units, 2, LANES), w_in.dtype),
        in_specs=[HBM],
        out_specs=VMEM,
        scratch_shapes=[pltpu.SemaphoreType.DMA((tiles,))],
        compiler_params=pltpu.CompilerParams(vmem_limit_bytes=2 * MIB),
        cost_estimate=pl.CostEstimate(flops=0, bytes_accessed=4 * w_in.size, transcendentals=0),
    )(*in_hbm(w_in))
    return loaded.reshape(tiles, units * 2, LANES)


def expert_kernel(exp_dev, experts, count, one_step, *refs):
    group_ref = refs[0]
    x_refs = refs[1 : 1 + count]
    win_ref, wout_hbm, send_ref, keep_ref, mixed, hidden, wout_ref, sem = refs[1 + count :]
    load = pltpu.make_async_copy(wout_hbm, wout_ref, sem)
    if one_step:
        load.start()
    else:
        pl.when(pl.program_id(0) == 0)(load.start)
    tiles, lines, _ = win_ref.shape
    width = tiles * LANES
    per = lines // exp_dev
    rows = sum(ref.shape[0] for ref in x_refs)
    x = jnp.concatenate([ref[:, :width] for ref in x_refs], axis=0)
    tail = jnp.concatenate([ref[:, width:] for ref in x_refs], axis=0)
    contract_last = (((1,), (1,)), ((), ()))
    column = lax.broadcasted_iota(jnp.int32, (16, tail.shape[1]), 1)
    wanted = lax.broadcasted_iota(jnp.int32, (16, tail.shape[1]), 0) + group_ref[0] * exp_dev
    select = (column % experts == wanted) & (column < 3 * experts)
    scale = lax.dot_general(
        select.astype(jnp.bfloat16), tail, contract_last, preferred_element_type=jnp.float32
    )
    for e in range(exp_dev):
        w = jnp.concatenate([win_ref[t, pl.ds(e * per, per), :] for t in range(tiles)], axis=1)
        both = lax.dot_general(w, x, contract_last, preferred_element_type=jnp.float32)
        for r in range(0, rows, LANES):
            mixed[...] = both[:, r : r + LANES]
            gate = mixed[pl.ds(0, per // 2, stride=2), :]
            up = mixed[pl.ds(1, per // 2, stride=2), :]
            act = gate / (1.0 + jnp.exp(-gate)) * up * scale[e : e + 1, r : r + LANES]
            hidden[pl.ds(e * per // 2, per // 2), r : r + LANES] = act.astype(jnp.bfloat16)
    if one_step:
        load.wait()
    else:
        pl.when(pl.program_id(0) == 0)(load.wait)
    chunk = min(512, width)
    pieces, piece, _ = keep_ref.shape
    for c in range(0, width, chunk):
        part = lax.dot_general(
            hidden[...],
            wout_ref[:, c : c + chunk],
            (((0,), (0,)), ((), ())),
            preferred_element_type=jnp.float32,
        )
        for p in range(pieces):
            keep_ref[p, :, c : c + chunk] = part[p * piece : (p + 1) * piece]
            other = part[(pieces + p) * piece : (pieces + p + 1) * piece]
            send_ref[p, :, c : c + chunk] = other.astype(jnp.bfloat16)


def run_experts(group, blocks, win, wout, exp_dev, experts):
    packed_width = blocks[0].shape[1]
    half_rows = sum(block.shape[0] for block in blocks) // 2
    count = len(blocks)
    width = wout.shape[1]
    lines = win.shape[1]
    one_step = half_rows <= LANES
    if one_step:
        x_block, out_block, grid = VMEM, VMEM, ()
        pieces, piece, rows = 1, half_rows, 2 * half_rows
        windows = 0
    else:
        pieces, piece, block = count // 2, blocks[0].shape[0], 16
        x_block = pl.BlockSpec((block, packed_width), lambda i: (i, 0))
        out_block = pl.BlockSpec((pieces, block, width), lambda i: (0, i, 0))
        grid = (piece // block,)
        rows = count * block
        windows = 2 * rows * (2 * packed_width + 3 * width)
    scratch = 2 * wout.size + rows * (6 * lines + 6 * width)
    send, keep = pl.pallas_call(
        functools.partial(expert_kernel, exp_dev, experts, count, one_step),
        grid=grid,
        out_shape=(
            jax.ShapeDtypeStruct((pieces, piece, width), jnp.bfloat16),
            jax.ShapeDtypeStruct((pieces, piece, width), jnp.float32),
        ),
        in_specs=[pl.BlockSpec(memory_space=pltpu.SMEM), *[x_block] * count, VMEM, HBM],
        out_specs=[out_block, out_block],
        scratch_shapes=[
            pltpu.VMEM((lines // exp_dev, LANES), jnp.float32),
            pltpu.VMEM((lines // 2, rows), jnp.bfloat16),
            pltpu.VMEM(wout.shape, wout.dtype),
            pltpu.SemaphoreType.DMA,
        ],
        compiler_params=pltpu.CompilerParams(vmem_limit_bytes=windows + scratch + 4 * MIB),
        cost_estimate=pl.CostEstimate(
            flops=6 * half_rows * width * lines,
            bytes_accessed=4 * half_rows * packed_width + 6 * half_rows * width,
            transcendentals=half_rows * lines,
        ),
    )(group, *blocks, pltpu.with_memory_space_constraint(win, pltpu.VMEM), *in_hbm(wout))
    return send.reshape(half_rows, width), keep.reshape(half_rows, width)


def body(tokens, expert_ids, route_weights, in_weights, out_weights):
    width = tokens.shape[1]
    exp_dev, units = in_weights.shape[:2]
    groups = lax.axis_size("expert")
    planes = lax.axis_size("batch")
    experts = exp_dev * groups
    far = planes - 1
    strides = [groups >> i for i in range(1, groups.bit_length() - 1)]
    w_in = in_weights.reshape(exp_dev * units, 2, width)
    w_out = out_weights.reshape(exp_dev * units, width)

    group = lax.axis_index("expert").astype(jnp.int32).reshape(1)
    x = pack(tokens, expert_ids, route_weights, experts)
    x, group = lax.optimization_barrier((x, group))
    for stride in strides[:-1]:
        x = stack(x, swap(x, "expert", stride))
    across = swap(x, "batch", far)
    mine = stack(x, swap(x, "expert", strides[-1]))
    mine, across, w_in = lax.optimization_barrier((mine, across, w_in))
    early = [mine, across]
    late = [swap(mine, "batch", b) for b in range(1, far)]
    late.append(swap(across, "expert", strides[-1]))
    early_core = [swap(block, "expert", 1) for block in early]
    win = load_weights(w_in)
    late, win = lax.optimization_barrier((late, win))
    late_core = [swap(block, "expert", 1) for block in late]
    blocks = []
    for (mine, across), rest in ((early, late), (early_core, late_core)):
        if 2 * mine.shape[0] * planes <= 2 * LANES:
            blocks += [mine] + rest[:-1] + [across, rest[-1]]
        else:
            blocks += [mine] + rest[:-1] + [jnp.concatenate([across, rest[-1]], axis=0)]

    send, total = run_experts(group, blocks, win, w_out, exp_dev, experts)
    total = total + swap(send, "expert", 1).astype(jnp.float32)
    size = total.shape[0] // planes
    rounded = total.astype(jnp.bfloat16)
    mine = total[:size]
    for b in range(1, far):
        piece = rounded[b * size : (b + 1) * size]
        mine = mine + swap(piece, "batch", b).astype(jnp.float32)
    size = size // 2
    piece = rounded[2 * far * size + size :]
    across = total[2 * far * size : 2 * far * size + size]
    across = across + swap(piece, "expert", strides[-1]).astype(jnp.float32)
    piece = mine[size:].astype(jnp.bfloat16)
    mine = mine[:size] + swap(piece, "expert", strides[-1]).astype(jnp.float32)
    mine = mine + swap(across.astype(jnp.bfloat16), "batch", far).astype(jnp.float32)
    for stride in reversed(strides[:-1]):
        size = size // 2
        piece = mine[size:].astype(jnp.bfloat16)
        mine = mine[:size] + swap(piece, "expert", stride).astype(jnp.float32)
    return mine.astype(jnp.bfloat16)


def solution(mesh):
    return jax.shard_map(
        body,
        mesh=mesh,
        in_specs=(
            P(("batch", "expert"), None),
            P(("batch", "expert"), None),
            P(("batch", "expert"), None),
            P("expert", "batch", None, None),
            P("expert", "batch", None),
        ),
        out_specs=P(("batch", "expert"), None),
        check_vma=False,
    )
```

time: 62.7 us -> 62.9 us (level)
  waiting for transfers between devices: 17.5 us -> 24.1 us
  starting transfers between devices: 29.2 us -> 22.7 us
    ppermute x23 -> x18, waiting for transfers between devices: 17.5 us -> 24.1 us  [swap(): return lax.ppermute(block, axis, [(i, i ^ flips) for i in range(size)])]
    ppermute x23 -> x18, starting transfers between devices: 29.2 us -> 22.7 us  [swap(): return lax.ppermute(block, axis, [(i, i ^ flips) for i in range(size)])]
  transfers between devices with their start and end apart: 23 -> 18, of which waited for: 11 -> 10; matrix products, arithmetic and copies ran while one was open for 0% -> 0% of each run, Pallas kernels for 9% -> 9%
where the time goes in v5:
time: 62.9 us; the launch traced here: 62.7 us
  waiting for transfers between devices  24.1 us (38%)
  starting transfers between devices  22.7 us (36%)
  Pallas kernels  14.4 us (23%)
  other arithmetic  1.19 us (2%)
    ppermute x18, waiting for transfers between devices, swap(): return lax.ppermute(block, axis, [(i, i ^ flips) for i in range(size)])  24.1 us
    ppermute x18, starting transfers between devices, swap(): return lax.ppermute(block, axis, [(i, i ^ flips) for i in range(size)])  22.7 us
    pallas_call x1, Pallas kernels, run_experts(): pl.pallas_call(functools.partial(expert_kernel, exp_dev, experts, count,...  8.05 us
    pallas_call x1, Pallas kernels, load_weights(): pl.pallas_call(load_kernel, out_shape=pltpu.VMEM((tiles, units, 2, LANES)...  5.36 us
  transfers between devices with their start and end apart: 18, of which 10 were waited for; matrix products, arithmetic and copies ran while one was open for 0% of the time, Pallas kernels for 9%

profile of v5, /device:TPU:0, one launch (start us, length us, event | category | flops | bytes accessed | tf_op | source)
XLA Modules:
  0.0 62.7 jit_solution(14876131333882841022)
XLA Ops:
  0.0 1.0 %shard_map.55.first_ref = bf16[8,4224]{1,0:T(8,128)(2,1)S(1)} custom-call(bf16[8,4096]{1,0:T(8,128)(2,1)} %tokens_hbm.1, s32[8,8]{1,0:T(8,128)} %ids_hbm.1, f32[8,8]{1,0:T(8,128)} %weights_hbm.1), custom_call_target="tpu_custom_call" | custom-call | tf_op jit(solution)/shard_map/pallas_call | solution.py:58
  1.0 4.1 %collective-permute-start = (bf16[8,4224]{1,0:T(8,128)(2,1)S(1)}, bf16[8,4224]{1,0:T(8,128)(2,1)S(1)}, u32[]{:S(2)}, u32[]{:S(2)}) collective-permute-start(bf16[8,4224]{1,0:T(8,128)(2,1)S(1)} %shard_map.55.first_ref), channel_id=1, source_target_pairs={{0,4},{1,5},{2,6},{3,7},{4,0},{5,1},{6,2},{7,3},{8,12},{9,13},{10,... | collective-permute-start | bytes 202760 | tf_op jit(solution)/shard_map/ppermute | solution.py:22
  5.1 3.7 %collective-permute-done.second_ref = bf16[8,4224]{1,0:T(8,128)(2,1)S(1)} collective-permute-done((bf16[8,4224]{1,0:T(8,128)(2,1)S(1)}, bf16[8,4224]{1,0:T(8,128)(2,1)S(1)}, u32[]{:S(2)}, u32[]{:S(2)}) %collective-permute-start) | collective-permute-done | bytes 67616 | tf_op jit(solution)/shard_map/ppermute | solution.py:22
  8.8 0.7 %collective-permute-start.1 = (bf16[16,4224]{1,0:T(8,128)(2,1)S(1)}, bf16[16,4224]{1,0:T(8,128)(2,1)S(1)}, u32[]{:S(2)}, u32[]{:S(2)}) collective-permute-start(bf16[16,4224]{1,0:T(8,128)(2,1)S(1)} %shard_map.56.first_ref), channel_id=1, source_target_pairs={{0,2},{1,3},{2,0},{3,1},{4,6},{5,7},{6,4},{7,5},{8,10},{9,11},{10,... | collective-permute-start | bytes 405512 | tf_op jit(solution)/shard_map/ppermute | solution.py:22
  9.5 2.4 %collective-permute-start.2 = (bf16[16,4224]{1,0:T(8,128)(2,1)S(1)}, bf16[16,4224]{1,0:T(8,128)(2,1)S(1)}, u32[]{:S(2)}, u32[]{:S(2)}) collective-permute-start(bf16[16,4224]{1,0:T(8,128)(2,1)S(1)} %shard_map.56.first_ref), channel_id=1, source_target_pairs={{0,24},{8,16},{16,8},{24,0},{1,25},{9,17},{17,9},{25,1},{2,26},{10... | collective-permute-start | bytes 405512 | tf_op jit(solution)/shard_map/ppermute | solution.py:22
  11.9 2.0 %collective-permute-done.1.second_ref = bf16[16,4224]{1,0:T(8,128)(2,1)S(1)} collective-permute-done((bf16[16,4224]{1,0:T(8,128)(2,1)S(1)}, bf16[16,4224]{1,0:T(8,128)(2,1)S(1)}, u32[]{:S(2)}, u32[]{:S(2)}) %collective-permute-start.1) | collective-permute-done | bytes 135200 | tf_op jit(solution)/shard_map/ppermute | solution.py:22
  13.9 1.5 %collective-permute-done.2.refs_4_ = bf16[16,4224]{1,0:T(8,128)(2,1)S(1)} collective-permute-done((bf16[16,4224]{1,0:T(8,128)(2,1)S(1)}, bf16[16,4224]{1,0:T(8,128)(2,1)S(1)}, u32[]{:S(2)}, u32[]{:S(2)}) %collective-permute-start.2) | collective-permute-done | bytes 135200 | tf_op jit(solution)/shard_map/ppermute | solution.py:22
  15.4 1.5 %collective-permute-start.4 = (bf16[32,4224]{1,0:T(8,128)(2,1)S(1)}, bf16[32,4224]{1,0:T(8,128)(2,1)S(1)}, u32[]{:S(2)}, u32[]{:S(2)}) collective-permute-start(bf16[32,4224]{1,0:T(8,128)(2,1)S(1)} %shard_map.57.refs_1_), channel_id=1, source_target_pairs={{0,16},{8,24},{16,0},{24,8},{1,17},{9,25},{17,1},{25,9},{2,18},{10... | collective-permute-start | bytes 811016 | tf_op jit(solution)/shard_map/ppermute | solution.py:22
  16.9 1.5 %collective-permute-start.3 = (bf16[32,4224]{1,0:T(8,128)(2,1)S(1)}, bf16[32,4224]{1,0:T(8,128)(2,1)S(1)}, u32[]{:S(2)}, u32[]{:S(2)}) collective-permute-start(bf16[32,4224]{1,0:T(8,128)(2,1)S(1)} %shard_map.57.refs_1_), channel_id=1, source_target_pairs={{0,8},{8,0},{16,24},{24,16},{1,9},{9,1},{17,25},{25,17},{2,10},{10... | collective-permute-start | bytes 811016 | tf_op jit(solution)/shard_map/ppermute | solution.py:22
  18.4 1.7 %collective-permute-start.5 = (bf16[16,4224]{1,0:T(8,128)(2,1)S(1)}, bf16[16,4224]{1,0:T(8,128)(2,1)S(1)}, u32[]{:S(2)}, u32[]{:S(2)}) collective-permute-start(bf16[16,4224]{1,0:T(8,128)(2,1)S(1)} %collective-permute-done.2.refs_4_), channel_id=1, source_target_pairs={{0,2},{1,3},{2,0},{3,1},{4,6},{5,7},{6,4},{7,5},{8,10},{9,11},{10,... | collective-permute-start | bytes 405512 | tf_op jit(solution)/shard_map/ppermute | solution.py:22
  20.1 0.0 collective-permute-start.6
  20.1 5.4 %shard_map.58 = bf16[32,768,2,128]{3,2,1,0:T(2,128)(2,1)S(1)} custom-call(bf16[768,2,4096]{2,1,0:T(2,128)(2,1)} %bitcast.10), custom_call_target="tpu_custom_call" | custom-call | bytes 25165824 | tf_op jit(solution)/shard_map/pallas_call | solution.py:105
  25.5 0.0 collective-permute-done.5.refs_5_
  25.5 0.0 collective-permute-done.4.refs_3_
  25.5 0.0 collective-permute-done.3.refs_2_
  25.5 0.6 collective-permute-start.7
  26.1 0.1 collective-permute-start.8
  26.2 0.4 collective-permute-start.9
  26.6 0.1 collective-permute-start.10
  26.7 1.2 %collective-permute-done.9.refs_9_ = bf16[16,4224]{1,0:T(8,128)(2,1)S(1)} collective-permute-done((bf16[16,4224]{1,0:T(8,128)(2,1)S(1)}, bf16[16,4224]{1,0:T(8,128)(2,1)S(1)}, u32[]{:S(2)}, u32[]{:S(2)}) %collective-permute-start.9) | collective-permute-done | bytes 135200 | tf_op jit(solution)/shard_map/ppermute | solution.py:22
  27.8 0.0 collective-permute-done.6.refs_6_
  27.9 0.2 collective-permute-done.10.refs_10_
  28.0 0.0 collective-permute-done.7.refs_7_
  28.0 0.0 collective-permute-done.8.refs_8_
  28.0 8.1 %shard_map.59 = (bf16[1,128,4096]{2,1,0:T(8,128)(2,1)S(1)}, f32[1,128,4096]{2,1,0:T(8,128)S(1)}) custom-call(s32[1]{0:T(128)} %bitcast.refs_0_, bf16[32,4224]{1,0:T(8,128)(2,1)S(1)} %shard_map.57.refs_1_, bf16[32,4224]{1,0:T(8,128)(2,1)S(1)} %collective-permute-done.3.refs_2_, bf16[32,4224]{1,0:T(8,128)(2,1)S(1)} %collective-permute-done.4.refs_3_, ...), custom_call_target="tpu_custom_call" | custom-call | flops 4831838208 | bytes 5308416 | tf_op jit(solution)/shard_map/pallas_call | solution.py:186
  36.1 0.4 collective-permute-start.11
  36.5 2.3 %collective-permute-done.11 = bf16[128,4096]{1,0:T(8,128)(2,1)S(1)} collective-permute-done((bf16[128,4096]{1,0:T(8,128)(2,1)S(1)}, bf16[128,4096]{1,0:T(8,128)(2,1)S(1)}, u32[]{:S(2)}, u32[]{:S(2)}) %collective-permute-start.11) | collective-permute-done | bytes 1048608 | tf_op jit(solution)/shard_map/ppermute | solution.py:22
  38.8 0.4 fusion.4
  39.2 0.4 collective-permute-start.15
  39.7 0.6 collective-permute-start.12
  40.3 0.5 collective-permute-start.13
  40.8 4.3 %collective-permute-done.15 = bf16[16,4096]{1,0:T(8,128)(2,1)S(1)} collective-permute-done((bf16[16,4096]{1,0:T(8,128)(2,1)S(1)}, bf16[16,4096]{1,0:T(8,128)(2,1)S(1)}, u32[]{:S(2)}, u32[]{:S(2)}) %collective-permute-start.15) | collective-permute-done | bytes 131104 | tf_op jit(solution)/shard_map/ppermute | solution.py:22
  45.1 0.3 collective-permute-start.16
  45.4 3.3 %collective-permute-done.12 = bf16[32,4096]{1,0:T(8,128)(2,1)S(1)} collective-permute-done((bf16[32,4096]{1,0:T(8,128)(2,1)S(1)}, bf16[32,4096]{1,0:T(8,128)(2,1)S(1)}, u32[]{:S(2)}, u32[]{:S(2)}) %collective-permute-start.12) | collective-permute-done | bytes 262176 | tf_op jit(solution)/shard_map/ppermute | solution.py:22
  48.7 0.0 collective-permute-done.13
  48.7 0.1 fusion
  48.9 4.1 %collective-permute-start.14 = (bf16[16,4096]{1,0:T(8,128)(2,1)S(1)}, bf16[16,4096]{1,0:T(8,128)(2,1)S(1)}, u32[]{:S(2)}, u32[]{:S(2)}) collective-permute-start(bf16[16,4096]{1,0:T(8,128)(2,1)S(1)} %slice.61), channel_id=1, source_target_pairs={{0,2},{1,3},{2,0},{3,1},{4,6},{5,7},{6,4},{7,5},{8,10},{9,11},{10,... | collective-permute-start | bytes 393224 | tf_op jit(solution)/shard_map/ppermute | solution.py:22
  53.0 0.0 collective-permute-done.16
  53.0 3.4 %collective-permute-done.14 = bf16[16,4096]{1,0:T(8,128)(2,1)S(1)} collective-permute-done((bf16[16,4096]{1,0:T(8,128)(2,1)S(1)}, bf16[16,4096]{1,0:T(8,128)(2,1)S(1)}, u32[]{:S(2)}, u32[]{:S(2)}) %collective-permute-start.14) | collective-permute-done | bytes 131104 | tf_op jit(solution)/shard_map/ppermute | solution.py:22
  56.5 3.3 %collective-permute-start.17 = (bf16[8,4096]{1,0:T(8,128)(2,1)S(1)}, bf16[8,4096]{1,0:T(8,128)(2,1)S(1)}, u32[]{:S(2)}, u32[]{:S(2)}) collective-permute-start(bf16[8,4096]{1,0:T(8,128)(2,1)S(1)} %slice.62), channel_id=1, source_target_pairs={{0,4},{1,5},{2,6},{3,7},{4,0},{5,1},{6,2},{7,3},{8,12},{9,13},{10,... | collective-permute-start | bytes 196616 | tf_op jit(solution)/shard_map/ppermute | solution.py:22
  59.8 2.2 %collective-permute-done.17 = bf16[8,4096]{1,0:T(8,128)(2,1)S(1)} collective-permute-done((bf16[8,4096]{1,0:T(8,128)(2,1)S(1)}, bf16[8,4096]{1,0:T(8,128)(2,1)S(1)}, u32[]{:S(2)}, u32[]{:S(2)}) %collective-permute-start.17) | collective-permute-done | bytes 65568 | tf_op jit(solution)/shard_map/ppermute | solution.py:22
  62.0 0.6 %fusion.3 = bf16[8,4096]{1,0:T(8,128)(2,1)} fusion(f32[16,4096]{1,0:T(8,128)S(1)} %fusion.2, bf16[8,4096]{1,0:T(8,128)(2,1)S(1)} %collective-permute-done.17), kind=kLoop, calls=%fused_computation.10 | loop fusion | flops 98304 | bytes 262144 | tf_op jit(solution)/shard_map/convert_element_type | solution.py:263
  (8 shorter events, 0.2 us)
Async XLA Ops:
  1.0 7.8 %collective-permute-start = (bf16[8,4224]{1,0:T(8,128)(2,1)S(1)}, bf16[8,4224]{1,0:T(8,128)(2,1)S(1)}, u32[]{:S(2)}, u32[]{:S(2)}) collective-permute-start(bf16[8,4224]{1,0:T(8,128)(2,1)S(1)} %shard_map.55.first_ref), channel_id=1, source_target_pairs={{0,4},{1,5},{2,6},{3,7},{4,0},{5,1},{6,2},{7,3},{8,12},{9,13},{10,... | collective-permute-start | bytes 202760 | tf_op jit(solution)/shard_map/ppermute | solution.py:22
  8.8 5.1 %collective-permute-start.1 = (bf16[16,4224]{1,0:T(8,128)(2,1)S(1)}, bf16[16,4224]{1,0:T(8,128)(2,1)S(1)}, u32[]{:S(2)}, u32[]{:S(2)}) collective-permute-start(bf16[16,4224]{1,0:T(8,128)(2,1)S(1)} %shard_map.56.first_ref), channel_id=1, source_target_pairs={{0,2},{1,3},{2,0},{3,1},{4,6},{5,7},{6,4},{7,5},{8,10},{9,11},{10,... | collective-permute-start | bytes 405512 | tf_op jit(solution)/shard_map/ppermute | solution.py:22
  9.5 5.9 %collective-permute-start.2 = (bf16[16,4224]{1,0:T(8,128)(2,1)S(1)}, bf16[16,4224]{1,0:T(8,128)(2,1)S(1)}, u32[]{:S(2)}, u32[]{:S(2)}) collective-permute-start(bf16[16,4224]{1,0:T(8,128)(2,1)S(1)} %shard_map.56.first_ref), channel_id=1, source_target_pairs={{0,24},{8,16},{16,8},{24,0},{1,25},{9,17},{17,9},{25,1},{2,26},{10... | collective-permute-start | bytes 405512 | tf_op jit(solution)/shard_map/ppermute | solution.py:22
  15.4 10.1 %collective-permute-start.4 = (bf16[32,4224]{1,0:T(8,128)(2,1)S(1)}, bf16[32,4224]{1,0:T(8,128)(2,1)S(1)}, u32[]{:S(2)}, u32[]{:S(2)}) collective-permute-start(bf16[32,4224]{1,0:T(8,128)(2,1)S(1)} %shard_map.57.refs_1_), channel_id=1, source_target_pairs={{0,16},{8,24},{16,0},{24,8},{1,17},{9,25},{17,1},{25,9},{2,18},{10... | collective-permute-start | bytes 811016 | tf_op jit(solution)/shard_map/ppermute | solution.py:22
  16.9 8.6 %collective-permute-start.3 = (bf16[32,4224]{1,0:T(8,128)(2,1)S(1)}, bf16[32,4224]{1,0:T(8,128)(2,1)S(1)}, u32[]{:S(2)}, u32[]{:S(2)}) collective-permute-start(bf16[32,4224]{1,0:T(8,128)(2,1)S(1)} %shard_map.57.refs_1_), channel_id=1, source_target_pairs={{0,8},{8,0},{16,24},{24,16},{1,9},{9,1},{17,25},{25,17},{2,10},{10... | collective-permute-start | bytes 811016 | tf_op jit(solution)/shard_map/ppermute | solution.py:22
  18.4 7.1 %collective-permute-start.5 = (bf16[16,4224]{1,0:T(8,128)(2,1)S(1)}, bf16[16,4224]{1,0:T(8,128)(2,1)S(1)}, u32[]{:S(2)}, u32[]{:S(2)}) collective-permute-start(bf16[16,4224]{1,0:T(8,128)(2,1)S(1)} %collective-permute-done.2.refs_4_), channel_id=1, source_target_pairs={{0,2},{1,3},{2,0},{3,1},{4,6},{5,7},{6,4},{7,5},{8,10},{9,11},{10,... | collective-permute-start | bytes 405512 | tf_op jit(solution)/shard_map/ppermute | solution.py:22
  20.1 7.7 %collective-permute-start.6 = (bf16[32,4224]{1,0:T(8,128)(2,1)S(1)}, bf16[32,4224]{1,0:T(8,128)(2,1)S(1)}, u32[]{:S(2)}, u32[]{:S(2)}) collective-permute-start(bf16[32,4224]{1,0:T(8,128)(2,1)S(1)} %shard_map.57.refs_1_), channel_id=1, source_target_pairs={{0,1},{1,0},{2,3},{3,2},{4,5},{5,4},{6,7},{7,6},{8,9},{9,8},{10,11... | collective-permute-start | bytes 811016 | tf_op jit(solution)/shard_map/ppermute | solution.py:22
  25.5 2.5 %collective-permute-start.7 = (bf16[32,4224]{1,0:T(8,128)(2,1)S(1)}, bf16[32,4224]{1,0:T(8,128)(2,1)S(1)}, u32[]{:S(2)}, u32[]{:S(2)}) collective-permute-start(bf16[32,4224]{1,0:T(8,128)(2,1)S(1)} %collective-permute-done.3.refs_2_), channel_id=1, source_target_pairs={{0,1},{1,0},{2,3},{3,2},{4,5},{5,4},{6,7},{7,6},{8,9},{9,8},{10,11... | collective-permute-start | bytes 811016 | tf_op jit(solution)/shard_map/ppermute | solution.py:22
  26.1 2.0 %collective-permute-start.8 = (bf16[32,4224]{1,0:T(8,128)(2,1)S(1)}, bf16[32,4224]{1,0:T(8,128)(2,1)S(1)}, u32[]{:S(2)}, u32[]{:S(2)}) collective-permute-start(bf16[32,4224]{1,0:T(8,128)(2,1)S(1)} %collective-permute-done.4.refs_3_), channel_id=1, source_target_pairs={{0,1},{1,0},{2,3},{3,2},{4,5},{5,4},{6,7},{7,6},{8,9},{9,8},{10,11... | collective-permute-start | bytes 811016 | tf_op jit(solution)/shard_map/ppermute | solution.py:22
  26.2 1.7 %collective-permute-start.9 = (bf16[16,4224]{1,0:T(8,128)(2,1)S(1)}, bf16[16,4224]{1,0:T(8,128)(2,1)S(1)}, u32[]{:S(2)}, u32[]{:S(2)}) collective-permute-start(bf16[16,4224]{1,0:T(8,128)(2,1)S(1)} %collective-permute-done.2.refs_4_), channel_id=1, source_target_pairs={{0,1},{1,0},{2,3},{3,2},{4,5},{5,4},{6,7},{7,6},{8,9},{9,8},{10,11... | collective-permute-start | bytes 405512 | tf_op jit(solution)/shard_map/ppermute | solution.py:22
  26.6 1.4 %collective-permute-start.10 = (bf16[16,4224]{1,0:T(8,128)(2,1)S(1)}, bf16[16,4224]{1,0:T(8,128)(2,1)S(1)}, u32[]{:S(2)}, u32[]{:S(2)}) collective-permute-start(bf16[16,4224]{1,0:T(8,128)(2,1)S(1)} %collective-permute-done.5.refs_5_), channel_id=1, source_target_pairs={{0,1},{1,0},{2,3},{3,2},{4,5},{5,4},{6,7},{7,6},{8,9},{9,8},{10,11... | collective-permute-start | bytes 405512 | tf_op jit(solution)/shard_map/ppermute | solution.py:22
  36.1 2.7 %collective-permute-start.11 = (bf16[128,4096]{1,0:T(8,128)(2,1)S(1)}, bf16[128,4096]{1,0:T(8,128)(2,1)S(1)}, u32[]{:S(2)}, u32[]{:S(2)}) collective-permute-start(bf16[128,4096]{1,0:T(8,128)(2,1)S(1)} %bitcast.9), channel_id=1, source_target_pairs={{0,1},{1,0},{2,3},{3,2},{4,5},{5,4},{6,7},{7,6},{8,9},{9,8},{10,11... | collective-permute-start | bytes 3145736 | tf_op jit(solution)/shard_map/ppermute | solution.py:22
  39.2 5.8 %collective-permute-start.15 = (bf16[16,4096]{1,0:T(8,128)(2,1)S(1)}, bf16[16,4096]{1,0:T(8,128)(2,1)S(1)}, u32[]{:S(2)}, u32[]{:S(2)}) collective-permute-start(bf16[16,4096]{1,0:T(8,128)(2,1)S(1)} %slice.44), channel_id=1, source_target_pairs={{0,2},{1,3},{2,0},{3,1},{4,6},{5,7},{6,4},{7,5},{8,10},{9,11},{10,... | collective-permute-start | bytes 393224 | tf_op jit(solution)/shard_map/ppermute | solution.py:22
  39.7 9.1 %collective-permute-start.12 = (bf16[32,4096]{1,0:T(8,128)(2,1)S(1)}, bf16[32,4096]{1,0:T(8,128)(2,1)S(1)}, u32[]{:S(2)}, u32[]{:S(2)}) collective-permute-start(bf16[32,4096]{1,0:T(8,128)(2,1)S(1)} %get-tuple-element.29), channel_id=1, source_target_pairs={{0,8},{8,0},{16,24},{24,16},{1,9},{9,1},{17,25},{25,17},{2,10},{10... | collective-permute-start | bytes 786440 | tf_op jit(solution)/shard_map/ppermute | solution.py:22
  40.3 8.4 %collective-permute-start.13 = (bf16[32,4096]{1,0:T(8,128)(2,1)S(1)}, bf16[32,4096]{1,0:T(8,128)(2,1)S(1)}, u32[]{:S(2)}, u32[]{:S(2)}) collective-permute-start(bf16[32,4096]{1,0:T(8,128)(2,1)S(1)} %get-tuple-element.30), channel_id=1, source_target_pairs={{0,16},{8,24},{16,0},{24,8},{1,17},{9,25},{17,1},{25,9},{2,18},{10... | collective-permute-start | bytes 786440 | tf_op jit(solution)/shard_map/ppermute | solution.py:22
  45.1 7.9 %collective-permute-start.16 = (bf16[16,4096]{1,0:T(8,128)(2,1)S(1)}, bf16[16,4096]{1,0:T(8,128)(2,1)S(1)}, u32[]{:S(2)}, u32[]{:S(2)}) collective-permute-start(bf16[16,4096]{1,0:T(8,128)(2,1)S(1)} %fusion.1), channel_id=1, source_target_pairs={{0,24},{8,16},{16,8},{24,0},{1,25},{9,17},{17,9},{25,1},{2,26},{10... | collective-permute-start | bytes 393224 | tf_op jit(solution)/shard_map/ppermute | solution.py:22
  48.9 7.6 %collective-permute-start.14 = (bf16[16,4096]{1,0:T(8,128)(2,1)S(1)}, bf16[16,4096]{1,0:T(8,128)(2,1)S(1)}, u32[]{:S(2)}, u32[]{:S(2)}) collective-permute-start(bf16[16,4096]{1,0:T(8,128)(2,1)S(1)} %slice.61), channel_id=1, source_target_pairs={{0,2},{1,3},{2,0},{3,1},{4,6},{5,7},{6,4},{7,5},{8,10},{9,11},{10,... | collective-permute-start | bytes 393224 | tf_op jit(solution)/shard_map/ppermute | solution.py:22
  56.5 5.5 %collective-permute-start.17 = (bf16[8,4096]{1,0:T(8,128)(2,1)S(1)}, bf16[8,4096]{1,0:T(8,128)(2,1)S(1)}, u32[]{:S(2)}, u32[]{:S(2)}) collective-permute-start(bf16[8,4096]{1,0:T(8,128)(2,1)S(1)} %slice.62), channel_id=1, source_target_pairs={{0,4},{1,5},{2,6},{3,7},{4,0},{5,1},{6,2},{7,3},{8,12},{9,13},{10,... | collective-permute-start | bytes 196616 | tf_op jit(solution)/shard_map/ppermute | solution.py:22

commit v6 on v5

--- a/solution.py
+++ b/solution.py
@@ -1,4 +1,5 @@
 import functools
+import math
 
 import jax
 import jax.numpy as jnp
@@ -15,6 +16,10 @@
 
 def in_hbm(*arrays):
     return [pltpu.with_memory_space_constraint(array, pltpu.HBM) for array in arrays]
+
+
+def in_vmem(*arrays):
+    return [pltpu.with_memory_space_constraint(array, pltpu.VMEM) for array in arrays]
 
 
 def swap(block, axis, flips):
@@ -70,28 +75,32 @@
     )(*in_hbm(tokens, expert_ids, route_weights))
 
 
-def stack_kernel(first_ref, second_ref, out_ref):
+def stack_kernel(count, first_ref, second_ref, *refs):
+    out_ref = refs[count]
     rows = first_ref.shape[0]
     out_ref[:rows, :] = first_ref[...]
     out_ref[rows:, :] = second_ref[...]
 
 
-def stack(first, second):
+def stack(first, second, held):
     rows, width = first.shape
     return pl.pallas_call(
-        stack_kernel,
-        out_shape=jax.ShapeDtypeStruct((rows + second.shape[0], width), first.dtype),
-        in_specs=[VMEM] * 2,
-        out_specs=VMEM,
+        functools.partial(stack_kernel, len(held)),
+        out_shape=[jax.ShapeDtypeStruct((rows + second.shape[0], width), first.dtype)]
+        + [pltpu.VMEM(array.shape, array.dtype) for array in held],
+        in_specs=[VMEM] * (2 + len(held)),
+        out_specs=[VMEM] * (1 + len(held)),
+        input_output_aliases={2 + i: 1 + i for i in range(len(held))},
         compiler_params=pltpu.CompilerParams(vmem_limit_bytes=2 * MIB),
-    )(first, second)
-
-
-def load_kernel(in_ref, in_vmem, sems):
-    tiles = in_vmem.shape[0]
+    )(first, second, *in_vmem(*held))
+
+
+def load_in_kernel(first, in_ref, in_vmem, sems):
     copies = [
-        pltpu.make_async_copy(in_ref.at[:, :, pl.ds(t * LANES, LANES)], in_vmem.at[t], sems.at[t])
-        for t in range(tiles)
+        pltpu.make_async_copy(
+            in_ref.at[:, :, pl.ds((first + t) * LANES, LANES)], in_vmem.at[t], sems.at[t]
+        )
+        for t in range(in_vmem.shape[0])
     ]
     for copy in copies:
         copy.start()
@@ -99,32 +108,45 @@
         copy.wait()
 
 
-def load_weights(w_in):
-    units, _, width = w_in.shape
-    tiles = width // LANES
-    loaded = pl.pallas_call(
-        load_kernel,
-        out_shape=pltpu.VMEM((tiles, units, 2, LANES), w_in.dtype),
+def load_out_kernel(out_ref, out_vmem, sems):
+    copies = []
+    step = out_ref.shape[0] // sems.shape[0]
+    for i in range(sems.shape[0]):
+        rows = pl.ds(i * step, step)
+        copies.append(pltpu.make_async_copy(out_ref.at[rows], out_vmem.at[rows], sems.at[i]))
+    for copy in copies:
+        copy.start()
+    for copy in copies:
+        copy.wait()
+
+
+def load(kernel, source, shape, copies):
+    return pl.pallas_call(
+        kernel,
+        out_shape=pltpu.VMEM(shape, source.dtype),
         in_specs=[HBM],
         out_specs=VMEM,
-        scratch_shapes=[pltpu.SemaphoreType.DMA((tiles,))],
+        scratch_shapes=[pltpu.SemaphoreType.DMA((copies,))],
         compiler_params=pltpu.CompilerParams(vmem_limit_bytes=2 * MIB),
-        cost_estimate=pl.CostEstimate(flops=0, bytes_accessed=4 * w_in.size, transcendentals=0),
-    )(*in_hbm(w_in))
-    return loaded.reshape(tiles, units * 2, LANES)
-
-
-def expert_kernel(exp_dev, experts, count, one_step, *refs):
+        cost_estimate=pl.CostEstimate(
+            flops=0, bytes_accessed=4 * math.prod(shape), transcendentals=0
+        ),
+    )(*in_hbm(source))
+
+
+def load_in(w_in, first, tiles):
+    units = w_in.shape[0]
+    kernel = functools.partial(load_in_kernel, first)
+    loaded = load(kernel, w_in, (tiles, units, 2, LANES), tiles)
+    return loaded.reshape(tiles, 2 * units, LANES)
+
+
+def expert_kernel(exp_dev, experts, count, *refs):
     group_ref = refs[0]
     x_refs = refs[1 : 1 + count]
-    win_ref, wout_hbm, send_ref, keep_ref, mixed, hidden, wout_ref, sem = refs[1 + count :]
-    load = pltpu.make_async_copy(wout_hbm, wout_ref, sem)
-    if one_step:
-        load.start()
-    else:
-        pl.when(pl.program_id(0) == 0)(load.start)
-    tiles, lines, _ = win_ref.shape
-    width = tiles * LANES
+    low_ref, high_ref, wout_ref, send_ref, keep_ref, mixed, hidden = refs[1 + count :]
+    lines = low_ref.shape[1]
+    width = wout_ref.shape[1]
     per = lines // exp_dev
     rows = sum(ref.shape[0] for ref in x_refs)
     x = jnp.concatenate([ref[:, :width] for ref in x_refs], axis=0)
@@ -137,7 +159,14 @@
         select.astype(jnp.bfloat16), tail, contract_last, preferred_element_type=jnp.float32
     )
     for e in range(exp_dev):
-        w = jnp.concatenate([win_ref[t, pl.ds(e * per, per), :] for t in range(tiles)], axis=1)
+        w = jnp.concatenate(
+            [
+                ref[t, pl.ds(e * per, per), :]
+                for ref in (low_ref, high_ref)
+                for t in range(ref.shape[0])
+            ],
+            axis=1,
+        )
         both = lax.dot_general(w, x, contract_last, preferred_element_type=jnp.float32)
         for r in range(0, rows, LANES):
             mixed[...] = both[:, r : r + LANES]
@@ -145,10 +174,6 @@
             up = mixed[pl.ds(1, per // 2, stride=2), :]
             act = gate / (1.0 + jnp.exp(-gate)) * up * scale[e : e + 1, r : r + LANES]
             hidden[pl.ds(e * per // 2, per // 2), r : r + LANES] = act.astype(jnp.bfloat16)
-    if one_step:
-        load.wait()
-    else:
-        pl.when(pl.program_id(0) == 0)(load.wait)
     chunk = min(512, width)
     pieces, piece, _ = keep_ref.shape
     for c in range(0, width, chunk):
@@ -164,12 +189,12 @@
             send_ref[p, :, c : c + chunk] = other.astype(jnp.bfloat16)
 
 
-def run_experts(group, blocks, win, wout, exp_dev, experts):
+def run_experts(group, blocks, low, high, wout, exp_dev, experts):
     packed_width = blocks[0].shape[1]
     half_rows = sum(block.shape[0] for block in blocks) // 2
     count = len(blocks)
     width = wout.shape[1]
-    lines = win.shape[1]
+    lines = low.shape[1]
     one_step = half_rows <= LANES
     if one_step:
         x_block, out_block, grid = VMEM, VMEM, ()
@@ -182,21 +207,19 @@
         grid = (piece // block,)
         rows = count * block
         windows = 2 * rows * (2 * packed_width + 3 * width)
-    scratch = 2 * wout.size + rows * (6 * lines + 6 * width)
+    scratch = rows * (6 * lines + 6 * width)
     send, keep = pl.pallas_call(
-        functools.partial(expert_kernel, exp_dev, experts, count, one_step),
+        functools.partial(expert_kernel, exp_dev, experts, count),
         grid=grid,
         out_shape=(
             jax.ShapeDtypeStruct((pieces, piece, width), jnp.bfloat16),
             jax.ShapeDtypeStruct((pieces, piece, width), jnp.float32),
         ),
-        in_specs=[pl.BlockSpec(memory_space=pltpu.SMEM), *[x_block] * count, VMEM, HBM],
+        in_specs=[pl.BlockSpec(memory_space=pltpu.SMEM), *[x_block] * count, VMEM, VMEM, VMEM],
         out_specs=[out_block, out_block],
         scratch_shapes=[
             pltpu.VMEM((lines // exp_dev, LANES), jnp.float32),
             pltpu.VMEM((lines // 2, rows), jnp.bfloat16),
-            pltpu.VMEM(wout.shape, wout.dtype),
-            pltpu.SemaphoreType.DMA,
         ],
         compiler_params=pltpu.CompilerParams(vmem_limit_bytes=windows + scratch + 4 * MIB),
         cost_estimate=pl.CostEstimate(
@@ -204,7 +227,7 @@
             bytes_accessed=4 * half_rows * packed_width + 6 * half_rows * width,
             transcendentals=half_rows * lines,
         ),
-    )(group, *blocks, pltpu.with_memory_space_constraint(win, pltpu.VMEM), *in_hbm(wout))
+    )(group, *blocks, *in_vmem(low, high, wout))
     return send.reshape(half_rows, width), keep.reshape(half_rows, width)
 
 
@@ -221,18 +244,24 @@
 
     group = lax.axis_index("expert").astype(jnp.int32).reshape(1)
     x = pack(tokens, expert_ids, route_weights, experts)
-    x, group = lax.optimization_barrier((x, group))
+    x, group, w_in, w_out = lax.optimization_barrier((x, group, w_in, w_out))
+    tiles = width // LANES
+    wout = load(load_out_kernel, w_out, w_out.shape, 8)
     for stride in strides[:-1]:
-        x = stack(x, swap(x, "expert", stride))
+        x, wout = stack(x, swap(x, "expert", stride), [wout])
+    x, w_in = lax.optimization_barrier((x, w_in))
     across = swap(x, "batch", far)
-    mine = stack(x, swap(x, "expert", strides[-1]))
+    mine = swap(x, "expert", strides[-1])
+    low = load_in(w_in, 0, tiles // 2)
+    across, mine, low = lax.optimization_barrier((across, mine, low))
+    mine, wout, low = stack(x, mine, [wout, low])
     mine, across, w_in = lax.optimization_barrier((mine, across, w_in))
     early = [mine, across]
     late = [swap(mine, "batch", b) for b in range(1, far)]
     late.append(swap(across, "expert", strides[-1]))
     early_core = [swap(block, "expert", 1) for block in early]
-    win = load_weights(w_in)
-    late, win = lax.optimization_barrier((late, win))
+    high = load_in(w_in, tiles // 2, tiles - tiles // 2)
+    late, high = lax.optimization_barrier((late, high))
     late_core = [swap(block, "expert", 1) for block in late]
     blocks = []
     for (mine, across), rest in ((early, late), (early_core, late_core)):
@@ -241,7 +270,7 @@
         else:
             blocks += [mine] + rest[:-1] + [jnp.concatenate([across, rest[-1]], axis=0)]
 
-    send, total = run_experts(group, blocks, win, w_out, exp_dev, experts)
+    send, total = run_experts(group, blocks, low, high, wout, exp_dev, experts)
     total = total + swap(send, "expert", 1).astype(jnp.float32)
     size = total.shape[0] // planes
     rounded = total.astype(jnp.bfloat16)

time: 62.9 us -> 61 us (0.970)
  starting transfers between devices: 22.7 us -> 20.5 us
  Pallas kernels: 14.4 us -> 15.6 us
  waiting for transfers between devices: 24.1 us -> 23.3 us
    ppermute x18, starting transfers between devices: 22.7 us -> 20.5 us  [swap(): return lax.ppermute(block, axis, [(i, i ^ flips) for i in range(size)])]
    pallas_call x4 -> x6, Pallas kernels: 13.4 us -> 14.6 us  [the longest x3 9.16 us: load(): pl.pallas_call(kernel, out_shape=pltpu.VMEM(shape, source.dtype), in_spec...]
    ppermute x18, waiting for transfers between devices: 24.1 us -> 23.3 us  [swap(): return lax.ppermute(block, axis, [(i, i ^ flips) for i in range(size)])]
  transfers between devices with their start and end apart: 18 -> 18, of which waited for: 10 -> 11; matrix products, arithmetic and copies ran while one was open for 0% -> 0% of each run, Pallas kernels for 9% -> 15%
where the time goes in v6:
time: 61 us; the launch traced here: 60.8 us
  waiting for transfers between devices  23.3 us (38%)
  starting transfers between devices  20.5 us (34%)
  Pallas kernels  15.6 us (26%)
  other arithmetic  1.19 us (2%)
    ppermute x18, waiting for transfers between devices, swap(): return lax.ppermute(block, axis, [(i, i ^ flips) for i in range(size)])  23.3 us
    ppermute x18, starting transfers between devices, swap(): return lax.ppermute(block, axis, [(i, i ^ flips) for i in range(size)])  20.5 us
    pallas_call x3, Pallas kernels, load(): pl.pallas_call(kernel, out_shape=pltpu.VMEM(shape, source.dtype), in_spec...  9.16 us
    pallas_call x1, Pallas kernels, run_experts(): pl.pallas_call(functools.partial(expert_kernel, exp_dev, experts, count),...  5.44 us
  transfers between devices with their start and end apart: 18, of which 11 were waited for; matrix products, arithmetic and copies ran while one was open for 0% of the time, Pallas kernels for 15%

profile of v6, /device:TPU:0, one launch (start us, length us, event | category | flops | bytes accessed | tf_op | source)
XLA Modules:
  0.0 60.8 jit_solution(17405086917017002933)
XLA Ops:
  0.0 1.0 %shard_map.55.first_ref = bf16[8,4224]{1,0:T(8,128)(2,1)S(1)} custom-call(bf16[8,4096]{1,0:T(8,128)(2,1)} %tokens_hbm.1, s32[8,8]{1,0:T(8,128)} %ids_hbm.1, f32[8,8]{1,0:T(8,128)} %weights_hbm.1), custom_call_target="tpu_custom_call" | custom-call | tf_op jit(solution)/shard_map/pallas_call | solution.py:63
  1.0 4.1 %collective-permute-start = (bf16[8,4224]{1,0:T(8,128)(2,1)S(1)}, bf16[8,4224]{1,0:T(8,128)(2,1)S(1)}, u32[]{:S(2)}, u32[]{:S(2)}) collective-permute-start(bf16[8,4224]{1,0:T(8,128)(2,1)S(1)} %shard_map.55.first_ref), channel_id=1, source_target_pairs={{0,4},{1,5},{2,6},{3,7},{4,0},{5,1},{6,2},{7,3},{8,12},{9,13},{10,... | collective-permute-start | bytes 202760 | tf_op jit(solution)/shard_map/ppermute | solution.py:27
  5.1 2.9 %shard_map.56.refs_0_ = bf16[768,4096]{1,0:T(8,128)(2,1)S(1)} custom-call(bf16[768,4096]{1,0:T(8,128)(2,1)} %bitcast.14), custom_call_target="tpu_custom_call" | custom-call | bytes 12582912 | tf_op jit(solution)/shard_map/pallas_call | solution.py:124
  8.0 0.9 %collective-permute-done.second_ref = bf16[8,4224]{1,0:T(8,128)(2,1)S(1)} collective-permute-done((bf16[8,4224]{1,0:T(8,128)(2,1)S(1)}, bf16[8,4224]{1,0:T(8,128)(2,1)S(1)}, u32[]{:S(2)}, u32[]{:S(2)}) %collective-permute-start) | collective-permute-done | bytes 67616 | tf_op jit(solution)/shard_map/ppermute | solution.py:27
  8.8 0.8 %collective-permute-start.2 = (bf16[16,4224]{1,0:T(8,128)(2,1)S(1)}, bf16[16,4224]{1,0:T(8,128)(2,1)S(1)}, u32[]{:S(2)}, u32[]{:S(2)}) collective-permute-start(bf16[16,4224]{1,0:T(8,128)(2,1)S(1)} %get-tuple-element.33.first_ref), channel_id=1, source_target_pairs={{0,2},{1,3},{2,0},{3,1},{4,6},{5,7},{6,4},{7,5},{8,10},{9,11},{10,... | collective-permute-start | bytes 405512 | tf_op jit(solution)/shard_map/ppermute | solution.py:27
  9.6 2.4 %collective-permute-start.1 = (bf16[16,4224]{1,0:T(8,128)(2,1)S(1)}, bf16[16,4224]{1,0:T(8,128)(2,1)S(1)}, u32[]{:S(2)}, u32[]{:S(2)}) collective-permute-start(bf16[16,4224]{1,0:T(8,128)(2,1)S(1)} %get-tuple-element.33.first_ref), channel_id=1, source_target_pairs={{0,24},{8,16},{16,8},{24,0},{1,25},{9,17},{17,9},{25,1},{2,26},{10... | collective-permute-start | bytes 405512 | tf_op jit(solution)/shard_map/ppermute | solution.py:27
  12.1 3.2 %shard_map.58 = bf16[16,768,2,128]{3,2,1,0:T(2,128)(2,1)S(1)} custom-call(bf16[768,2,4096]{2,1,0:T(2,128)(2,1)} %bitcast.12), custom_call_target="tpu_custom_call" | custom-call | bytes 12582912 | tf_op jit(solution)/shard_map/pallas_call | solution.py:124
  15.3 0.0 collective-permute-done.2.second_ref
  15.3 0.3 collective-permute-done.1.refs_4_
  15.6 1.6 %collective-permute-start.4 = (bf16[32,4224]{1,0:T(8,128)(2,1)S(1)}, bf16[32,4224]{1,0:T(8,128)(2,1)S(1)}, u32[]{:S(2)}, u32[]{:S(2)}) collective-permute-start(bf16[32,4224]{1,0:T(8,128)(2,1)S(1)} %get-tuple-element.40.refs_1_), channel_id=1, source_target_pairs={{0,16},{8,24},{16,0},{24,8},{1,17},{9,25},{17,1},{25,9},{2,18},{10... | collective-permute-start | bytes 811016 | tf_op jit(solution)/shard_map/ppermute | solution.py:27
  17.2 1.5 %collective-permute-start.3 = (bf16[32,4224]{1,0:T(8,128)(2,1)S(1)}, bf16[32,4224]{1,0:T(8,128)(2,1)S(1)}, u32[]{:S(2)}, u32[]{:S(2)}) collective-permute-start(bf16[32,4224]{1,0:T(8,128)(2,1)S(1)} %get-tuple-element.40.refs_1_), channel_id=1, source_target_pairs={{0,8},{8,0},{16,24},{24,16},{1,9},{9,1},{17,25},{25,17},{2,10},{10... | collective-permute-start | bytes 811016 | tf_op jit(solution)/shard_map/ppermute | solution.py:27
  18.7 1.5 %collective-permute-start.5 = (bf16[16,4224]{1,0:T(8,128)(2,1)S(1)}, bf16[16,4224]{1,0:T(8,128)(2,1)S(1)}, u32[]{:S(2)}, u32[]{:S(2)}) collective-permute-start(bf16[16,4224]{1,0:T(8,128)(2,1)S(1)} %collective-permute-done.1.refs_4_), channel_id=1, source_target_pairs={{0,2},{1,3},{2,0},{3,1},{4,6},{5,7},{6,4},{7,5},{8,10},{9,11},{10,... | collective-permute-start | bytes 405512 | tf_op jit(solution)/shard_map/ppermute | solution.py:27
  20.2 0.0 collective-permute-start.6
  20.2 3.2 %shard_map.60 = bf16[16,768,2,128]{3,2,1,0:T(2,128)(2,1)S(1)} custom-call(bf16[768,2,4096]{2,1,0:T(2,128)(2,1)} %bitcast.13), custom_call_target="tpu_custom_call" | custom-call | bytes 12582912 | tf_op jit(solution)/shard_map/pallas_call | solution.py:124
  23.3 0.3 collective-permute-done.5.refs_5_
  23.7 0.0 collective-permute-done.4.refs_3_
  23.7 0.0 collective-permute-done.3.refs_2_
  23.7 0.3 collective-permute-start.7
  23.9 0.2 collective-permute-start.8
  24.2 0.3 collective-permute-start.9
  24.5 0.2 collective-permute-start.10
  24.7 1.1 %collective-permute-done.9.refs_9_ = bf16[16,4224]{1,0:T(8,128)(2,1)S(1)} collective-permute-done((bf16[16,4224]{1,0:T(8,128)(2,1)S(1)}, bf16[16,4224]{1,0:T(8,128)(2,1)S(1)}, u32[]{:S(2)}, u32[]{:S(2)}) %collective-permute-start.9) | collective-permute-done | bytes 135200 | tf_op jit(solution)/shard_map/ppermute | solution.py:27
  25.8 0.0 collective-permute-done.6.refs_6_
  25.8 0.2 collective-permute-done.10.refs_10_
  26.0 0.0 collective-permute-done.7.refs_7_
  26.0 0.0 collective-permute-done.8.refs_8_
  26.0 5.4 %shard_map.61 = (bf16[1,128,4096]{2,1,0:T(8,128)(2,1)S(1)}, f32[1,128,4096]{2,1,0:T(8,128)S(1)}) custom-call(s32[1]{0:T(128)} %bitcast.refs_0_, bf16[32,4224]{1,0:T(8,128)(2,1)S(1)} %get-tuple-element.40.refs_1_, bf16[32,4224]{1,0:T(8,128)(2,1)S(1)} %collective-permute-done.3.refs_2_, bf16[32,4224]{1,0:T(8,128)(2,1)S(1)} %collective-permute-done.4.refs_3_, ...), custom_call_target="tpu_custom_call" | custom-call | flops 4831838208 | bytes 5308416 | tf_op jit(solution)/shard_map/pallas_call | solution.py:211
  31.4 0.3 collective-permute-start.11
  31.8 2.4 %collective-permute-done.11 = bf16[128,4096]{1,0:T(8,128)(2,1)S(1)} collective-permute-done((bf16[128,4096]{1,0:T(8,128)(2,1)S(1)}, bf16[128,4096]{1,0:T(8,128)(2,1)S(1)}, u32[]{:S(2)}, u32[]{:S(2)}) %collective-permute-start.11) | collective-permute-done | bytes 1048608 | tf_op jit(solution)/shard_map/ppermute | solution.py:27
  34.2 0.4 fusion.4
  34.6 1.6 %collective-permute-start.15 = (bf16[16,4096]{1,0:T(8,128)(2,1)S(1)}, bf16[16,4096]{1,0:T(8,128)(2,1)S(1)}, u32[]{:S(2)}, u32[]{:S(2)}) collective-permute-start(bf16[16,4096]{1,0:T(8,128)(2,1)S(1)} %slice.44), channel_id=1, source_target_pairs={{0,2},{1,3},{2,0},{3,1},{4,6},{5,7},{6,4},{7,5},{8,10},{9,11},{10,... | collective-permute-start | bytes 393224 | tf_op jit(solution)/shard_map/ppermute | solution.py:27
  36.2 1.5 %collective-permute-start.12 = (bf16[32,4096]{1,0:T(8,128)(2,1)S(1)}, bf16[32,4096]{1,0:T(8,128)(2,1)S(1)}, u32[]{:S(2)}, u32[]{:S(2)}) collective-permute-start(bf16[32,4096]{1,0:T(8,128)(2,1)S(1)} %get-tuple-element.53), channel_id=1, source_target_pairs={{0,8},{8,0},{16,24},{24,16},{1,9},{9,1},{17,25},{25,17},{2,10},{10... | collective-permute-start | bytes 786440 | tf_op jit(solution)/shard_map/ppermute | solution.py:27
  37.7 0.5 collective-permute-start.13
  38.2 2.1 %collective-permute-done.15 = bf16[16,4096]{1,0:T(8,128)(2,1)S(1)} collective-permute-done((bf16[16,4096]{1,0:T(8,128)(2,1)S(1)}, bf16[16,4096]{1,0:T(8,128)(2,1)S(1)}, u32[]{:S(2)}, u32[]{:S(2)}) %collective-permute-start.15) | collective-permute-done | bytes 131104 | tf_op jit(solution)/shard_map/ppermute | solution.py:27
  40.3 1.3 %collective-permute-start.16 = (bf16[16,4096]{1,0:T(8,128)(2,1)S(1)}, bf16[16,4096]{1,0:T(8,128)(2,1)S(1)}, u32[]{:S(2)}, u32[]{:S(2)}) collective-permute-start(bf16[16,4096]{1,0:T(8,128)(2,1)S(1)} %fusion.1), channel_id=1, source_target_pairs={{0,24},{8,16},{16,8},{24,0},{1,25},{9,17},{17,9},{25,1},{2,26},{10... | collective-permute-start | bytes 393224 | tf_op jit(solution)/shard_map/ppermute | solution.py:27
  41.7 3.8 %collective-permute-done.12 = bf16[32,4096]{1,0:T(8,128)(2,1)S(1)} collective-permute-done((bf16[32,4096]{1,0:T(8,128)(2,1)S(1)}, bf16[32,4096]{1,0:T(8,128)(2,1)S(1)}, u32[]{:S(2)}, u32[]{:S(2)}) %collective-permute-start.12) | collective-permute-done | bytes 262176 | tf_op jit(solution)/shard_map/ppermute | solution.py:27
  45.4 2.9 %collective-permute-done.13 = bf16[32,4096]{1,0:T(8,128)(2,1)S(1)} collective-permute-done((bf16[32,4096]{1,0:T(8,128)(2,1)S(1)}, bf16[32,4096]{1,0:T(8,128)(2,1)S(1)}, u32[]{:S(2)}, u32[]{:S(2)}) %collective-permute-start.13) | collective-permute-done | bytes 262176 | tf_op jit(solution)/shard_map/ppermute | solution.py:27
  48.3 0.1 fusion
  48.4 0.6 collective-permute-start.14
  49.0 0.0 collective-permute-done.16
  49.0 5.2 %collective-permute-done.14 = bf16[16,4096]{1,0:T(8,128)(2,1)S(1)} collective-permute-done((bf16[16,4096]{1,0:T(8,128)(2,1)S(1)}, bf16[16,4096]{1,0:T(8,128)(2,1)S(1)}, u32[]{:S(2)}, u32[]{:S(2)}) %collective-permute-start.14) | collective-permute-done | bytes 131104 | tf_op jit(solution)/shard_map/ppermute | solution.py:27
  54.2 1.8 %collective-permute-start.17 = (bf16[8,4096]{1,0:T(8,128)(2,1)S(1)}, bf16[8,4096]{1,0:T(8,128)(2,1)S(1)}, u32[]{:S(2)}, u32[]{:S(2)}) collective-permute-start(bf16[8,4096]{1,0:T(8,128)(2,1)S(1)} %slice.62), channel_id=1, source_target_pairs={{0,4},{1,5},{2,6},{3,7},{4,0},{5,1},{6,2},{7,3},{8,12},{9,13},{10,... | collective-permute-start | bytes 196616 | tf_op jit(solution)/shard_map/ppermute | solution.py:27
  56.0 4.2 %collective-permute-done.17 = bf16[8,4096]{1,0:T(8,128)(2,1)S(1)} collective-permute-done((bf16[8,4096]{1,0:T(8,128)(2,1)S(1)}, bf16[8,4096]{1,0:T(8,128)(2,1)S(1)}, u32[]{:S(2)}, u32[]{:S(2)}) %collective-permute-start.17) | collective-permute-done | bytes 65568 | tf_op jit(solution)/shard_map/ppermute | solution.py:27
  60.2 0.6 %fusion.3 = bf16[8,4096]{1,0:T(8,128)(2,1)} fusion(f32[16,4096]{1,0:T(8,128)S(1)} %fusion.2, bf16[8,4096]{1,0:T(8,128)(2,1)S(1)} %collective-permute-done.17), kind=kLoop, calls=%fused_computation.10 | loop fusion | flops 98304 | bytes 262144 | tf_op jit(solution)/shard_map/convert_element_type | solution.py:292
  (8 shorter events, 0.2 us)
Async XLA Ops:
  1.0 7.8 %collective-permute-start = (bf16[8,4224]{1,0:T(8,128)(2,1)S(1)}, bf16[8,4224]{1,0:T(8,128)(2,1)S(1)}, u32[]{:S(2)}, u32[]{:S(2)}) collective-permute-start(bf16[8,4224]{1,0:T(8,128)(2,1)S(1)} %shard_map.55.first_ref), channel_id=1, source_target_pairs={{0,4},{1,5},{2,6},{3,7},{4,0},{5,1},{6,2},{7,3},{8,12},{9,13},{10,... | collective-permute-start | bytes 202760 | tf_op jit(solution)/shard_map/ppermute | solution.py:27
  8.8 6.4 %collective-permute-start.2 = (bf16[16,4224]{1,0:T(8,128)(2,1)S(1)}, bf16[16,4224]{1,0:T(8,128)(2,1)S(1)}, u32[]{:S(2)}, u32[]{:S(2)}) collective-permute-start(bf16[16,4224]{1,0:T(8,128)(2,1)S(1)} %get-tuple-element.33.first_ref), channel_id=1, source_target_pairs={{0,2},{1,3},{2,0},{3,1},{4,6},{5,7},{6,4},{7,5},{8,10},{9,11},{10,... | collective-permute-start | bytes 405512 | tf_op jit(solution)/shard_map/ppermute | solution.py:27
  9.6 5.9 %collective-permute-start.1 = (bf16[16,4224]{1,0:T(8,128)(2,1)S(1)}, bf16[16,4224]{1,0:T(8,128)(2,1)S(1)}, u32[]{:S(2)}, u32[]{:S(2)}) collective-permute-start(bf16[16,4224]{1,0:T(8,128)(2,1)S(1)} %get-tuple-element.33.first_ref), channel_id=1, source_target_pairs={{0,24},{8,16},{16,8},{24,0},{1,25},{9,17},{17,9},{25,1},{2,26},{10... | collective-permute-start | bytes 405512 | tf_op jit(solution)/shard_map/ppermute | solution.py:27
  15.6 8.1 %collective-permute-start.4 = (bf16[32,4224]{1,0:T(8,128)(2,1)S(1)}, bf16[32,4224]{1,0:T(8,128)(2,1)S(1)}, u32[]{:S(2)}, u32[]{:S(2)}) collective-permute-start(bf16[32,4224]{1,0:T(8,128)(2,1)S(1)} %get-tuple-element.40.refs_1_), channel_id=1, source_target_pairs={{0,16},{8,24},{16,0},{24,8},{1,17},{9,25},{17,1},{25,9},{2,18},{10... | collective-permute-start | bytes 811016 | tf_op jit(solution)/shard_map/ppermute | solution.py:27
  17.2 6.5 %collective-permute-start.3 = (bf16[32,4224]{1,0:T(8,128)(2,1)S(1)}, bf16[32,4224]{1,0:T(8,128)(2,1)S(1)}, u32[]{:S(2)}, u32[]{:S(2)}) collective-permute-start(bf16[32,4224]{1,0:T(8,128)(2,1)S(1)} %get-tuple-element.40.refs_1_), channel_id=1, source_target_pairs={{0,8},{8,0},{16,24},{24,16},{1,9},{9,1},{17,25},{25,17},{2,10},{10... | collective-permute-start | bytes 811016 | tf_op jit(solution)/shard_map/ppermute | solution.py:27
  18.7 5.0 %collective-permute-start.5 = (bf16[16,4224]{1,0:T(8,128)(2,1)S(1)}, bf16[16,4224]{1,0:T(8,128)(2,1)S(1)}, u32[]{:S(2)}, u32[]{:S(2)}) collective-permute-start(bf16[16,4224]{1,0:T(8,128)(2,1)S(1)} %collective-permute-done.1.refs_4_), channel_id=1, source_target_pairs={{0,2},{1,3},{2,0},{3,1},{4,6},{5,7},{6,4},{7,5},{8,10},{9,11},{10,... | collective-permute-start | bytes 405512 | tf_op jit(solution)/shard_map/ppermute | solution.py:27
  20.2 5.6 %collective-permute-start.6 = (bf16[32,4224]{1,0:T(8,128)(2,1)S(1)}, bf16[32,4224]{1,0:T(8,128)(2,1)S(1)}, u32[]{:S(2)}, u32[]{:S(2)}) collective-permute-start(bf16[32,4224]{1,0:T(8,128)(2,1)S(1)} %get-tuple-element.40.refs_1_), channel_id=1, source_target_pairs={{0,1},{1,0},{2,3},{3,2},{4,5},{5,4},{6,7},{7,6},{8,9},{9,8},{10,11... | collective-permute-start | bytes 811016 | tf_op jit(solution)/shard_map/ppermute | solution.py:27
  23.7 2.3 %collective-permute-start.7 = (bf16[32,4224]{1,0:T(8,128)(2,1)S(1)}, bf16[32,4224]{1,0:T(8,128)(2,1)S(1)}, u32[]{:S(2)}, u32[]{:S(2)}) collective-permute-start(bf16[32,4224]{1,0:T(8,128)(2,1)S(1)} %collective-permute-done.3.refs_2_), channel_id=1, source_target_pairs={{0,1},{1,0},{2,3},{3,2},{4,5},{5,4},{6,7},{7,6},{8,9},{9,8},{10,11... | collective-permute-start | bytes 811016 | tf_op jit(solution)/shard_map/ppermute | solution.py:27
  23.9 2.1 %collective-permute-start.8 = (bf16[32,4224]{1,0:T(8,128)(2,1)S(1)}, bf16[32,4224]{1,0:T(8,128)(2,1)S(1)}, u32[]{:S(2)}, u32[]{:S(2)}) collective-permute-start(bf16[32,4224]{1,0:T(8,128)(2,1)S(1)} %collective-permute-done.4.refs_3_), channel_id=1, source_target_pairs={{0,1},{1,0},{2,3},{3,2},{4,5},{5,4},{6,7},{7,6},{8,9},{9,8},{10,11... | collective-permute-start | bytes 811016 | tf_op jit(solution)/shard_map/ppermute | solution.py:27
  24.2 1.6 %collective-permute-start.9 = (bf16[16,4224]{1,0:T(8,128)(2,1)S(1)}, bf16[16,4224]{1,0:T(8,128)(2,1)S(1)}, u32[]{:S(2)}, u32[]{:S(2)}) collective-permute-start(bf16[16,4224]{1,0:T(8,128)(2,1)S(1)} %collective-permute-done.1.refs_4_), channel_id=1, source_target_pairs={{0,1},{1,0},{2,3},{3,2},{4,5},{5,4},{6,7},{7,6},{8,9},{9,8},{10,11... | collective-permute-start | bytes 405512 | tf_op jit(solution)/shard_map/ppermute | solution.py:27
  24.5 1.5 %collective-permute-start.10 = (bf16[16,4224]{1,0:T(8,128)(2,1)S(1)}, bf16[16,4224]{1,0:T(8,128)(2,1)S(1)}, u32[]{:S(2)}, u32[]{:S(2)}) collective-permute-start(bf16[16,4224]{1,0:T(8,128)(2,1)S(1)} %collective-permute-done.5.refs_5_), channel_id=1, source_target_pairs={{0,1},{1,0},{2,3},{3,2},{4,5},{5,4},{6,7},{7,6},{8,9},{9,8},{10,11... | collective-permute-start | bytes 405512 | tf_op jit(solution)/shard_map/ppermute | solution.py:27
  31.4 2.7 %collective-permute-start.11 = (bf16[128,4096]{1,0:T(8,128)(2,1)S(1)}, bf16[128,4096]{1,0:T(8,128)(2,1)S(1)}, u32[]{:S(2)}, u32[]{:S(2)}) collective-permute-start(bf16[128,4096]{1,0:T(8,128)(2,1)S(1)} %bitcast.11), channel_id=1, source_target_pairs={{0,1},{1,0},{2,3},{3,2},{4,5},{5,4},{6,7},{7,6},{8,9},{9,8},{10,11... | collective-permute-start | bytes 3145736 | tf_op jit(solution)/shard_map/ppermute | solution.py:27
  34.6 5.7 %collective-permute-start.15 = (bf16[16,4096]{1,0:T(8,128)(2,1)S(1)}, bf16[16,4096]{1,0:T(8,128)(2,1)S(1)}, u32[]{:S(2)}, u32[]{:S(2)}) collective-permute-start(bf16[16,4096]{1,0:T(8,128)(2,1)S(1)} %slice.44), channel_id=1, source_target_pairs={{0,2},{1,3},{2,0},{3,1},{4,6},{5,7},{6,4},{7,5},{8,10},{9,11},{10,... | collective-permute-start | bytes 393224 | tf_op jit(solution)/shard_map/ppermute | solution.py:27
  36.2 9.3 %collective-permute-start.12 = (bf16[32,4096]{1,0:T(8,128)(2,1)S(1)}, bf16[32,4096]{1,0:T(8,128)(2,1)S(1)}, u32[]{:S(2)}, u32[]{:S(2)}) collective-permute-start(bf16[32,4096]{1,0:T(8,128)(2,1)S(1)} %get-tuple-element.53), channel_id=1, source_target_pairs={{0,8},{8,0},{16,24},{24,16},{1,9},{9,1},{17,25},{25,17},{2,10},{10... | collective-permute-start | bytes 786440 | tf_op jit(solution)/shard_map/ppermute | solution.py:27
  37.7 10.6 %collective-permute-start.13 = (bf16[32,4096]{1,0:T(8,128)(2,1)S(1)}, bf16[32,4096]{1,0:T(8,128)(2,1)S(1)}, u32[]{:S(2)}, u32[]{:S(2)}) collective-permute-start(bf16[32,4096]{1,0:T(8,128)(2,1)S(1)} %get-tuple-element.54), channel_id=1, source_target_pairs={{0,16},{8,24},{16,0},{24,8},{1,17},{9,25},{17,1},{25,9},{2,18},{10... | collective-permute-start | bytes 786440 | tf_op jit(solution)/shard_map/ppermute | solution.py:27
  40.3 8.7 %collective-permute-start.16 = (bf16[16,4096]{1,0:T(8,128)(2,1)S(1)}, bf16[16,4096]{1,0:T(8,128)(2,1)S(1)}, u32[]{:S(2)}, u32[]{:S(2)}) collective-permute-start(bf16[16,4096]{1,0:T(8,128)(2,1)S(1)} %fusion.1), channel_id=1, source_target_pairs={{0,24},{8,16},{16,8},{24,0},{1,25},{9,17},{17,9},{25,1},{2,26},{10... | collective-permute-start | bytes 393224 | tf_op jit(solution)/shard_map/ppermute | solution.py:27
  48.4 5.7 %collective-permute-start.14 = (bf16[16,4096]{1,0:T(8,128)(2,1)S(1)}, bf16[16,4096]{1,0:T(8,128)(2,1)S(1)}, u32[]{:S(2)}, u32[]{:S(2)}) collective-permute-start(bf16[16,4096]{1,0:T(8,128)(2,1)S(1)} %slice.61), channel_id=1, source_target_pairs={{0,2},{1,3},{2,0},{3,1},{4,6},{5,7},{6,4},{7,5},{8,10},{9,11},{10,... | collective-permute-start | bytes 393224 | tf_op jit(solution)/shard_map/ppermute | solution.py:27
  54.2 5.9 %collective-permute-start.17 = (bf16[8,4096]{1,0:T(8,128)(2,1)S(1)}, bf16[8,4096]{1,0:T(8,128)(2,1)S(1)}, u32[]{:S(2)}, u32[]{:S(2)}) collective-permute-start(bf16[8,4096]{1,0:T(8,128)(2,1)S(1)} %slice.62), channel_id=1, source_target_pairs={{0,4},{1,5},{2,6},{3,7},{4,0},{5,1},{6,2},{7,3},{8,12},{9,13},{10,... | collective-permute-start | bytes 196616 | tf_op jit(solution)/shard_map/ppermute | solution.py:27

commit v7 on v6

--- a/solution.py
+++ b/solution.py
@@ -231,6 +231,12 @@
     return send.reshape(half_rows, width), keep.reshape(half_rows, width)
 
 
+def halve(rows, stride):
+    size = rows.shape[0] // 2
+    sent = rows[size:].astype(jnp.bfloat16)
+    return rows[:size] + swap(sent, "expert", stride).astype(jnp.float32)
+
+
 def body(tokens, expert_ids, route_weights, in_weights, out_weights):
     width = tokens.shape[1]
     exp_dev, units = in_weights.shape[:2]
@@ -278,17 +284,13 @@
     for b in range(1, far):
         piece = rounded[b * size : (b + 1) * size]
         mine = mine + swap(piece, "batch", b).astype(jnp.float32)
-    size = size // 2
-    piece = rounded[2 * far * size + size :]
-    across = total[2 * far * size : 2 * far * size + size]
-    across = across + swap(piece, "expert", strides[-1]).astype(jnp.float32)
-    piece = mine[size:].astype(jnp.bfloat16)
-    mine = mine[:size] + swap(piece, "expert", strides[-1]).astype(jnp.float32)
-    mine = mine + swap(across.astype(jnp.bfloat16), "batch", far).astype(jnp.float32)
-    for stride in reversed(strides[:-1]):
-        size = size // 2
-        piece = mine[size:].astype(jnp.bfloat16)
-        mine = mine[:size] + swap(piece, "expert", stride).astype(jnp.float32)
+    across = total[far * size :]
+    for stride in reversed(strides):
+        across = halve(across, stride)
+    across = swap(across.astype(jnp.bfloat16), "batch", far).astype(jnp.float32)
+    for stride in reversed(strides):
+        mine = halve(mine, stride)
+    mine = mine + across
     return mine.astype(jnp.bfloat16)
 
 

time: 61 us -> 57.5 us (0.943)
  waiting for transfers between devices: 23.3 us -> 15.8 us
  starting transfers between devices: 20.5 us -> 24.4 us
    ppermute x18 -> x19, waiting for transfers between devices: 23.3 us -> 15.8 us  [swap(): return lax.ppermute(block, axis, [(i, i ^ flips) for i in range(size)])]
    ppermute x18 -> x19, starting transfers between devices: 20.5 us -> 24.4 us  [swap(): return lax.ppermute(block, axis, [(i, i ^ flips) for i in range(size)])]
  transfers between devices with their start and end apart: 18 -> 19, of which waited for: 11 -> 11; matrix products, arithmetic and copies ran while one was open for 0% -> 0% of each run, Pallas kernels for 15% -> 16%
where the time goes in v7:
time: 57.5 us; the launch traced here: 57.3 us
  starting transfers between devices  24.4 us (42%)
  waiting for transfers between devices  15.8 us (27%)
  Pallas kernels  15.6 us (27%)
  other arithmetic  1.2 us (2%)
    ppermute x19, starting transfers between devices, swap(): return lax.ppermute(block, axis, [(i, i ^ flips) for i in range(size)])  24.4 us
    ppermute x19, waiting for transfers between devices, swap(): return lax.ppermute(block, axis, [(i, i ^ flips) for i in range(size)])  15.8 us
    pallas_call x3, Pallas kernels, load(): pl.pallas_call(kernel, out_shape=pltpu.VMEM(shape, source.dtype), in_spec...  9.16 us
    pallas_call x1, Pallas kernels, run_experts(): pl.pallas_call(functools.partial(expert_kernel, exp_dev, experts, count),...  5.44 us
  transfers between devices with their start and end apart: 19, of which 11 were waited for; matrix products, arithmetic and copies ran while one was open for 0% of the time, Pallas kernels for 16%

profile of v7, /device:TPU:0, one launch (start us, length us, event | category | flops | bytes accessed | tf_op | source)
XLA Modules:
  0.0 57.3 jit_solution(5443251683567110471)
XLA Ops:
  0.0 1.0 %shard_map.55.first_ref = bf16[8,4224]{1,0:T(8,128)(2,1)S(1)} custom-call(bf16[8,4096]{1,0:T(8,128)(2,1)} %tokens_hbm.1, s32[8,8]{1,0:T(8,128)} %ids_hbm.1, f32[8,8]{1,0:T(8,128)} %weights_hbm.1), custom_call_target="tpu_custom_call" | custom-call | tf_op jit(solution)/shard_map/pallas_call | solution.py:63
  1.0 4.1 %collective-permute-start = (bf16[8,4224]{1,0:T(8,128)(2,1)S(1)}, bf16[8,4224]{1,0:T(8,128)(2,1)S(1)}, u32[]{:S(2)}, u32[]{:S(2)}) collective-permute-start(bf16[8,4224]{1,0:T(8,128)(2,1)S(1)} %shard_map.55.first_ref), channel_id=1, source_target_pairs={{0,4},{1,5},{2,6},{3,7},{4,0},{5,1},{6,2},{7,3},{8,12},{9,13},{10,... | collective-permute-start | bytes 202760 | tf_op jit(solution)/shard_map/ppermute | solution.py:27
  5.1 2.9 %shard_map.56.refs_0_ = bf16[768,4096]{1,0:T(8,128)(2,1)S(1)} custom-call(bf16[768,4096]{1,0:T(8,128)(2,1)} %bitcast.14), custom_call_target="tpu_custom_call" | custom-call | bytes 12582912 | tf_op jit(solution)/shard_map/pallas_call | solution.py:124
  8.0 0.9 %collective-permute-done.second_ref = bf16[8,4224]{1,0:T(8,128)(2,1)S(1)} collective-permute-done((bf16[8,4224]{1,0:T(8,128)(2,1)S(1)}, bf16[8,4224]{1,0:T(8,128)(2,1)S(1)}, u32[]{:S(2)}, u32[]{:S(2)}) %collective-permute-start) | collective-permute-done | bytes 67616 | tf_op jit(solution)/shard_map/ppermute | solution.py:27
  8.8 0.8 %collective-permute-start.2 = (bf16[16,4224]{1,0:T(8,128)(2,1)S(1)}, bf16[16,4224]{1,0:T(8,128)(2,1)S(1)}, u32[]{:S(2)}, u32[]{:S(2)}) collective-permute-start(bf16[16,4224]{1,0:T(8,128)(2,1)S(1)} %get-tuple-element.33.first_ref), channel_id=1, source_target_pairs={{0,2},{1,3},{2,0},{3,1},{4,6},{5,7},{6,4},{7,5},{8,10},{9,11},{10,... | collective-permute-start | bytes 405512 | tf_op jit(solution)/shard_map/ppermute | solution.py:27
  9.6 2.4 %collective-permute-start.1 = (bf16[16,4224]{1,0:T(8,128)(2,1)S(1)}, bf16[16,4224]{1,0:T(8,128)(2,1)S(1)}, u32[]{:S(2)}, u32[]{:S(2)}) collective-permute-start(bf16[16,4224]{1,0:T(8,128)(2,1)S(1)} %get-tuple-element.33.first_ref), channel_id=1, source_target_pairs={{0,24},{8,16},{16,8},{24,0},{1,25},{9,17},{17,9},{25,1},{2,26},{10... | collective-permute-start | bytes 405512 | tf_op jit(solution)/shard_map/ppermute | solution.py:27
  12.1 3.2 %shard_map.58 = bf16[16,768,2,128]{3,2,1,0:T(2,128)(2,1)S(1)} custom-call(bf16[768,2,4096]{2,1,0:T(2,128)(2,1)} %bitcast.12), custom_call_target="tpu_custom_call" | custom-call | bytes 12582912 | tf_op jit(solution)/shard_map/pallas_call | solution.py:124
  15.3 0.0 collective-permute-done.2.second_ref
  15.3 0.3 collective-permute-done.1.refs_4_
  15.6 1.6 %collective-permute-start.4 = (bf16[32,4224]{1,0:T(8,128)(2,1)S(1)}, bf16[32,4224]{1,0:T(8,128)(2,1)S(1)}, u32[]{:S(2)}, u32[]{:S(2)}) collective-permute-start(bf16[32,4224]{1,0:T(8,128)(2,1)S(1)} %get-tuple-element.40.refs_1_), channel_id=1, source_target_pairs={{0,16},{8,24},{16,0},{24,8},{1,17},{9,25},{17,1},{25,9},{2,18},{10... | collective-permute-start | bytes 811016 | tf_op jit(solution)/shard_map/ppermute | solution.py:27
  17.2 1.5 %collective-permute-start.3 = (bf16[32,4224]{1,0:T(8,128)(2,1)S(1)}, bf16[32,4224]{1,0:T(8,128)(2,1)S(1)}, u32[]{:S(2)}, u32[]{:S(2)}) collective-permute-start(bf16[32,4224]{1,0:T(8,128)(2,1)S(1)} %get-tuple-element.40.refs_1_), channel_id=1, source_target_pairs={{0,8},{8,0},{16,24},{24,16},{1,9},{9,1},{17,25},{25,17},{2,10},{10... | collective-permute-start | bytes 811016 | tf_op jit(solution)/shard_map/ppermute | solution.py:27
  18.7 1.5 %collective-permute-start.5 = (bf16[16,4224]{1,0:T(8,128)(2,1)S(1)}, bf16[16,4224]{1,0:T(8,128)(2,1)S(1)}, u32[]{:S(2)}, u32[]{:S(2)}) collective-permute-start(bf16[16,4224]{1,0:T(8,128)(2,1)S(1)} %collective-permute-done.1.refs_4_), channel_id=1, source_target_pairs={{0,2},{1,3},{2,0},{3,1},{4,6},{5,7},{6,4},{7,5},{8,10},{9,11},{10,... | collective-permute-start | bytes 405512 | tf_op jit(solution)/shard_map/ppermute | solution.py:27
  20.2 0.0 collective-permute-start.6
  20.2 3.2 %shard_map.60 = bf16[16,768,2,128]{3,2,1,0:T(2,128)(2,1)S(1)} custom-call(bf16[768,2,4096]{2,1,0:T(2,128)(2,1)} %bitcast.13), custom_call_target="tpu_custom_call" | custom-call | bytes 12582912 | tf_op jit(solution)/shard_map/pallas_call | solution.py:124
  23.3 0.3 collective-permute-done.5.refs_5_
  23.7 0.0 collective-permute-done.4.refs_3_
  23.7 0.0 collective-permute-done.3.refs_2_
  23.7 0.3 collective-permute-start.7
  23.9 0.2 collective-permute-start.8
  24.2 0.3 collective-permute-start.9
  24.5 0.2 collective-permute-start.10
  24.7 1.1 %collective-permute-done.9.refs_9_ = bf16[16,4224]{1,0:T(8,128)(2,1)S(1)} collective-permute-done((bf16[16,4224]{1,0:T(8,128)(2,1)S(1)}, bf16[16,4224]{1,0:T(8,128)(2,1)S(1)}, u32[]{:S(2)}, u32[]{:S(2)}) %collective-permute-start.9) | collective-permute-done | bytes 135200 | tf_op jit(solution)/shard_map/ppermute | solution.py:27
  25.8 0.0 collective-permute-done.6.refs_6_
  25.8 0.2 collective-permute-done.10.refs_10_
  26.0 0.0 collective-permute-done.7.refs_7_
  26.0 0.0 collective-permute-done.8.refs_8_
  26.0 5.4 %shard_map.61 = (bf16[1,128,4096]{2,1,0:T(8,128)(2,1)S(1)}, f32[1,128,4096]{2,1,0:T(8,128)S(1)}) custom-call(s32[1]{0:T(128)} %bitcast.refs_0_, bf16[32,4224]{1,0:T(8,128)(2,1)S(1)} %get-tuple-element.40.refs_1_, bf16[32,4224]{1,0:T(8,128)(2,1)S(1)} %collective-permute-done.3.refs_2_, bf16[32,4224]{1,0:T(8,128)(2,1)S(1)} %collective-permute-done.4.refs_3_, ...), custom_call_target="tpu_custom_call" | custom-call | flops 4831838208 | bytes 5308416 | tf_op jit(solution)/shard_map/pallas_call | solution.py:211
  31.4 0.3 collective-permute-start.11
  31.8 2.4 %collective-permute-done.11 = bf16[128,4096]{1,0:T(8,128)(2,1)S(1)} collective-permute-done((bf16[128,4096]{1,0:T(8,128)(2,1)S(1)}, bf16[128,4096]{1,0:T(8,128)(2,1)S(1)}, u32[]{:S(2)}, u32[]{:S(2)}) %collective-permute-start.11) | collective-permute-done | bytes 1048608 | tf_op jit(solution)/shard_map/ppermute | solution.py:27
  34.2 0.4 fusion.4
  34.6 1.6 %collective-permute-start.16 = (bf16[16,4096]{1,0:T(8,128)(2,1)S(1)}, bf16[16,4096]{1,0:T(8,128)(2,1)S(1)}, u32[]{:S(2)}, u32[]{:S(2)}) collective-permute-start(bf16[16,4096]{1,0:T(8,128)(2,1)S(1)} %slice.59), channel_id=1, source_target_pairs={{0,2},{1,3},{2,0},{3,1},{4,6},{5,7},{6,4},{7,5},{8,10},{9,11},{10,... | collective-permute-start | bytes 393224 | tf_op jit(solution)/shard_map/ppermute | solution.py:27
  36.2 1.5 %collective-permute-start.12 = (bf16[32,4096]{1,0:T(8,128)(2,1)S(1)}, bf16[32,4096]{1,0:T(8,128)(2,1)S(1)}, u32[]{:S(2)}, u32[]{:S(2)}) collective-permute-start(bf16[32,4096]{1,0:T(8,128)(2,1)S(1)} %get-tuple-element.53), channel_id=1, source_target_pairs={{0,8},{8,0},{16,24},{24,16},{1,9},{9,1},{17,25},{25,17},{2,10},{10... | collective-permute-start | bytes 786440 | tf_op jit(solution)/shard_map/ppermute | solution.py:27
  37.7 0.5 collective-permute-start.13
  38.2 2.1 %collective-permute-done.16 = bf16[16,4096]{1,0:T(8,128)(2,1)S(1)} collective-permute-done((bf16[16,4096]{1,0:T(8,128)(2,1)S(1)}, bf16[16,4096]{1,0:T(8,128)(2,1)S(1)}, u32[]{:S(2)}, u32[]{:S(2)}) %collective-permute-start.16) | collective-permute-done | bytes 131104 | tf_op jit(solution)/shard_map/ppermute | solution.py:27
  40.3 3.2 %collective-permute-start.17 = (bf16[8,4096]{1,0:T(8,128)(2,1)S(1)}, bf16[8,4096]{1,0:T(8,128)(2,1)S(1)}, u32[]{:S(2)}, u32[]{:S(2)}) collective-permute-start(bf16[8,4096]{1,0:T(8,128)(2,1)S(1)} %slice.79), channel_id=1, source_target_pairs={{0,4},{1,5},{2,6},{3,7},{4,0},{5,1},{6,2},{7,3},{8,12},{9,13},{10,... | collective-permute-start | bytes 196616 | tf_op jit(solution)/shard_map/ppermute | solution.py:27
  43.5 0.8 %collective-permute-done.12 = bf16[32,4096]{1,0:T(8,128)(2,1)S(1)} collective-permute-done((bf16[32,4096]{1,0:T(8,128)(2,1)S(1)}, bf16[32,4096]{1,0:T(8,128)(2,1)S(1)}, u32[]{:S(2)}, u32[]{:S(2)}) %collective-permute-start.12) | collective-permute-done | bytes 262176 | tf_op jit(solution)/shard_map/ppermute | solution.py:27
  44.4 1.2 %collective-permute-done.13 = bf16[32,4096]{1,0:T(8,128)(2,1)S(1)} collective-permute-done((bf16[32,4096]{1,0:T(8,128)(2,1)S(1)}, bf16[32,4096]{1,0:T(8,128)(2,1)S(1)}, u32[]{:S(2)}, u32[]{:S(2)}) %collective-permute-start.13) | collective-permute-done | bytes 262176 | tf_op jit(solution)/shard_map/ppermute | solution.py:27
  45.5 0.1 fusion
  45.6 0.6 %collective-permute-start.14 = (bf16[16,4096]{1,0:T(8,128)(2,1)S(1)}, bf16[16,4096]{1,0:T(8,128)(2,1)S(1)}, u32[]{:S(2)}, u32[]{:S(2)}) collective-permute-start(bf16[16,4096]{1,0:T(8,128)(2,1)S(1)} %slice.78), channel_id=1, source_target_pairs={{0,2},{1,3},{2,0},{3,1},{4,6},{5,7},{6,4},{7,5},{8,10},{9,11},{10,... | collective-permute-start | bytes 393224 | tf_op jit(solution)/shard_map/ppermute | solution.py:27
  46.2 0.0 collective-permute-done.17
  46.2 1.2 %collective-permute-start.18 = (bf16[8,4096]{1,0:T(8,128)(2,1)S(1)}, bf16[8,4096]{1,0:T(8,128)(2,1)S(1)}, u32[]{:S(2)}, u32[]{:S(2)}) collective-permute-start(bf16[8,4096]{1,0:T(8,128)(2,1)S(1)} %fusion.1), channel_id=1, source_target_pairs={{0,24},{8,16},{16,8},{24,0},{1,25},{9,17},{17,9},{25,1},{2,26},{10... | collective-permute-start | bytes 196616 | tf_op jit(solution)/shard_map/ppermute | solution.py:27
  47.5 3.2 %collective-permute-done.14 = bf16[16,4096]{1,0:T(8,128)(2,1)S(1)} collective-permute-done((bf16[16,4096]{1,0:T(8,128)(2,1)S(1)}, bf16[16,4096]{1,0:T(8,128)(2,1)S(1)}, u32[]{:S(2)}, u32[]{:S(2)}) %collective-permute-start.14) | collective-permute-done | bytes 131104 | tf_op jit(solution)/shard_map/ppermute | solution.py:27
  50.7 2.6 %collective-permute-start.15 = (bf16[8,4096]{1,0:T(8,128)(2,1)S(1)}, bf16[8,4096]{1,0:T(8,128)(2,1)S(1)}, u32[]{:S(2)}, u32[]{:S(2)}) collective-permute-start(bf16[8,4096]{1,0:T(8,128)(2,1)S(1)} %slice.80), channel_id=1, source_target_pairs={{0,4},{1,5},{2,6},{3,7},{4,0},{5,1},{6,2},{7,3},{8,12},{9,13},{10,... | collective-permute-start | bytes 196616 | tf_op jit(solution)/shard_map/ppermute | solution.py:27
  53.3 0.0 collective-permute-done.18
  53.3 3.3 %collective-permute-done.15 = bf16[8,4096]{1,0:T(8,128)(2,1)S(1)} collective-permute-done((bf16[8,4096]{1,0:T(8,128)(2,1)S(1)}, bf16[8,4096]{1,0:T(8,128)(2,1)S(1)}, u32[]{:S(2)}, u32[]{:S(2)}) %collective-permute-start.15) | collective-permute-done | bytes 65568 | tf_op jit(solution)/shard_map/ppermute | solution.py:27
  56.6 0.7 %fusion.3 = bf16[8,4096]{1,0:T(8,128)(2,1)} fusion(f32[16,4096]{1,0:T(8,128)S(1)} %slice_add_fusion.2, bf16[8,4096]{1,0:T(8,128)(2,1)S(1)} %collective-permute-done.18, bf16[8,4096]{1,0:T(8,128)(2,1)S(1)} %collective-permute-done.15), kind=kLoop, calls=%fused_computation.12 | loop fusion | flops 163840 | bytes 327680 | tf_op jit(solution)/shard_map/convert_element_type | solution.py:294
  (10 shorter events, 0.2 us)
Async XLA Ops:
  1.0 7.8 %collective-permute-start = (bf16[8,4224]{1,0:T(8,128)(2,1)S(1)}, bf16[8,4224]{1,0:T(8,128)(2,1)S(1)}, u32[]{:S(2)}, u32[]{:S(2)}) collective-permute-start(bf16[8,4224]{1,0:T(8,128)(2,1)S(1)} %shard_map.55.first_ref), channel_id=1, source_target_pairs={{0,4},{1,5},{2,6},{3,7},{4,0},{5,1},{6,2},{7,3},{8,12},{9,13},{10,... | collective-permute-start | bytes 202760 | tf_op jit(solution)/shard_map/ppermute | solution.py:27
  8.8 6.4 %collective-permute-start.2 = (bf16[16,4224]{1,0:T(8,128)(2,1)S(1)}, bf16[16,4224]{1,0:T(8,128)(2,1)S(1)}, u32[]{:S(2)}, u32[]{:S(2)}) collective-permute-start(bf16[16,4224]{1,0:T(8,128)(2,1)S(1)} %get-tuple-element.33.first_ref), channel_id=1, source_target_pairs={{0,2},{1,3},{2,0},{3,1},{4,6},{5,7},{6,4},{7,5},{8,10},{9,11},{10,... | collective-permute-start | bytes 405512 | tf_op jit(solution)/shard_map/ppermute | solution.py:27
  9.6 5.9 %collective-permute-start.1 = (bf16[16,4224]{1,0:T(8,128)(2,1)S(1)}, bf16[16,4224]{1,0:T(8,128)(2,1)S(1)}, u32[]{:S(2)}, u32[]{:S(2)}) collective-permute-start(bf16[16,4224]{1,0:T(8,128)(2,1)S(1)} %get-tuple-element.33.first_ref), channel_id=1, source_target_pairs={{0,24},{8,16},{16,8},{24,0},{1,25},{9,17},{17,9},{25,1},{2,26},{10... | collective-permute-start | bytes 405512 | tf_op jit(solution)/shard_map/ppermute | solution.py:27
  15.6 8.1 %collective-permute-start.4 = (bf16[32,4224]{1,0:T(8,128)(2,1)S(1)}, bf16[32,4224]{1,0:T(8,128)(2,1)S(1)}, u32[]{:S(2)}, u32[]{:S(2)}) collective-permute-start(bf16[32,4224]{1,0:T(8,128)(2,1)S(1)} %get-tuple-element.40.refs_1_), channel_id=1, source_target_pairs={{0,16},{8,24},{16,0},{24,8},{1,17},{9,25},{17,1},{25,9},{2,18},{10... | collective-permute-start | bytes 811016 | tf_op jit(solution)/shard_map/ppermute | solution.py:27
  17.2 6.5 %collective-permute-start.3 = (bf16[32,4224]{1,0:T(8,128)(2,1)S(1)}, bf16[32,4224]{1,0:T(8,128)(2,1)S(1)}, u32[]{:S(2)}, u32[]{:S(2)}) collective-permute-start(bf16[32,4224]{1,0:T(8,128)(2,1)S(1)} %get-tuple-element.40.refs_1_), channel_id=1, source_target_pairs={{0,8},{8,0},{16,24},{24,16},{1,9},{9,1},{17,25},{25,17},{2,10},{10... | collective-permute-start | bytes 811016 | tf_op jit(solution)/shard_map/ppermute | solution.py:27
  18.7 5.0 %collective-permute-start.5 = (bf16[16,4224]{1,0:T(8,128)(2,1)S(1)}, bf16[16,4224]{1,0:T(8,128)(2,1)S(1)}, u32[]{:S(2)}, u32[]{:S(2)}) collective-permute-start(bf16[16,4224]{1,0:T(8,128)(2,1)S(1)} %collective-permute-done.1.refs_4_), channel_id=1, source_target_pairs={{0,2},{1,3},{2,0},{3,1},{4,6},{5,7},{6,4},{7,5},{8,10},{9,11},{10,... | collective-permute-start | bytes 405512 | tf_op jit(solution)/shard_map/ppermute | solution.py:27
  20.2 5.6 %collective-permute-start.6 = (bf16[32,4224]{1,0:T(8,128)(2,1)S(1)}, bf16[32,4224]{1,0:T(8,128)(2,1)S(1)}, u32[]{:S(2)}, u32[]{:S(2)}) collective-permute-start(bf16[32,4224]{1,0:T(8,128)(2,1)S(1)} %get-tuple-element.40.refs_1_), channel_id=1, source_target_pairs={{0,1},{1,0},{2,3},{3,2},{4,5},{5,4},{6,7},{7,6},{8,9},{9,8},{10,11... | collective-permute-start | bytes 811016 | tf_op jit(solution)/shard_map/ppermute | solution.py:27
  23.7 2.3 %collective-permute-start.7 = (bf16[32,4224]{1,0:T(8,128)(2,1)S(1)}, bf16[32,4224]{1,0:T(8,128)(2,1)S(1)}, u32[]{:S(2)}, u32[]{:S(2)}) collective-permute-start(bf16[32,4224]{1,0:T(8,128)(2,1)S(1)} %collective-permute-done.3.refs_2_), channel_id=1, source_target_pairs={{0,1},{1,0},{2,3},{3,2},{4,5},{5,4},{6,7},{7,6},{8,9},{9,8},{10,11... | collective-permute-start | bytes 811016 | tf_op jit(solution)/shard_map/ppermute | solution.py:27
  23.9 2.1 %collective-permute-start.8 = (bf16[32,4224]{1,0:T(8,128)(2,1)S(1)}, bf16[32,4224]{1,0:T(8,128)(2,1)S(1)}, u32[]{:S(2)}, u32[]{:S(2)}) collective-permute-start(bf16[32,4224]{1,0:T(8,128)(2,1)S(1)} %collective-permute-done.4.refs_3_), channel_id=1, source_target_pairs={{0,1},{1,0},{2,3},{3,2},{4,5},{5,4},{6,7},{7,6},{8,9},{9,8},{10,11... | collective-permute-start | bytes 811016 | tf_op jit(solution)/shard_map/ppermute | solution.py:27
  24.2 1.6 %collective-permute-start.9 = (bf16[16,4224]{1,0:T(8,128)(2,1)S(1)}, bf16[16,4224]{1,0:T(8,128)(2,1)S(1)}, u32[]{:S(2)}, u32[]{:S(2)}) collective-permute-start(bf16[16,4224]{1,0:T(8,128)(2,1)S(1)} %collective-permute-done.1.refs_4_), channel_id=1, source_target_pairs={{0,1},{1,0},{2,3},{3,2},{4,5},{5,4},{6,7},{7,6},{8,9},{9,8},{10,11... | collective-permute-start | bytes 405512 | tf_op jit(solution)/shard_map/ppermute | solution.py:27
  24.5 1.5 %collective-permute-start.10 = (bf16[16,4224]{1,0:T(8,128)(2,1)S(1)}, bf16[16,4224]{1,0:T(8,128)(2,1)S(1)}, u32[]{:S(2)}, u32[]{:S(2)}) collective-permute-start(bf16[16,4224]{1,0:T(8,128)(2,1)S(1)} %collective-permute-done.5.refs_5_), channel_id=1, source_target_pairs={{0,1},{1,0},{2,3},{3,2},{4,5},{5,4},{6,7},{7,6},{8,9},{9,8},{10,11... | collective-permute-start | bytes 405512 | tf_op jit(solution)/shard_map/ppermute | solution.py:27
  31.4 2.7 %collective-permute-start.11 = (bf16[128,4096]{1,0:T(8,128)(2,1)S(1)}, bf16[128,4096]{1,0:T(8,128)(2,1)S(1)}, u32[]{:S(2)}, u32[]{:S(2)}) collective-permute-start(bf16[128,4096]{1,0:T(8,128)(2,1)S(1)} %bitcast.11), channel_id=1, source_target_pairs={{0,1},{1,0},{2,3},{3,2},{4,5},{5,4},{6,7},{7,6},{8,9},{9,8},{10,11... | collective-permute-start | bytes 3145736 | tf_op jit(solution)/shard_map/ppermute | solution.py:27
  34.6 5.7 %collective-permute-start.16 = (bf16[16,4096]{1,0:T(8,128)(2,1)S(1)}, bf16[16,4096]{1,0:T(8,128)(2,1)S(1)}, u32[]{:S(2)}, u32[]{:S(2)}) collective-permute-start(bf16[16,4096]{1,0:T(8,128)(2,1)S(1)} %slice.59), channel_id=1, source_target_pairs={{0,2},{1,3},{2,0},{3,1},{4,6},{5,7},{6,4},{7,5},{8,10},{9,11},{10,... | collective-permute-start | bytes 393224 | tf_op jit(solution)/shard_map/ppermute | solution.py:27
  36.2 8.2 %collective-permute-start.12 = (bf16[32,4096]{1,0:T(8,128)(2,1)S(1)}, bf16[32,4096]{1,0:T(8,128)(2,1)S(1)}, u32[]{:S(2)}, u32[]{:S(2)}) collective-permute-start(bf16[32,4096]{1,0:T(8,128)(2,1)S(1)} %get-tuple-element.53), channel_id=1, source_target_pairs={{0,8},{8,0},{16,24},{24,16},{1,9},{9,1},{17,25},{25,17},{2,10},{10... | collective-permute-start | bytes 786440 | tf_op jit(solution)/shard_map/ppermute | solution.py:27
  37.7 7.8 %collective-permute-start.13 = (bf16[32,4096]{1,0:T(8,128)(2,1)S(1)}, bf16[32,4096]{1,0:T(8,128)(2,1)S(1)}, u32[]{:S(2)}, u32[]{:S(2)}) collective-permute-start(bf16[32,4096]{1,0:T(8,128)(2,1)S(1)} %get-tuple-element.54), channel_id=1, source_target_pairs={{0,16},{8,24},{16,0},{24,8},{1,17},{9,25},{17,1},{25,9},{2,18},{10... | collective-permute-start | bytes 786440 | tf_op jit(solution)/shard_map/ppermute | solution.py:27
  40.3 5.9 %collective-permute-start.17 = (bf16[8,4096]{1,0:T(8,128)(2,1)S(1)}, bf16[8,4096]{1,0:T(8,128)(2,1)S(1)}, u32[]{:S(2)}, u32[]{:S(2)}) collective-permute-start(bf16[8,4096]{1,0:T(8,128)(2,1)S(1)} %slice.79), channel_id=1, source_target_pairs={{0,4},{1,5},{2,6},{3,7},{4,0},{5,1},{6,2},{7,3},{8,12},{9,13},{10,... | collective-permute-start | bytes 196616 | tf_op jit(solution)/shard_map/ppermute | solution.py:27
  45.6 5.0 %collective-permute-start.14 = (bf16[16,4096]{1,0:T(8,128)(2,1)S(1)}, bf16[16,4096]{1,0:T(8,128)(2,1)S(1)}, u32[]{:S(2)}, u32[]{:S(2)}) collective-permute-start(bf16[16,4096]{1,0:T(8,128)(2,1)S(1)} %slice.78), channel_id=1, source_target_pairs={{0,2},{1,3},{2,0},{3,1},{4,6},{5,7},{6,4},{7,5},{8,10},{9,11},{10,... | collective-permute-start | bytes 393224 | tf_op jit(solution)/shard_map/ppermute | solution.py:27
  46.2 7.1 %collective-permute-start.18 = (bf16[8,4096]{1,0:T(8,128)(2,1)S(1)}, bf16[8,4096]{1,0:T(8,128)(2,1)S(1)}, u32[]{:S(2)}, u32[]{:S(2)}) collective-permute-start(bf16[8,4096]{1,0:T(8,128)(2,1)S(1)} %fusion.1), channel_id=1, source_target_pairs={{0,24},{8,16},{16,8},{24,0},{1,25},{9,17},{17,9},{25,1},{2,26},{10... | collective-permute-start | bytes 196616 | tf_op jit(solution)/shard_map/ppermute | solution.py:27
  50.7 5.9 %collective-permute-start.15 = (bf16[8,4096]{1,0:T(8,128)(2,1)S(1)}, bf16[8,4096]{1,0:T(8,128)(2,1)S(1)}, u32[]{:S(2)}, u32[]{:S(2)}) collective-permute-start(bf16[8,4096]{1,0:T(8,128)(2,1)S(1)} %slice.80), channel_id=1, source_target_pairs={{0,4},{1,5},{2,6},{3,7},{4,0},{5,1},{6,2},{7,3},{8,12},{9,13},{10,... | collective-permute-start | bytes 196616 | tf_op jit(solution)/shard_map/ppermute | solution.py:27

commit v8 on v7

--- a/solution.py
+++ b/solution.py
@@ -144,7 +144,9 @@
 def expert_kernel(exp_dev, experts, count, *refs):
     group_ref = refs[0]
     x_refs = refs[1 : 1 + count]
-    low_ref, high_ref, wout_ref, send_ref, keep_ref, mixed, hidden = refs[1 + count :]
+    low_ref, high_ref, wout_ref = refs[1 + count : 4 + count]
+    send_refs, keep_refs = refs[4 + count : 6 + count], refs[6 + count : 8 + count]
+    mixed, hidden = refs[8 + count :]
     lines = low_ref.shape[1]
     width = wout_ref.shape[1]
     per = lines // exp_dev
@@ -175,7 +177,8 @@
             act = gate / (1.0 + jnp.exp(-gate)) * up * scale[e : e + 1, r : r + LANES]
             hidden[pl.ds(e * per // 2, per // 2), r : r + LANES] = act.astype(jnp.bfloat16)
     chunk = min(512, width)
-    pieces, piece, _ = keep_ref.shape
+    ahead, piece, _ = keep_refs[0].shape
+    pieces = ahead + keep_refs[1].shape[0]
     for c in range(0, width, chunk):
         part = lax.dot_general(
             hidden[...],
@@ -183,40 +186,45 @@
             (((0,), (0,)), ((), ())),
             preferred_element_type=jnp.float32,
         )
-        for p in range(pieces):
-            keep_ref[p, :, c : c + chunk] = part[p * piece : (p + 1) * piece]
-            other = part[(pieces + p) * piece : (pieces + p + 1) * piece]
-            send_ref[p, :, c : c + chunk] = other.astype(jnp.bfloat16)
-
-
-def run_experts(group, blocks, low, high, wout, exp_dev, experts):
+        for p in range(2 * pieces):
+            targets = keep_refs if p < pieces else send_refs
+            q = p % pieces
+            target = targets[0].at[q] if q < ahead else targets[1].at[q - ahead]
+            target[:, c : c + chunk] = part[p * piece : (p + 1) * piece].astype(target.dtype)
+
+
+def run_experts(group, blocks, pieces, low, high, wout, exp_dev, experts):
     packed_width = blocks[0].shape[1]
     half_rows = sum(block.shape[0] for block in blocks) // 2
+    piece = half_rows // pieces
+    ahead = pieces - 2
     count = len(blocks)
     width = wout.shape[1]
     lines = low.shape[1]
-    one_step = half_rows <= LANES
-    if one_step:
-        x_block, out_block, grid = VMEM, VMEM, ()
-        pieces, piece, rows = 1, half_rows, 2 * half_rows
-        windows = 0
+    if half_rows <= LANES:
+        x_block, out_blocks, grid = VMEM, [VMEM] * 4, ()
+        rows, windows = 2 * half_rows, 0
     else:
-        pieces, piece, block = count // 2, blocks[0].shape[0], 16
+        block = 16
         x_block = pl.BlockSpec((block, packed_width), lambda i: (i, 0))
-        out_block = pl.BlockSpec((pieces, block, width), lambda i: (0, i, 0))
+        out_blocks = [
+            pl.BlockSpec((n, block, width), lambda i: (0, i, 0)) for n in (ahead, 2, ahead, 2)
+        ]
         grid = (piece // block,)
         rows = count * block
         windows = 2 * rows * (2 * packed_width + 3 * width)
     scratch = rows * (6 * lines + 6 * width)
-    send, keep = pl.pallas_call(
+    return pl.pallas_call(
         functools.partial(expert_kernel, exp_dev, experts, count),
         grid=grid,
         out_shape=(
-            jax.ShapeDtypeStruct((pieces, piece, width), jnp.bfloat16),
-            jax.ShapeDtypeStruct((pieces, piece, width), jnp.float32),
+            jax.ShapeDtypeStruct((ahead, piece, width), jnp.bfloat16),
+            jax.ShapeDtypeStruct((2, piece, width), jnp.bfloat16),
+            jax.ShapeDtypeStruct((ahead, piece, width), jnp.float32),
+            jax.ShapeDtypeStruct((2, piece, width), jnp.float32),
         ),
         in_specs=[pl.BlockSpec(memory_space=pltpu.SMEM), *[x_block] * count, VMEM, VMEM, VMEM],
-        out_specs=[out_block, out_block],
+        out_specs=out_blocks,
         scratch_shapes=[
             pltpu.VMEM((lines // exp_dev, LANES), jnp.float32),
             pltpu.VMEM((lines // 2, rows), jnp.bfloat16),
@@ -228,7 +236,6 @@
             transcendentals=half_rows * lines,
         ),
     )(group, *blocks, *in_vmem(low, high, wout))
-    return send.reshape(half_rows, width), keep.reshape(half_rows, width)
 
 
 def halve(rows, stride):
@@ -271,20 +278,20 @@
     late_core = [swap(block, "expert", 1) for block in late]
     blocks = []
     for (mine, across), rest in ((early, late), (early_core, late_core)):
-        if 2 * mine.shape[0] * planes <= 2 * LANES:
-            blocks += [mine] + rest[:-1] + [across, rest[-1]]
+        if mine.shape[0] * planes <= LANES:
+            blocks += rest[:-1] + [mine, across, rest[-1]]
         else:
-            blocks += [mine] + rest[:-1] + [jnp.concatenate([across, rest[-1]], axis=0)]
-
-    send, total = run_experts(group, blocks, low, high, wout, exp_dev, experts)
-    total = total + swap(send, "expert", 1).astype(jnp.float32)
-    size = total.shape[0] // planes
-    rounded = total.astype(jnp.bfloat16)
-    mine = total[:size]
-    for b in range(1, far):
-        piece = rounded[b * size : (b + 1) * size]
-        mine = mine + swap(piece, "batch", b).astype(jnp.float32)
-    across = total[far * size :]
+            blocks += rest[:-1] + [mine, jnp.concatenate([across, rest[-1]], axis=0)]
+
+    sends = run_experts(group, blocks, planes, low, high, wout, exp_dev, experts)
+    first, second, kept, total = sends
+    arrived, second = lax.optimization_barrier((swap(first, "expert", 1), second))
+    first = (kept + arrived.astype(jnp.float32)).astype(jnp.bfloat16)
+    moved = [swap(first[b - 1], "batch", b) for b in range(1, far)]
+    total = total + swap(second, "expert", 1).astype(jnp.float32)
+    mine, across = total[0], total[1]
+    for rows in moved:
+        mine = mine + rows.astype(jnp.float32)
     for stride in reversed(strides):
         across = halve(across, stride)
     across = swap(across.astype(jnp.bfloat16), "batch", far).astype(jnp.float32)

time: 57.5 us -> 58.9 us (1.024)
  starting transfers between devices: 24.4 us -> 25.8 us
    ppermute x19 -> x20, starting transfers between devices: 24.4 us -> 25.8 us  [swap(): return lax.ppermute(block, axis, [(i, i ^ flips) for i in range(size)])]
    ppermute x19 -> x20, waiting for transfers between devices: 15.8 us -> 16 us  [swap(): return lax.ppermute(block, axis, [(i, i ^ flips) for i in range(size)])]
  transfers between devices with their start and end apart: 19 -> 20, of which waited for: 11 -> 11; matrix products, arithmetic and copies ran while one was open for 0% -> 1% of each run, Pallas kernels for 16% -> 16%
where the time goes in v8:
time: 58.9 us; the launch traced here: 58.7 us
  starting transfers between devices  25.8 us (44%)
  waiting for transfers between devices  16 us (27%)
  Pallas kernels  15.6 us (26%)
  other arithmetic  1.05 us (2%)
    ppermute x20, starting transfers between devices, swap(): return lax.ppermute(block, axis, [(i, i ^ flips) for i in range(size)])  25.8 us
    ppermute x20, waiting for transfers between devices, swap(): return lax.ppermute(block, axis, [(i, i ^ flips) for i in range(size)])  16 us
    pallas_call x3, Pallas kernels, load(): pl.pallas_call(kernel, out_shape=pltpu.VMEM(shape, source.dtype), in_spec...  9.16 us
    pallas_call x1, Pallas kernels, run_experts(): pl.pallas_call(functools.partial(expert_kernel, exp_dev, experts, count),...  5.45 us
  transfers between devices with their start and end apart: 20, of which 11 were waited for; matrix products, arithmetic and copies ran while one was open for 1% of the time, Pallas kernels for 16%

profile of v8, /device:TPU:0, one launch (start us, length us, event | category | flops | bytes accessed | tf_op | source)
XLA Modules:
  0.0 58.7 jit_solution(15750374685839676307)
XLA Ops:
  0.0 1.0 %shard_map.55.first_ref = bf16[8,4224]{1,0:T(8,128)(2,1)S(1)} custom-call(bf16[8,4096]{1,0:T(8,128)(2,1)} %tokens_hbm.1, s32[8,8]{1,0:T(8,128)} %ids_hbm.1, f32[8,8]{1,0:T(8,128)} %weights_hbm.1), custom_call_target="tpu_custom_call" | custom-call | tf_op jit(solution)/shard_map/pallas_call | solution.py:63
  1.0 4.1 %collective-permute-start = (bf16[8,4224]{1,0:T(8,128)(2,1)S(1)}, bf16[8,4224]{1,0:T(8,128)(2,1)S(1)}, u32[]{:S(2)}, u32[]{:S(2)}) collective-permute-start(bf16[8,4224]{1,0:T(8,128)(2,1)S(1)} %shard_map.55.first_ref), channel_id=1, source_target_pairs={{0,4},{1,5},{2,6},{3,7},{4,0},{5,1},{6,2},{7,3},{8,12},{9,13},{10,... | collective-permute-start | bytes 202760 | tf_op jit(solution)/shard_map/ppermute | solution.py:27
  5.1 2.9 %shard_map.56.refs_0_ = bf16[768,4096]{1,0:T(8,128)(2,1)S(1)} custom-call(bf16[768,4096]{1,0:T(8,128)(2,1)} %bitcast.25), custom_call_target="tpu_custom_call" | custom-call | bytes 12582912 | tf_op jit(solution)/shard_map/pallas_call | solution.py:124
  8.0 0.9 %collective-permute-done.second_ref = bf16[8,4224]{1,0:T(8,128)(2,1)S(1)} collective-permute-done((bf16[8,4224]{1,0:T(8,128)(2,1)S(1)}, bf16[8,4224]{1,0:T(8,128)(2,1)S(1)}, u32[]{:S(2)}, u32[]{:S(2)}) %collective-permute-start) | collective-permute-done | bytes 67616 | tf_op jit(solution)/shard_map/ppermute | solution.py:27
  8.8 0.8 %collective-permute-start.2 = (bf16[16,4224]{1,0:T(8,128)(2,1)S(1)}, bf16[16,4224]{1,0:T(8,128)(2,1)S(1)}, u32[]{:S(2)}, u32[]{:S(2)}) collective-permute-start(bf16[16,4224]{1,0:T(8,128)(2,1)S(1)} %get-tuple-element.37.first_ref), channel_id=1, source_target_pairs={{0,2},{1,3},{2,0},{3,1},{4,6},{5,7},{6,4},{7,5},{8,10},{9,11},{10,... | collective-permute-start | bytes 405512 | tf_op jit(solution)/shard_map/ppermute | solution.py:27
  9.6 2.4 %collective-permute-start.1 = (bf16[16,4224]{1,0:T(8,128)(2,1)S(1)}, bf16[16,4224]{1,0:T(8,128)(2,1)S(1)}, u32[]{:S(2)}, u32[]{:S(2)}) collective-permute-start(bf16[16,4224]{1,0:T(8,128)(2,1)S(1)} %get-tuple-element.37.first_ref), channel_id=1, source_target_pairs={{0,24},{8,16},{16,8},{24,0},{1,25},{9,17},{17,9},{25,1},{2,26},{10... | collective-permute-start | bytes 405512 | tf_op jit(solution)/shard_map/ppermute | solution.py:27
  12.1 3.2 %shard_map.58 = bf16[16,768,2,128]{3,2,1,0:T(2,128)(2,1)S(1)} custom-call(bf16[768,2,4096]{2,1,0:T(2,128)(2,1)} %bitcast.23), custom_call_target="tpu_custom_call" | custom-call | bytes 12582912 | tf_op jit(solution)/shard_map/pallas_call | solution.py:124
  15.3 0.0 collective-permute-done.2.second_ref
  15.3 0.3 collective-permute-done.1.refs_4_
  15.6 1.6 %collective-permute-start.4 = (bf16[32,4224]{1,0:T(8,128)(2,1)S(1)}, bf16[32,4224]{1,0:T(8,128)(2,1)S(1)}, u32[]{:S(2)}, u32[]{:S(2)}) collective-permute-start(bf16[32,4224]{1,0:T(8,128)(2,1)S(1)} %get-tuple-element.44.refs_3_), channel_id=1, source_target_pairs={{0,16},{8,24},{16,0},{24,8},{1,17},{9,25},{17,1},{25,9},{2,18},{10... | collective-permute-start | bytes 811016 | tf_op jit(solution)/shard_map/ppermute | solution.py:27
  17.2 1.5 %collective-permute-start.3 = (bf16[32,4224]{1,0:T(8,128)(2,1)S(1)}, bf16[32,4224]{1,0:T(8,128)(2,1)S(1)}, u32[]{:S(2)}, u32[]{:S(2)}) collective-permute-start(bf16[32,4224]{1,0:T(8,128)(2,1)S(1)} %get-tuple-element.44.refs_3_), channel_id=1, source_target_pairs={{0,8},{8,0},{16,24},{24,16},{1,9},{9,1},{17,25},{25,17},{2,10},{10... | collective-permute-start | bytes 811016 | tf_op jit(solution)/shard_map/ppermute | solution.py:27
  18.7 1.5 %collective-permute-start.5 = (bf16[16,4224]{1,0:T(8,128)(2,1)S(1)}, bf16[16,4224]{1,0:T(8,128)(2,1)S(1)}, u32[]{:S(2)}, u32[]{:S(2)}) collective-permute-start(bf16[16,4224]{1,0:T(8,128)(2,1)S(1)} %collective-permute-done.1.refs_4_), channel_id=1, source_target_pairs={{0,2},{1,3},{2,0},{3,1},{4,6},{5,7},{6,4},{7,5},{8,10},{9,11},{10,... | collective-permute-start | bytes 405512 | tf_op jit(solution)/shard_map/ppermute | solution.py:27
  20.2 0.0 collective-permute-start.8
  20.2 3.2 %shard_map.60 = bf16[16,768,2,128]{3,2,1,0:T(2,128)(2,1)S(1)} custom-call(bf16[768,2,4096]{2,1,0:T(2,128)(2,1)} %bitcast.24), custom_call_target="tpu_custom_call" | custom-call | bytes 12582912 | tf_op jit(solution)/shard_map/pallas_call | solution.py:124
  23.3 0.3 collective-permute-done.5.refs_5_
  23.7 0.0 collective-permute-done.4.refs_2_
  23.7 0.0 collective-permute-done.3.refs_1_
  23.7 0.3 collective-permute-start.6
  23.9 0.2 collective-permute-start.7
  24.2 0.3 collective-permute-start.9
  24.5 0.2 collective-permute-start.10
  24.7 1.1 %collective-permute-done.9.refs_9_ = bf16[16,4224]{1,0:T(8,128)(2,1)S(1)} collective-permute-done((bf16[16,4224]{1,0:T(8,128)(2,1)S(1)}, bf16[16,4224]{1,0:T(8,128)(2,1)S(1)}, u32[]{:S(2)}, u32[]{:S(2)}) %collective-permute-start.9) | collective-permute-done | bytes 135200 | tf_op jit(solution)/shard_map/ppermute | solution.py:27
  25.8 0.0 collective-permute-done.8.refs_8_
  25.8 0.2 collective-permute-done.10.refs_10_
  26.0 0.0 collective-permute-done.6.refs_6_
  26.0 0.0 collective-permute-done.7.refs_7_
  26.0 5.4 %shard_map.61 = (bf16[2,32,4096]{2,1,0:T(8,128)(2,1)S(1)}, bf16[2,32,4096]{2,1,0:T(8,128)(2,1)S(1)}, f32[2,32,4096]{2,1,0:T(8,128)S(1)}, f32[2,32,4096]{2,1,0:T(8,128)S(1)}) custom-call(s32[1]{0:T(128)} %bitcast.refs_0_, bf16[32,4224]{1,0:T(8,128)(2,1)S(1)} %collective-permute-done.3.refs_1_, bf16[32,4224]{1,0:T(8,128)(2,1)S(1)} %collective-permute-done.4.refs_2_, ...), custom_call_target="tpu_custom_call" | custom-call | flops 4831838208 | bytes 5308416 | tf_op jit(solution)/shard_map/pallas_call | solution.py:217
  31.5 0.3 collective-permute-start.11
  31.8 1.7 %collective-permute-done.11 = bf16[2,32,4096]{2,1,0:T(8,128)(2,1)S(1)} collective-permute-done((bf16[2,32,4096]{2,1,0:T(8,128)(2,1)S(1)}, bf16[2,32,4096]{2,1,0:T(8,128)(2,1)S(1)}, u32[]{:S(2)}, u32[]{:S(2)}) %collective-permute-start.11) | collective-permute-done | bytes 524320 | tf_op jit(solution)/shard_map/ppermute | solution.py:27
  33.4 0.3 collective-permute-start.12
  33.7 0.1 add_convert_fusion
  33.9 1.4 %collective-permute-start.13 = (bf16[32,4096]{1,0:T(8,128)(2,1)S(1)}, bf16[32,4096]{1,0:T(8,128)(2,1)S(1)}, u32[]{:S(2)}, u32[]{:S(2)}) collective-permute-start(bf16[32,4096]{1,0:T(8,128)(2,1)S(1)} %get-tuple-element.59), channel_id=1, source_target_pairs={{0,8},{8,0},{16,24},{24,16},{1,9},{9,1},{17,25},{25,17},{2,10},{10... | collective-permute-start | bytes 786440 | tf_op jit(solution)/shard_map/ppermute | solution.py:27
  35.3 0.5 collective-permute-start.14
  35.8 0.0 collective-permute-done.12
  35.8 0.1 convert_add_fusion
  35.9 1.6 %collective-permute-start.17 = (bf16[16,4096]{1,0:T(8,128)(2,1)S(1)}, bf16[16,4096]{1,0:T(8,128)(2,1)S(1)}, u32[]{:S(2)}, u32[]{:S(2)}) collective-permute-start(bf16[16,4096]{1,0:T(8,128)(2,1)S(1)} %fusion.3), channel_id=1, source_target_pairs={{0,2},{1,3},{2,0},{3,1},{4,6},{5,7},{6,4},{7,5},{8,10},{9,11},{10,... | collective-permute-start | bytes 393224 | tf_op jit(solution)/shard_map/ppermute | solution.py:27
  37.5 4.9 %collective-permute-done.13 = bf16[32,4096]{1,0:T(8,128)(2,1)S(1)} collective-permute-done((bf16[32,4096]{1,0:T(8,128)(2,1)S(1)}, bf16[32,4096]{1,0:T(8,128)(2,1)S(1)}, u32[]{:S(2)}, u32[]{:S(2)}) %collective-permute-start.13) | collective-permute-done | bytes 262176 | tf_op jit(solution)/shard_map/ppermute | solution.py:27
  42.4 1.1 %collective-permute-done.14 = bf16[32,4096]{1,0:T(8,128)(2,1)S(1)} collective-permute-done((bf16[32,4096]{1,0:T(8,128)(2,1)S(1)}, bf16[32,4096]{1,0:T(8,128)(2,1)S(1)}, u32[]{:S(2)}, u32[]{:S(2)}) %collective-permute-start.14) | collective-permute-done | bytes 262176 | tf_op jit(solution)/shard_map/ppermute | solution.py:27
  43.5 0.1 fusion.1
  43.7 1.6 %collective-permute-start.15 = (bf16[16,4096]{1,0:T(8,128)(2,1)S(1)}, bf16[16,4096]{1,0:T(8,128)(2,1)S(1)}, u32[]{:S(2)}, u32[]{:S(2)}) collective-permute-start(bf16[16,4096]{1,0:T(8,128)(2,1)S(1)} %slice.92), channel_id=1, source_target_pairs={{0,2},{1,3},{2,0},{3,1},{4,6},{5,7},{6,4},{7,5},{8,10},{9,11},{10,... | collective-permute-start | bytes 393224 | tf_op jit(solution)/shard_map/ppermute | solution.py:27
  45.2 0.0 collective-permute-done.17
  45.3 2.4 %collective-permute-start.18 = (bf16[8,4096]{1,0:T(8,128)(2,1)S(1)}, bf16[8,4096]{1,0:T(8,128)(2,1)S(1)}, u32[]{:S(2)}, u32[]{:S(2)}) collective-permute-start(bf16[8,4096]{1,0:T(8,128)(2,1)S(1)} %slice.93), channel_id=1, source_target_pairs={{0,4},{1,5},{2,6},{3,7},{4,0},{5,1},{6,2},{7,3},{8,12},{9,13},{10,... | collective-permute-start | bytes 196616 | tf_op jit(solution)/shard_map/ppermute | solution.py:27
  47.7 1.7 %collective-permute-done.15 = bf16[16,4096]{1,0:T(8,128)(2,1)S(1)} collective-permute-done((bf16[16,4096]{1,0:T(8,128)(2,1)S(1)}, bf16[16,4096]{1,0:T(8,128)(2,1)S(1)}, u32[]{:S(2)}, u32[]{:S(2)}) %collective-permute-start.15) | collective-permute-done | bytes 131104 | tf_op jit(solution)/shard_map/ppermute | solution.py:27
  49.4 3.3 %collective-permute-start.16 = (bf16[8,4096]{1,0:T(8,128)(2,1)S(1)}, bf16[8,4096]{1,0:T(8,128)(2,1)S(1)}, u32[]{:S(2)}, u32[]{:S(2)}) collective-permute-start(bf16[8,4096]{1,0:T(8,128)(2,1)S(1)} %slice.94), channel_id=1, source_target_pairs={{0,4},{1,5},{2,6},{3,7},{4,0},{5,1},{6,2},{7,3},{8,12},{9,13},{10,... | collective-permute-start | bytes 196616 | tf_op jit(solution)/shard_map/ppermute | solution.py:27
  52.8 0.0 collective-permute-done.18
  52.8 1.4 %collective-permute-start.19 = (bf16[8,4096]{1,0:T(8,128)(2,1)S(1)}, bf16[8,4096]{1,0:T(8,128)(2,1)S(1)}, u32[]{:S(2)}, u32[]{:S(2)}) collective-permute-start(bf16[8,4096]{1,0:T(8,128)(2,1)S(1)} %fusion.4), channel_id=1, source_target_pairs={{0,24},{8,16},{16,8},{24,0},{1,25},{9,17},{17,9},{25,1},{2,26},{10... | collective-permute-start | bytes 196616 | tf_op jit(solution)/shard_map/ppermute | solution.py:27
  54.2 0.9 %collective-permute-done.16 = bf16[8,4096]{1,0:T(8,128)(2,1)S(1)} collective-permute-done((bf16[8,4096]{1,0:T(8,128)(2,1)S(1)}, bf16[8,4096]{1,0:T(8,128)(2,1)S(1)}, u32[]{:S(2)}, u32[]{:S(2)}) %collective-permute-start.16) | collective-permute-done | bytes 65568 | tf_op jit(solution)/shard_map/ppermute | solution.py:27
  55.0 3.0 %collective-permute-done.19 = bf16[8,4096]{1,0:T(8,128)(2,1)S(1)} collective-permute-done((bf16[8,4096]{1,0:T(8,128)(2,1)S(1)}, bf16[8,4096]{1,0:T(8,128)(2,1)S(1)}, u32[]{:S(2)}, u32[]{:S(2)}) %collective-permute-start.19) | collective-permute-done | bytes 65568 | tf_op jit(solution)/shard_map/ppermute | solution.py:27
  58.0 0.7 %fusion.6 = bf16[8,4096]{1,0:T(8,128)(2,1)} fusion(f32[16,4096]{1,0:T(8,128)S(1)} %slice_add_fusion, bf16[8,4096]{1,0:T(8,128)(2,1)S(1)} %collective-permute-done.19, bf16[8,4096]{1,0:T(8,128)(2,1)S(1)} %collective-permute-done.16), kind=kLoop, calls=%fused_computation.19 | loop fusion | flops 163840 | bytes 327680 | tf_op jit(solution)/shard_map/convert_element_type | solution.py:301
  (10 shorter events, 0.2 us)
Async XLA Ops:
  1.0 7.8 %collective-permute-start = (bf16[8,4224]{1,0:T(8,128)(2,1)S(1)}, bf16[8,4224]{1,0:T(8,128)(2,1)S(1)}, u32[]{:S(2)}, u32[]{:S(2)}) collective-permute-start(bf16[8,4224]{1,0:T(8,128)(2,1)S(1)} %shard_map.55.first_ref), channel_id=1, source_target_pairs={{0,4},{1,5},{2,6},{3,7},{4,0},{5,1},{6,2},{7,3},{8,12},{9,13},{10,... | collective-permute-start | bytes 202760 | tf_op jit(solution)/shard_map/ppermute | solution.py:27
  8.8 6.4 %collective-permute-start.2 = (bf16[16,4224]{1,0:T(8,128)(2,1)S(1)}, bf16[16,4224]{1,0:T(8,128)(2,1)S(1)}, u32[]{:S(2)}, u32[]{:S(2)}) collective-permute-start(bf16[16,4224]{1,0:T(8,128)(2,1)S(1)} %get-tuple-element.37.first_ref), channel_id=1, source_target_pairs={{0,2},{1,3},{2,0},{3,1},{4,6},{5,7},{6,4},{7,5},{8,10},{9,11},{10,... | collective-permute-start | bytes 405512 | tf_op jit(solution)/shard_map/ppermute | solution.py:27
  9.6 5.9 %collective-permute-start.1 = (bf16[16,4224]{1,0:T(8,128)(2,1)S(1)}, bf16[16,4224]{1,0:T(8,128)(2,1)S(1)}, u32[]{:S(2)}, u32[]{:S(2)}) collective-permute-start(bf16[16,4224]{1,0:T(8,128)(2,1)S(1)} %get-tuple-element.37.first_ref), channel_id=1, source_target_pairs={{0,24},{8,16},{16,8},{24,0},{1,25},{9,17},{17,9},{25,1},{2,26},{10... | collective-permute-start | bytes 405512 | tf_op jit(solution)/shard_map/ppermute | solution.py:27
  15.6 8.1 %collective-permute-start.4 = (bf16[32,4224]{1,0:T(8,128)(2,1)S(1)}, bf16[32,4224]{1,0:T(8,128)(2,1)S(1)}, u32[]{:S(2)}, u32[]{:S(2)}) collective-permute-start(bf16[32,4224]{1,0:T(8,128)(2,1)S(1)} %get-tuple-element.44.refs_3_), channel_id=1, source_target_pairs={{0,16},{8,24},{16,0},{24,8},{1,17},{9,25},{17,1},{25,9},{2,18},{10... | collective-permute-start | bytes 811016 | tf_op jit(solution)/shard_map/ppermute | solution.py:27
  17.2 6.5 %collective-permute-start.3 = (bf16[32,4224]{1,0:T(8,128)(2,1)S(1)}, bf16[32,4224]{1,0:T(8,128)(2,1)S(1)}, u32[]{:S(2)}, u32[]{:S(2)}) collective-permute-start(bf16[32,4224]{1,0:T(8,128)(2,1)S(1)} %get-tuple-element.44.refs_3_), channel_id=1, source_target_pairs={{0,8},{8,0},{16,24},{24,16},{1,9},{9,1},{17,25},{25,17},{2,10},{10... | collective-permute-start | bytes 811016 | tf_op jit(solution)/shard_map/ppermute | solution.py:27
  18.7 5.0 %collective-permute-start.5 = (bf16[16,4224]{1,0:T(8,128)(2,1)S(1)}, bf16[16,4224]{1,0:T(8,128)(2,1)S(1)}, u32[]{:S(2)}, u32[]{:S(2)}) collective-permute-start(bf16[16,4224]{1,0:T(8,128)(2,1)S(1)} %collective-permute-done.1.refs_4_), channel_id=1, source_target_pairs={{0,2},{1,3},{2,0},{3,1},{4,6},{5,7},{6,4},{7,5},{8,10},{9,11},{10,... | collective-permute-start | bytes 405512 | tf_op jit(solution)/shard_map/ppermute | solution.py:27
  20.2 5.6 %collective-permute-start.8 = (bf16[32,4224]{1,0:T(8,128)(2,1)S(1)}, bf16[32,4224]{1,0:T(8,128)(2,1)S(1)}, u32[]{:S(2)}, u32[]{:S(2)}) collective-permute-start(bf16[32,4224]{1,0:T(8,128)(2,1)S(1)} %get-tuple-element.44.refs_3_), channel_id=1, source_target_pairs={{0,1},{1,0},{2,3},{3,2},{4,5},{5,4},{6,7},{7,6},{8,9},{9,8},{10,11... | collective-permute-start | bytes 811016 | tf_op jit(solution)/shard_map/ppermute | solution.py:27
  23.7 2.3 %collective-permute-start.6 = (bf16[32,4224]{1,0:T(8,128)(2,1)S(1)}, bf16[32,4224]{1,0:T(8,128)(2,1)S(1)}, u32[]{:S(2)}, u32[]{:S(2)}) collective-permute-start(bf16[32,4224]{1,0:T(8,128)(2,1)S(1)} %collective-permute-done.3.refs_1_), channel_id=1, source_target_pairs={{0,1},{1,0},{2,3},{3,2},{4,5},{5,4},{6,7},{7,6},{8,9},{9,8},{10,11... | collective-permute-start | bytes 811016 | tf_op jit(solution)/shard_map/ppermute | solution.py:27
  23.9 2.1 %collective-permute-start.7 = (bf16[32,4224]{1,0:T(8,128)(2,1)S(1)}, bf16[32,4224]{1,0:T(8,128)(2,1)S(1)}, u32[]{:S(2)}, u32[]{:S(2)}) collective-permute-start(bf16[32,4224]{1,0:T(8,128)(2,1)S(1)} %collective-permute-done.4.refs_2_), channel_id=1, source_target_pairs={{0,1},{1,0},{2,3},{3,2},{4,5},{5,4},{6,7},{7,6},{8,9},{9,8},{10,11... | collective-permute-start | bytes 811016 | tf_op jit(solution)/shard_map/ppermute | solution.py:27
  24.2 1.6 %collective-permute-start.9 = (bf16[16,4224]{1,0:T(8,128)(2,1)S(1)}, bf16[16,4224]{1,0:T(8,128)(2,1)S(1)}, u32[]{:S(2)}, u32[]{:S(2)}) collective-permute-start(bf16[16,4224]{1,0:T(8,128)(2,1)S(1)} %collective-permute-done.1.refs_4_), channel_id=1, source_target_pairs={{0,1},{1,0},{2,3},{3,2},{4,5},{5,4},{6,7},{7,6},{8,9},{9,8},{10,11... | collective-permute-start | bytes 405512 | tf_op jit(solution)/shard_map/ppermute | solution.py:27
  24.5 1.5 %collective-permute-start.10 = (bf16[16,4224]{1,0:T(8,128)(2,1)S(1)}, bf16[16,4224]{1,0:T(8,128)(2,1)S(1)}, u32[]{:S(2)}, u32[]{:S(2)}) collective-permute-start(bf16[16,4224]{1,0:T(8,128)(2,1)S(1)} %collective-permute-done.5.refs_5_), channel_id=1, source_target_pairs={{0,1},{1,0},{2,3},{3,2},{4,5},{5,4},{6,7},{7,6},{8,9},{9,8},{10,11... | collective-permute-start | bytes 405512 | tf_op jit(solution)/shard_map/ppermute | solution.py:27
  31.5 2.0 %collective-permute-start.11 = (bf16[2,32,4096]{2,1,0:T(8,128)(2,1)S(1)}, bf16[2,32,4096]{2,1,0:T(8,128)(2,1)S(1)}, u32[]{:S(2)}, u32[]{:S(2)}) collective-permute-start(bf16[2,32,4096]{2,1,0:T(8,128)(2,1)S(1)} %get-tuple-element.54), channel_id=1, source_target_pairs={{0,1},{1,0},{2,3},{3,2},{4,5},{5,4},{6,7},{7,6},{8,9},{9,8},{10,11... | collective-permute-start | bytes 1572872 | tf_op jit(solution)/shard_map/ppermute | solution.py:27
  33.4 2.3 %collective-permute-start.12 = (bf16[2,32,4096]{2,1,0:T(8,128)(2,1)S(1)}, bf16[2,32,4096]{2,1,0:T(8,128)(2,1)S(1)}, u32[]{:S(2)}, u32[]{:S(2)}) collective-permute-start(bf16[2,32,4096]{2,1,0:T(8,128)(2,1)S(1)} %get-tuple-element.56), channel_id=1, source_target_pairs={{0,1},{1,0},{2,3},{3,2},{4,5},{5,4},{6,7},{7,6},{8,9},{9,8},{10,11... | collective-permute-start | bytes 1572872 | tf_op jit(solution)/shard_map/ppermute | solution.py:27
  33.9 8.5 %collective-permute-start.13 = (bf16[32,4096]{1,0:T(8,128)(2,1)S(1)}, bf16[32,4096]{1,0:T(8,128)(2,1)S(1)}, u32[]{:S(2)}, u32[]{:S(2)}) collective-permute-start(bf16[32,4096]{1,0:T(8,128)(2,1)S(1)} %get-tuple-element.59), channel_id=1, source_target_pairs={{0,8},{8,0},{16,24},{24,16},{1,9},{9,1},{17,25},{25,17},{2,10},{10... | collective-permute-start | bytes 786440 | tf_op jit(solution)/shard_map/ppermute | solution.py:27
  35.3 8.3 %collective-permute-start.14 = (bf16[32,4096]{1,0:T(8,128)(2,1)S(1)}, bf16[32,4096]{1,0:T(8,128)(2,1)S(1)}, u32[]{:S(2)}, u32[]{:S(2)}) collective-permute-start(bf16[32,4096]{1,0:T(8,128)(2,1)S(1)} %get-tuple-element.60), channel_id=1, source_target_pairs={{0,16},{8,24},{16,0},{24,8},{1,17},{9,25},{17,1},{25,9},{2,18},{10... | collective-permute-start | bytes 786440 | tf_op jit(solution)/shard_map/ppermute | solution.py:27
  35.9 9.3 %collective-permute-start.17 = (bf16[16,4096]{1,0:T(8,128)(2,1)S(1)}, bf16[16,4096]{1,0:T(8,128)(2,1)S(1)}, u32[]{:S(2)}, u32[]{:S(2)}) collective-permute-start(bf16[16,4096]{1,0:T(8,128)(2,1)S(1)} %fusion.3), channel_id=1, source_target_pairs={{0,2},{1,3},{2,0},{3,1},{4,6},{5,7},{6,4},{7,5},{8,10},{9,11},{10,... | collective-permute-start | bytes 393224 | tf_op jit(solution)/shard_map/ppermute | solution.py:27
  43.7 5.7 %collective-permute-start.15 = (bf16[16,4096]{1,0:T(8,128)(2,1)S(1)}, bf16[16,4096]{1,0:T(8,128)(2,1)S(1)}, u32[]{:S(2)}, u32[]{:S(2)}) collective-permute-start(bf16[16,4096]{1,0:T(8,128)(2,1)S(1)} %slice.92), channel_id=1, source_target_pairs={{0,2},{1,3},{2,0},{3,1},{4,6},{5,7},{6,4},{7,5},{8,10},{9,11},{10,... | collective-permute-start | bytes 393224 | tf_op jit(solution)/shard_map/ppermute | solution.py:27
  45.3 7.5 %collective-permute-start.18 = (bf16[8,4096]{1,0:T(8,128)(2,1)S(1)}, bf16[8,4096]{1,0:T(8,128)(2,1)S(1)}, u32[]{:S(2)}, u32[]{:S(2)}) collective-permute-start(bf16[8,4096]{1,0:T(8,128)(2,1)S(1)} %slice.93), channel_id=1, source_target_pairs={{0,4},{1,5},{2,6},{3,7},{4,0},{5,1},{6,2},{7,3},{8,12},{9,13},{10,... | collective-permute-start | bytes 196616 | tf_op jit(solution)/shard_map/ppermute | solution.py:27
  49.4 5.6 %collective-permute-start.16 = (bf16[8,4096]{1,0:T(8,128)(2,1)S(1)}, bf16[8,4096]{1,0:T(8,128)(2,1)S(1)}, u32[]{:S(2)}, u32[]{:S(2)}) collective-permute-start(bf16[8,4096]{1,0:T(8,128)(2,1)S(1)} %slice.94), channel_id=1, source_target_pairs={{0,4},{1,5},{2,6},{3,7},{4,0},{5,1},{6,2},{7,3},{8,12},{9,13},{10,... | collective-permute-start | bytes 196616 | tf_op jit(solution)/shard_map/ppermute | solution.py:27
  52.8 5.2 %collective-permute-start.19 = (bf16[8,4096]{1,0:T(8,128)(2,1)S(1)}, bf16[8,4096]{1,0:T(8,128)(2,1)S(1)}, u32[]{:S(2)}, u32[]{:S(2)}) collective-permute-start(bf16[8,4096]{1,0:T(8,128)(2,1)S(1)} %fusion.4), channel_id=1, source_target_pairs={{0,24},{8,16},{16,8},{24,0},{1,25},{9,17},{17,9},{25,1},{2,26},{10... | collective-permute-start | bytes 196616 | tf_op jit(solution)/shard_map/ppermute | solution.py:27

commit v9 on v8

--- a/solution.py
+++ b/solution.py
@@ -292,12 +292,11 @@
     mine, across = total[0], total[1]
     for rows in moved:
         mine = mine + rows.astype(jnp.float32)
-    for stride in reversed(strides):
-        across = halve(across, stride)
-    across = swap(across.astype(jnp.bfloat16), "batch", far).astype(jnp.float32)
-    for stride in reversed(strides):
+    across = halve(across, strides[-1])
+    mine = halve(mine, strides[-1])
+    mine = mine + swap(across.astype(jnp.bfloat16), "batch", far).astype(jnp.float32)
+    for stride in reversed(strides[:-1]):
         mine = halve(mine, stride)
-    mine = mine + across
     return mine.astype(jnp.bfloat16)
 
 

time: 58.9 us -> 58 us (0.985)
  starting transfers between devices: 25.8 us -> 21.6 us
  waiting for transfers between devices: 16 us -> 19.3 us
    ppermute x20 -> x19, starting transfers between devices: 25.8 us -> 21.6 us  [swap(): return lax.ppermute(block, axis, [(i, i ^ flips) for i in range(size)])]
    ppermute x20 -> x19, waiting for transfers between devices: 16 us -> 19.3 us  [swap(): return lax.ppermute(block, axis, [(i, i ^ flips) for i in range(size)])]
  transfers between devices with their start and end apart: 20 -> 19, of which waited for: 11 -> 11; matrix products, arithmetic and copies ran while one was open for 1% -> 1% of each run, Pallas kernels for 16% -> 16%
where the time goes in v9:
time: 58 us; the launch traced here: 57.8 us
  starting transfers between devices  21.6 us (37%)
  waiting for transfers between devices  19.3 us (33%)
  Pallas kernels  15.6 us (27%)
  other arithmetic  1.04 us (2%)
    ppermute x19, starting transfers between devices, swap(): return lax.ppermute(block, axis, [(i, i ^ flips) for i in range(size)])  21.6 us
    ppermute x19, waiting for transfers between devices, swap(): return lax.ppermute(block, axis, [(i, i ^ flips) for i in range(size)])  19.3 us
    pallas_call x3, Pallas kernels, load(): pl.pallas_call(kernel, out_shape=pltpu.VMEM(shape, source.dtype), in_spec...  9.16 us
    pallas_call x1, Pallas kernels, run_experts(): pl.pallas_call(functools.partial(expert_kernel, exp_dev, experts, count),...  5.45 us
  transfers between devices with their start and end apart: 19, of which 11 were waited for; matrix products, arithmetic and copies ran while one was open for 1% of the time, Pallas kernels for 16%

profile of v9, /device:TPU:0, one launch (start us, length us, event | category | flops | bytes accessed | tf_op | source)
XLA Modules:
  0.0 57.8 jit_solution(621629566156337552)
XLA Ops:
  0.0 1.0 %shard_map.55.first_ref = bf16[8,4224]{1,0:T(8,128)(2,1)S(1)} custom-call(bf16[8,4096]{1,0:T(8,128)(2,1)} %tokens_hbm.1, s32[8,8]{1,0:T(8,128)} %ids_hbm.1, f32[8,8]{1,0:T(8,128)} %weights_hbm.1), custom_call_target="tpu_custom_call" | custom-call | tf_op jit(solution)/shard_map/pallas_call | solution.py:63
  1.0 4.1 %collective-permute-start = (bf16[8,4224]{1,0:T(8,128)(2,1)S(1)}, bf16[8,4224]{1,0:T(8,128)(2,1)S(1)}, u32[]{:S(2)}, u32[]{:S(2)}) collective-permute-start(bf16[8,4224]{1,0:T(8,128)(2,1)S(1)} %shard_map.55.first_ref), channel_id=1, source_target_pairs={{0,4},{1,5},{2,6},{3,7},{4,0},{5,1},{6,2},{7,3},{8,12},{9,13},{10,... | collective-permute-start | bytes 202760 | tf_op jit(solution)/shard_map/ppermute | solution.py:27
  5.1 2.9 %shard_map.56.refs_0_ = bf16[768,4096]{1,0:T(8,128)(2,1)S(1)} custom-call(bf16[768,4096]{1,0:T(8,128)(2,1)} %bitcast.27), custom_call_target="tpu_custom_call" | custom-call | bytes 12582912 | tf_op jit(solution)/shard_map/pallas_call | solution.py:124
  8.0 0.9 %collective-permute-done.second_ref = bf16[8,4224]{1,0:T(8,128)(2,1)S(1)} collective-permute-done((bf16[8,4224]{1,0:T(8,128)(2,1)S(1)}, bf16[8,4224]{1,0:T(8,128)(2,1)S(1)}, u32[]{:S(2)}, u32[]{:S(2)}) %collective-permute-start) | collective-permute-done | bytes 67616 | tf_op jit(solution)/shard_map/ppermute | solution.py:27
  8.8 0.8 %collective-permute-start.2 = (bf16[16,4224]{1,0:T(8,128)(2,1)S(1)}, bf16[16,4224]{1,0:T(8,128)(2,1)S(1)}, u32[]{:S(2)}, u32[]{:S(2)}) collective-permute-start(bf16[16,4224]{1,0:T(8,128)(2,1)S(1)} %get-tuple-element.37.first_ref), channel_id=1, source_target_pairs={{0,2},{1,3},{2,0},{3,1},{4,6},{5,7},{6,4},{7,5},{8,10},{9,11},{10,... | collective-permute-start | bytes 405512 | tf_op jit(solution)/shard_map/ppermute | solution.py:27
  9.6 2.4 %collective-permute-start.1 = (bf16[16,4224]{1,0:T(8,128)(2,1)S(1)}, bf16[16,4224]{1,0:T(8,128)(2,1)S(1)}, u32[]{:S(2)}, u32[]{:S(2)}) collective-permute-start(bf16[16,4224]{1,0:T(8,128)(2,1)S(1)} %get-tuple-element.37.first_ref), channel_id=1, source_target_pairs={{0,24},{8,16},{16,8},{24,0},{1,25},{9,17},{17,9},{25,1},{2,26},{10... | collective-permute-start | bytes 405512 | tf_op jit(solution)/shard_map/ppermute | solution.py:27
  12.1 3.2 %shard_map.58 = bf16[16,768,2,128]{3,2,1,0:T(2,128)(2,1)S(1)} custom-call(bf16[768,2,4096]{2,1,0:T(2,128)(2,1)} %bitcast.25), custom_call_target="tpu_custom_call" | custom-call | bytes 12582912 | tf_op jit(solution)/shard_map/pallas_call | solution.py:124
  15.3 0.0 collective-permute-done.2.second_ref
  15.3 0.3 collective-permute-done.1.refs_4_
  15.6 1.6 %collective-permute-start.4 = (bf16[32,4224]{1,0:T(8,128)(2,1)S(1)}, bf16[32,4224]{1,0:T(8,128)(2,1)S(1)}, u32[]{:S(2)}, u32[]{:S(2)}) collective-permute-start(bf16[32,4224]{1,0:T(8,128)(2,1)S(1)} %get-tuple-element.44.refs_3_), channel_id=1, source_target_pairs={{0,16},{8,24},{16,0},{24,8},{1,17},{9,25},{17,1},{25,9},{2,18},{10... | collective-permute-start | bytes 811016 | tf_op jit(solution)/shard_map/ppermute | solution.py:27
  17.2 1.5 %collective-permute-start.3 = (bf16[32,4224]{1,0:T(8,128)(2,1)S(1)}, bf16[32,4224]{1,0:T(8,128)(2,1)S(1)}, u32[]{:S(2)}, u32[]{:S(2)}) collective-permute-start(bf16[32,4224]{1,0:T(8,128)(2,1)S(1)} %get-tuple-element.44.refs_3_), channel_id=1, source_target_pairs={{0,8},{8,0},{16,24},{24,16},{1,9},{9,1},{17,25},{25,17},{2,10},{10... | collective-permute-start | bytes 811016 | tf_op jit(solution)/shard_map/ppermute | solution.py:27
  18.7 1.5 %collective-permute-start.5 = (bf16[16,4224]{1,0:T(8,128)(2,1)S(1)}, bf16[16,4224]{1,0:T(8,128)(2,1)S(1)}, u32[]{:S(2)}, u32[]{:S(2)}) collective-permute-start(bf16[16,4224]{1,0:T(8,128)(2,1)S(1)} %collective-permute-done.1.refs_4_), channel_id=1, source_target_pairs={{0,2},{1,3},{2,0},{3,1},{4,6},{5,7},{6,4},{7,5},{8,10},{9,11},{10,... | collective-permute-start | bytes 405512 | tf_op jit(solution)/shard_map/ppermute | solution.py:27
  20.2 0.0 collective-permute-start.8
  20.2 3.2 %shard_map.60 = bf16[16,768,2,128]{3,2,1,0:T(2,128)(2,1)S(1)} custom-call(bf16[768,2,4096]{2,1,0:T(2,128)(2,1)} %bitcast.26), custom_call_target="tpu_custom_call" | custom-call | bytes 12582912 | tf_op jit(solution)/shard_map/pallas_call | solution.py:124
  23.3 0.3 collective-permute-done.5.refs_5_
  23.7 0.0 collective-permute-done.4.refs_2_
  23.7 0.0 collective-permute-done.3.refs_1_
  23.7 0.3 collective-permute-start.6
  23.9 0.2 collective-permute-start.7
  24.2 0.3 collective-permute-start.9
  24.5 0.2 collective-permute-start.10
  24.7 1.1 %collective-permute-done.9.refs_9_ = bf16[16,4224]{1,0:T(8,128)(2,1)S(1)} collective-permute-done((bf16[16,4224]{1,0:T(8,128)(2,1)S(1)}, bf16[16,4224]{1,0:T(8,128)(2,1)S(1)}, u32[]{:S(2)}, u32[]{:S(2)}) %collective-permute-start.9) | collective-permute-done | bytes 135200 | tf_op jit(solution)/shard_map/ppermute | solution.py:27
  25.8 0.0 collective-permute-done.8.refs_8_
  25.8 0.2 collective-permute-done.10.refs_10_
  26.0 0.0 collective-permute-done.6.refs_6_
  26.0 0.0 collective-permute-done.7.refs_7_
  26.0 5.4 %shard_map.61 = (bf16[2,32,4096]{2,1,0:T(8,128)(2,1)S(1)}, bf16[2,32,4096]{2,1,0:T(8,128)(2,1)S(1)}, f32[2,32,4096]{2,1,0:T(8,128)S(1)}, f32[2,32,4096]{2,1,0:T(8,128)S(1)}) custom-call(s32[1]{0:T(128)} %bitcast.refs_0_, bf16[32,4224]{1,0:T(8,128)(2,1)S(1)} %collective-permute-done.3.refs_1_, bf16[32,4224]{1,0:T(8,128)(2,1)S(1)} %collective-permute-done.4.refs_2_, ...), custom_call_target="tpu_custom_call" | custom-call | flops 4831838208 | bytes 5308416 | tf_op jit(solution)/shard_map/pallas_call | solution.py:217
  31.5 0.3 collective-permute-start.11
  31.8 1.7 %collective-permute-done.11 = bf16[2,32,4096]{2,1,0:T(8,128)(2,1)S(1)} collective-permute-done((bf16[2,32,4096]{2,1,0:T(8,128)(2,1)S(1)}, bf16[2,32,4096]{2,1,0:T(8,128)(2,1)S(1)}, u32[]{:S(2)}, u32[]{:S(2)}) %collective-permute-start.11) | collective-permute-done | bytes 524320 | tf_op jit(solution)/shard_map/ppermute | solution.py:27
  33.4 0.3 collective-permute-start.12
  33.7 0.1 add_convert_fusion
  33.9 1.4 %collective-permute-start.13 = (bf16[32,4096]{1,0:T(8,128)(2,1)S(1)}, bf16[32,4096]{1,0:T(8,128)(2,1)S(1)}, u32[]{:S(2)}, u32[]{:S(2)}) collective-permute-start(bf16[32,4096]{1,0:T(8,128)(2,1)S(1)} %get-tuple-element.59), channel_id=1, source_target_pairs={{0,8},{8,0},{16,24},{24,16},{1,9},{9,1},{17,25},{25,17},{2,10},{10... | collective-permute-start | bytes 786440 | tf_op jit(solution)/shard_map/ppermute | solution.py:27
  35.3 0.5 collective-permute-start.14
  35.8 0.0 collective-permute-done.12
  35.8 0.1 convert_add_fusion
  35.9 1.6 %collective-permute-start.16 = (bf16[16,4096]{1,0:T(8,128)(2,1)S(1)}, bf16[16,4096]{1,0:T(8,128)(2,1)S(1)}, u32[]{:S(2)}, u32[]{:S(2)}) collective-permute-start(bf16[16,4096]{1,0:T(8,128)(2,1)S(1)} %fusion.5), channel_id=1, source_target_pairs={{0,2},{1,3},{2,0},{3,1},{4,6},{5,7},{6,4},{7,5},{8,10},{9,11},{10,... | collective-permute-start | bytes 393224 | tf_op jit(solution)/shard_map/ppermute | solution.py:27
  37.5 4.9 %collective-permute-done.13 = bf16[32,4096]{1,0:T(8,128)(2,1)S(1)} collective-permute-done((bf16[32,4096]{1,0:T(8,128)(2,1)S(1)}, bf16[32,4096]{1,0:T(8,128)(2,1)S(1)}, u32[]{:S(2)}, u32[]{:S(2)}) %collective-permute-start.13) | collective-permute-done | bytes 262176 | tf_op jit(solution)/shard_map/ppermute | solution.py:27
  42.4 1.1 %collective-permute-done.14 = bf16[32,4096]{1,0:T(8,128)(2,1)S(1)} collective-permute-done((bf16[32,4096]{1,0:T(8,128)(2,1)S(1)}, bf16[32,4096]{1,0:T(8,128)(2,1)S(1)}, u32[]{:S(2)}, u32[]{:S(2)}) %collective-permute-start.14) | collective-permute-done | bytes 262176 | tf_op jit(solution)/shard_map/ppermute | solution.py:27
  43.5 0.1 fusion.1
  43.7 1.6 %collective-permute-start.15 = (bf16[16,4096]{1,0:T(8,128)(2,1)S(1)}, bf16[16,4096]{1,0:T(8,128)(2,1)S(1)}, u32[]{:S(2)}, u32[]{:S(2)}) collective-permute-start(bf16[16,4096]{1,0:T(8,128)(2,1)S(1)} %slice.79), channel_id=1, source_target_pairs={{0,2},{1,3},{2,0},{3,1},{4,6},{5,7},{6,4},{7,5},{8,10},{9,11},{10,... | collective-permute-start | bytes 393224 | tf_op jit(solution)/shard_map/ppermute | solution.py:27
  45.2 0.0 collective-permute-done.16
  45.3 0.6 %collective-permute-start.17 = (bf16[16,4096]{1,0:T(8,128)(2,1)S(1)}, bf16[16,4096]{1,0:T(8,128)(2,1)S(1)}, u32[]{:S(2)}, u32[]{:S(2)}) collective-permute-start(bf16[16,4096]{1,0:T(8,128)(2,1)S(1)} %fusion.3), channel_id=1, source_target_pairs={{0,24},{8,16},{16,8},{24,0},{1,25},{9,17},{17,9},{25,1},{2,26},{10... | collective-permute-start | bytes 393224 | tf_op jit(solution)/shard_map/ppermute | solution.py:27
  45.9 2.8 %collective-permute-done.15 = bf16[16,4096]{1,0:T(8,128)(2,1)S(1)} collective-permute-done((bf16[16,4096]{1,0:T(8,128)(2,1)S(1)}, bf16[16,4096]{1,0:T(8,128)(2,1)S(1)}, u32[]{:S(2)}, u32[]{:S(2)}) %collective-permute-start.15) | collective-permute-done | bytes 131104 | tf_op jit(solution)/shard_map/ppermute | solution.py:27
  48.7 2.5 %collective-permute-done.17 = bf16[16,4096]{1,0:T(8,128)(2,1)S(1)} collective-permute-done((bf16[16,4096]{1,0:T(8,128)(2,1)S(1)}, bf16[16,4096]{1,0:T(8,128)(2,1)S(1)}, u32[]{:S(2)}, u32[]{:S(2)}) %collective-permute-start.17) | collective-permute-done | bytes 131104 | tf_op jit(solution)/shard_map/ppermute | solution.py:27
  51.3 2.4 %collective-permute-start.18 = (bf16[8,4096]{1,0:T(8,128)(2,1)S(1)}, bf16[8,4096]{1,0:T(8,128)(2,1)S(1)}, u32[]{:S(2)}, u32[]{:S(2)}) collective-permute-start(bf16[8,4096]{1,0:T(8,128)(2,1)S(1)} %slice.80), channel_id=1, source_target_pairs={{0,4},{1,5},{2,6},{3,7},{4,0},{5,1},{6,2},{7,3},{8,12},{9,13},{10,... | collective-permute-start | bytes 196616 | tf_op jit(solution)/shard_map/ppermute | solution.py:27
  53.7 3.5 %collective-permute-done.18 = bf16[8,4096]{1,0:T(8,128)(2,1)S(1)} collective-permute-done((bf16[8,4096]{1,0:T(8,128)(2,1)S(1)}, bf16[8,4096]{1,0:T(8,128)(2,1)S(1)}, u32[]{:S(2)}, u32[]{:S(2)}) %collective-permute-start.18) | collective-permute-done | bytes 65568 | tf_op jit(solution)/shard_map/ppermute | solution.py:27
  57.2 0.6 %fusion.6 = bf16[8,4096]{1,0:T(8,128)(2,1)} fusion(f32[16,4096]{1,0:T(8,128)S(1)} %fusion.4, bf16[8,4096]{1,0:T(8,128)(2,1)S(1)} %collective-permute-done.18), kind=kLoop, calls=%fused_computation.17 | loop fusion | flops 98304 | bytes 262144 | tf_op jit(solution)/shard_map/convert_element_type | solution.py:300
  (8 shorter events, 0.2 us)
Async XLA Ops:
  1.0 7.8 %collective-permute-start = (bf16[8,4224]{1,0:T(8,128)(2,1)S(1)}, bf16[8,4224]{1,0:T(8,128)(2,1)S(1)}, u32[]{:S(2)}, u32[]{:S(2)}) collective-permute-start(bf16[8,4224]{1,0:T(8,128)(2,1)S(1)} %shard_map.55.first_ref), channel_id=1, source_target_pairs={{0,4},{1,5},{2,6},{3,7},{4,0},{5,1},{6,2},{7,3},{8,12},{9,13},{10,... | collective-permute-start | bytes 202760 | tf_op jit(solution)/shard_map/ppermute | solution.py:27
  8.8 6.4 %collective-permute-start.2 = (bf16[16,4224]{1,0:T(8,128)(2,1)S(1)}, bf16[16,4224]{1,0:T(8,128)(2,1)S(1)}, u32[]{:S(2)}, u32[]{:S(2)}) collective-permute-start(bf16[16,4224]{1,0:T(8,128)(2,1)S(1)} %get-tuple-element.37.first_ref), channel_id=1, source_target_pairs={{0,2},{1,3},{2,0},{3,1},{4,6},{5,7},{6,4},{7,5},{8,10},{9,11},{10,... | collective-permute-start | bytes 405512 | tf_op jit(solution)/shard_map/ppermute | solution.py:27
  9.6 5.9 %collective-permute-start.1 = (bf16[16,4224]{1,0:T(8,128)(2,1)S(1)}, bf16[16,4224]{1,0:T(8,128)(2,1)S(1)}, u32[]{:S(2)}, u32[]{:S(2)}) collective-permute-start(bf16[16,4224]{1,0:T(8,128)(2,1)S(1)} %get-tuple-element.37.first_ref), channel_id=1, source_target_pairs={{0,24},{8,16},{16,8},{24,0},{1,25},{9,17},{17,9},{25,1},{2,26},{10... | collective-permute-start | bytes 405512 | tf_op jit(solution)/shard_map/ppermute | solution.py:27
  15.6 8.1 %collective-permute-start.4 = (bf16[32,4224]{1,0:T(8,128)(2,1)S(1)}, bf16[32,4224]{1,0:T(8,128)(2,1)S(1)}, u32[]{:S(2)}, u32[]{:S(2)}) collective-permute-start(bf16[32,4224]{1,0:T(8,128)(2,1)S(1)} %get-tuple-element.44.refs_3_), channel_id=1, source_target_pairs={{0,16},{8,24},{16,0},{24,8},{1,17},{9,25},{17,1},{25,9},{2,18},{10... | collective-permute-start | bytes 811016 | tf_op jit(solution)/shard_map/ppermute | solution.py:27
  17.2 6.5 %collective-permute-start.3 = (bf16[32,4224]{1,0:T(8,128)(2,1)S(1)}, bf16[32,4224]{1,0:T(8,128)(2,1)S(1)}, u32[]{:S(2)}, u32[]{:S(2)}) collective-permute-start(bf16[32,4224]{1,0:T(8,128)(2,1)S(1)} %get-tuple-element.44.refs_3_), channel_id=1, source_target_pairs={{0,8},{8,0},{16,24},{24,16},{1,9},{9,1},{17,25},{25,17},{2,10},{10... | collective-permute-start | bytes 811016 | tf_op jit(solution)/shard_map/ppermute | solution.py:27
  18.7 5.0 %collective-permute-start.5 = (bf16[16,4224]{1,0:T(8,128)(2,1)S(1)}, bf16[16,4224]{1,0:T(8,128)(2,1)S(1)}, u32[]{:S(2)}, u32[]{:S(2)}) collective-permute-start(bf16[16,4224]{1,0:T(8,128)(2,1)S(1)} %collective-permute-done.1.refs_4_), channel_id=1, source_target_pairs={{0,2},{1,3},{2,0},{3,1},{4,6},{5,7},{6,4},{7,5},{8,10},{9,11},{10,... | collective-permute-start | bytes 405512 | tf_op jit(solution)/shard_map/ppermute | solution.py:27
  20.2 5.6 %collective-permute-start.8 = (bf16[32,4224]{1,0:T(8,128)(2,1)S(1)}, bf16[32,4224]{1,0:T(8,128)(2,1)S(1)}, u32[]{:S(2)}, u32[]{:S(2)}) collective-permute-start(bf16[32,4224]{1,0:T(8,128)(2,1)S(1)} %get-tuple-element.44.refs_3_), channel_id=1, source_target_pairs={{0,1},{1,0},{2,3},{3,2},{4,5},{5,4},{6,7},{7,6},{8,9},{9,8},{10,11... | collective-permute-start | bytes 811016 | tf_op jit(solution)/shard_map/ppermute | solution.py:27
  23.7 2.3 %collective-permute-start.6 = (bf16[32,4224]{1,0:T(8,128)(2,1)S(1)}, bf16[32,4224]{1,0:T(8,128)(2,1)S(1)}, u32[]{:S(2)}, u32[]{:S(2)}) collective-permute-start(bf16[32,4224]{1,0:T(8,128)(2,1)S(1)} %collective-permute-done.3.refs_1_), channel_id=1, source_target_pairs={{0,1},{1,0},{2,3},{3,2},{4,5},{5,4},{6,7},{7,6},{8,9},{9,8},{10,11... | collective-permute-start | bytes 811016 | tf_op jit(solution)/shard_map/ppermute | solution.py:27
  23.9 2.1 %collective-permute-start.7 = (bf16[32,4224]{1,0:T(8,128)(2,1)S(1)}, bf16[32,4224]{1,0:T(8,128)(2,1)S(1)}, u32[]{:S(2)}, u32[]{:S(2)}) collective-permute-start(bf16[32,4224]{1,0:T(8,128)(2,1)S(1)} %collective-permute-done.4.refs_2_), channel_id=1, source_target_pairs={{0,1},{1,0},{2,3},{3,2},{4,5},{5,4},{6,7},{7,6},{8,9},{9,8},{10,11... | collective-permute-start | bytes 811016 | tf_op jit(solution)/shard_map/ppermute | solution.py:27
  24.2 1.6 %collective-permute-start.9 = (bf16[16,4224]{1,0:T(8,128)(2,1)S(1)}, bf16[16,4224]{1,0:T(8,128)(2,1)S(1)}, u32[]{:S(2)}, u32[]{:S(2)}) collective-permute-start(bf16[16,4224]{1,0:T(8,128)(2,1)S(1)} %collective-permute-done.1.refs_4_), channel_id=1, source_target_pairs={{0,1},{1,0},{2,3},{3,2},{4,5},{5,4},{6,7},{7,6},{8,9},{9,8},{10,11... | collective-permute-start | bytes 405512 | tf_op jit(solution)/shard_map/ppermute | solution.py:27
  24.5 1.5 %collective-permute-start.10 = (bf16[16,4224]{1,0:T(8,128)(2,1)S(1)}, bf16[16,4224]{1,0:T(8,128)(2,1)S(1)}, u32[]{:S(2)}, u32[]{:S(2)}) collective-permute-start(bf16[16,4224]{1,0:T(8,128)(2,1)S(1)} %collective-permute-done.5.refs_5_), channel_id=1, source_target_pairs={{0,1},{1,0},{2,3},{3,2},{4,5},{5,4},{6,7},{7,6},{8,9},{9,8},{10,11... | collective-permute-start | bytes 405512 | tf_op jit(solution)/shard_map/ppermute | solution.py:27
  31.5 2.0 %collective-permute-start.11 = (bf16[2,32,4096]{2,1,0:T(8,128)(2,1)S(1)}, bf16[2,32,4096]{2,1,0:T(8,128)(2,1)S(1)}, u32[]{:S(2)}, u32[]{:S(2)}) collective-permute-start(bf16[2,32,4096]{2,1,0:T(8,128)(2,1)S(1)} %get-tuple-element.54), channel_id=1, source_target_pairs={{0,1},{1,0},{2,3},{3,2},{4,5},{5,4},{6,7},{7,6},{8,9},{9,8},{10,11... | collective-permute-start | bytes 1572872 | tf_op jit(solution)/shard_map/ppermute | solution.py:27
  33.4 2.3 %collective-permute-start.12 = (bf16[2,32,4096]{2,1,0:T(8,128)(2,1)S(1)}, bf16[2,32,4096]{2,1,0:T(8,128)(2,1)S(1)}, u32[]{:S(2)}, u32[]{:S(2)}) collective-permute-start(bf16[2,32,4096]{2,1,0:T(8,128)(2,1)S(1)} %get-tuple-element.56), channel_id=1, source_target_pairs={{0,1},{1,0},{2,3},{3,2},{4,5},{5,4},{6,7},{7,6},{8,9},{9,8},{10,11... | collective-permute-start | bytes 1572872 | tf_op jit(solution)/shard_map/ppermute | solution.py:27
  33.9 8.5 %collective-permute-start.13 = (bf16[32,4096]{1,0:T(8,128)(2,1)S(1)}, bf16[32,4096]{1,0:T(8,128)(2,1)S(1)}, u32[]{:S(2)}, u32[]{:S(2)}) collective-permute-start(bf16[32,4096]{1,0:T(8,128)(2,1)S(1)} %get-tuple-element.59), channel_id=1, source_target_pairs={{0,8},{8,0},{16,24},{24,16},{1,9},{9,1},{17,25},{25,17},{2,10},{10... | collective-permute-start | bytes 786440 | tf_op jit(solution)/shard_map/ppermute | solution.py:27
  35.3 8.3 %collective-permute-start.14 = (bf16[32,4096]{1,0:T(8,128)(2,1)S(1)}, bf16[32,4096]{1,0:T(8,128)(2,1)S(1)}, u32[]{:S(2)}, u32[]{:S(2)}) collective-permute-start(bf16[32,4096]{1,0:T(8,128)(2,1)S(1)} %get-tuple-element.60), channel_id=1, source_target_pairs={{0,16},{8,24},{16,0},{24,8},{1,17},{9,25},{17,1},{25,9},{2,18},{10... | collective-permute-start | bytes 786440 | tf_op jit(solution)/shard_map/ppermute | solution.py:27
  35.9 9.3 %collective-permute-start.16 = (bf16[16,4096]{1,0:T(8,128)(2,1)S(1)}, bf16[16,4096]{1,0:T(8,128)(2,1)S(1)}, u32[]{:S(2)}, u32[]{:S(2)}) collective-permute-start(bf16[16,4096]{1,0:T(8,128)(2,1)S(1)} %fusion.5), channel_id=1, source_target_pairs={{0,2},{1,3},{2,0},{3,1},{4,6},{5,7},{6,4},{7,5},{8,10},{9,11},{10,... | collective-permute-start | bytes 393224 | tf_op jit(solution)/shard_map/ppermute | solution.py:27
  43.7 5.0 %collective-permute-start.15 = (bf16[16,4096]{1,0:T(8,128)(2,1)S(1)}, bf16[16,4096]{1,0:T(8,128)(2,1)S(1)}, u32[]{:S(2)}, u32[]{:S(2)}) collective-permute-start(bf16[16,4096]{1,0:T(8,128)(2,1)S(1)} %slice.79), channel_id=1, source_target_pairs={{0,2},{1,3},{2,0},{3,1},{4,6},{5,7},{6,4},{7,5},{8,10},{9,11},{10,... | collective-permute-start | bytes 393224 | tf_op jit(solution)/shard_map/ppermute | solution.py:27
  45.3 5.9 %collective-permute-start.17 = (bf16[16,4096]{1,0:T(8,128)(2,1)S(1)}, bf16[16,4096]{1,0:T(8,128)(2,1)S(1)}, u32[]{:S(2)}, u32[]{:S(2)}) collective-permute-start(bf16[16,4096]{1,0:T(8,128)(2,1)S(1)} %fusion.3), channel_id=1, source_target_pairs={{0,24},{8,16},{16,8},{24,0},{1,25},{9,17},{17,9},{25,1},{2,26},{10... | collective-permute-start | bytes 393224 | tf_op jit(solution)/shard_map/ppermute | solution.py:27
  51.3 5.9 %collective-permute-start.18 = (bf16[8,4096]{1,0:T(8,128)(2,1)S(1)}, bf16[8,4096]{1,0:T(8,128)(2,1)S(1)}, u32[]{:S(2)}, u32[]{:S(2)}) collective-permute-start(bf16[8,4096]{1,0:T(8,128)(2,1)S(1)} %slice.80), channel_id=1, source_target_pairs={{0,4},{1,5},{2,6},{3,7},{4,0},{5,1},{6,2},{7,3},{8,12},{9,13},{10,... | collective-permute-start | bytes 196616 | tf_op jit(solution)/shard_map/ppermute | solution.py:27

commit v10 on v7

--- a/solution.py
+++ b/solution.py
@@ -279,16 +279,28 @@
     send, total = run_experts(group, blocks, low, high, wout, exp_dev, experts)
     total = total + swap(send, "expert", 1).astype(jnp.float32)
     size = total.shape[0] // planes
+    half = size // 2
     rounded = total.astype(jnp.bfloat16)
-    mine = total[:size]
-    for b in range(1, far):
-        piece = rounded[b * size : (b + 1) * size]
-        mine = mine + swap(piece, "batch", b).astype(jnp.float32)
-    across = total[far * size :]
-    for stride in reversed(strides):
+    starts = [b * size for b in range(1, far)]
+    onward = [
+        swap(rounded[start + half : start + size], "batch", b)
+        for b, start in zip(range(1, far), starts)
+    ]
+    across = halve(total[far * size :], strides[-1])
+    onward, staying = lax.optimization_barrier(
+        (onward, [rounded[start : start + half] for start in starts])
+    )
+    sent = total[half:size]
+    for rows in onward:
+        sent = sent + rows.astype(jnp.float32)
+    mine = total[:half]
+    for b, rows in zip(range(1, far), staying):
+        mine = mine + swap(rows, "batch", b).astype(jnp.float32)
+    mine = mine + swap(sent.astype(jnp.bfloat16), "expert", strides[-1]).astype(jnp.float32)
+    for stride in reversed(strides[:-1]):
         across = halve(across, stride)
     across = swap(across.astype(jnp.bfloat16), "batch", far).astype(jnp.float32)
-    for stride in reversed(strides):
+    for stride in reversed(strides[:-1]):
         mine = halve(mine, stride)
     mine = mine + across
     return mine.astype(jnp.bfloat16)

time: 57.5 us -> 58.9 us (1.024)
  waiting for transfers between devices: 15.8 us -> 17 us
    ppermute x19 -> x21, waiting for transfers between devices: 15.8 us -> 17 us  [swap(): return lax.ppermute(block, axis, [(i, i ^ flips) for i in range(size)])]
    ppermute x19 -> x21, starting transfers between devices: 24.4 us -> 24.7 us  [swap(): return lax.ppermute(block, axis, [(i, i ^ flips) for i in range(size)])]
  transfers between devices with their start and end apart: 19 -> 21, of which waited for: 11 -> 14; matrix products, arithmetic and copies ran while one was open for 0% -> 0% of each run, Pallas kernels for 16% -> 16%
where the time goes in v10:
time: 58.9 us; the launch traced here: 58.8 us
  starting transfers between devices  24.7 us (42%)
  waiting for transfers between devices  17 us (29%)
  Pallas kernels  15.6 us (26%)
  other arithmetic  1.2 us (2%)
    ppermute x21, starting transfers between devices, swap(): return lax.ppermute(block, axis, [(i, i ^ flips) for i in range(size)])  24.7 us
    ppermute x21, waiting for transfers between devices, swap(): return lax.ppermute(block, axis, [(i, i ^ flips) for i in range(size)])  17 us
    pallas_call x3, Pallas kernels, load(): pl.pallas_call(kernel, out_shape=pltpu.VMEM(shape, source.dtype), in_spec...  9.16 us
    pallas_call x1, Pallas kernels, run_experts(): pl.pallas_call(functools.partial(expert_kernel, exp_dev, experts, count),...  5.44 us
  transfers between devices with their start and end apart: 21, of which 14 were waited for; matrix products, arithmetic and copies ran while one was open for 0% of the time, Pallas kernels for 16%

profile of v10, /device:TPU:0, one launch (start us, length us, event | category | flops | bytes accessed | tf_op | source)
XLA Modules:
  0.0 58.8 jit_solution(10471905876970125600)
XLA Ops:
  0.0 1.0 %shard_map.55.first_ref = bf16[8,4224]{1,0:T(8,128)(2,1)S(1)} custom-call(bf16[8,4096]{1,0:T(8,128)(2,1)} %tokens_hbm.1, s32[8,8]{1,0:T(8,128)} %ids_hbm.1, f32[8,8]{1,0:T(8,128)} %weights_hbm.1), custom_call_target="tpu_custom_call" | custom-call | tf_op jit(solution)/shard_map/pallas_call | solution.py:63
  1.0 4.1 %collective-permute-start = (bf16[8,4224]{1,0:T(8,128)(2,1)S(1)}, bf16[8,4224]{1,0:T(8,128)(2,1)S(1)}, u32[]{:S(2)}, u32[]{:S(2)}) collective-permute-start(bf16[8,4224]{1,0:T(8,128)(2,1)S(1)} %shard_map.55.first_ref), channel_id=1, source_target_pairs={{0,4},{1,5},{2,6},{3,7},{4,0},{5,1},{6,2},{7,3},{8,12},{9,13},{10,... | collective-permute-start | bytes 202760 | tf_op jit(solution)/shard_map/ppermute | solution.py:27
  5.1 2.9 %shard_map.56.refs_0_ = bf16[768,4096]{1,0:T(8,128)(2,1)S(1)} custom-call(bf16[768,4096]{1,0:T(8,128)(2,1)} %bitcast.14), custom_call_target="tpu_custom_call" | custom-call | bytes 12582912 | tf_op jit(solution)/shard_map/pallas_call | solution.py:124
  8.0 0.9 %collective-permute-done.second_ref = bf16[8,4224]{1,0:T(8,128)(2,1)S(1)} collective-permute-done((bf16[8,4224]{1,0:T(8,128)(2,1)S(1)}, bf16[8,4224]{1,0:T(8,128)(2,1)S(1)}, u32[]{:S(2)}, u32[]{:S(2)}) %collective-permute-start) | collective-permute-done | bytes 67616 | tf_op jit(solution)/shard_map/ppermute | solution.py:27
  8.8 0.8 %collective-permute-start.2 = (bf16[16,4224]{1,0:T(8,128)(2,1)S(1)}, bf16[16,4224]{1,0:T(8,128)(2,1)S(1)}, u32[]{:S(2)}, u32[]{:S(2)}) collective-permute-start(bf16[16,4224]{1,0:T(8,128)(2,1)S(1)} %get-tuple-element.37.first_ref), channel_id=1, source_target_pairs={{0,2},{1,3},{2,0},{3,1},{4,6},{5,7},{6,4},{7,5},{8,10},{9,11},{10,... | collective-permute-start | bytes 405512 | tf_op jit(solution)/shard_map/ppermute | solution.py:27
  9.6 2.4 %collective-permute-start.1 = (bf16[16,4224]{1,0:T(8,128)(2,1)S(1)}, bf16[16,4224]{1,0:T(8,128)(2,1)S(1)}, u32[]{:S(2)}, u32[]{:S(2)}) collective-permute-start(bf16[16,4224]{1,0:T(8,128)(2,1)S(1)} %get-tuple-element.37.first_ref), channel_id=1, source_target_pairs={{0,24},{8,16},{16,8},{24,0},{1,25},{9,17},{17,9},{25,1},{2,26},{10... | collective-permute-start | bytes 405512 | tf_op jit(solution)/shard_map/ppermute | solution.py:27
  12.1 3.2 %shard_map.58 = bf16[16,768,2,128]{3,2,1,0:T(2,128)(2,1)S(1)} custom-call(bf16[768,2,4096]{2,1,0:T(2,128)(2,1)} %bitcast.12), custom_call_target="tpu_custom_call" | custom-call | bytes 12582912 | tf_op jit(solution)/shard_map/pallas_call | solution.py:124
  15.3 0.0 collective-permute-done.2.second_ref
  15.3 0.3 collective-permute-done.1.refs_4_
  15.6 1.6 %collective-permute-start.4 = (bf16[32,4224]{1,0:T(8,128)(2,1)S(1)}, bf16[32,4224]{1,0:T(8,128)(2,1)S(1)}, u32[]{:S(2)}, u32[]{:S(2)}) collective-permute-start(bf16[32,4224]{1,0:T(8,128)(2,1)S(1)} %get-tuple-element.44.refs_1_), channel_id=1, source_target_pairs={{0,16},{8,24},{16,0},{24,8},{1,17},{9,25},{17,1},{25,9},{2,18},{10... | collective-permute-start | bytes 811016 | tf_op jit(solution)/shard_map/ppermute | solution.py:27
  17.2 1.5 %collective-permute-start.3 = (bf16[32,4224]{1,0:T(8,128)(2,1)S(1)}, bf16[32,4224]{1,0:T(8,128)(2,1)S(1)}, u32[]{:S(2)}, u32[]{:S(2)}) collective-permute-start(bf16[32,4224]{1,0:T(8,128)(2,1)S(1)} %get-tuple-element.44.refs_1_), channel_id=1, source_target_pairs={{0,8},{8,0},{16,24},{24,16},{1,9},{9,1},{17,25},{25,17},{2,10},{10... | collective-permute-start | bytes 811016 | tf_op jit(solution)/shard_map/ppermute | solution.py:27
  18.7 1.5 %collective-permute-start.5 = (bf16[16,4224]{1,0:T(8,128)(2,1)S(1)}, bf16[16,4224]{1,0:T(8,128)(2,1)S(1)}, u32[]{:S(2)}, u32[]{:S(2)}) collective-permute-start(bf16[16,4224]{1,0:T(8,128)(2,1)S(1)} %collective-permute-done.1.refs_4_), channel_id=1, source_target_pairs={{0,2},{1,3},{2,0},{3,1},{4,6},{5,7},{6,4},{7,5},{8,10},{9,11},{10,... | collective-permute-start | bytes 405512 | tf_op jit(solution)/shard_map/ppermute | solution.py:27
  20.2 0.0 collective-permute-start.6
  20.2 3.2 %shard_map.60 = bf16[16,768,2,128]{3,2,1,0:T(2,128)(2,1)S(1)} custom-call(bf16[768,2,4096]{2,1,0:T(2,128)(2,1)} %bitcast.13), custom_call_target="tpu_custom_call" | custom-call | bytes 12582912 | tf_op jit(solution)/shard_map/pallas_call | solution.py:124
  23.3 0.3 collective-permute-done.5.refs_5_
  23.7 0.0 collective-permute-done.4.refs_3_
  23.7 0.0 collective-permute-done.3.refs_2_
  23.7 0.3 collective-permute-start.7
  23.9 0.2 collective-permute-start.8
  24.2 0.3 collective-permute-start.9
  24.5 0.2 collective-permute-start.10
  24.7 1.1 %collective-permute-done.9.refs_9_ = bf16[16,4224]{1,0:T(8,128)(2,1)S(1)} collective-permute-done((bf16[16,4224]{1,0:T(8,128)(2,1)S(1)}, bf16[16,4224]{1,0:T(8,128)(2,1)S(1)}, u32[]{:S(2)}, u32[]{:S(2)}) %collective-permute-start.9) | collective-permute-done | bytes 135200 | tf_op jit(solution)/shard_map/ppermute | solution.py:27
  25.8 0.0 collective-permute-done.6.refs_6_
  25.8 0.2 collective-permute-done.10.refs_10_
  26.0 0.0 collective-permute-done.7.refs_7_
  26.0 0.0 collective-permute-done.8.refs_8_
  26.0 5.4 %shard_map.61 = (bf16[1,128,4096]{2,1,0:T(8,128)(2,1)S(1)}, f32[1,128,4096]{2,1,0:T(8,128)S(1)}) custom-call(s32[1]{0:T(128)} %bitcast.refs_0_, bf16[32,4224]{1,0:T(8,128)(2,1)S(1)} %get-tuple-element.44.refs_1_, bf16[32,4224]{1,0:T(8,128)(2,1)S(1)} %collective-permute-done.3.refs_2_, bf16[32,4224]{1,0:T(8,128)(2,1)S(1)} %collective-permute-done.4.refs_3_, ...), custom_call_target="tpu_custom_call" | custom-call | flops 4831838208 | bytes 5308416 | tf_op jit(solution)/shard_map/pallas_call | solution.py:211
  31.4 0.3 collective-permute-start.11
  31.8 2.4 %collective-permute-done.11 = bf16[128,4096]{1,0:T(8,128)(2,1)S(1)} collective-permute-done((bf16[128,4096]{1,0:T(8,128)(2,1)S(1)}, bf16[128,4096]{1,0:T(8,128)(2,1)S(1)}, u32[]{:S(2)}, u32[]{:S(2)}) %collective-permute-start.11) | collective-permute-done | bytes 1048608 | tf_op jit(solution)/shard_map/ppermute | solution.py:27
  34.2 0.4 fusion.7
  34.6 0.9 %collective-permute-start.13 = (bf16[16,4096]{1,0:T(8,128)(2,1)S(1)}, bf16[16,4096]{1,0:T(8,128)(2,1)S(1)}, u32[]{:S(2)}, u32[]{:S(2)}) collective-permute-start(bf16[16,4096]{1,0:T(8,128)(2,1)S(1)} %get-tuple-element.66), channel_id=1, source_target_pairs={{0,16},{8,24},{16,0},{24,8},{1,17},{9,25},{17,1},{25,9},{2,18},{10... | collective-permute-start | bytes 393224 | tf_op jit(solution)/shard_map/ppermute | solution.py:27
  35.5 1.1 %collective-permute-start.12 = (bf16[16,4096]{1,0:T(8,128)(2,1)S(1)}, bf16[16,4096]{1,0:T(8,128)(2,1)S(1)}, u32[]{:S(2)}, u32[]{:S(2)}) collective-permute-start(bf16[16,4096]{1,0:T(8,128)(2,1)S(1)} %get-tuple-element.67), channel_id=1, source_target_pairs={{0,8},{8,0},{16,24},{24,16},{1,9},{9,1},{17,25},{25,17},{2,10},{10... | collective-permute-start | bytes 393224 | tf_op jit(solution)/shard_map/ppermute | solution.py:27
  36.6 1.5 %collective-permute-start.18 = (bf16[16,4096]{1,0:T(8,128)(2,1)S(1)}, bf16[16,4096]{1,0:T(8,128)(2,1)S(1)}, u32[]{:S(2)}, u32[]{:S(2)}) collective-permute-start(bf16[16,4096]{1,0:T(8,128)(2,1)S(1)} %get-tuple-element.63), channel_id=1, source_target_pairs={{0,2},{1,3},{2,0},{3,1},{4,6},{5,7},{6,4},{7,5},{8,10},{9,11},{10,... | collective-permute-start | bytes 393224 | tf_op jit(solution)/shard_map/ppermute | solution.py:27
  38.1 2.2 %collective-permute-done.13 = bf16[16,4096]{1,0:T(8,128)(2,1)S(1)} collective-permute-done((bf16[16,4096]{1,0:T(8,128)(2,1)S(1)}, bf16[16,4096]{1,0:T(8,128)(2,1)S(1)}, u32[]{:S(2)}, u32[]{:S(2)}) %collective-permute-start.13) | collective-permute-done | bytes 131104 | tf_op jit(solution)/shard_map/ppermute | solution.py:27
  40.3 0.4 collective-permute-done.12
  40.8 0.9 %collective-permute-done.18 = bf16[16,4096]{1,0:T(8,128)(2,1)S(1)} collective-permute-done((bf16[16,4096]{1,0:T(8,128)(2,1)S(1)}, bf16[16,4096]{1,0:T(8,128)(2,1)S(1)}, u32[]{:S(2)}, u32[]{:S(2)}) %collective-permute-start.18) | collective-permute-done | bytes 131104 | tf_op jit(solution)/shard_map/ppermute | solution.py:27
  41.6 0.1 slice_add_fusion
  41.7 3.3 %collective-permute-start.19 = (bf16[8,4096]{1,0:T(8,128)(2,1)S(1)}, bf16[8,4096]{1,0:T(8,128)(2,1)S(1)}, u32[]{:S(2)}, u32[]{:S(2)}) collective-permute-start(bf16[8,4096]{1,0:T(8,128)(2,1)S(1)} %slice.87), channel_id=1, source_target_pairs={{0,4},{1,5},{2,6},{3,7},{4,0},{5,1},{6,2},{7,3},{8,12},{9,13},{10,... | collective-permute-start | bytes 196616 | tf_op jit(solution)/shard_map/ppermute | solution.py:27
  45.0 1.0 %collective-permute-start.14 = (bf16[16,4096]{1,0:T(8,128)(2,1)S(1)}, bf16[16,4096]{1,0:T(8,128)(2,1)S(1)}, u32[]{:S(2)}, u32[]{:S(2)}) collective-permute-start(bf16[16,4096]{1,0:T(8,128)(2,1)S(1)} %get-tuple-element.55), channel_id=1, source_target_pairs={{0,8},{8,0},{16,24},{24,16},{1,9},{9,1},{17,25},{25,17},{2,10},{10... | collective-permute-start | bytes 393224 | tf_op jit(solution)/shard_map/ppermute | solution.py:27
  46.0 1.1 %collective-permute-start.15 = (bf16[16,4096]{1,0:T(8,128)(2,1)S(1)}, bf16[16,4096]{1,0:T(8,128)(2,1)S(1)}, u32[]{:S(2)}, u32[]{:S(2)}) collective-permute-start(bf16[16,4096]{1,0:T(8,128)(2,1)S(1)} %get-tuple-element.56), channel_id=1, source_target_pairs={{0,16},{8,24},{16,0},{24,8},{1,17},{9,25},{17,1},{25,9},{2,18},{10... | collective-permute-start | bytes 393224 | tf_op jit(solution)/shard_map/ppermute | solution.py:27
  47.1 0.6 %collective-permute-start.16 = (bf16[16,4096]{1,0:T(8,128)(2,1)S(1)}, bf16[16,4096]{1,0:T(8,128)(2,1)S(1)}, u32[]{:S(2)}, u32[]{:S(2)}) collective-permute-start(bf16[16,4096]{1,0:T(8,128)(2,1)S(1)} %get-tuple-element.62), channel_id=1, source_target_pairs={{0,2},{1,3},{2,0},{3,1},{4,6},{5,7},{6,4},{7,5},{8,10},{9,11},{10,... | collective-permute-start | bytes 393224 | tf_op jit(solution)/shard_map/ppermute | solution.py:27
  47.8 0.0 collective-permute-done.19
  47.8 1.5 %collective-permute-start.20 = (bf16[8,4096]{1,0:T(8,128)(2,1)S(1)}, bf16[8,4096]{1,0:T(8,128)(2,1)S(1)}, u32[]{:S(2)}, u32[]{:S(2)}) collective-permute-start(bf16[8,4096]{1,0:T(8,128)(2,1)S(1)} %fusion.4), channel_id=1, source_target_pairs={{0,24},{8,16},{16,8},{24,0},{1,25},{9,17},{17,9},{25,1},{2,26},{10... | collective-permute-start | bytes 196616 | tf_op jit(solution)/shard_map/ppermute | solution.py:27
  49.3 1.3 %collective-permute-done.14 = bf16[16,4096]{1,0:T(8,128)(2,1)S(1)} collective-permute-done((bf16[16,4096]{1,0:T(8,128)(2,1)S(1)}, bf16[16,4096]{1,0:T(8,128)(2,1)S(1)}, u32[]{:S(2)}, u32[]{:S(2)}) %collective-permute-start.14) | collective-permute-done | bytes 131104 | tf_op jit(solution)/shard_map/ppermute | solution.py:27
  50.5 1.0 %collective-permute-done.15 = bf16[16,4096]{1,0:T(8,128)(2,1)S(1)} collective-permute-done((bf16[16,4096]{1,0:T(8,128)(2,1)S(1)}, bf16[16,4096]{1,0:T(8,128)(2,1)S(1)}, u32[]{:S(2)}, u32[]{:S(2)}) %collective-permute-start.15) | collective-permute-done | bytes 131104 | tf_op jit(solution)/shard_map/ppermute | solution.py:27
  51.5 0.6 collective-permute-done.16
  52.1 0.1 fusion.3
  52.2 0.4 collective-permute-start.17
  52.6 0.4 collective-permute-done.20
  53.0 5.1 %collective-permute-done.17 = bf16[8,4096]{1,0:T(8,128)(2,1)S(1)} collective-permute-done((bf16[8,4096]{1,0:T(8,128)(2,1)S(1)}, bf16[8,4096]{1,0:T(8,128)(2,1)S(1)}, u32[]{:S(2)}, u32[]{:S(2)}) %collective-permute-start.17) | collective-permute-done | bytes 65568 | tf_op jit(solution)/shard_map/ppermute | solution.py:27
  58.1 0.7 %fusion.6 = bf16[8,4096]{1,0:T(8,128)(2,1)} fusion(f32[16,4096]{1,0:T(8,128)S(1)} %fusion.3, bf16[8,4096]{1,0:T(8,128)(2,1)S(1)} %collective-permute-done.20, bf16[8,4096]{1,0:T(8,128)(2,1)S(1)} %collective-permute-done.17), kind=kLoop, calls=%fused_computation.14 | loop fusion | flops 163840 | bytes 327680 | tf_op jit(solution)/shard_map/convert_element_type | solution.py:306
  (6 shorter events, 0.1 us)
Async XLA Ops:
  1.0 7.8 %collective-permute-start = (bf16[8,4224]{1,0:T(8,128)(2,1)S(1)}, bf16[8,4224]{1,0:T(8,128)(2,1)S(1)}, u32[]{:S(2)}, u32[]{:S(2)}) collective-permute-start(bf16[8,4224]{1,0:T(8,128)(2,1)S(1)} %shard_map.55.first_ref), channel_id=1, source_target_pairs={{0,4},{1,5},{2,6},{3,7},{4,0},{5,1},{6,2},{7,3},{8,12},{9,13},{10,... | collective-permute-start | bytes 202760 | tf_op jit(solution)/shard_map/ppermute | solution.py:27
  8.8 6.4 %collective-permute-start.2 = (bf16[16,4224]{1,0:T(8,128)(2,1)S(1)}, bf16[16,4224]{1,0:T(8,128)(2,1)S(1)}, u32[]{:S(2)}, u32[]{:S(2)}) collective-permute-start(bf16[16,4224]{1,0:T(8,128)(2,1)S(1)} %get-tuple-element.37.first_ref), channel_id=1, source_target_pairs={{0,2},{1,3},{2,0},{3,1},{4,6},{5,7},{6,4},{7,5},{8,10},{9,11},{10,... | collective-permute-start | bytes 405512 | tf_op jit(solution)/shard_map/ppermute | solution.py:27
  9.6 5.9 %collective-permute-start.1 = (bf16[16,4224]{1,0:T(8,128)(2,1)S(1)}, bf16[16,4224]{1,0:T(8,128)(2,1)S(1)}, u32[]{:S(2)}, u32[]{:S(2)}) collective-permute-start(bf16[16,4224]{1,0:T(8,128)(2,1)S(1)} %get-tuple-element.37.first_ref), channel_id=1, source_target_pairs={{0,24},{8,16},{16,8},{24,0},{1,25},{9,17},{17,9},{25,1},{2,26},{10... | collective-permute-start | bytes 405512 | tf_op jit(solution)/shard_map/ppermute | solution.py:27
  15.6 8.1 %collective-permute-start.4 = (bf16[32,4224]{1,0:T(8,128)(2,1)S(1)}, bf16[32,4224]{1,0:T(8,128)(2,1)S(1)}, u32[]{:S(2)}, u32[]{:S(2)}) collective-permute-start(bf16[32,4224]{1,0:T(8,128)(2,1)S(1)} %get-tuple-element.44.refs_1_), channel_id=1, source_target_pairs={{0,16},{8,24},{16,0},{24,8},{1,17},{9,25},{17,1},{25,9},{2,18},{10... | collective-permute-start | bytes 811016 | tf_op jit(solution)/shard_map/ppermute | solution.py:27
  17.2 6.5 %collective-permute-start.3 = (bf16[32,4224]{1,0:T(8,128)(2,1)S(1)}, bf16[32,4224]{1,0:T(8,128)(2,1)S(1)}, u32[]{:S(2)}, u32[]{:S(2)}) collective-permute-start(bf16[32,4224]{1,0:T(8,128)(2,1)S(1)} %get-tuple-element.44.refs_1_), channel_id=1, source_target_pairs={{0,8},{8,0},{16,24},{24,16},{1,9},{9,1},{17,25},{25,17},{2,10},{10... | collective-permute-start | bytes 811016 | tf_op jit(solution)/shard_map/ppermute | solution.py:27
  18.7 5.0 %collective-permute-start.5 = (bf16[16,4224]{1,0:T(8,128)(2,1)S(1)}, bf16[16,4224]{1,0:T(8,128)(2,1)S(1)}, u32[]{:S(2)}, u32[]{:S(2)}) collective-permute-start(bf16[16,4224]{1,0:T(8,128)(2,1)S(1)} %collective-permute-done.1.refs_4_), channel_id=1, source_target_pairs={{0,2},{1,3},{2,0},{3,1},{4,6},{5,7},{6,4},{7,5},{8,10},{9,11},{10,... | collective-permute-start | bytes 405512 | tf_op jit(solution)/shard_map/ppermute | solution.py:27
  20.2 5.6 %collective-permute-start.6 = (bf16[32,4224]{1,0:T(8,128)(2,1)S(1)}, bf16[32,4224]{1,0:T(8,128)(2,1)S(1)}, u32[]{:S(2)}, u32[]{:S(2)}) collective-permute-start(bf16[32,4224]{1,0:T(8,128)(2,1)S(1)} %get-tuple-element.44.refs_1_), channel_id=1, source_target_pairs={{0,1},{1,0},{2,3},{3,2},{4,5},{5,4},{6,7},{7,6},{8,9},{9,8},{10,11... | collective-permute-start | bytes 811016 | tf_op jit(solution)/shard_map/ppermute | solution.py:27
  23.7 2.3 %collective-permute-start.7 = (bf16[32,4224]{1,0:T(8,128)(2,1)S(1)}, bf16[32,4224]{1,0:T(8,128)(2,1)S(1)}, u32[]{:S(2)}, u32[]{:S(2)}) collective-permute-start(bf16[32,4224]{1,0:T(8,128)(2,1)S(1)} %collective-permute-done.3.refs_2_), channel_id=1, source_target_pairs={{0,1},{1,0},{2,3},{3,2},{4,5},{5,4},{6,7},{7,6},{8,9},{9,8},{10,11... | collective-permute-start | bytes 811016 | tf_op jit(solution)/shard_map/ppermute | solution.py:27
  23.9 2.1 %collective-permute-start.8 = (bf16[32,4224]{1,0:T(8,128)(2,1)S(1)}, bf16[32,4224]{1,0:T(8,128)(2,1)S(1)}, u32[]{:S(2)}, u32[]{:S(2)}) collective-permute-start(bf16[32,4224]{1,0:T(8,128)(2,1)S(1)} %collective-permute-done.4.refs_3_), channel_id=1, source_target_pairs={{0,1},{1,0},{2,3},{3,2},{4,5},{5,4},{6,7},{7,6},{8,9},{9,8},{10,11... | collective-permute-start | bytes 811016 | tf_op jit(solution)/shard_map/ppermute | solution.py:27
  24.2 1.6 %collective-permute-start.9 = (bf16[16,4224]{1,0:T(8,128)(2,1)S(1)}, bf16[16,4224]{1,0:T(8,128)(2,1)S(1)}, u32[]{:S(2)}, u32[]{:S(2)}) collective-permute-start(bf16[16,4224]{1,0:T(8,128)(2,1)S(1)} %collective-permute-done.1.refs_4_), channel_id=1, source_target_pairs={{0,1},{1,0},{2,3},{3,2},{4,5},{5,4},{6,7},{7,6},{8,9},{9,8},{10,11... | collective-permute-start | bytes 405512 | tf_op jit(solution)/shard_map/ppermute | solution.py:27
  24.5 1.5 %collective-permute-start.10 = (bf16[16,4224]{1,0:T(8,128)(2,1)S(1)}, bf16[16,4224]{1,0:T(8,128)(2,1)S(1)}, u32[]{:S(2)}, u32[]{:S(2)}) collective-permute-start(bf16[16,4224]{1,0:T(8,128)(2,1)S(1)} %collective-permute-done.5.refs_5_), channel_id=1, source_target_pairs={{0,1},{1,0},{2,3},{3,2},{4,5},{5,4},{6,7},{7,6},{8,9},{9,8},{10,11... | collective-permute-start | bytes 405512 | tf_op jit(solution)/shard_map/ppermute | solution.py:27
  31.4 2.7 %collective-permute-start.11 = (bf16[128,4096]{1,0:T(8,128)(2,1)S(1)}, bf16[128,4096]{1,0:T(8,128)(2,1)S(1)}, u32[]{:S(2)}, u32[]{:S(2)}) collective-permute-start(bf16[128,4096]{1,0:T(8,128)(2,1)S(1)} %bitcast.11), channel_id=1, source_target_pairs={{0,1},{1,0},{2,3},{3,2},{4,5},{5,4},{6,7},{7,6},{8,9},{9,8},{10,11... | collective-permute-start | bytes 3145736 | tf_op jit(solution)/shard_map/ppermute | solution.py:27
  34.6 5.7 %collective-permute-start.13 = (bf16[16,4096]{1,0:T(8,128)(2,1)S(1)}, bf16[16,4096]{1,0:T(8,128)(2,1)S(1)}, u32[]{:S(2)}, u32[]{:S(2)}) collective-permute-start(bf16[16,4096]{1,0:T(8,128)(2,1)S(1)} %get-tuple-element.66), channel_id=1, source_target_pairs={{0,16},{8,24},{16,0},{24,8},{1,17},{9,25},{17,1},{25,9},{2,18},{10... | collective-permute-start | bytes 393224 | tf_op jit(solution)/shard_map/ppermute | solution.py:27
  35.5 5.3 %collective-permute-start.12 = (bf16[16,4096]{1,0:T(8,128)(2,1)S(1)}, bf16[16,4096]{1,0:T(8,128)(2,1)S(1)}, u32[]{:S(2)}, u32[]{:S(2)}) collective-permute-start(bf16[16,4096]{1,0:T(8,128)(2,1)S(1)} %get-tuple-element.67), channel_id=1, source_target_pairs={{0,8},{8,0},{16,24},{24,16},{1,9},{9,1},{17,25},{25,17},{2,10},{10... | collective-permute-start | bytes 393224 | tf_op jit(solution)/shard_map/ppermute | solution.py:27
  36.6 5.0 %collective-permute-start.18 = (bf16[16,4096]{1,0:T(8,128)(2,1)S(1)}, bf16[16,4096]{1,0:T(8,128)(2,1)S(1)}, u32[]{:S(2)}, u32[]{:S(2)}) collective-permute-start(bf16[16,4096]{1,0:T(8,128)(2,1)S(1)} %get-tuple-element.63), channel_id=1, source_target_pairs={{0,2},{1,3},{2,0},{3,1},{4,6},{5,7},{6,4},{7,5},{8,10},{9,11},{10,... | collective-permute-start | bytes 393224 | tf_op jit(solution)/shard_map/ppermute | solution.py:27
  41.7 6.0 %collective-permute-start.19 = (bf16[8,4096]{1,0:T(8,128)(2,1)S(1)}, bf16[8,4096]{1,0:T(8,128)(2,1)S(1)}, u32[]{:S(2)}, u32[]{:S(2)}) collective-permute-start(bf16[8,4096]{1,0:T(8,128)(2,1)S(1)} %slice.87), channel_id=1, source_target_pairs={{0,4},{1,5},{2,6},{3,7},{4,0},{5,1},{6,2},{7,3},{8,12},{9,13},{10,... | collective-permute-start | bytes 196616 | tf_op jit(solution)/shard_map/ppermute | solution.py:27
  45.0 5.5 %collective-permute-start.14 = (bf16[16,4096]{1,0:T(8,128)(2,1)S(1)}, bf16[16,4096]{1,0:T(8,128)(2,1)S(1)}, u32[]{:S(2)}, u32[]{:S(2)}) collective-permute-start(bf16[16,4096]{1,0:T(8,128)(2,1)S(1)} %get-tuple-element.55), channel_id=1, source_target_pairs={{0,8},{8,0},{16,24},{24,16},{1,9},{9,1},{17,25},{25,17},{2,10},{10... | collective-permute-start | bytes 393224 | tf_op jit(solution)/shard_map/ppermute | solution.py:27
  46.0 5.5 %collective-permute-start.15 = (bf16[16,4096]{1,0:T(8,128)(2,1)S(1)}, bf16[16,4096]{1,0:T(8,128)(2,1)S(1)}, u32[]{:S(2)}, u32[]{:S(2)}) collective-permute-start(bf16[16,4096]{1,0:T(8,128)(2,1)S(1)} %get-tuple-element.56), channel_id=1, source_target_pairs={{0,16},{8,24},{16,0},{24,8},{1,17},{9,25},{17,1},{25,9},{2,18},{10... | collective-permute-start | bytes 393224 | tf_op jit(solution)/shard_map/ppermute | solution.py:27
  47.1 5.0 %collective-permute-start.16 = (bf16[16,4096]{1,0:T(8,128)(2,1)S(1)}, bf16[16,4096]{1,0:T(8,128)(2,1)S(1)}, u32[]{:S(2)}, u32[]{:S(2)}) collective-permute-start(bf16[16,4096]{1,0:T(8,128)(2,1)S(1)} %get-tuple-element.62), channel_id=1, source_target_pairs={{0,2},{1,3},{2,0},{3,1},{4,6},{5,7},{6,4},{7,5},{8,10},{9,11},{10,... | collective-permute-start | bytes 393224 | tf_op jit(solution)/shard_map/ppermute | solution.py:27
  47.8 5.2 %collective-permute-start.20 = (bf16[8,4096]{1,0:T(8,128)(2,1)S(1)}, bf16[8,4096]{1,0:T(8,128)(2,1)S(1)}, u32[]{:S(2)}, u32[]{:S(2)}) collective-permute-start(bf16[8,4096]{1,0:T(8,128)(2,1)S(1)} %fusion.4), channel_id=1, source_target_pairs={{0,24},{8,16},{16,8},{24,0},{1,25},{9,17},{17,9},{25,1},{2,26},{10... | collective-permute-start | bytes 196616 | tf_op jit(solution)/shard_map/ppermute | solution.py:27
  52.2 5.9 %collective-permute-start.17 = (bf16[8,4096]{1,0:T(8,128)(2,1)S(1)}, bf16[8,4096]{1,0:T(8,128)(2,1)S(1)}, u32[]{:S(2)}, u32[]{:S(2)}) collective-permute-start(bf16[8,4096]{1,0:T(8,128)(2,1)S(1)} %slice.88), channel_id=1, source_target_pairs={{0,4},{1,5},{2,6},{3,7},{4,0},{5,1},{6,2},{7,3},{8,12},{9,13},{10,... | collective-permute-start | bytes 196616 | tf_op jit(solution)/shard_map/ppermute | solution.py:27

commit v11 on v8

--- a/solution.py
+++ b/solution.py
@@ -197,7 +197,7 @@
     packed_width = blocks[0].shape[1]
     half_rows = sum(block.shape[0] for block in blocks) // 2
     piece = half_rows // pieces
-    ahead = pieces - 2
+    ahead, after = 1, pieces - 1
     count = len(blocks)
     width = wout.shape[1]
     lines = low.shape[1]
@@ -208,7 +208,7 @@
         block = 16
         x_block = pl.BlockSpec((block, packed_width), lambda i: (i, 0))
         out_blocks = [
-            pl.BlockSpec((n, block, width), lambda i: (0, i, 0)) for n in (ahead, 2, ahead, 2)
+            pl.BlockSpec((n, block, width), lambda i: (0, i, 0)) for n in (ahead, after) * 2
         ]
         grid = (piece // block,)
         rows = count * block
@@ -219,9 +219,9 @@
         grid=grid,
         out_shape=(
             jax.ShapeDtypeStruct((ahead, piece, width), jnp.bfloat16),
-            jax.ShapeDtypeStruct((2, piece, width), jnp.bfloat16),
+            jax.ShapeDtypeStruct((after, piece, width), jnp.bfloat16),
             jax.ShapeDtypeStruct((ahead, piece, width), jnp.float32),
-            jax.ShapeDtypeStruct((2, piece, width), jnp.float32),
+            jax.ShapeDtypeStruct((after, piece, width), jnp.float32),
         ),
         in_specs=[pl.BlockSpec(memory_space=pltpu.SMEM), *[x_block] * count, VMEM, VMEM, VMEM],
         out_specs=out_blocks,
@@ -279,23 +279,32 @@
     blocks = []
     for (mine, across), rest in ((early, late), (early_core, late_core)):
         if mine.shape[0] * planes <= LANES:
-            blocks += rest[:-1] + [mine, across, rest[-1]]
+            blocks += [across, rest[-1], mine] + rest[:-1]
         else:
-            blocks += rest[:-1] + [mine, jnp.concatenate([across, rest[-1]], axis=0)]
+            blocks += [jnp.concatenate([across, rest[-1]], axis=0), mine] + rest[:-1]
 
     sends = run_experts(group, blocks, planes, low, high, wout, exp_dev, experts)
-    first, second, kept, total = sends
-    arrived, second = lax.optimization_barrier((swap(first, "expert", 1), second))
-    first = (kept + arrived.astype(jnp.float32)).astype(jnp.bfloat16)
-    moved = [swap(first[b - 1], "batch", b) for b in range(1, far)]
+    first, second, across, total = sends
+    across = across[0] + swap(first, "expert", 1)[0].astype(jnp.float32)
     total = total + swap(second, "expert", 1).astype(jnp.float32)
-    mine, across = total[0], total[1]
-    for rows in moved:
-        mine = mine + rows.astype(jnp.float32)
-    for stride in reversed(strides):
+    half = total.shape[1] // 2
+    rounded = total.astype(jnp.bfloat16)
+    onward = [swap(rounded[b, half:], "batch", b) for b in range(1, far)]
+    across = halve(across, strides[-1])
+    onward, staying = lax.optimization_barrier(
+        (onward, [rounded[b, :half] for b in range(1, far)])
+    )
+    sent = total[0, half:]
+    for rows in onward:
+        sent = sent + rows.astype(jnp.float32)
+    mine = total[0, :half]
+    for b, rows in zip(range(1, far), staying):
+        mine = mine + swap(rows, "batch", b).astype(jnp.float32)
+    mine = mine + swap(sent.astype(jnp.bfloat16), "expert", strides[-1]).astype(jnp.float32)
+    for stride in reversed(strides[:-1]):
         across = halve(across, stride)
     across = swap(across.astype(jnp.bfloat16), "batch", far).astype(jnp.float32)
-    for stride in reversed(strides):
+    for stride in reversed(strides[:-1]):
         mine = halve(mine, stride)
     mine = mine + across
     return mine.astype(jnp.bfloat16)

time: 58.9 us -> 56.4 us (0.958)
  waiting for transfers between devices: 16 us -> 12.7 us
  starting transfers between devices: 25.8 us -> 26.6 us
    ppermute x20 -> x22, waiting for transfers between devices: 16 us -> 12.7 us  [swap(): return lax.ppermute(block, axis, [(i, i ^ flips) for i in range(size)])]
    ppermute x20 -> x22, starting transfers between devices: 25.8 us -> 26.6 us  [swap(): return lax.ppermute(block, axis, [(i, i ^ flips) for i in range(size)])]
  transfers between devices with their start and end apart: 20 -> 22, of which waited for: 11 -> 11; matrix products, arithmetic and copies ran while one was open for 1% -> 1% of each run, Pallas kernels for 16% -> 16%
where the time goes in v11:
time: 56.4 us; the launch traced here: 56.2 us
  starting transfers between devices  26.6 us (47%)
  Pallas kernels  15.6 us (28%)
  waiting for transfers between devices  12.7 us (23%)
  other arithmetic  1.11 us (2%)
    ppermute x22, starting transfers between devices, swap(): return lax.ppermute(block, axis, [(i, i ^ flips) for i in range(size)])  26.6 us
    ppermute x22, waiting for transfers between devices, swap(): return lax.ppermute(block, axis, [(i, i ^ flips) for i in range(size)])  12.7 us
    pallas_call x3, Pallas kernels, load(): pl.pallas_call(kernel, out_shape=pltpu.VMEM(shape, source.dtype), in_spec...  9.16 us
    pallas_call x1, Pallas kernels, run_experts(): pl.pallas_call(functools.partial(expert_kernel, exp_dev, experts, count),...  5.44 us
  transfers between devices with their start and end apart: 22, of which 11 were waited for; matrix products, arithmetic and copies ran while one was open for 1% of the time, Pallas kernels for 16%

profile of v11, /device:TPU:0, one launch (start us, length us, event | category | flops | bytes accessed | tf_op | source)
XLA Modules:
  0.0 56.2 jit_solution(11776690082047535688)
XLA Ops:
  0.0 1.0 %shard_map.55.first_ref = bf16[8,4224]{1,0:T(8,128)(2,1)S(1)} custom-call(bf16[8,4096]{1,0:T(8,128)(2,1)} %tokens_hbm.1, s32[8,8]{1,0:T(8,128)} %ids_hbm.1, f32[8,8]{1,0:T(8,128)} %weights_hbm.1), custom_call_target="tpu_custom_call" | custom-call | tf_op jit(solution)/shard_map/pallas_call | solution.py:63
  1.0 4.1 %collective-permute-start = (bf16[8,4224]{1,0:T(8,128)(2,1)S(1)}, bf16[8,4224]{1,0:T(8,128)(2,1)S(1)}, u32[]{:S(2)}, u32[]{:S(2)}) collective-permute-start(bf16[8,4224]{1,0:T(8,128)(2,1)S(1)} %shard_map.55.first_ref), channel_id=1, source_target_pairs={{0,4},{1,5},{2,6},{3,7},{4,0},{5,1},{6,2},{7,3},{8,12},{9,13},{10,... | collective-permute-start | bytes 202760 | tf_op jit(solution)/shard_map/ppermute | solution.py:27
  5.1 2.9 %shard_map.56.refs_0_ = bf16[768,4096]{1,0:T(8,128)(2,1)S(1)} custom-call(bf16[768,4096]{1,0:T(8,128)(2,1)} %bitcast.39), custom_call_target="tpu_custom_call" | custom-call | bytes 12582912 | tf_op jit(solution)/shard_map/pallas_call | solution.py:124
  8.0 0.9 %collective-permute-done.second_ref = bf16[8,4224]{1,0:T(8,128)(2,1)S(1)} collective-permute-done((bf16[8,4224]{1,0:T(8,128)(2,1)S(1)}, bf16[8,4224]{1,0:T(8,128)(2,1)S(1)}, u32[]{:S(2)}, u32[]{:S(2)}) %collective-permute-start) | collective-permute-done | bytes 67616 | tf_op jit(solution)/shard_map/ppermute | solution.py:27
  8.8 0.8 %collective-permute-start.2 = (bf16[16,4224]{1,0:T(8,128)(2,1)S(1)}, bf16[16,4224]{1,0:T(8,128)(2,1)S(1)}, u32[]{:S(2)}, u32[]{:S(2)}) collective-permute-start(bf16[16,4224]{1,0:T(8,128)(2,1)S(1)} %get-tuple-element.39.first_ref), channel_id=1, source_target_pairs={{0,2},{1,3},{2,0},{3,1},{4,6},{5,7},{6,4},{7,5},{8,10},{9,11},{10,... | collective-permute-start | bytes 405512 | tf_op jit(solution)/shard_map/ppermute | solution.py:27
  9.6 2.4 %collective-permute-start.1 = (bf16[16,4224]{1,0:T(8,128)(2,1)S(1)}, bf16[16,4224]{1,0:T(8,128)(2,1)S(1)}, u32[]{:S(2)}, u32[]{:S(2)}) collective-permute-start(bf16[16,4224]{1,0:T(8,128)(2,1)S(1)} %get-tuple-element.39.first_ref), channel_id=1, source_target_pairs={{0,24},{8,16},{16,8},{24,0},{1,25},{9,17},{17,9},{25,1},{2,26},{10... | collective-permute-start | bytes 405512 | tf_op jit(solution)/shard_map/ppermute | solution.py:27
  12.1 3.2 %shard_map.58 = bf16[16,768,2,128]{3,2,1,0:T(2,128)(2,1)S(1)} custom-call(bf16[768,2,4096]{2,1,0:T(2,128)(2,1)} %bitcast.37), custom_call_target="tpu_custom_call" | custom-call | bytes 12582912 | tf_op jit(solution)/shard_map/pallas_call | solution.py:124
  15.3 0.0 collective-permute-done.2.second_ref
  15.3 0.3 collective-permute-done.1.refs_1_
  15.6 1.6 %collective-permute-start.4 = (bf16[32,4224]{1,0:T(8,128)(2,1)S(1)}, bf16[32,4224]{1,0:T(8,128)(2,1)S(1)}, u32[]{:S(2)}, u32[]{:S(2)}) collective-permute-start(bf16[32,4224]{1,0:T(8,128)(2,1)S(1)} %get-tuple-element.47.refs_3_), channel_id=1, source_target_pairs={{0,16},{8,24},{16,0},{24,8},{1,17},{9,25},{17,1},{25,9},{2,18},{10... | collective-permute-start | bytes 811016 | tf_op jit(solution)/shard_map/ppermute | solution.py:27
  17.2 1.5 %collective-permute-start.3 = (bf16[32,4224]{1,0:T(8,128)(2,1)S(1)}, bf16[32,4224]{1,0:T(8,128)(2,1)S(1)}, u32[]{:S(2)}, u32[]{:S(2)}) collective-permute-start(bf16[32,4224]{1,0:T(8,128)(2,1)S(1)} %get-tuple-element.47.refs_3_), channel_id=1, source_target_pairs={{0,8},{8,0},{16,24},{24,16},{1,9},{9,1},{17,25},{25,17},{2,10},{10... | collective-permute-start | bytes 811016 | tf_op jit(solution)/shard_map/ppermute | solution.py:27
  18.7 1.5 %collective-permute-start.5 = (bf16[16,4224]{1,0:T(8,128)(2,1)S(1)}, bf16[16,4224]{1,0:T(8,128)(2,1)S(1)}, u32[]{:S(2)}, u32[]{:S(2)}) collective-permute-start(bf16[16,4224]{1,0:T(8,128)(2,1)S(1)} %collective-permute-done.1.refs_1_), channel_id=1, source_target_pairs={{0,2},{1,3},{2,0},{3,1},{4,6},{5,7},{6,4},{7,5},{8,10},{9,11},{10,... | collective-permute-start | bytes 405512 | tf_op jit(solution)/shard_map/ppermute | solution.py:27
  20.2 0.0 collective-permute-start.8
  20.2 3.2 %shard_map.60 = bf16[16,768,2,128]{3,2,1,0:T(2,128)(2,1)S(1)} custom-call(bf16[768,2,4096]{2,1,0:T(2,128)(2,1)} %bitcast.38), custom_call_target="tpu_custom_call" | custom-call | bytes 12582912 | tf_op jit(solution)/shard_map/pallas_call | solution.py:124
  23.3 0.3 collective-permute-done.5.refs_2_
  23.7 0.0 collective-permute-done.4.refs_5_
  23.7 0.0 collective-permute-done.3.refs_4_
  23.7 0.3 collective-permute-start.9
  23.9 0.2 collective-permute-start.10
  24.2 0.3 collective-permute-start.6
  24.5 0.2 collective-permute-start.7
  24.7 1.1 %collective-permute-done.6.refs_6_ = bf16[16,4224]{1,0:T(8,128)(2,1)S(1)} collective-permute-done((bf16[16,4224]{1,0:T(8,128)(2,1)S(1)}, bf16[16,4224]{1,0:T(8,128)(2,1)S(1)}, u32[]{:S(2)}, u32[]{:S(2)}) %collective-permute-start.6) | collective-permute-done | bytes 135200 | tf_op jit(solution)/shard_map/ppermute | solution.py:27
  25.8 0.0 collective-permute-done.8.refs_8_
  25.8 0.2 collective-permute-done.7.refs_7_
  26.0 0.0 collective-permute-done.9.refs_9_
  26.0 0.0 collective-permute-done.10.refs_10_
  26.0 5.4 %shard_map.61 = (bf16[1,32,4096]{2,1,0:T(8,128)(2,1)S(1)}, bf16[3,32,4096]{2,1,0:T(8,128)(2,1)S(1)}, f32[1,32,4096]{2,1,0:T(8,128)S(1)}, f32[3,32,4096]{2,1,0:T(8,128)S(1)}) custom-call(s32[1]{0:T(128)} %bitcast.refs_0_, bf16[16,4224]{1,0:T(8,128)(2,1)S(1)} %collective-permute-done.1.refs_1_, bf16[16,4224]{1,0:T(8,128)(2,1)S(1)} %collective-permute-done.5.refs_2_, ...), custom_call_target="tpu_custom_call" | custom-call | flops 4831838208 | bytes 5308416 | tf_op jit(solution)/shard_map/pallas_call | solution.py:217
  31.5 0.3 collective-permute-start.18
  31.8 0.2 collective-permute-start.11
  32.0 1.0 %collective-permute-done.18 = bf16[1,32,4096]{2,1,0:T(8,128)(2,1)S(1)} collective-permute-done((bf16[1,32,4096]{2,1,0:T(8,128)(2,1)S(1)}, bf16[1,32,4096]{2,1,0:T(8,128)(2,1)S(1)}, u32[]{:S(2)}, u32[]{:S(2)}) %collective-permute-start.18) | collective-permute-done | bytes 262176 | tf_op jit(solution)/shard_map/ppermute | solution.py:27
  33.1 1.6 %collective-permute-start.19 = (bf16[16,4096]{1,0:T(8,128)(2,1)S(1)}, bf16[16,4096]{1,0:T(8,128)(2,1)S(1)}, u32[]{:S(2)}, u32[]{:S(2)}) collective-permute-start(bf16[16,4096]{1,0:T(8,128)(2,1)S(1)} %fusion.7), channel_id=1, source_target_pairs={{0,2},{1,3},{2,0},{3,1},{4,6},{5,7},{6,4},{7,5},{8,10},{9,11},{10,... | collective-permute-start | bytes 393224 | tf_op jit(solution)/shard_map/ppermute | solution.py:27
  34.7 0.0 collective-permute-done.11
  34.7 0.3 fusion.11
  35.0 0.6 %collective-permute-start.13 = (bf16[16,4096]{1,0:T(8,128)(2,1)S(1)}, bf16[16,4096]{1,0:T(8,128)(2,1)S(1)}, u32[]{:S(2)}, u32[]{:S(2)}) collective-permute-start(bf16[16,4096]{1,0:T(8,128)(2,1)S(1)} %get-tuple-element.67), channel_id=1, source_target_pairs={{0,16},{8,24},{16,0},{24,8},{1,17},{9,25},{17,1},{25,9},{2,18},{10... | collective-permute-start | bytes 393224 | tf_op jit(solution)/shard_map/ppermute | solution.py:27
  35.6 1.4 %collective-permute-start.12 = (bf16[16,4096]{1,0:T(8,128)(2,1)S(1)}, bf16[16,4096]{1,0:T(8,128)(2,1)S(1)}, u32[]{:S(2)}, u32[]{:S(2)}) collective-permute-start(bf16[16,4096]{1,0:T(8,128)(2,1)S(1)} %get-tuple-element.68), channel_id=1, source_target_pairs={{0,8},{8,0},{16,24},{24,16},{1,9},{9,1},{17,25},{25,17},{2,10},{10... | collective-permute-start | bytes 393224 | tf_op jit(solution)/shard_map/ppermute | solution.py:27
  37.0 1.8 %collective-permute-done.19 = bf16[16,4096]{1,0:T(8,128)(2,1)S(1)} collective-permute-done((bf16[16,4096]{1,0:T(8,128)(2,1)S(1)}, bf16[16,4096]{1,0:T(8,128)(2,1)S(1)}, u32[]{:S(2)}, u32[]{:S(2)}) %collective-permute-start.19) | collective-permute-done | bytes 131104 | tf_op jit(solution)/shard_map/ppermute | solution.py:27
  38.9 3.2 %collective-permute-start.20 = (bf16[8,4096]{1,0:T(8,128)(2,1)S(1)}, bf16[8,4096]{1,0:T(8,128)(2,1)S(1)}, u32[]{:S(2)}, u32[]{:S(2)}) collective-permute-start(bf16[8,4096]{1,0:T(8,128)(2,1)S(1)} %slice.102), channel_id=1, source_target_pairs={{0,4},{1,5},{2,6},{3,7},{4,0},{5,1},{6,2},{7,3},{8,12},{9,13},{10,... | collective-permute-start | bytes 196616 | tf_op jit(solution)/shard_map/ppermute | solution.py:27
  42.1 0.0 collective-permute-done.13
  42.1 0.0 collective-permute-done.12
  42.1 0.7 %collective-permute-start.16 = (bf16[16,4096]{1,0:T(8,128)(2,1)S(1)}, bf16[16,4096]{1,0:T(8,128)(2,1)S(1)}, u32[]{:S(2)}, u32[]{:S(2)}) collective-permute-start(bf16[16,4096]{1,0:T(8,128)(2,1)S(1)} %fusion.3), channel_id=1, source_target_pairs={{0,2},{1,3},{2,0},{3,1},{4,6},{5,7},{6,4},{7,5},{8,10},{9,11},{10,... | collective-permute-start | bytes 393224 | tf_op jit(solution)/shard_map/ppermute | solution.py:27
  42.8 1.5 %collective-permute-start.14 = (bf16[16,4096]{1,0:T(8,128)(2,1)S(1)}, bf16[16,4096]{1,0:T(8,128)(2,1)S(1)}, u32[]{:S(2)}, u32[]{:S(2)}) collective-permute-start(bf16[16,4096]{1,0:T(8,128)(2,1)S(1)} %get-tuple-element.57), channel_id=1, source_target_pairs={{0,8},{8,0},{16,24},{24,16},{1,9},{9,1},{17,25},{25,17},{2,10},{10... | collective-permute-start | bytes 393224 | tf_op jit(solution)/shard_map/ppermute | solution.py:27
  44.3 0.6 %collective-permute-start.15 = (bf16[16,4096]{1,0:T(8,128)(2,1)S(1)}, bf16[16,4096]{1,0:T(8,128)(2,1)S(1)}, u32[]{:S(2)}, u32[]{:S(2)}) collective-permute-start(bf16[16,4096]{1,0:T(8,128)(2,1)S(1)} %get-tuple-element.58), channel_id=1, source_target_pairs={{0,16},{8,24},{16,0},{24,8},{1,17},{9,25},{17,1},{25,9},{2,18},{10... | collective-permute-start | bytes 393224 | tf_op jit(solution)/shard_map/ppermute | solution.py:27
  44.9 0.0 collective-permute-done.20
  44.9 1.7 %collective-permute-start.21 = (bf16[8,4096]{1,0:T(8,128)(2,1)S(1)}, bf16[8,4096]{1,0:T(8,128)(2,1)S(1)}, u32[]{:S(2)}, u32[]{:S(2)}) collective-permute-start(bf16[8,4096]{1,0:T(8,128)(2,1)S(1)} %fusion.8), channel_id=1, source_target_pairs={{0,24},{8,16},{16,8},{24,0},{1,25},{9,17},{17,9},{25,1},{2,26},{10... | collective-permute-start | bytes 196616 | tf_op jit(solution)/shard_map/ppermute | solution.py:27
  46.7 0.5 collective-permute-done.16
  47.2 1.3 %collective-permute-done.14 = bf16[16,4096]{1,0:T(8,128)(2,1)S(1)} collective-permute-done((bf16[16,4096]{1,0:T(8,128)(2,1)S(1)}, bf16[16,4096]{1,0:T(8,128)(2,1)S(1)}, u32[]{:S(2)}, u32[]{:S(2)}) %collective-permute-start.14) | collective-permute-done | bytes 131104 | tf_op jit(solution)/shard_map/ppermute | solution.py:27
  48.5 1.1 %collective-permute-done.15 = bf16[16,4096]{1,0:T(8,128)(2,1)S(1)} collective-permute-done((bf16[16,4096]{1,0:T(8,128)(2,1)S(1)}, bf16[16,4096]{1,0:T(8,128)(2,1)S(1)}, u32[]{:S(2)}, u32[]{:S(2)}) %collective-permute-start.15) | collective-permute-done | bytes 131104 | tf_op jit(solution)/shard_map/ppermute | solution.py:27
  49.6 0.1 fusion.6
  49.6 1.8 %collective-permute-start.17 = (bf16[8,4096]{1,0:T(8,128)(2,1)S(1)}, bf16[8,4096]{1,0:T(8,128)(2,1)S(1)}, u32[]{:S(2)}, u32[]{:S(2)}) collective-permute-start(bf16[8,4096]{1,0:T(8,128)(2,1)S(1)} %slice.103), channel_id=1, source_target_pairs={{0,4},{1,5},{2,6},{3,7},{4,0},{5,1},{6,2},{7,3},{8,12},{9,13},{10,... | collective-permute-start | bytes 196616 | tf_op jit(solution)/shard_map/ppermute | solution.py:27
  51.5 0.0 collective-permute-done.21
  51.5 4.1 %collective-permute-done.17 = bf16[8,4096]{1,0:T(8,128)(2,1)S(1)} collective-permute-done((bf16[8,4096]{1,0:T(8,128)(2,1)S(1)}, bf16[8,4096]{1,0:T(8,128)(2,1)S(1)}, u32[]{:S(2)}, u32[]{:S(2)}) %collective-permute-start.17) | collective-permute-done | bytes 65568 | tf_op jit(solution)/shard_map/ppermute | solution.py:27
  55.6 0.7 %fusion.10 = bf16[8,4096]{1,0:T(8,128)(2,1)} fusion(f32[16,4096]{1,0:T(8,128)S(1)} %fusion.6, bf16[8,4096]{1,0:T(8,128)(2,1)S(1)} %collective-permute-done.21, bf16[8,4096]{1,0:T(8,128)(2,1)S(1)} %collective-permute-done.17), kind=kLoop, calls=%fused_computation.20 | loop fusion | flops 163840 | bytes 327680 | tf_op jit(solution)/shard_map/convert_element_type | solution.py:310
  (10 shorter events, 0.2 us)
Async XLA Ops:
  1.0 7.8 %collective-permute-start = (bf16[8,4224]{1,0:T(8,128)(2,1)S(1)}, bf16[8,4224]{1,0:T(8,128)(2,1)S(1)}, u32[]{:S(2)}, u32[]{:S(2)}) collective-permute-start(bf16[8,4224]{1,0:T(8,128)(2,1)S(1)} %shard_map.55.first_ref), channel_id=1, source_target_pairs={{0,4},{1,5},{2,6},{3,7},{4,0},{5,1},{6,2},{7,3},{8,12},{9,13},{10,... | collective-permute-start | bytes 202760 | tf_op jit(solution)/shard_map/ppermute | solution.py:27
  8.8 6.4 %collective-permute-start.2 = (bf16[16,4224]{1,0:T(8,128)(2,1)S(1)}, bf16[16,4224]{1,0:T(8,128)(2,1)S(1)}, u32[]{:S(2)}, u32[]{:S(2)}) collective-permute-start(bf16[16,4224]{1,0:T(8,128)(2,1)S(1)} %get-tuple-element.39.first_ref), channel_id=1, source_target_pairs={{0,2},{1,3},{2,0},{3,1},{4,6},{5,7},{6,4},{7,5},{8,10},{9,11},{10,... | collective-permute-start | bytes 405512 | tf_op jit(solution)/shard_map/ppermute | solution.py:27
  9.6 5.9 %collective-permute-start.1 = (bf16[16,4224]{1,0:T(8,128)(2,1)S(1)}, bf16[16,4224]{1,0:T(8,128)(2,1)S(1)}, u32[]{:S(2)}, u32[]{:S(2)}) collective-permute-start(bf16[16,4224]{1,0:T(8,128)(2,1)S(1)} %get-tuple-element.39.first_ref), channel_id=1, source_target_pairs={{0,24},{8,16},{16,8},{24,0},{1,25},{9,17},{17,9},{25,1},{2,26},{10... | collective-permute-start | bytes 405512 | tf_op jit(solution)/shard_map/ppermute | solution.py:27
  15.6 8.1 %collective-permute-start.4 = (bf16[32,4224]{1,0:T(8,128)(2,1)S(1)}, bf16[32,4224]{1,0:T(8,128)(2,1)S(1)}, u32[]{:S(2)}, u32[]{:S(2)}) collective-permute-start(bf16[32,4224]{1,0:T(8,128)(2,1)S(1)} %get-tuple-element.47.refs_3_), channel_id=1, source_target_pairs={{0,16},{8,24},{16,0},{24,8},{1,17},{9,25},{17,1},{25,9},{2,18},{10... | collective-permute-start | bytes 811016 | tf_op jit(solution)/shard_map/ppermute | solution.py:27
  17.2 6.5 %collective-permute-start.3 = (bf16[32,4224]{1,0:T(8,128)(2,1)S(1)}, bf16[32,4224]{1,0:T(8,128)(2,1)S(1)}, u32[]{:S(2)}, u32[]{:S(2)}) collective-permute-start(bf16[32,4224]{1,0:T(8,128)(2,1)S(1)} %get-tuple-element.47.refs_3_), channel_id=1, source_target_pairs={{0,8},{8,0},{16,24},{24,16},{1,9},{9,1},{17,25},{25,17},{2,10},{10... | collective-permute-start | bytes 811016 | tf_op jit(solution)/shard_map/ppermute | solution.py:27
  18.7 5.0 %collective-permute-start.5 = (bf16[16,4224]{1,0:T(8,128)(2,1)S(1)}, bf16[16,4224]{1,0:T(8,128)(2,1)S(1)}, u32[]{:S(2)}, u32[]{:S(2)}) collective-permute-start(bf16[16,4224]{1,0:T(8,128)(2,1)S(1)} %collective-permute-done.1.refs_1_), channel_id=1, source_target_pairs={{0,2},{1,3},{2,0},{3,1},{4,6},{5,7},{6,4},{7,5},{8,10},{9,11},{10,... | collective-permute-start | bytes 405512 | tf_op jit(solution)/shard_map/ppermute | solution.py:27
  20.2 5.6 %collective-permute-start.8 = (bf16[32,4224]{1,0:T(8,128)(2,1)S(1)}, bf16[32,4224]{1,0:T(8,128)(2,1)S(1)}, u32[]{:S(2)}, u32[]{:S(2)}) collective-permute-start(bf16[32,4224]{1,0:T(8,128)(2,1)S(1)} %get-tuple-element.47.refs_3_), channel_id=1, source_target_pairs={{0,1},{1,0},{2,3},{3,2},{4,5},{5,4},{6,7},{7,6},{8,9},{9,8},{10,11... | collective-permute-start | bytes 811016 | tf_op jit(solution)/shard_map/ppermute | solution.py:27
  23.7 2.3 %collective-permute-start.9 = (bf16[32,4224]{1,0:T(8,128)(2,1)S(1)}, bf16[32,4224]{1,0:T(8,128)(2,1)S(1)}, u32[]{:S(2)}, u32[]{:S(2)}) collective-permute-start(bf16[32,4224]{1,0:T(8,128)(2,1)S(1)} %collective-permute-done.3.refs_4_), channel_id=1, source_target_pairs={{0,1},{1,0},{2,3},{3,2},{4,5},{5,4},{6,7},{7,6},{8,9},{9,8},{10,11... | collective-permute-start | bytes 811016 | tf_op jit(solution)/shard_map/ppermute | solution.py:27
  23.9 2.1 %collective-permute-start.10 = (bf16[32,4224]{1,0:T(8,128)(2,1)S(1)}, bf16[32,4224]{1,0:T(8,128)(2,1)S(1)}, u32[]{:S(2)}, u32[]{:S(2)}) collective-permute-start(bf16[32,4224]{1,0:T(8,128)(2,1)S(1)} %collective-permute-done.4.refs_5_), channel_id=1, source_target_pairs={{0,1},{1,0},{2,3},{3,2},{4,5},{5,4},{6,7},{7,6},{8,9},{9,8},{10,11... | collective-permute-start | bytes 811016 | tf_op jit(solution)/shard_map/ppermute | solution.py:27
  24.2 1.6 %collective-permute-start.6 = (bf16[16,4224]{1,0:T(8,128)(2,1)S(1)}, bf16[16,4224]{1,0:T(8,128)(2,1)S(1)}, u32[]{:S(2)}, u32[]{:S(2)}) collective-permute-start(bf16[16,4224]{1,0:T(8,128)(2,1)S(1)} %collective-permute-done.1.refs_1_), channel_id=1, source_target_pairs={{0,1},{1,0},{2,3},{3,2},{4,5},{5,4},{6,7},{7,6},{8,9},{9,8},{10,11... | collective-permute-start | bytes 405512 | tf_op jit(solution)/shard_map/ppermute | solution.py:27
  24.5 1.5 %collective-permute-start.7 = (bf16[16,4224]{1,0:T(8,128)(2,1)S(1)}, bf16[16,4224]{1,0:T(8,128)(2,1)S(1)}, u32[]{:S(2)}, u32[]{:S(2)}) collective-permute-start(bf16[16,4224]{1,0:T(8,128)(2,1)S(1)} %collective-permute-done.5.refs_2_), channel_id=1, source_target_pairs={{0,1},{1,0},{2,3},{3,2},{4,5},{5,4},{6,7},{7,6},{8,9},{9,8},{10,11... | collective-permute-start | bytes 405512 | tf_op jit(solution)/shard_map/ppermute | solution.py:27
  31.5 1.6 %collective-permute-start.18 = (bf16[1,32,4096]{2,1,0:T(8,128)(2,1)S(1)}, bf16[1,32,4096]{2,1,0:T(8,128)(2,1)S(1)}, u32[]{:S(2)}, u32[]{:S(2)}) collective-permute-start(bf16[1,32,4096]{2,1,0:T(8,128)(2,1)S(1)} %get-tuple-element.62), channel_id=1, source_target_pairs={{0,1},{1,0},{2,3},{3,2},{4,5},{5,4},{6,7},{7,6},{8,9},{9,8},{10,11... | collective-permute-start | bytes 786440 | tf_op jit(solution)/shard_map/ppermute | solution.py:27
  31.8 2.9 %collective-permute-start.11 = (bf16[3,32,4096]{2,1,0:T(8,128)(2,1)S(1)}, bf16[3,32,4096]{2,1,0:T(8,128)(2,1)S(1)}, u32[]{:S(2)}, u32[]{:S(2)}) collective-permute-start(bf16[3,32,4096]{2,1,0:T(8,128)(2,1)S(1)} %get-tuple-element.56), channel_id=1, source_target_pairs={{0,1},{1,0},{2,3},{3,2},{4,5},{5,4},{6,7},{7,6},{8,9},{9,8},{10,11... | collective-permute-start | bytes 2359304 | tf_op jit(solution)/shard_map/ppermute | solution.py:27
  33.1 5.7 %collective-permute-start.19 = (bf16[16,4096]{1,0:T(8,128)(2,1)S(1)}, bf16[16,4096]{1,0:T(8,128)(2,1)S(1)}, u32[]{:S(2)}, u32[]{:S(2)}) collective-permute-start(bf16[16,4096]{1,0:T(8,128)(2,1)S(1)} %fusion.7), channel_id=1, source_target_pairs={{0,2},{1,3},{2,0},{3,1},{4,6},{5,7},{6,4},{7,5},{8,10},{9,11},{10,... | collective-permute-start | bytes 393224 | tf_op jit(solution)/shard_map/ppermute | solution.py:27
  35.0 7.1 %collective-permute-start.13 = (bf16[16,4096]{1,0:T(8,128)(2,1)S(1)}, bf16[16,4096]{1,0:T(8,128)(2,1)S(1)}, u32[]{:S(2)}, u32[]{:S(2)}) collective-permute-start(bf16[16,4096]{1,0:T(8,128)(2,1)S(1)} %get-tuple-element.67), channel_id=1, source_target_pairs={{0,16},{8,24},{16,0},{24,8},{1,17},{9,25},{17,1},{25,9},{2,18},{10... | collective-permute-start | bytes 393224 | tf_op jit(solution)/shard_map/ppermute | solution.py:27
  35.6 6.5 %collective-permute-start.12 = (bf16[16,4096]{1,0:T(8,128)(2,1)S(1)}, bf16[16,4096]{1,0:T(8,128)(2,1)S(1)}, u32[]{:S(2)}, u32[]{:S(2)}) collective-permute-start(bf16[16,4096]{1,0:T(8,128)(2,1)S(1)} %get-tuple-element.68), channel_id=1, source_target_pairs={{0,8},{8,0},{16,24},{24,16},{1,9},{9,1},{17,25},{25,17},{2,10},{10... | collective-permute-start | bytes 393224 | tf_op jit(solution)/shard_map/ppermute | solution.py:27
  38.9 6.0 %collective-permute-start.20 = (bf16[8,4096]{1,0:T(8,128)(2,1)S(1)}, bf16[8,4096]{1,0:T(8,128)(2,1)S(1)}, u32[]{:S(2)}, u32[]{:S(2)}) collective-permute-start(bf16[8,4096]{1,0:T(8,128)(2,1)S(1)} %slice.102), channel_id=1, source_target_pairs={{0,4},{1,5},{2,6},{3,7},{4,0},{5,1},{6,2},{7,3},{8,12},{9,13},{10,... | collective-permute-start | bytes 196616 | tf_op jit(solution)/shard_map/ppermute | solution.py:27
  42.1 5.0 %collective-permute-start.16 = (bf16[16,4096]{1,0:T(8,128)(2,1)S(1)}, bf16[16,4096]{1,0:T(8,128)(2,1)S(1)}, u32[]{:S(2)}, u32[]{:S(2)}) collective-permute-start(bf16[16,4096]{1,0:T(8,128)(2,1)S(1)} %fusion.3), channel_id=1, source_target_pairs={{0,2},{1,3},{2,0},{3,1},{4,6},{5,7},{6,4},{7,5},{8,10},{9,11},{10,... | collective-permute-start | bytes 393224 | tf_op jit(solution)/shard_map/ppermute | solution.py:27
  42.8 5.7 %collective-permute-start.14 = (bf16[16,4096]{1,0:T(8,128)(2,1)S(1)}, bf16[16,4096]{1,0:T(8,128)(2,1)S(1)}, u32[]{:S(2)}, u32[]{:S(2)}) collective-permute-start(bf16[16,4096]{1,0:T(8,128)(2,1)S(1)} %get-tuple-element.57), channel_id=1, source_target_pairs={{0,8},{8,0},{16,24},{24,16},{1,9},{9,1},{17,25},{25,17},{2,10},{10... | collective-permute-start | bytes 393224 | tf_op jit(solution)/shard_map/ppermute | solution.py:27
  44.3 5.2 %collective-permute-start.15 = (bf16[16,4096]{1,0:T(8,128)(2,1)S(1)}, bf16[16,4096]{1,0:T(8,128)(2,1)S(1)}, u32[]{:S(2)}, u32[]{:S(2)}) collective-permute-start(bf16[16,4096]{1,0:T(8,128)(2,1)S(1)} %get-tuple-element.58), channel_id=1, source_target_pairs={{0,16},{8,24},{16,0},{24,8},{1,17},{9,25},{17,1},{25,9},{2,18},{10... | collective-permute-start | bytes 393224 | tf_op jit(solution)/shard_map/ppermute | solution.py:27
  44.9 6.5 %collective-permute-start.21 = (bf16[8,4096]{1,0:T(8,128)(2,1)S(1)}, bf16[8,4096]{1,0:T(8,128)(2,1)S(1)}, u32[]{:S(2)}, u32[]{:S(2)}) collective-permute-start(bf16[8,4096]{1,0:T(8,128)(2,1)S(1)} %fusion.8), channel_id=1, source_target_pairs={{0,24},{8,16},{16,8},{24,0},{1,25},{9,17},{17,9},{25,1},{2,26},{10... | collective-permute-start | bytes 196616 | tf_op jit(solution)/shard_map/ppermute | solution.py:27
  49.6 5.9 %collective-permute-start.17 = (bf16[8,4096]{1,0:T(8,128)(2,1)S(1)}, bf16[8,4096]{1,0:T(8,128)(2,1)S(1)}, u32[]{:S(2)}, u32[]{:S(2)}) collective-permute-start(bf16[8,4096]{1,0:T(8,128)(2,1)S(1)} %slice.103), channel_id=1, source_target_pairs={{0,4},{1,5},{2,6},{3,7},{4,0},{5,1},{6,2},{7,3},{8,12},{9,13},{10,... | collective-permute-start | bytes 196616 | tf_op jit(solution)/shard_map/ppermute | solution.py:27

commit v12 on v7

--- a/solution.py
+++ b/solution.py
@@ -278,18 +278,40 @@
 
     send, total = run_experts(group, blocks, low, high, wout, exp_dev, experts)
     total = total + swap(send, "expert", 1).astype(jnp.float32)
-    size = total.shape[0] // planes
+    total = total.reshape(planes, -1, width)
+    half = total.shape[1] // 2
     rounded = total.astype(jnp.bfloat16)
-    mine = total[:size]
-    for b in range(1, far):
-        piece = rounded[b * size : (b + 1) * size]
-        mine = mine + swap(piece, "batch", b).astype(jnp.float32)
-    across = total[far * size :]
-    for stride in reversed(strides):
+    across = halve(total[far], strides[-1])
+    onward = [swap(rounded[b, half:], "batch", b) for b in range(1, far)]
+    own = tokens.shape[0]
+    onward, middle = lax.optimization_barrier(
+        (onward, [rounded[b, own:half] for b in range(1, far)])
+    )
+    sent = total[0, half:]
+    for rows in onward:
+        sent = sent + rows.astype(jnp.float32)
+    middle = [swap(rows, "batch", b) for b, rows in zip(range(1, far), middle)]
+    middle, last = lax.optimization_barrier(
+        (middle, [rounded[b, :own] for b in range(1, far)])
+    )
+    arrived = swap(sent.astype(jnp.bfloat16), "expert", strides[-1]).astype(jnp.float32)
+    mine = total[0, :own] + arrived[:own]
+    rest = total[0, own:half] + arrived[own:]
+    for rows in middle:
+        rest = rest + rows.astype(jnp.float32)
+    for stride in reversed(strides[:-1]):
         across = halve(across, stride)
     across = swap(across.astype(jnp.bfloat16), "batch", far).astype(jnp.float32)
-    for stride in reversed(strides):
-        mine = halve(mine, stride)
+    size = half
+    for stride in reversed(strides[:-1]):
+        size = size // 2
+        sent = rest[size - own :].astype(jnp.bfloat16)
+        arrived = swap(sent, "expert", stride).astype(jnp.float32)
+        mine = mine + arrived[:own]
+        if size > own:
+            rest = rest[: size - own] + arrived[own:]
+    for b, rows in zip(range(1, far), last):
+        mine = mine + swap(rows, "batch", b).astype(jnp.float32)
     mine = mine + across
     return mine.astype(jnp.bfloat16)
 

time: 57.5 us -> 57.5 us (level)
  starting transfers between devices: 24.4 us -> 27 us
  waiting for transfers between devices: 15.8 us -> 13.3 us
    ppermute x19 -> x23, starting transfers between devices: 24.4 us -> 27 us  [swap(): return lax.ppermute(block, axis, [(i, i ^ flips) for i in range(size)])]
    ppermute x19 -> x23, waiting for transfers between devices: 15.8 us -> 13.3 us  [swap(): return lax.ppermute(block, axis, [(i, i ^ flips) for i in range(size)])]
  transfers between devices with their start and end apart: 19 -> 23, of which waited for: 11 -> 10; matrix products, arithmetic and copies ran while one was open for 0% -> 1% of each run, Pallas kernels for 16% -> 16%
where the time goes in v12:
time: 57.5 us; the launch traced here: 57.3 us
  starting transfers between devices  27 us (47%)
  Pallas kernels  15.6 us (27%)
  waiting for transfers between devices  13.3 us (23%)
  other arithmetic  1.2 us (2%)
    ppermute x23, starting transfers between devices, swap(): return lax.ppermute(block, axis, [(i, i ^ flips) for i in range(size)])  27 us
    ppermute x23, waiting for transfers between devices, swap(): return lax.ppermute(block, axis, [(i, i ^ flips) for i in range(size)])  13.3 us
    pallas_call x3, Pallas kernels, load(): pl.pallas_call(kernel, out_shape=pltpu.VMEM(shape, source.dtype), in_spec...  9.16 us
    pallas_call x1, Pallas kernels, run_experts(): pl.pallas_call(functools.partial(expert_kernel, exp_dev, experts, count),...  5.44 us
  transfers between devices with their start and end apart: 23, of which 10 were waited for; matrix products, arithmetic and copies ran while one was open for 1% of the time, Pallas kernels for 16%

profile of v12, /device:TPU:0, one launch (start us, length us, event | category | flops | bytes accessed | tf_op | source)
XLA Modules:
  0.0 57.3 jit_solution(17717151889022614733)
XLA Ops:
  0.0 1.0 %shard_map.55.first_ref = bf16[8,4224]{1,0:T(8,128)(2,1)S(1)} custom-call(bf16[8,4096]{1,0:T(8,128)(2,1)} %tokens_hbm.1, s32[8,8]{1,0:T(8,128)} %ids_hbm.1, f32[8,8]{1,0:T(8,128)} %weights_hbm.1), custom_call_target="tpu_custom_call" | custom-call | tf_op jit(solution)/shard_map/pallas_call | solution.py:63
  1.0 4.1 %collective-permute-start = (bf16[8,4224]{1,0:T(8,128)(2,1)S(1)}, bf16[8,4224]{1,0:T(8,128)(2,1)S(1)}, u32[]{:S(2)}, u32[]{:S(2)}) collective-permute-start(bf16[8,4224]{1,0:T(8,128)(2,1)S(1)} %shard_map.55.first_ref), channel_id=1, source_target_pairs={{0,4},{1,5},{2,6},{3,7},{4,0},{5,1},{6,2},{7,3},{8,12},{9,13},{10,... | collective-permute-start | bytes 202760 | tf_op jit(solution)/shard_map/ppermute | solution.py:27
  5.1 2.9 %shard_map.56.refs_0_ = bf16[768,4096]{1,0:T(8,128)(2,1)S(1)} custom-call(bf16[768,4096]{1,0:T(8,128)(2,1)} %bitcast.46), custom_call_target="tpu_custom_call" | custom-call | bytes 12582912 | tf_op jit(solution)/shard_map/pallas_call | solution.py:124
  8.0 0.9 %collective-permute-done.second_ref = bf16[8,4224]{1,0:T(8,128)(2,1)S(1)} collective-permute-done((bf16[8,4224]{1,0:T(8,128)(2,1)S(1)}, bf16[8,4224]{1,0:T(8,128)(2,1)S(1)}, u32[]{:S(2)}, u32[]{:S(2)}) %collective-permute-start) | collective-permute-done | bytes 67616 | tf_op jit(solution)/shard_map/ppermute | solution.py:27
  8.8 0.8 %collective-permute-start.2 = (bf16[16,4224]{1,0:T(8,128)(2,1)S(1)}, bf16[16,4224]{1,0:T(8,128)(2,1)S(1)}, u32[]{:S(2)}, u32[]{:S(2)}) collective-permute-start(bf16[16,4224]{1,0:T(8,128)(2,1)S(1)} %get-tuple-element.41.first_ref), channel_id=1, source_target_pairs={{0,2},{1,3},{2,0},{3,1},{4,6},{5,7},{6,4},{7,5},{8,10},{9,11},{10,... | collective-permute-start | bytes 405512 | tf_op jit(solution)/shard_map/ppermute | solution.py:27
  9.6 2.4 %collective-permute-start.1 = (bf16[16,4224]{1,0:T(8,128)(2,1)S(1)}, bf16[16,4224]{1,0:T(8,128)(2,1)S(1)}, u32[]{:S(2)}, u32[]{:S(2)}) collective-permute-start(bf16[16,4224]{1,0:T(8,128)(2,1)S(1)} %get-tuple-element.41.first_ref), channel_id=1, source_target_pairs={{0,24},{8,16},{16,8},{24,0},{1,25},{9,17},{17,9},{25,1},{2,26},{10... | collective-permute-start | bytes 405512 | tf_op jit(solution)/shard_map/ppermute | solution.py:27
  12.1 3.2 %shard_map.58 = bf16[16,768,2,128]{3,2,1,0:T(2,128)(2,1)S(1)} custom-call(bf16[768,2,4096]{2,1,0:T(2,128)(2,1)} %bitcast.40), custom_call_target="tpu_custom_call" | custom-call | bytes 12582912 | tf_op jit(solution)/shard_map/pallas_call | solution.py:124
  15.3 0.0 collective-permute-done.2.second_ref
  15.3 0.3 collective-permute-done.1.refs_4_
  15.6 1.6 %collective-permute-start.4 = (bf16[32,4224]{1,0:T(8,128)(2,1)S(1)}, bf16[32,4224]{1,0:T(8,128)(2,1)S(1)}, u32[]{:S(2)}, u32[]{:S(2)}) collective-permute-start(bf16[32,4224]{1,0:T(8,128)(2,1)S(1)} %get-tuple-element.48.refs_1_), channel_id=1, source_target_pairs={{0,16},{8,24},{16,0},{24,8},{1,17},{9,25},{17,1},{25,9},{2,18},{10... | collective-permute-start | bytes 811016 | tf_op jit(solution)/shard_map/ppermute | solution.py:27
  17.2 1.5 %collective-permute-start.3 = (bf16[32,4224]{1,0:T(8,128)(2,1)S(1)}, bf16[32,4224]{1,0:T(8,128)(2,1)S(1)}, u32[]{:S(2)}, u32[]{:S(2)}) collective-permute-start(bf16[32,4224]{1,0:T(8,128)(2,1)S(1)} %get-tuple-element.48.refs_1_), channel_id=1, source_target_pairs={{0,8},{8,0},{16,24},{24,16},{1,9},{9,1},{17,25},{25,17},{2,10},{10... | collective-permute-start | bytes 811016 | tf_op jit(solution)/shard_map/ppermute | solution.py:27
  18.7 1.5 %collective-permute-start.5 = (bf16[16,4224]{1,0:T(8,128)(2,1)S(1)}, bf16[16,4224]{1,0:T(8,128)(2,1)S(1)}, u32[]{:S(2)}, u32[]{:S(2)}) collective-permute-start(bf16[16,4224]{1,0:T(8,128)(2,1)S(1)} %collective-permute-done.1.refs_4_), channel_id=1, source_target_pairs={{0,2},{1,3},{2,0},{3,1},{4,6},{5,7},{6,4},{7,5},{8,10},{9,11},{10,... | collective-permute-start | bytes 405512 | tf_op jit(solution)/shard_map/ppermute | solution.py:27
  20.2 0.0 collective-permute-start.6
  20.2 3.2 %shard_map.60 = bf16[16,768,2,128]{3,2,1,0:T(2,128)(2,1)S(1)} custom-call(bf16[768,2,4096]{2,1,0:T(2,128)(2,1)} %bitcast.41), custom_call_target="tpu_custom_call" | custom-call | bytes 12582912 | tf_op jit(solution)/shard_map/pallas_call | solution.py:124
  23.3 0.3 collective-permute-done.5.refs_5_
  23.7 0.0 collective-permute-done.4.refs_3_
  23.7 0.0 collective-permute-done.3.refs_2_
  23.7 0.3 collective-permute-start.7
  23.9 0.2 collective-permute-start.8
  24.2 0.3 collective-permute-start.9
  24.5 0.2 collective-permute-start.10
  24.7 1.1 %collective-permute-done.9.refs_9_ = bf16[16,4224]{1,0:T(8,128)(2,1)S(1)} collective-permute-done((bf16[16,4224]{1,0:T(8,128)(2,1)S(1)}, bf16[16,4224]{1,0:T(8,128)(2,1)S(1)}, u32[]{:S(2)}, u32[]{:S(2)}) %collective-permute-start.9) | collective-permute-done | bytes 135200 | tf_op jit(solution)/shard_map/ppermute | solution.py:27
  25.8 0.0 collective-permute-done.6.refs_6_
  25.8 0.2 collective-permute-done.10.refs_10_
  26.0 0.0 collective-permute-done.7.refs_7_
  26.0 0.0 collective-permute-done.8.refs_8_
  26.0 5.4 %shard_map.61 = (bf16[1,128,4096]{2,1,0:T(8,128)(2,1)S(1)}, f32[1,128,4096]{2,1,0:T(8,128)S(1)}) custom-call(s32[1]{0:T(128)} %bitcast.refs_0_, bf16[32,4224]{1,0:T(8,128)(2,1)S(1)} %get-tuple-element.48.refs_1_, bf16[32,4224]{1,0:T(8,128)(2,1)S(1)} %collective-permute-done.3.refs_2_, bf16[32,4224]{1,0:T(8,128)(2,1)S(1)} %collective-permute-done.4.refs_3_, ...), custom_call_target="tpu_custom_call" | custom-call | flops 4831838208 | bytes 5308416 | tf_op jit(solution)/shard_map/pallas_call | solution.py:211
  31.4 0.3 collective-permute-start.11
  31.8 2.4 %collective-permute-done.11 = bf16[128,4096]{1,0:T(8,128)(2,1)S(1)} collective-permute-done((bf16[128,4096]{1,0:T(8,128)(2,1)S(1)}, bf16[128,4096]{1,0:T(8,128)(2,1)S(1)}, u32[]{:S(2)}, u32[]{:S(2)}) %collective-permute-start.11) | collective-permute-done | bytes 1048608 | tf_op jit(solution)/shard_map/ppermute | solution.py:27
  34.2 0.2 bitcast_add_fusion
  34.4 1.6 %collective-permute-start.20 = (bf16[16,4096]{1,0:T(8,128)(2,1)S(1)}, bf16[16,4096]{1,0:T(8,128)(2,1)S(1)}, u32[]{:S(2)}, u32[]{:S(2)}) collective-permute-start(bf16[16,4096]{1,0:T(8,128)(2,1)S(1)} %slice.125), channel_id=1, source_target_pairs={{0,2},{1,3},{2,0},{3,1},{4,6},{5,7},{6,4},{7,5},{8,10},{9,11},{10,... | collective-permute-start | bytes 393224 | tf_op jit(solution)/shard_map/ppermute | solution.py:27
  36.0 0.1 convert_element_type.54
  36.2 0.6 %collective-permute-start.13 = (bf16[16,4096]{1,0:T(8,128)(2,1)S(1)}, bf16[16,4096]{1,0:T(8,128)(2,1)S(1)}, u32[]{:S(2)}, u32[]{:S(2)}) collective-permute-start(bf16[16,4096]{1,0:T(8,128)(2,1)S(1)} %get-tuple-element.71), channel_id=1, source_target_pairs={{0,16},{8,24},{16,0},{24,8},{1,17},{9,25},{17,1},{25,9},{2,18},{10... | collective-permute-start | bytes 393224 | tf_op jit(solution)/shard_map/ppermute | solution.py:27
  36.8 1.4 %collective-permute-start.12 = (bf16[16,4096]{1,0:T(8,128)(2,1)S(1)}, bf16[16,4096]{1,0:T(8,128)(2,1)S(1)}, u32[]{:S(2)}, u32[]{:S(2)}) collective-permute-start(bf16[16,4096]{1,0:T(8,128)(2,1)S(1)} %get-tuple-element.72), channel_id=1, source_target_pairs={{0,8},{8,0},{16,24},{24,16},{1,9},{9,1},{17,25},{25,17},{2,10},{10... | collective-permute-start | bytes 393224 | tf_op jit(solution)/shard_map/ppermute | solution.py:27
  38.2 2.0 %collective-permute-done.20 = bf16[16,4096]{1,0:T(8,128)(2,1)S(1)} collective-permute-done((bf16[16,4096]{1,0:T(8,128)(2,1)S(1)}, bf16[16,4096]{1,0:T(8,128)(2,1)S(1)}, u32[]{:S(2)}, u32[]{:S(2)}) %collective-permute-start.20) | collective-permute-done | bytes 131104 | tf_op jit(solution)/shard_map/ppermute | solution.py:27
  40.2 3.2 %collective-permute-start.21 = (bf16[8,4096]{1,0:T(8,128)(2,1)S(1)}, bf16[8,4096]{1,0:T(8,128)(2,1)S(1)}, u32[]{:S(2)}, u32[]{:S(2)}) collective-permute-start(bf16[8,4096]{1,0:T(8,128)(2,1)S(1)} %slice.126), channel_id=1, source_target_pairs={{0,4},{1,5},{2,6},{3,7},{4,0},{5,1},{6,2},{7,3},{8,12},{9,13},{10,... | collective-permute-start | bytes 196616 | tf_op jit(solution)/shard_map/ppermute | solution.py:27
  43.4 0.0 collective-permute-done.13
  43.4 0.0 collective-permute-done.12
  43.4 1.5 %collective-permute-start.15 = (bf16[8,4096]{1,0:T(8,128)(2,1)S(1)}, bf16[8,4096]{1,0:T(8,128)(2,1)S(1)}, u32[]{:S(2)}, u32[]{:S(2)}) collective-permute-start(bf16[8,4096]{1,0:T(8,128)(2,1)S(1)} %get-tuple-element.61), channel_id=1, source_target_pairs={{0,8},{8,0},{16,24},{24,16},{1,9},{9,1},{17,25},{25,17},{2,10},{10... | collective-permute-start | bytes 196616 | tf_op jit(solution)/shard_map/ppermute | solution.py:27
  44.9 0.5 collective-permute-start.16
  45.4 0.8 %collective-permute-start.14 = (bf16[16,4096]{1,0:T(8,128)(2,1)S(1)}, bf16[16,4096]{1,0:T(8,128)(2,1)S(1)}, u32[]{:S(2)}, u32[]{:S(2)}) collective-permute-start(bf16[16,4096]{1,0:T(8,128)(2,1)S(1)} %fusion.2), channel_id=1, source_target_pairs={{0,2},{1,3},{2,0},{3,1},{4,6},{5,7},{6,4},{7,5},{8,10},{9,11},{10,... | collective-permute-start | bytes 393224 | tf_op jit(solution)/shard_map/ppermute | solution.py:27
  46.2 0.0 collective-permute-done.21
  46.2 1.6 %collective-permute-start.22 = (bf16[8,4096]{1,0:T(8,128)(2,1)S(1)}, bf16[8,4096]{1,0:T(8,128)(2,1)S(1)}, u32[]{:S(2)}, u32[]{:S(2)}) collective-permute-start(bf16[8,4096]{1,0:T(8,128)(2,1)S(1)} %fusion.3), channel_id=1, source_target_pairs={{0,24},{8,16},{16,8},{24,0},{1,25},{9,17},{17,9},{25,1},{2,26},{10... | collective-permute-start | bytes 196616 | tf_op jit(solution)/shard_map/ppermute | solution.py:27
  47.7 0.0 collective-permute-done.15
  47.7 2.1 %collective-permute-done.16 = bf16[8,4096]{1,0:T(8,128)(2,1)S(1)} collective-permute-done((bf16[8,4096]{1,0:T(8,128)(2,1)S(1)}, bf16[8,4096]{1,0:T(8,128)(2,1)S(1)}, u32[]{:S(2)}, u32[]{:S(2)}) %collective-permute-start.16) | collective-permute-done | bytes 65568 | tf_op jit(solution)/shard_map/ppermute | solution.py:27
  49.9 0.0 collective-permute-start.18
  49.9 1.5 %collective-permute-start.19 = (bf16[8,4096]{1,0:T(8,128)(2,1)S(1)}, bf16[8,4096]{1,0:T(8,128)(2,1)S(1)}, u32[]{:S(2)}, u32[]{:S(2)}) collective-permute-start(bf16[8,4096]{1,0:T(8,128)(2,1)S(1)} %get-tuple-element.66), channel_id=1, source_target_pairs={{0,16},{8,24},{16,0},{24,8},{1,17},{9,25},{17,1},{25,9},{2,18},{10... | collective-permute-start | bytes 196616 | tf_op jit(solution)/shard_map/ppermute | solution.py:27
  51.4 0.0 collective-permute-done.14
  51.4 1.3 %collective-permute-start.17 = (bf16[8,4096]{1,0:T(8,128)(2,1)S(1)}, bf16[8,4096]{1,0:T(8,128)(2,1)S(1)}, u32[]{:S(2)}, u32[]{:S(2)}) collective-permute-start(bf16[8,4096]{1,0:T(8,128)(2,1)S(1)} %fusion.6), channel_id=1, source_target_pairs={{0,4},{1,5},{2,6},{3,7},{4,0},{5,1},{6,2},{7,3},{8,12},{9,13},{10,... | collective-permute-start | bytes 196616 | tf_op jit(solution)/shard_map/ppermute | solution.py:27
  52.7 0.0 collective-permute-done.22
  52.7 1.4 %collective-permute-done.18 = bf16[8,4096]{1,0:T(8,128)(2,1)S(1)} collective-permute-done((bf16[8,4096]{1,0:T(8,128)(2,1)S(1)}, bf16[8,4096]{1,0:T(8,128)(2,1)S(1)}, u32[]{:S(2)}, u32[]{:S(2)}) %collective-permute-start.18) | collective-permute-done | bytes 65568 | tf_op jit(solution)/shard_map/ppermute | solution.py:27
  54.2 0.0 collective-permute-done.19
  54.2 2.5 %collective-permute-done.17 = bf16[8,4096]{1,0:T(8,128)(2,1)S(1)} collective-permute-done((bf16[8,4096]{1,0:T(8,128)(2,1)S(1)}, bf16[8,4096]{1,0:T(8,128)(2,1)S(1)}, u32[]{:S(2)}, u32[]{:S(2)}) %collective-permute-start.17) | collective-permute-done | bytes 65568 | tf_op jit(solution)/shard_map/ppermute | solution.py:27
  56.7 0.7 %fusion.11 = bf16[8,4096]{1,0:T(8,128)(2,1)} fusion(f32[16,4096]{1,0:T(8,128)S(1)} %convert_element_type.58, f32[4,32,4096]{2,1,0:T(8,128)S(1)} %bitcast.45, bf16[8,4096]{1,0:T(8,128)(2,1)S(1)} %collective-permute-done.22, bf16[8,4096]{1,0:T(8,128)(2,1)S(1)} %collective-permute-done.19, bf16[8,4096]{1,0:T(8,128)(2,1)S(1)} %collective-permute-done.18, ...), kind=kLoop, calls=%fused_computation.20 | loop fusion | flops 327680 | bytes 589824 | tf_op jit(solution)/shard_map/convert_element_type | solution.py:316
  (11 shorter events, 0.2 us)
Async XLA Ops:
  1.0 7.8 %collective-permute-start = (bf16[8,4224]{1,0:T(8,128)(2,1)S(1)}, bf16[8,4224]{1,0:T(8,128)(2,1)S(1)}, u32[]{:S(2)}, u32[]{:S(2)}) collective-permute-start(bf16[8,4224]{1,0:T(8,128)(2,1)S(1)} %shard_map.55.first_ref), channel_id=1, source_target_pairs={{0,4},{1,5},{2,6},{3,7},{4,0},{5,1},{6,2},{7,3},{8,12},{9,13},{10,... | collective-permute-start | bytes 202760 | tf_op jit(solution)/shard_map/ppermute | solution.py:27
  8.8 6.4 %collective-permute-start.2 = (bf16[16,4224]{1,0:T(8,128)(2,1)S(1)}, bf16[16,4224]{1,0:T(8,128)(2,1)S(1)}, u32[]{:S(2)}, u32[]{:S(2)}) collective-permute-start(bf16[16,4224]{1,0:T(8,128)(2,1)S(1)} %get-tuple-element.41.first_ref), channel_id=1, source_target_pairs={{0,2},{1,3},{2,0},{3,1},{4,6},{5,7},{6,4},{7,5},{8,10},{9,11},{10,... | collective-permute-start | bytes 405512 | tf_op jit(solution)/shard_map/ppermute | solution.py:27
  9.6 5.9 %collective-permute-start.1 = (bf16[16,4224]{1,0:T(8,128)(2,1)S(1)}, bf16[16,4224]{1,0:T(8,128)(2,1)S(1)}, u32[]{:S(2)}, u32[]{:S(2)}) collective-permute-start(bf16[16,4224]{1,0:T(8,128)(2,1)S(1)} %get-tuple-element.41.first_ref), channel_id=1, source_target_pairs={{0,24},{8,16},{16,8},{24,0},{1,25},{9,17},{17,9},{25,1},{2,26},{10... | collective-permute-start | bytes 405512 | tf_op jit(solution)/shard_map/ppermute | solution.py:27
  15.6 8.1 %collective-permute-start.4 = (bf16[32,4224]{1,0:T(8,128)(2,1)S(1)}, bf16[32,4224]{1,0:T(8,128)(2,1)S(1)}, u32[]{:S(2)}, u32[]{:S(2)}) collective-permute-start(bf16[32,4224]{1,0:T(8,128)(2,1)S(1)} %get-tuple-element.48.refs_1_), channel_id=1, source_target_pairs={{0,16},{8,24},{16,0},{24,8},{1,17},{9,25},{17,1},{25,9},{2,18},{10... | collective-permute-start | bytes 811016 | tf_op jit(solution)/shard_map/ppermute | solution.py:27
  17.2 6.5 %collective-permute-start.3 = (bf16[32,4224]{1,0:T(8,128)(2,1)S(1)}, bf16[32,4224]{1,0:T(8,128)(2,1)S(1)}, u32[]{:S(2)}, u32[]{:S(2)}) collective-permute-start(bf16[32,4224]{1,0:T(8,128)(2,1)S(1)} %get-tuple-element.48.refs_1_), channel_id=1, source_target_pairs={{0,8},{8,0},{16,24},{24,16},{1,9},{9,1},{17,25},{25,17},{2,10},{10... | collective-permute-start | bytes 811016 | tf_op jit(solution)/shard_map/ppermute | solution.py:27
  18.7 5.0 %collective-permute-start.5 = (bf16[16,4224]{1,0:T(8,128)(2,1)S(1)}, bf16[16,4224]{1,0:T(8,128)(2,1)S(1)}, u32[]{:S(2)}, u32[]{:S(2)}) collective-permute-start(bf16[16,4224]{1,0:T(8,128)(2,1)S(1)} %collective-permute-done.1.refs_4_), channel_id=1, source_target_pairs={{0,2},{1,3},{2,0},{3,1},{4,6},{5,7},{6,4},{7,5},{8,10},{9,11},{10,... | collective-permute-start | bytes 405512 | tf_op jit(solution)/shard_map/ppermute | solution.py:27
  20.2 5.6 %collective-permute-start.6 = (bf16[32,4224]{1,0:T(8,128)(2,1)S(1)}, bf16[32,4224]{1,0:T(8,128)(2,1)S(1)}, u32[]{:S(2)}, u32[]{:S(2)}) collective-permute-start(bf16[32,4224]{1,0:T(8,128)(2,1)S(1)} %get-tuple-element.48.refs_1_), channel_id=1, source_target_pairs={{0,1},{1,0},{2,3},{3,2},{4,5},{5,4},{6,7},{7,6},{8,9},{9,8},{10,11... | collective-permute-start | bytes 811016 | tf_op jit(solution)/shard_map/ppermute | solution.py:27
  23.7 2.3 %collective-permute-start.7 = (bf16[32,4224]{1,0:T(8,128)(2,1)S(1)}, bf16[32,4224]{1,0:T(8,128)(2,1)S(1)}, u32[]{:S(2)}, u32[]{:S(2)}) collective-permute-start(bf16[32,4224]{1,0:T(8,128)(2,1)S(1)} %collective-permute-done.3.refs_2_), channel_id=1, source_target_pairs={{0,1},{1,0},{2,3},{3,2},{4,5},{5,4},{6,7},{7,6},{8,9},{9,8},{10,11... | collective-permute-start | bytes 811016 | tf_op jit(solution)/shard_map/ppermute | solution.py:27
  23.9 2.1 %collective-permute-start.8 = (bf16[32,4224]{1,0:T(8,128)(2,1)S(1)}, bf16[32,4224]{1,0:T(8,128)(2,1)S(1)}, u32[]{:S(2)}, u32[]{:S(2)}) collective-permute-start(bf16[32,4224]{1,0:T(8,128)(2,1)S(1)} %collective-permute-done.4.refs_3_), channel_id=1, source_target_pairs={{0,1},{1,0},{2,3},{3,2},{4,5},{5,4},{6,7},{7,6},{8,9},{9,8},{10,11... | collective-permute-start | bytes 811016 | tf_op jit(solution)/shard_map/ppermute | solution.py:27
  24.2 1.6 %collective-permute-start.9 = (bf16[16,4224]{1,0:T(8,128)(2,1)S(1)}, bf16[16,4224]{1,0:T(8,128)(2,1)S(1)}, u32[]{:S(2)}, u32[]{:S(2)}) collective-permute-start(bf16[16,4224]{1,0:T(8,128)(2,1)S(1)} %collective-permute-done.1.refs_4_), channel_id=1, source_target_pairs={{0,1},{1,0},{2,3},{3,2},{4,5},{5,4},{6,7},{7,6},{8,9},{9,8},{10,11... | collective-permute-start | bytes 405512 | tf_op jit(solution)/shard_map/ppermute | solution.py:27
  24.5 1.5 %collective-permute-start.10 = (bf16[16,4224]{1,0:T(8,128)(2,1)S(1)}, bf16[16,4224]{1,0:T(8,128)(2,1)S(1)}, u32[]{:S(2)}, u32[]{:S(2)}) collective-permute-start(bf16[16,4224]{1,0:T(8,128)(2,1)S(1)} %collective-permute-done.5.refs_5_), channel_id=1, source_target_pairs={{0,1},{1,0},{2,3},{3,2},{4,5},{5,4},{6,7},{7,6},{8,9},{9,8},{10,11... | collective-permute-start | bytes 405512 | tf_op jit(solution)/shard_map/ppermute | solution.py:27
  31.4 2.7 %collective-permute-start.11 = (bf16[128,4096]{1,0:T(8,128)(2,1)S(1)}, bf16[128,4096]{1,0:T(8,128)(2,1)S(1)}, u32[]{:S(2)}, u32[]{:S(2)}) collective-permute-start(bf16[128,4096]{1,0:T(8,128)(2,1)S(1)} %bitcast.39), channel_id=1, source_target_pairs={{0,1},{1,0},{2,3},{3,2},{4,5},{5,4},{6,7},{7,6},{8,9},{9,8},{10,11... | collective-permute-start | bytes 3145736 | tf_op jit(solution)/shard_map/ppermute | solution.py:27
  34.4 5.7 %collective-permute-start.20 = (bf16[16,4096]{1,0:T(8,128)(2,1)S(1)}, bf16[16,4096]{1,0:T(8,128)(2,1)S(1)}, u32[]{:S(2)}, u32[]{:S(2)}) collective-permute-start(bf16[16,4096]{1,0:T(8,128)(2,1)S(1)} %slice.125), channel_id=1, source_target_pairs={{0,2},{1,3},{2,0},{3,1},{4,6},{5,7},{6,4},{7,5},{8,10},{9,11},{10,... | collective-permute-start | bytes 393224 | tf_op jit(solution)/shard_map/ppermute | solution.py:27
  36.2 7.2 %collective-permute-start.13 = (bf16[16,4096]{1,0:T(8,128)(2,1)S(1)}, bf16[16,4096]{1,0:T(8,128)(2,1)S(1)}, u32[]{:S(2)}, u32[]{:S(2)}) collective-permute-start(bf16[16,4096]{1,0:T(8,128)(2,1)S(1)} %get-tuple-element.71), channel_id=1, source_target_pairs={{0,16},{8,24},{16,0},{24,8},{1,17},{9,25},{17,1},{25,9},{2,18},{10... | collective-permute-start | bytes 393224 | tf_op jit(solution)/shard_map/ppermute | solution.py:27
  36.8 6.6 %collective-permute-start.12 = (bf16[16,4096]{1,0:T(8,128)(2,1)S(1)}, bf16[16,4096]{1,0:T(8,128)(2,1)S(1)}, u32[]{:S(2)}, u32[]{:S(2)}) collective-permute-start(bf16[16,4096]{1,0:T(8,128)(2,1)S(1)} %get-tuple-element.72), channel_id=1, source_target_pairs={{0,8},{8,0},{16,24},{24,16},{1,9},{9,1},{17,25},{25,17},{2,10},{10... | collective-permute-start | bytes 393224 | tf_op jit(solution)/shard_map/ppermute | solution.py:27
  40.2 5.9 %collective-permute-start.21 = (bf16[8,4096]{1,0:T(8,128)(2,1)S(1)}, bf16[8,4096]{1,0:T(8,128)(2,1)S(1)}, u32[]{:S(2)}, u32[]{:S(2)}) collective-permute-start(bf16[8,4096]{1,0:T(8,128)(2,1)S(1)} %slice.126), channel_id=1, source_target_pairs={{0,4},{1,5},{2,6},{3,7},{4,0},{5,1},{6,2},{7,3},{8,12},{9,13},{10,... | collective-permute-start | bytes 196616 | tf_op jit(solution)/shard_map/ppermute | solution.py:27
  43.4 4.3 %collective-permute-start.15 = (bf16[8,4096]{1,0:T(8,128)(2,1)S(1)}, bf16[8,4096]{1,0:T(8,128)(2,1)S(1)}, u32[]{:S(2)}, u32[]{:S(2)}) collective-permute-start(bf16[8,4096]{1,0:T(8,128)(2,1)S(1)} %get-tuple-element.61), channel_id=1, source_target_pairs={{0,8},{8,0},{16,24},{24,16},{1,9},{9,1},{17,25},{25,17},{2,10},{10... | collective-permute-start | bytes 196616 | tf_op jit(solution)/shard_map/ppermute | solution.py:27
  44.9 5.0 %collective-permute-start.16 = (bf16[8,4096]{1,0:T(8,128)(2,1)S(1)}, bf16[8,4096]{1,0:T(8,128)(2,1)S(1)}, u32[]{:S(2)}, u32[]{:S(2)}) collective-permute-start(bf16[8,4096]{1,0:T(8,128)(2,1)S(1)} %get-tuple-element.62), channel_id=1, source_target_pairs={{0,16},{8,24},{16,0},{24,8},{1,17},{9,25},{17,1},{25,9},{2,18},{10... | collective-permute-start | bytes 196616 | tf_op jit(solution)/shard_map/ppermute | solution.py:27
  45.4 6.0 %collective-permute-start.14 = (bf16[16,4096]{1,0:T(8,128)(2,1)S(1)}, bf16[16,4096]{1,0:T(8,128)(2,1)S(1)}, u32[]{:S(2)}, u32[]{:S(2)}) collective-permute-start(bf16[16,4096]{1,0:T(8,128)(2,1)S(1)} %fusion.2), channel_id=1, source_target_pairs={{0,2},{1,3},{2,0},{3,1},{4,6},{5,7},{6,4},{7,5},{8,10},{9,11},{10,... | collective-permute-start | bytes 393224 | tf_op jit(solution)/shard_map/ppermute | solution.py:27
  46.2 6.5 %collective-permute-start.22 = (bf16[8,4096]{1,0:T(8,128)(2,1)S(1)}, bf16[8,4096]{1,0:T(8,128)(2,1)S(1)}, u32[]{:S(2)}, u32[]{:S(2)}) collective-permute-start(bf16[8,4096]{1,0:T(8,128)(2,1)S(1)} %fusion.3), channel_id=1, source_target_pairs={{0,24},{8,16},{16,8},{24,0},{1,25},{9,17},{17,9},{25,1},{2,26},{10... | collective-permute-start | bytes 196616 | tf_op jit(solution)/shard_map/ppermute | solution.py:27
  49.9 4.3 %collective-permute-start.18 = (bf16[8,4096]{1,0:T(8,128)(2,1)S(1)}, bf16[8,4096]{1,0:T(8,128)(2,1)S(1)}, u32[]{:S(2)}, u32[]{:S(2)}) collective-permute-start(bf16[8,4096]{1,0:T(8,128)(2,1)S(1)} %get-tuple-element.65), channel_id=1, source_target_pairs={{0,8},{8,0},{16,24},{24,16},{1,9},{9,1},{17,25},{25,17},{2,10},{10... | collective-permute-start | bytes 196616 | tf_op jit(solution)/shard_map/ppermute | solution.py:27
  49.9 4.3 %collective-permute-start.19 = (bf16[8,4096]{1,0:T(8,128)(2,1)S(1)}, bf16[8,4096]{1,0:T(8,128)(2,1)S(1)}, u32[]{:S(2)}, u32[]{:S(2)}) collective-permute-start(bf16[8,4096]{1,0:T(8,128)(2,1)S(1)} %get-tuple-element.66), channel_id=1, source_target_pairs={{0,16},{8,24},{16,0},{24,8},{1,17},{9,25},{17,1},{25,9},{2,18},{10... | collective-permute-start | bytes 196616 | tf_op jit(solution)/shard_map/ppermute | solution.py:27
  51.4 5.2 %collective-permute-start.17 = (bf16[8,4096]{1,0:T(8,128)(2,1)S(1)}, bf16[8,4096]{1,0:T(8,128)(2,1)S(1)}, u32[]{:S(2)}, u32[]{:S(2)}) collective-permute-start(bf16[8,4096]{1,0:T(8,128)(2,1)S(1)} %fusion.6), channel_id=1, source_target_pairs={{0,4},{1,5},{2,6},{3,7},{4,0},{5,1},{6,2},{7,3},{8,12},{9,13},{10,... | collective-permute-start | bytes 196616 | tf_op jit(solution)/shard_map/ppermute | solution.py:27

commit v13 on v11

--- a/solution.py
+++ b/solution.py
@@ -179,13 +179,9 @@
     chunk = min(512, width)
     ahead, piece, _ = keep_refs[0].shape
     pieces = ahead + keep_refs[1].shape[0]
+    by_row = hidden[...].T
     for c in range(0, width, chunk):
-        part = lax.dot_general(
-            hidden[...],
-            wout_ref[:, c : c + chunk],
-            (((0,), (0,)), ((), ())),
-            preferred_element_type=jnp.float32,
-        )
+        part = jnp.dot(by_row, wout_ref[:, c : c + chunk], preferred_element_type=jnp.float32)
         for p in range(2 * pieces):
             targets = keep_refs if p < pieces else send_refs
             q = p % pieces

time: 56.4 us -> 56.4 us (level)
  no operation moved by 1% of the time
where the time goes in v13:
time: 56.4 us; the launch traced here: 56.2 us
  starting transfers between devices  26.4 us (47%)
  Pallas kernels  15.6 us (28%)
  waiting for transfers between devices  12.9 us (23%)
  other arithmetic  1.11 us (2%)
    ppermute x22, starting transfers between devices, swap(): return lax.ppermute(block, axis, [(i, i ^ flips) for i in range(size)])  26.4 us
    ppermute x22, waiting for transfers between devices, swap(): return lax.ppermute(block, axis, [(i, i ^ flips) for i in range(size)])  12.9 us
    pallas_call x3, Pallas kernels, load(): pl.pallas_call(kernel, out_shape=pltpu.VMEM(shape, source.dtype), in_spec...  9.16 us
    pallas_call x1, Pallas kernels, run_experts(): pl.pallas_call(functools.partial(expert_kernel, exp_dev, experts, count),...  5.39 us
  transfers between devices with their start and end apart: 22, of which 11 were waited for; matrix products, arithmetic and copies ran while one was open for 1% of the time, Pallas kernels for 16%

profile of v13, /device:TPU:0, one launch (start us, length us, event | category | flops | bytes accessed | tf_op | source)
XLA Modules:
  0.0 56.2 jit_solution(13651614212786954489)
XLA Ops:
  0.0 1.0 %shard_map.55.first_ref = bf16[8,4224]{1,0:T(8,128)(2,1)S(1)} custom-call(bf16[8,4096]{1,0:T(8,128)(2,1)} %tokens_hbm.1, s32[8,8]{1,0:T(8,128)} %ids_hbm.1, f32[8,8]{1,0:T(8,128)} %weights_hbm.1), custom_call_target="tpu_custom_call" | custom-call | tf_op jit(solution)/shard_map/pallas_call | solution.py:63
  1.0 4.1 %collective-permute-start = (bf16[8,4224]{1,0:T(8,128)(2,1)S(1)}, bf16[8,4224]{1,0:T(8,128)(2,1)S(1)}, u32[]{:S(2)}, u32[]{:S(2)}) collective-permute-start(bf16[8,4224]{1,0:T(8,128)(2,1)S(1)} %shard_map.55.first_ref), channel_id=1, source_target_pairs={{0,4},{1,5},{2,6},{3,7},{4,0},{5,1},{6,2},{7,3},{8,12},{9,13},{10,... | collective-permute-start | bytes 202760 | tf_op jit(solution)/shard_map/ppermute | solution.py:27
  5.1 2.9 %shard_map.56.refs_0_ = bf16[768,4096]{1,0:T(8,128)(2,1)S(1)} custom-call(bf16[768,4096]{1,0:T(8,128)(2,1)} %bitcast.39), custom_call_target="tpu_custom_call" | custom-call | bytes 12582912 | tf_op jit(solution)/shard_map/pallas_call | solution.py:124
  8.0 0.9 %collective-permute-done.second_ref = bf16[8,4224]{1,0:T(8,128)(2,1)S(1)} collective-permute-done((bf16[8,4224]{1,0:T(8,128)(2,1)S(1)}, bf16[8,4224]{1,0:T(8,128)(2,1)S(1)}, u32[]{:S(2)}, u32[]{:S(2)}) %collective-permute-start) | collective-permute-done | bytes 67616 | tf_op jit(solution)/shard_map/ppermute | solution.py:27
  8.8 0.8 %collective-permute-start.2 = (bf16[16,4224]{1,0:T(8,128)(2,1)S(1)}, bf16[16,4224]{1,0:T(8,128)(2,1)S(1)}, u32[]{:S(2)}, u32[]{:S(2)}) collective-permute-start(bf16[16,4224]{1,0:T(8,128)(2,1)S(1)} %get-tuple-element.39.first_ref), channel_id=1, source_target_pairs={{0,2},{1,3},{2,0},{3,1},{4,6},{5,7},{6,4},{7,5},{8,10},{9,11},{10,... | collective-permute-start | bytes 405512 | tf_op jit(solution)/shard_map/ppermute | solution.py:27
  9.6 2.4 %collective-permute-start.1 = (bf16[16,4224]{1,0:T(8,128)(2,1)S(1)}, bf16[16,4224]{1,0:T(8,128)(2,1)S(1)}, u32[]{:S(2)}, u32[]{:S(2)}) collective-permute-start(bf16[16,4224]{1,0:T(8,128)(2,1)S(1)} %get-tuple-element.39.first_ref), channel_id=1, source_target_pairs={{0,24},{8,16},{16,8},{24,0},{1,25},{9,17},{17,9},{25,1},{2,26},{10... | collective-permute-start | bytes 405512 | tf_op jit(solution)/shard_map/ppermute | solution.py:27
  12.1 3.2 %shard_map.58 = bf16[16,768,2,128]{3,2,1,0:T(2,128)(2,1)S(1)} custom-call(bf16[768,2,4096]{2,1,0:T(2,128)(2,1)} %bitcast.37), custom_call_target="tpu_custom_call" | custom-call | bytes 12582912 | tf_op jit(solution)/shard_map/pallas_call | solution.py:124
  15.3 0.0 collective-permute-done.2.second_ref
  15.3 0.3 collective-permute-done.1.refs_1_
  15.6 1.6 %collective-permute-start.4 = (bf16[32,4224]{1,0:T(8,128)(2,1)S(1)}, bf16[32,4224]{1,0:T(8,128)(2,1)S(1)}, u32[]{:S(2)}, u32[]{:S(2)}) collective-permute-start(bf16[32,4224]{1,0:T(8,128)(2,1)S(1)} %get-tuple-element.47.refs_3_), channel_id=1, source_target_pairs={{0,16},{8,24},{16,0},{24,8},{1,17},{9,25},{17,1},{25,9},{2,18},{10... | collective-permute-start | bytes 811016 | tf_op jit(solution)/shard_map/ppermute | solution.py:27
  17.2 1.5 %collective-permute-start.3 = (bf16[32,4224]{1,0:T(8,128)(2,1)S(1)}, bf16[32,4224]{1,0:T(8,128)(2,1)S(1)}, u32[]{:S(2)}, u32[]{:S(2)}) collective-permute-start(bf16[32,4224]{1,0:T(8,128)(2,1)S(1)} %get-tuple-element.47.refs_3_), channel_id=1, source_target_pairs={{0,8},{8,0},{16,24},{24,16},{1,9},{9,1},{17,25},{25,17},{2,10},{10... | collective-permute-start | bytes 811016 | tf_op jit(solution)/shard_map/ppermute | solution.py:27
  18.7 1.5 %collective-permute-start.5 = (bf16[16,4224]{1,0:T(8,128)(2,1)S(1)}, bf16[16,4224]{1,0:T(8,128)(2,1)S(1)}, u32[]{:S(2)}, u32[]{:S(2)}) collective-permute-start(bf16[16,4224]{1,0:T(8,128)(2,1)S(1)} %collective-permute-done.1.refs_1_), channel_id=1, source_target_pairs={{0,2},{1,3},{2,0},{3,1},{4,6},{5,7},{6,4},{7,5},{8,10},{9,11},{10,... | collective-permute-start | bytes 405512 | tf_op jit(solution)/shard_map/ppermute | solution.py:27
  20.2 0.0 collective-permute-start.8
  20.2 3.2 %shard_map.60 = bf16[16,768,2,128]{3,2,1,0:T(2,128)(2,1)S(1)} custom-call(bf16[768,2,4096]{2,1,0:T(2,128)(2,1)} %bitcast.38), custom_call_target="tpu_custom_call" | custom-call | bytes 12582912 | tf_op jit(solution)/shard_map/pallas_call | solution.py:124
  23.3 0.3 collective-permute-done.5.refs_2_
  23.7 0.0 collective-permute-done.4.refs_5_
  23.7 0.0 collective-permute-done.3.refs_4_
  23.7 0.3 collective-permute-start.9
  23.9 0.2 collective-permute-start.10
  24.2 0.3 collective-permute-start.6
  24.5 0.2 collective-permute-start.7
  24.7 1.1 %collective-permute-done.6.refs_6_ = bf16[16,4224]{1,0:T(8,128)(2,1)S(1)} collective-permute-done((bf16[16,4224]{1,0:T(8,128)(2,1)S(1)}, bf16[16,4224]{1,0:T(8,128)(2,1)S(1)}, u32[]{:S(2)}, u32[]{:S(2)}) %collective-permute-start.6) | collective-permute-done | bytes 135200 | tf_op jit(solution)/shard_map/ppermute | solution.py:27
  25.8 0.0 collective-permute-done.8.refs_8_
  25.8 0.2 collective-permute-done.7.refs_7_
  26.0 0.0 collective-permute-done.9.refs_9_
  26.0 0.0 collective-permute-done.10.refs_10_
  26.0 5.4 %shard_map.61 = (bf16[1,32,4096]{2,1,0:T(8,128)(2,1)S(1)}, bf16[3,32,4096]{2,1,0:T(8,128)(2,1)S(1)}, f32[1,32,4096]{2,1,0:T(8,128)S(1)}, f32[3,32,4096]{2,1,0:T(8,128)S(1)}) custom-call(s32[1]{0:T(128)} %bitcast.refs_0_, bf16[16,4224]{1,0:T(8,128)(2,1)S(1)} %collective-permute-done.1.refs_1_, bf16[16,4224]{1,0:T(8,128)(2,1)S(1)} %collective-permute-done.5.refs_2_, ...), custom_call_target="tpu_custom_call" | custom-call | flops 4831838208 | bytes 5308416 | tf_op jit(solution)/shard_map/pallas_call | solution.py:213
  31.4 0.3 collective-permute-start.18
  31.7 0.2 collective-permute-start.11
  32.0 1.0 %collective-permute-done.18 = bf16[1,32,4096]{2,1,0:T(8,128)(2,1)S(1)} collective-permute-done((bf16[1,32,4096]{2,1,0:T(8,128)(2,1)S(1)}, bf16[1,32,4096]{2,1,0:T(8,128)(2,1)S(1)}, u32[]{:S(2)}, u32[]{:S(2)}) %collective-permute-start.18) | collective-permute-done | bytes 262176 | tf_op jit(solution)/shard_map/ppermute | solution.py:27
  33.1 1.6 %collective-permute-start.19 = (bf16[16,4096]{1,0:T(8,128)(2,1)S(1)}, bf16[16,4096]{1,0:T(8,128)(2,1)S(1)}, u32[]{:S(2)}, u32[]{:S(2)}) collective-permute-start(bf16[16,4096]{1,0:T(8,128)(2,1)S(1)} %fusion.7), channel_id=1, source_target_pairs={{0,2},{1,3},{2,0},{3,1},{4,6},{5,7},{6,4},{7,5},{8,10},{9,11},{10,... | collective-permute-start | bytes 393224 | tf_op jit(solution)/shard_map/ppermute | solution.py:27
  34.7 0.0 collective-permute-done.11
  34.7 0.3 fusion.11
  35.0 0.6 %collective-permute-start.13 = (bf16[16,4096]{1,0:T(8,128)(2,1)S(1)}, bf16[16,4096]{1,0:T(8,128)(2,1)S(1)}, u32[]{:S(2)}, u32[]{:S(2)}) collective-permute-start(bf16[16,4096]{1,0:T(8,128)(2,1)S(1)} %get-tuple-element.67), channel_id=1, source_target_pairs={{0,16},{8,24},{16,0},{24,8},{1,17},{9,25},{17,1},{25,9},{2,18},{10... | collective-permute-start | bytes 393224 | tf_op jit(solution)/shard_map/ppermute | solution.py:27
  35.5 1.4 %collective-permute-start.12 = (bf16[16,4096]{1,0:T(8,128)(2,1)S(1)}, bf16[16,4096]{1,0:T(8,128)(2,1)S(1)}, u32[]{:S(2)}, u32[]{:S(2)}) collective-permute-start(bf16[16,4096]{1,0:T(8,128)(2,1)S(1)} %get-tuple-element.68), channel_id=1, source_target_pairs={{0,8},{8,0},{16,24},{24,16},{1,9},{9,1},{17,25},{25,17},{2,10},{10... | collective-permute-start | bytes 393224 | tf_op jit(solution)/shard_map/ppermute | solution.py:27
  37.0 1.8 %collective-permute-done.19 = bf16[16,4096]{1,0:T(8,128)(2,1)S(1)} collective-permute-done((bf16[16,4096]{1,0:T(8,128)(2,1)S(1)}, bf16[16,4096]{1,0:T(8,128)(2,1)S(1)}, u32[]{:S(2)}, u32[]{:S(2)}) %collective-permute-start.19) | collective-permute-done | bytes 131104 | tf_op jit(solution)/shard_map/ppermute | solution.py:27
  38.9 3.2 %collective-permute-start.20 = (bf16[8,4096]{1,0:T(8,128)(2,1)S(1)}, bf16[8,4096]{1,0:T(8,128)(2,1)S(1)}, u32[]{:S(2)}, u32[]{:S(2)}) collective-permute-start(bf16[8,4096]{1,0:T(8,128)(2,1)S(1)} %slice.102), channel_id=1, source_target_pairs={{0,4},{1,5},{2,6},{3,7},{4,0},{5,1},{6,2},{7,3},{8,12},{9,13},{10,... | collective-permute-start | bytes 196616 | tf_op jit(solution)/shard_map/ppermute | solution.py:27
  42.0 0.0 collective-permute-done.13
  42.0 0.0 collective-permute-done.12
  42.1 0.7 %collective-permute-start.16 = (bf16[16,4096]{1,0:T(8,128)(2,1)S(1)}, bf16[16,4096]{1,0:T(8,128)(2,1)S(1)}, u32[]{:S(2)}, u32[]{:S(2)}) collective-permute-start(bf16[16,4096]{1,0:T(8,128)(2,1)S(1)} %fusion.3), channel_id=1, source_target_pairs={{0,2},{1,3},{2,0},{3,1},{4,6},{5,7},{6,4},{7,5},{8,10},{9,11},{10,... | collective-permute-start | bytes 393224 | tf_op jit(solution)/shard_map/ppermute | solution.py:27
  42.8 1.5 %collective-permute-start.14 = (bf16[16,4096]{1,0:T(8,128)(2,1)S(1)}, bf16[16,4096]{1,0:T(8,128)(2,1)S(1)}, u32[]{:S(2)}, u32[]{:S(2)}) collective-permute-start(bf16[16,4096]{1,0:T(8,128)(2,1)S(1)} %get-tuple-element.57), channel_id=1, source_target_pairs={{0,8},{8,0},{16,24},{24,16},{1,9},{9,1},{17,25},{25,17},{2,10},{10... | collective-permute-start | bytes 393224 | tf_op jit(solution)/shard_map/ppermute | solution.py:27
  44.3 0.6 %collective-permute-start.15 = (bf16[16,4096]{1,0:T(8,128)(2,1)S(1)}, bf16[16,4096]{1,0:T(8,128)(2,1)S(1)}, u32[]{:S(2)}, u32[]{:S(2)}) collective-permute-start(bf16[16,4096]{1,0:T(8,128)(2,1)S(1)} %get-tuple-element.58), channel_id=1, source_target_pairs={{0,16},{8,24},{16,0},{24,8},{1,17},{9,25},{17,1},{25,9},{2,18},{10... | collective-permute-start | bytes 393224 | tf_op jit(solution)/shard_map/ppermute | solution.py:27
  44.9 0.0 collective-permute-done.20
  44.9 1.5 %collective-permute-start.21 = (bf16[8,4096]{1,0:T(8,128)(2,1)S(1)}, bf16[8,4096]{1,0:T(8,128)(2,1)S(1)}, u32[]{:S(2)}, u32[]{:S(2)}) collective-permute-start(bf16[8,4096]{1,0:T(8,128)(2,1)S(1)} %fusion.8), channel_id=1, source_target_pairs={{0,24},{8,16},{16,8},{24,0},{1,25},{9,17},{17,9},{25,1},{2,26},{10... | collective-permute-start | bytes 196616 | tf_op jit(solution)/shard_map/ppermute | solution.py:27
  46.4 0.8 %collective-permute-done.16 = bf16[16,4096]{1,0:T(8,128)(2,1)S(1)} collective-permute-done((bf16[16,4096]{1,0:T(8,128)(2,1)S(1)}, bf16[16,4096]{1,0:T(8,128)(2,1)S(1)}, u32[]{:S(2)}, u32[]{:S(2)}) %collective-permute-start.16) | collective-permute-done | bytes 131104 | tf_op jit(solution)/shard_map/ppermute | solution.py:27
  47.1 1.3 %collective-permute-done.14 = bf16[16,4096]{1,0:T(8,128)(2,1)S(1)} collective-permute-done((bf16[16,4096]{1,0:T(8,128)(2,1)S(1)}, bf16[16,4096]{1,0:T(8,128)(2,1)S(1)}, u32[]{:S(2)}, u32[]{:S(2)}) %collective-permute-start.14) | collective-permute-done | bytes 131104 | tf_op jit(solution)/shard_map/ppermute | solution.py:27
  48.4 1.1 %collective-permute-done.15 = bf16[16,4096]{1,0:T(8,128)(2,1)S(1)} collective-permute-done((bf16[16,4096]{1,0:T(8,128)(2,1)S(1)}, bf16[16,4096]{1,0:T(8,128)(2,1)S(1)}, u32[]{:S(2)}, u32[]{:S(2)}) %collective-permute-start.15) | collective-permute-done | bytes 131104 | tf_op jit(solution)/shard_map/ppermute | solution.py:27
  49.5 0.1 fusion.6
  49.6 1.8 %collective-permute-start.17 = (bf16[8,4096]{1,0:T(8,128)(2,1)S(1)}, bf16[8,4096]{1,0:T(8,128)(2,1)S(1)}, u32[]{:S(2)}, u32[]{:S(2)}) collective-permute-start(bf16[8,4096]{1,0:T(8,128)(2,1)S(1)} %slice.103), channel_id=1, source_target_pairs={{0,4},{1,5},{2,6},{3,7},{4,0},{5,1},{6,2},{7,3},{8,12},{9,13},{10,... | collective-permute-start | bytes 196616 | tf_op jit(solution)/shard_map/ppermute | solution.py:27
  51.4 0.0 collective-permute-done.21
  51.4 4.1 %collective-permute-done.17 = bf16[8,4096]{1,0:T(8,128)(2,1)S(1)} collective-permute-done((bf16[8,4096]{1,0:T(8,128)(2,1)S(1)}, bf16[8,4096]{1,0:T(8,128)(2,1)S(1)}, u32[]{:S(2)}, u32[]{:S(2)}) %collective-permute-start.17) | collective-permute-done | bytes 65568 | tf_op jit(solution)/shard_map/ppermute | solution.py:27
  55.5 0.7 %fusion.10 = bf16[8,4096]{1,0:T(8,128)(2,1)} fusion(f32[16,4096]{1,0:T(8,128)S(1)} %fusion.6, bf16[8,4096]{1,0:T(8,128)(2,1)S(1)} %collective-permute-done.21, bf16[8,4096]{1,0:T(8,128)(2,1)S(1)} %collective-permute-done.17), kind=kLoop, calls=%fused_computation.20 | loop fusion | flops 163840 | bytes 327680 | tf_op jit(solution)/shard_map/convert_element_type | solution.py:306
  (10 shorter events, 0.2 us)
Async XLA Ops:
  1.0 7.8 %collective-permute-start = (bf16[8,4224]{1,0:T(8,128)(2,1)S(1)}, bf16[8,4224]{1,0:T(8,128)(2,1)S(1)}, u32[]{:S(2)}, u32[]{:S(2)}) collective-permute-start(bf16[8,4224]{1,0:T(8,128)(2,1)S(1)} %shard_map.55.first_ref), channel_id=1, source_target_pairs={{0,4},{1,5},{2,6},{3,7},{4,0},{5,1},{6,2},{7,3},{8,12},{9,13},{10,... | collective-permute-start | bytes 202760 | tf_op jit(solution)/shard_map/ppermute | solution.py:27
  8.8 6.4 %collective-permute-start.2 = (bf16[16,4224]{1,0:T(8,128)(2,1)S(1)}, bf16[16,4224]{1,0:T(8,128)(2,1)S(1)}, u32[]{:S(2)}, u32[]{:S(2)}) collective-permute-start(bf16[16,4224]{1,0:T(8,128)(2,1)S(1)} %get-tuple-element.39.first_ref), channel_id=1, source_target_pairs={{0,2},{1,3},{2,0},{3,1},{4,6},{5,7},{6,4},{7,5},{8,10},{9,11},{10,... | collective-permute-start | bytes 405512 | tf_op jit(solution)/shard_map/ppermute | solution.py:27
  9.6 5.9 %collective-permute-start.1 = (bf16[16,4224]{1,0:T(8,128)(2,1)S(1)}, bf16[16,4224]{1,0:T(8,128)(2,1)S(1)}, u32[]{:S(2)}, u32[]{:S(2)}) collective-permute-start(bf16[16,4224]{1,0:T(8,128)(2,1)S(1)} %get-tuple-element.39.first_ref), channel_id=1, source_target_pairs={{0,24},{8,16},{16,8},{24,0},{1,25},{9,17},{17,9},{25,1},{2,26},{10... | collective-permute-start | bytes 405512 | tf_op jit(solution)/shard_map/ppermute | solution.py:27
  15.6 8.1 %collective-permute-start.4 = (bf16[32,4224]{1,0:T(8,128)(2,1)S(1)}, bf16[32,4224]{1,0:T(8,128)(2,1)S(1)}, u32[]{:S(2)}, u32[]{:S(2)}) collective-permute-start(bf16[32,4224]{1,0:T(8,128)(2,1)S(1)} %get-tuple-element.47.refs_3_), channel_id=1, source_target_pairs={{0,16},{8,24},{16,0},{24,8},{1,17},{9,25},{17,1},{25,9},{2,18},{10... | collective-permute-start | bytes 811016 | tf_op jit(solution)/shard_map/ppermute | solution.py:27
  17.2 6.5 %collective-permute-start.3 = (bf16[32,4224]{1,0:T(8,128)(2,1)S(1)}, bf16[32,4224]{1,0:T(8,128)(2,1)S(1)}, u32[]{:S(2)}, u32[]{:S(2)}) collective-permute-start(bf16[32,4224]{1,0:T(8,128)(2,1)S(1)} %get-tuple-element.47.refs_3_), channel_id=1, source_target_pairs={{0,8},{8,0},{16,24},{24,16},{1,9},{9,1},{17,25},{25,17},{2,10},{10... | collective-permute-start | bytes 811016 | tf_op jit(solution)/shard_map/ppermute | solution.py:27
  18.7 5.0 %collective-permute-start.5 = (bf16[16,4224]{1,0:T(8,128)(2,1)S(1)}, bf16[16,4224]{1,0:T(8,128)(2,1)S(1)}, u32[]{:S(2)}, u32[]{:S(2)}) collective-permute-start(bf16[16,4224]{1,0:T(8,128)(2,1)S(1)} %collective-permute-done.1.refs_1_), channel_id=1, source_target_pairs={{0,2},{1,3},{2,0},{3,1},{4,6},{5,7},{6,4},{7,5},{8,10},{9,11},{10,... | collective-permute-start | bytes 405512 | tf_op jit(solution)/shard_map/ppermute | solution.py:27
  20.2 5.6 %collective-permute-start.8 = (bf16[32,4224]{1,0:T(8,128)(2,1)S(1)}, bf16[32,4224]{1,0:T(8,128)(2,1)S(1)}, u32[]{:S(2)}, u32[]{:S(2)}) collective-permute-start(bf16[32,4224]{1,0:T(8,128)(2,1)S(1)} %get-tuple-element.47.refs_3_), channel_id=1, source_target_pairs={{0,1},{1,0},{2,3},{3,2},{4,5},{5,4},{6,7},{7,6},{8,9},{9,8},{10,11... | collective-permute-start | bytes 811016 | tf_op jit(solution)/shard_map/ppermute | solution.py:27
  23.7 2.3 %collective-permute-start.9 = (bf16[32,4224]{1,0:T(8,128)(2,1)S(1)}, bf16[32,4224]{1,0:T(8,128)(2,1)S(1)}, u32[]{:S(2)}, u32[]{:S(2)}) collective-permute-start(bf16[32,4224]{1,0:T(8,128)(2,1)S(1)} %collective-permute-done.3.refs_4_), channel_id=1, source_target_pairs={{0,1},{1,0},{2,3},{3,2},{4,5},{5,4},{6,7},{7,6},{8,9},{9,8},{10,11... | collective-permute-start | bytes 811016 | tf_op jit(solution)/shard_map/ppermute | solution.py:27
  23.9 2.1 %collective-permute-start.10 = (bf16[32,4224]{1,0:T(8,128)(2,1)S(1)}, bf16[32,4224]{1,0:T(8,128)(2,1)S(1)}, u32[]{:S(2)}, u32[]{:S(2)}) collective-permute-start(bf16[32,4224]{1,0:T(8,128)(2,1)S(1)} %collective-permute-done.4.refs_5_), channel_id=1, source_target_pairs={{0,1},{1,0},{2,3},{3,2},{4,5},{5,4},{6,7},{7,6},{8,9},{9,8},{10,11... | collective-permute-start | bytes 811016 | tf_op jit(solution)/shard_map/ppermute | solution.py:27
  24.2 1.6 %collective-permute-start.6 = (bf16[16,4224]{1,0:T(8,128)(2,1)S(1)}, bf16[16,4224]{1,0:T(8,128)(2,1)S(1)}, u32[]{:S(2)}, u32[]{:S(2)}) collective-permute-start(bf16[16,4224]{1,0:T(8,128)(2,1)S(1)} %collective-permute-done.1.refs_1_), channel_id=1, source_target_pairs={{0,1},{1,0},{2,3},{3,2},{4,5},{5,4},{6,7},{7,6},{8,9},{9,8},{10,11... | collective-permute-start | bytes 405512 | tf_op jit(solution)/shard_map/ppermute | solution.py:27
  24.5 1.5 %collective-permute-start.7 = (bf16[16,4224]{1,0:T(8,128)(2,1)S(1)}, bf16[16,4224]{1,0:T(8,128)(2,1)S(1)}, u32[]{:S(2)}, u32[]{:S(2)}) collective-permute-start(bf16[16,4224]{1,0:T(8,128)(2,1)S(1)} %collective-permute-done.5.refs_2_), channel_id=1, source_target_pairs={{0,1},{1,0},{2,3},{3,2},{4,5},{5,4},{6,7},{7,6},{8,9},{9,8},{10,11... | collective-permute-start | bytes 405512 | tf_op jit(solution)/shard_map/ppermute | solution.py:27
  31.4 1.6 %collective-permute-start.18 = (bf16[1,32,4096]{2,1,0:T(8,128)(2,1)S(1)}, bf16[1,32,4096]{2,1,0:T(8,128)(2,1)S(1)}, u32[]{:S(2)}, u32[]{:S(2)}) collective-permute-start(bf16[1,32,4096]{2,1,0:T(8,128)(2,1)S(1)} %get-tuple-element.62), channel_id=1, source_target_pairs={{0,1},{1,0},{2,3},{3,2},{4,5},{5,4},{6,7},{7,6},{8,9},{9,8},{10,11... | collective-permute-start | bytes 786440 | tf_op jit(solution)/shard_map/ppermute | solution.py:27
  31.7 2.9 %collective-permute-start.11 = (bf16[3,32,4096]{2,1,0:T(8,128)(2,1)S(1)}, bf16[3,32,4096]{2,1,0:T(8,128)(2,1)S(1)}, u32[]{:S(2)}, u32[]{:S(2)}) collective-permute-start(bf16[3,32,4096]{2,1,0:T(8,128)(2,1)S(1)} %get-tuple-element.56), channel_id=1, source_target_pairs={{0,1},{1,0},{2,3},{3,2},{4,5},{5,4},{6,7},{7,6},{8,9},{9,8},{10,11... | collective-permute-start | bytes 2359304 | tf_op jit(solution)/shard_map/ppermute | solution.py:27
  33.1 5.7 %collective-permute-start.19 = (bf16[16,4096]{1,0:T(8,128)(2,1)S(1)}, bf16[16,4096]{1,0:T(8,128)(2,1)S(1)}, u32[]{:S(2)}, u32[]{:S(2)}) collective-permute-start(bf16[16,4096]{1,0:T(8,128)(2,1)S(1)} %fusion.7), channel_id=1, source_target_pairs={{0,2},{1,3},{2,0},{3,1},{4,6},{5,7},{6,4},{7,5},{8,10},{9,11},{10,... | collective-permute-start | bytes 393224 | tf_op jit(solution)/shard_map/ppermute | solution.py:27
  35.0 7.1 %collective-permute-start.13 = (bf16[16,4096]{1,0:T(8,128)(2,1)S(1)}, bf16[16,4096]{1,0:T(8,128)(2,1)S(1)}, u32[]{:S(2)}, u32[]{:S(2)}) collective-permute-start(bf16[16,4096]{1,0:T(8,128)(2,1)S(1)} %get-tuple-element.67), channel_id=1, source_target_pairs={{0,16},{8,24},{16,0},{24,8},{1,17},{9,25},{17,1},{25,9},{2,18},{10... | collective-permute-start | bytes 393224 | tf_op jit(solution)/shard_map/ppermute | solution.py:27
  35.5 6.5 %collective-permute-start.12 = (bf16[16,4096]{1,0:T(8,128)(2,1)S(1)}, bf16[16,4096]{1,0:T(8,128)(2,1)S(1)}, u32[]{:S(2)}, u32[]{:S(2)}) collective-permute-start(bf16[16,4096]{1,0:T(8,128)(2,1)S(1)} %get-tuple-element.68), channel_id=1, source_target_pairs={{0,8},{8,0},{16,24},{24,16},{1,9},{9,1},{17,25},{25,17},{2,10},{10... | collective-permute-start | bytes 393224 | tf_op jit(solution)/shard_map/ppermute | solution.py:27
  38.9 6.0 %collective-permute-start.20 = (bf16[8,4096]{1,0:T(8,128)(2,1)S(1)}, bf16[8,4096]{1,0:T(8,128)(2,1)S(1)}, u32[]{:S(2)}, u32[]{:S(2)}) collective-permute-start(bf16[8,4096]{1,0:T(8,128)(2,1)S(1)} %slice.102), channel_id=1, source_target_pairs={{0,4},{1,5},{2,6},{3,7},{4,0},{5,1},{6,2},{7,3},{8,12},{9,13},{10,... | collective-permute-start | bytes 196616 | tf_op jit(solution)/shard_map/ppermute | solution.py:27
  42.1 5.0 %collective-permute-start.16 = (bf16[16,4096]{1,0:T(8,128)(2,1)S(1)}, bf16[16,4096]{1,0:T(8,128)(2,1)S(1)}, u32[]{:S(2)}, u32[]{:S(2)}) collective-permute-start(bf16[16,4096]{1,0:T(8,128)(2,1)S(1)} %fusion.3), channel_id=1, source_target_pairs={{0,2},{1,3},{2,0},{3,1},{4,6},{5,7},{6,4},{7,5},{8,10},{9,11},{10,... | collective-permute-start | bytes 393224 | tf_op jit(solution)/shard_map/ppermute | solution.py:27
  42.8 5.7 %collective-permute-start.14 = (bf16[16,4096]{1,0:T(8,128)(2,1)S(1)}, bf16[16,4096]{1,0:T(8,128)(2,1)S(1)}, u32[]{:S(2)}, u32[]{:S(2)}) collective-permute-start(bf16[16,4096]{1,0:T(8,128)(2,1)S(1)} %get-tuple-element.57), channel_id=1, source_target_pairs={{0,8},{8,0},{16,24},{24,16},{1,9},{9,1},{17,25},{25,17},{2,10},{10... | collective-permute-start | bytes 393224 | tf_op jit(solution)/shard_map/ppermute | solution.py:27
  44.3 5.2 %collective-permute-start.15 = (bf16[16,4096]{1,0:T(8,128)(2,1)S(1)}, bf16[16,4096]{1,0:T(8,128)(2,1)S(1)}, u32[]{:S(2)}, u32[]{:S(2)}) collective-permute-start(bf16[16,4096]{1,0:T(8,128)(2,1)S(1)} %get-tuple-element.58), channel_id=1, source_target_pairs={{0,16},{8,24},{16,0},{24,8},{1,17},{9,25},{17,1},{25,9},{2,18},{10... | collective-permute-start | bytes 393224 | tf_op jit(solution)/shard_map/ppermute | solution.py:27
  44.9 6.5 %collective-permute-start.21 = (bf16[8,4096]{1,0:T(8,128)(2,1)S(1)}, bf16[8,4096]{1,0:T(8,128)(2,1)S(1)}, u32[]{:S(2)}, u32[]{:S(2)}) collective-permute-start(bf16[8,4096]{1,0:T(8,128)(2,1)S(1)} %fusion.8), channel_id=1, source_target_pairs={{0,24},{8,16},{16,8},{24,0},{1,25},{9,17},{17,9},{25,1},{2,26},{10... | collective-permute-start | bytes 196616 | tf_op jit(solution)/shard_map/ppermute | solution.py:27
  49.6 5.9 %collective-permute-start.17 = (bf16[8,4096]{1,0:T(8,128)(2,1)S(1)}, bf16[8,4096]{1,0:T(8,128)(2,1)S(1)}, u32[]{:S(2)}, u32[]{:S(2)}) collective-permute-start(bf16[8,4096]{1,0:T(8,128)(2,1)S(1)} %slice.103), channel_id=1, source_target_pairs={{0,4},{1,5},{2,6},{3,7},{4,0},{5,1},{6,2},{7,3},{8,12},{9,13},{10,... | collective-permute-start | bytes 196616 | tf_op jit(solution)/shard_map/ppermute | solution.py:27
